TPU v7x, 32 devices: a whole 2x2x4 slice. The times are simulated.
32 devices in a mesh: groups: 2 (over y), frame: 16 (over z, x, core).
Axes of the slice: x: 2, y: 2, z: 4, core: 2. Of those that a mesh axis runs over, the one named last changes fastest.
Arguments:
- queries: bfloat16 [8192, 1536], P(('groups', 'frame')), parts along dimension 0, may hold values from -14 to 14
- key_heads: bfloat16 [8192, 1536], P(('groups', 'frame')), parts along dimension 0, may hold values from -14 to 14
- value_heads: bfloat16 [8192, 1536], P(('groups', 'frame')), parts along dimension 0, may hold values from -6 to 6
- tile_lists: int32 [16, 8], P('frame'), may hold values from 0 to 1
Outputs:
- attended: bfloat16 [8192, 1536], P(('groups', 'frame')), parts along dimension 0
There are 2 independent parts, one for each index of `groups`. A program takes and returns all parts, laid end to end along the dimension named above; an argument that names none is the same for every part. Nothing has to cross between parts.
Inputs may be any that keep to these rules, and one draw needn't show every extreme that they name: `tile_lists`: entry l of a frame's row names a block of the frame 2^l before it, entry 4 + l one of the frame 2^l after it; entries for frames outside the video are not read.
All inputs are finite; a program needn't handle non-finite values.
Results may differ from a plain program's by a relative error of at most 0.0049.
Values may be sent and summed in bfloat16 or wider, within the bound.
No kernel may reach another device: no remote copies, remote signals or barrier semaphores. Data moves between devices by JAX's collectives and lax.ppermute only.
A program may use at most 64 MiB of HBM per device.

v0:
```python
import math

import jax
import jax.numpy as jnp
from jax import lax
from jax.sharding import PartitionSpec as P

HEADS = 12
HD = 128
TILE = 128


def from_behind(block, axis, distance):
    devices = range(lax.axis_size(axis))
    route = [(i - distance, i) for i in devices if i - distance in devices]
    return lax.ppermute(block, axis, route)


def attend_block(block_queries, block_keys, block_values, usable):
    scale = 1.0 / math.sqrt(HD)

    def one_head(head):
        offset = head * HD
        head_queries = lax.dynamic_slice_in_dim(block_queries, offset, HD, 1)
        head_keys = lax.dynamic_slice_in_dim(block_keys, offset, HD, 1)
        head_values = lax.dynamic_slice_in_dim(block_values, offset, HD, 1)
        scores = (
            lax.dot_general(
                head_queries,
                head_keys,
                (((1,), (1,)), ((), ())),
                preferred_element_type=jnp.float32,
            )
            * scale
        )
        scores = jnp.where(usable[None, :], scores, -jnp.inf)
        peak = jnp.max(scores, axis=1, keepdims=True)
        raised = jnp.exp(scores - peak)
        weights = (raised / jnp.sum(raised, axis=1, keepdims=True)).astype(jnp.bfloat16)
        return jnp.dot(weights, head_values, preferred_element_type=jnp.float32).astype(
            jnp.bfloat16
        )

    per_head = lax.map(one_head, jnp.arange(HEADS, dtype=jnp.int32))
    return jnp.transpose(per_head, (1, 0, 2)).reshape(block_queries.shape[0], HEADS * HD)


def select_tile(tiled, wanted):
    return lax.dynamic_index_in_dim(tiled, wanted, 0, keepdims=False)


def send_upward(outgoing, distance):
    return from_behind(outgoing, "frame", distance)


def send_downward(outgoing, distance):
    return from_behind(outgoing, "frame", -distance)


def body(queries, key_heads, value_heads, tile_lists):
    cycle_size = lax.axis_size("frame")
    levels = cycle_size.bit_length() - 1
    own_index = lax.axis_index("frame")
    width = key_heads.shape[1]
    tile_count = key_heads.shape[0] // TILE
    key_tiles = key_heads.reshape(tile_count, TILE, width)
    value_tiles = value_heads.reshape(tile_count, TILE, width)
    lower_parts = []
    upper_parts = []
    lower_usable = []
    upper_usable = []
    for level in range(levels):
        distance = 1 << level
        below_wants = from_behind(tile_lists[:, level : level + 1], "frame", -distance)[0, 0]
        above_wants = from_behind(
            tile_lists[:, levels + level : levels + level + 1], "frame", distance
        )[0, 0]
        outgoing_up = jnp.stack(
            [select_tile(key_tiles, below_wants), select_tile(value_tiles, below_wants)]
        )
        from_lower = send_upward(outgoing_up, distance)
        outgoing_down = jnp.stack(
            [select_tile(key_tiles, above_wants), select_tile(value_tiles, above_wants)]
        )
        from_upper = send_downward(outgoing_down, distance)
        lower_parts.append(from_lower)
        upper_parts.append(from_upper)
        lower_usable.append(jnp.broadcast_to(own_index - distance >= 0, (TILE,)))
        upper_usable.append(jnp.broadcast_to(own_index + distance < cycle_size, (TILE,)))
    arrived = lower_parts + upper_parts
    key_all = jnp.concatenate([key_heads] + [piece[0] for piece in arrived], axis=0)
    value_all = jnp.concatenate([value_heads] + [piece[1] for piece in arrived], axis=0)
    usable = jnp.concatenate(
        [jnp.ones((key_heads.shape[0],), dtype=bool)] + lower_usable + upper_usable, axis=0
    )
    return attend_block(queries, key_all, value_all, usable)


def solution(mesh):
    in_specs = (
        P(("groups", "frame"), None),
        P(("groups", "frame"), None),
        P(("groups", "frame"), None),
        P("frame", None),
    )
    out_specs = P(("groups", "frame"), None)
    return jax.shard_map(body, mesh=mesh, in_specs=in_specs, out_specs=out_specs, check_vma=False)
```

profile of v0, /device:TPU:3, one launch (start us, length us, event | category | flops | bytes accessed | tf_op | source)
XLA Modules:
  0.0 207.4 jit_solution(14479701534994291148)
XLA Ops:
  0.0 1.6 fusion.25
  1.6 2.6 %collective-permute-start = (s32[1,1]{1,0:T(1,128)}, s32[1,1]{1,0:T(1,128)}, u32[]{:S(2)}, u32[]{:S(2)}) collective-permute-start(s32[1,1]{1,0:T(1,128)} %get-tuple-element.97), channel_id=1, source_target_pairs={{1,0},{2,1},{3,2},{4,3},{5,4},{6,5},{7,6},{8,7},{9,8},{10,9},{11,1... | collective-permute-start | bytes 20 | tf_op jit(solution)/shard_map/ppermute | solution.py:16
  4.2 1.9 collective-permute-start.2
  8.7 5.1 %collective-permute-start.8 = (s32[1,1]{1,0:T(1,128)}, s32[1,1]{1,0:T(1,128)}, u32[]{:S(2)}, u32[]{:S(2)}) collective-permute-start(s32[1,1]{1,0:T(1,128)} %get-tuple-element.93), channel_id=1, source_target_pairs={{0,1},{1,2},{2,3},{3,4},{4,5},{5,6},{6,7},{7,8},{8,9},{9,10},{10,1... | collective-permute-start | bytes 20 | tf_op jit(solution)/shard_map/ppermute | solution.py:16
  13.9 2.6 %constant_dynamic-update-slice_fusion.1 = (bf16[1280,1536]{1,0:T(8,128)(2,1)}, bf16[1280,1536]{1,0:T(8,128)(2,1)}) fusion(bf16[256,1536]{1,0:T(8,128)(2,1)} %param.7, bf16[256,1536]{1,0:T(8,128)(2,1)} %param.8), kind=kLoop, calls=%fused_computation.53 | loop fusion | bytes 3145728
  18.6 3.1 %collective-permute-start.10 = (s32[1,1]{1,0:T(1,128)}, s32[1,1]{1,0:T(1,128)}, u32[]{:S(2)}, u32[]{:S(2)}) collective-permute-start(s32[1,1]{1,0:T(1,128)} %get-tuple-element.92), channel_id=1, source_target_pairs={{0,2},{1,3},{2,4},{3,5},{4,6},{5,7},{6,8},{7,9},{8,10},{9,11},{10,... | collective-permute-start | bytes 20 | tf_op jit(solution)/shard_map/ppermute | solution.py:16
  23.0 4.7 %collective-permute-start.12 = (s32[1,1]{1,0:T(1,128)}, s32[1,1]{1,0:T(1,128)}, u32[]{:S(2)}, u32[]{:S(2)}) collective-permute-start(s32[1,1]{1,0:T(1,128)} %get-tuple-element.98), channel_id=1, source_target_pairs={{0,4},{1,5},{2,6},{3,7},{4,8},{5,9},{6,10},{7,11},{8,12},{9,13},{1... | collective-permute-start | bytes 20 | tf_op jit(solution)/shard_map/ppermute | solution.py:16
  28.8 3.3 %collective-permute-start.14 = (s32[1,1]{1,0:T(1,128)}, s32[1,1]{1,0:T(1,128)}, u32[]{:S(2)}, u32[]{:S(2)}) collective-permute-start(s32[1,1]{1,0:T(1,128)} %get-tuple-element.91), channel_id=1, source_target_pairs={{0,8},{1,9},{2,10},{3,11},{4,12},{5,13},{6,14},{7,15},{16,24},{17,... | collective-permute-start | bytes 20 | tf_op jit(solution)/shard_map/ppermute | solution.py:16
  45.4 1.9 collective-permute-start.1
  47.4 2.1 %collective-permute-start.3 = (bf16[2,128,1536]{2,1,0:T(8,128)(2,1)S(1)}, bf16[2,128,1536]{2,1,0:T(8,128)(2,1)S(1)}, u32[]{:S(2)}, u32[]{:S(2)}) collective-permute-start(bf16[2,128,1536]{2,1,0:T(8,128)(2,1)S(1)} %pad_maximum_fusion.1), channel_id=1, source_target_pairs={{0,2},{1,3},{2,4},{3,5},{4,6},{5,7},{6,8},{7,9},{8,10},{9,11},{10,... | collective-permute-start | bytes 2359304 | tf_op jit(solution)/shard_map/ppermute | solution.py:16
  49.6 1.5 collective-permute-start.5
  52.6 2.6 %collective-permute-start.9 = (bf16[2,128,1536]{2,1,0:T(8,128)(2,1)S(1)}, bf16[2,128,1536]{2,1,0:T(8,128)(2,1)S(1)}, u32[]{:S(2)}, u32[]{:S(2)}) collective-permute-start(bf16[2,128,1536]{2,1,0:T(8,128)(2,1)S(1)} %pad_maximum_fusion.4), channel_id=1, source_target_pairs={{1,0},{2,1},{3,2},{4,3},{5,4},{6,5},{7,6},{8,7},{9,8},{10,9},{11,1... | collective-permute-start | bytes 2359304 | tf_op jit(solution)/shard_map/ppermute | solution.py:16
  55.5 6.5 %collective-permute-done.1 = bf16[2,128,1536]{2,1,0:T(8,128)(2,1)S(1)} collective-permute-done((bf16[2,128,1536]{2,1,0:T(8,128)(2,1)S(1)}, bf16[2,128,1536]{2,1,0:T(8,128)(2,1)S(1)}, u32[]{:S(2)}, u32[]{:S(2)}) %collective-permute-start.1) | collective-permute-done | bytes 786464 | tf_op jit(solution)/shard_map/ppermute | solution.py:16
  61.9 10.3 %collective-permute-start.11 = (bf16[2,128,1536]{2,1,0:T(8,128)(2,1)S(1)}, bf16[2,128,1536]{2,1,0:T(8,128)(2,1)S(1)}, u32[]{:S(2)}, u32[]{:S(2)}) collective-permute-start(bf16[2,128,1536]{2,1,0:T(8,128)(2,1)S(1)} %pad_maximum_fusion.5), channel_id=1, source_target_pairs={{2,0},{3,1},{4,2},{5,3},{6,4},{7,5},{8,6},{9,7},{10,8},{11,9},{12,... | collective-permute-start | bytes 2359304 | tf_op jit(solution)/shard_map/ppermute | solution.py:16
  73.1 26.5 %collective-permute-done.3 = bf16[2,128,1536]{2,1,0:T(8,128)(2,1)S(1)} collective-permute-done((bf16[2,128,1536]{2,1,0:T(8,128)(2,1)S(1)}, bf16[2,128,1536]{2,1,0:T(8,128)(2,1)S(1)}, u32[]{:S(2)}, u32[]{:S(2)}) %collective-permute-start.3) | collective-permute-done | bytes 786464 | tf_op jit(solution)/shard_map/ppermute | solution.py:16
  104.1 2.8 %collective-permute-done.7 = bf16[2,128,1536]{2,1,0:T(8,128)(2,1)S(1)} collective-permute-done((bf16[2,128,1536]{2,1,0:T(8,128)(2,1)S(1)}, bf16[2,128,1536]{2,1,0:T(8,128)(2,1)S(1)}, u32[]{:S(2)}, u32[]{:S(2)}) %collective-permute-start.7) | collective-permute-done | bytes 786464 | tf_op jit(solution)/shard_map/ppermute | solution.py:16
  109.6 9.0 %collective-permute-done.13 = bf16[2,128,1536]{2,1,0:T(8,128)(2,1)S(1)} collective-permute-done((bf16[2,128,1536]{2,1,0:T(8,128)(2,1)S(1)}, bf16[2,128,1536]{2,1,0:T(8,128)(2,1)S(1)}, u32[]{:S(2)}, u32[]{:S(2)}) %collective-permute-start.13) | collective-permute-done | bytes 786464 | tf_op jit(solution)/shard_map/ppermute | solution.py:16
  119.5 30.7 %collective-permute-done.15 = bf16[2,128,1536]{2,1,0:T(8,128)(2,1)S(1)} collective-permute-done((bf16[2,128,1536]{2,1,0:T(8,128)(2,1)S(1)}, bf16[2,128,1536]{2,1,0:T(8,128)(2,1)S(1)}, u32[]{:S(2)}, u32[]{:S(2)}) %collective-permute-start.15) | collective-permute-done | bytes 786464 | tf_op jit(solution)/shard_map/ppermute | solution.py:16
  151.1 55.1 %while.10 = (s32[]{:T(128)}, bf16[12,256,128]{1,2,0:T(8,128)(2,1)S(1)}, pred[1280]{0:T(1024)(128)(4,1)S(1)}, s32[12]{0:T(128)S(1)}, bf16[256,1536]{1,0:T(8,128)(...) while((s32[]{:T(128)}, ...), condition=%wide.region_3.4_spmd, body=%wide.region_0.3_spmd.sunk | while | flops 170425856 | bytes 4988335 | solution.py:44
  152.4 1.4 fusion.31
  157.0 1.4 fusion.31
  161.6 1.4 fusion.31
  166.2 1.4 fusion.31
  170.8 1.4 fusion.31
  175.4 1.4 fusion.31
  180.0 1.4 fusion.31
  184.5 1.4 fusion.31
  189.1 1.4 fusion.31
  190.9 1.4 fusion.33
  193.7 1.4 fusion.31
  198.3 1.4 fusion.31
  202.9 1.4 fusion.31
  (118 shorter events, 47.3 us)
Async XLA Ops:
  0.0 44.4 %copy-start = (bf16[256,1536]{1,0:T(8,128)(2,1)S(1)}, bf16[256,1536]{1,0:T(8,128)(2,1)}, u32[]{:S(2)}) copy-start(bf16[256,1536]{1,0:T(8,128)(2,1)} %param.7) | copy-start | bytes 2359300
  0.0 44.4 %copy-start.1 = (bf16[256,1536]{1,0:T(8,128)(2,1)S(1)}, bf16[256,1536]{1,0:T(8,128)(2,1)}, u32[]{:S(2)}) copy-start(bf16[256,1536]{1,0:T(8,128)(2,1)} %param.8) | copy-start | bytes 2359300
  1.6 17.0 %collective-permute-start = (s32[1,1]{1,0:T(1,128)}, s32[1,1]{1,0:T(1,128)}, u32[]{:S(2)}, u32[]{:S(2)}) collective-permute-start(s32[1,1]{1,0:T(1,128)} %get-tuple-element.97), channel_id=1, source_target_pairs={{1,0},{2,1},{3,2},{4,3},{5,4},{6,5},{7,6},{8,7},{9,8},{10,9},{11,1... | collective-permute-start | bytes 20 | tf_op jit(solution)/shard_map/ppermute | solution.py:16
  4.2 18.7 %collective-permute-start.2 = (s32[1,1]{1,0:T(1,128)}, s32[1,1]{1,0:T(1,128)}, u32[]{:S(2)}, u32[]{:S(2)}) collective-permute-start(s32[1,1]{1,0:T(1,128)} %get-tuple-element.96), channel_id=1, source_target_pairs={{2,0},{3,1},{4,2},{5,3},{6,4},{7,5},{8,6},{9,7},{10,8},{11,9},{12,... | collective-permute-start | bytes 20 | tf_op jit(solution)/shard_map/ppermute | solution.py:16
  6.1 22.7 %collective-permute-start.4 = (s32[1,1]{1,0:T(1,128)}, s32[1,1]{1,0:T(1,128)}, u32[]{:S(2)}, u32[]{:S(2)}) collective-permute-start(s32[1,1]{1,0:T(1,128)} %get-tuple-element.95), channel_id=1, source_target_pairs={{4,0},{5,1},{6,2},{7,3},{8,4},{9,5},{10,6},{11,7},{12,8},{13,9},{1... | collective-permute-start | bytes 20 | tf_op jit(solution)/shard_map/ppermute | solution.py:16
  7.4 26.0 %collective-permute-start.6 = (s32[1,1]{1,0:T(1,128)}, s32[1,1]{1,0:T(1,128)}, u32[]{:S(2)}, u32[]{:S(2)}) collective-permute-start(s32[1,1]{1,0:T(1,128)} %get-tuple-element.94), channel_id=1, source_target_pairs={{8,0},{9,1},{10,2},{11,3},{12,4},{13,5},{14,6},{15,7},{24,16},{25,... | collective-permute-start | bytes 20 | tf_op jit(solution)/shard_map/ppermute | solution.py:16
  8.7 25.8 %collective-permute-start.8 = (s32[1,1]{1,0:T(1,128)}, s32[1,1]{1,0:T(1,128)}, u32[]{:S(2)}, u32[]{:S(2)}) collective-permute-start(s32[1,1]{1,0:T(1,128)} %get-tuple-element.93), channel_id=1, source_target_pairs={{0,1},{1,2},{2,3},{3,4},{4,5},{5,6},{6,7},{7,8},{8,9},{9,10},{10,1... | collective-permute-start | bytes 20 | tf_op jit(solution)/shard_map/ppermute | solution.py:16
  18.6 17.2 %collective-permute-start.10 = (s32[1,1]{1,0:T(1,128)}, s32[1,1]{1,0:T(1,128)}, u32[]{:S(2)}, u32[]{:S(2)}) collective-permute-start(s32[1,1]{1,0:T(1,128)} %get-tuple-element.92), channel_id=1, source_target_pairs={{0,2},{1,3},{2,4},{3,5},{4,6},{5,7},{6,8},{7,9},{8,10},{9,11},{10,... | collective-permute-start | bytes 20 | tf_op jit(solution)/shard_map/ppermute | solution.py:16
  23.0 14.1 %collective-permute-start.12 = (s32[1,1]{1,0:T(1,128)}, s32[1,1]{1,0:T(1,128)}, u32[]{:S(2)}, u32[]{:S(2)}) collective-permute-start(s32[1,1]{1,0:T(1,128)} %get-tuple-element.98), channel_id=1, source_target_pairs={{0,4},{1,5},{2,6},{3,7},{4,8},{5,9},{6,10},{7,11},{8,12},{9,13},{1... | collective-permute-start | bytes 20 | tf_op jit(solution)/shard_map/ppermute | solution.py:16
  28.8 9.6 %collective-permute-start.14 = (s32[1,1]{1,0:T(1,128)}, s32[1,1]{1,0:T(1,128)}, u32[]{:S(2)}, u32[]{:S(2)}) collective-permute-start(s32[1,1]{1,0:T(1,128)} %get-tuple-element.91), channel_id=1, source_target_pairs={{0,8},{1,9},{2,10},{3,11},{4,12},{5,13},{6,14},{7,15},{16,24},{17,... | collective-permute-start | bytes 20 | tf_op jit(solution)/shard_map/ppermute | solution.py:16
  45.4 16.6 %collective-permute-start.1 = (bf16[2,128,1536]{2,1,0:T(8,128)(2,1)S(1)}, bf16[2,128,1536]{2,1,0:T(8,128)(2,1)S(1)}, u32[]{:S(2)}, u32[]{:S(2)}) collective-permute-start(bf16[2,128,1536]{2,1,0:T(8,128)(2,1)S(1)} %pad_maximum_fusion), channel_id=1, source_target_pairs={{0,1},{1,2},{2,3},{3,4},{4,5},{5,6},{6,7},{7,8},{8,9},{9,10},{10,1... | collective-permute-start | bytes 2359304 | tf_op jit(solution)/shard_map/ppermute | solution.py:16
  47.4 52.3 %collective-permute-start.3 = (bf16[2,128,1536]{2,1,0:T(8,128)(2,1)S(1)}, bf16[2,128,1536]{2,1,0:T(8,128)(2,1)S(1)}, u32[]{:S(2)}, u32[]{:S(2)}) collective-permute-start(bf16[2,128,1536]{2,1,0:T(8,128)(2,1)S(1)} %pad_maximum_fusion.1), channel_id=1, source_target_pairs={{0,2},{1,3},{2,4},{3,5},{4,6},{5,7},{6,8},{7,9},{8,10},{9,11},{10,... | collective-permute-start | bytes 2359304 | tf_op jit(solution)/shard_map/ppermute | solution.py:16
  49.6 52.2 %collective-permute-start.5 = (bf16[2,128,1536]{2,1,0:T(8,128)(2,1)S(1)}, bf16[2,128,1536]{2,1,0:T(8,128)(2,1)S(1)}, u32[]{:S(2)}, u32[]{:S(2)}) collective-permute-start(bf16[2,128,1536]{2,1,0:T(8,128)(2,1)S(1)} %pad_maximum_fusion.2), channel_id=1, source_target_pairs={{0,4},{1,5},{2,6},{3,7},{4,8},{5,9},{6,10},{7,11},{8,12},{9,13},{1... | collective-permute-start | bytes 2359304 | tf_op jit(solution)/shard_map/ppermute | solution.py:16
  51.2 55.7 %collective-permute-start.7 = (bf16[2,128,1536]{2,1,0:T(8,128)(2,1)S(1)}, bf16[2,128,1536]{2,1,0:T(8,128)(2,1)S(1)}, u32[]{:S(2)}, u32[]{:S(2)}) collective-permute-start(bf16[2,128,1536]{2,1,0:T(8,128)(2,1)S(1)} %pad_maximum_fusion.3), channel_id=1, source_target_pairs={{0,8},{1,9},{2,10},{3,11},{4,12},{5,13},{6,14},{7,15},{16,24},{17,... | collective-permute-start | bytes 2359304 | tf_op jit(solution)/shard_map/ppermute | solution.py:16
  52.6 55.2 %collective-permute-start.9 = (bf16[2,128,1536]{2,1,0:T(8,128)(2,1)S(1)}, bf16[2,128,1536]{2,1,0:T(8,128)(2,1)S(1)}, u32[]{:S(2)}, u32[]{:S(2)}) collective-permute-start(bf16[2,128,1536]{2,1,0:T(8,128)(2,1)S(1)} %pad_maximum_fusion.4), channel_id=1, source_target_pairs={{1,0},{2,1},{3,2},{4,3},{5,4},{6,5},{7,6},{8,7},{9,8},{10,9},{11,1... | collective-permute-start | bytes 2359304 | tf_op jit(solution)/shard_map/ppermute | solution.py:16
  61.9 46.8 %collective-permute-start.11 = (bf16[2,128,1536]{2,1,0:T(8,128)(2,1)S(1)}, bf16[2,128,1536]{2,1,0:T(8,128)(2,1)S(1)}, u32[]{:S(2)}, u32[]{:S(2)}) collective-permute-start(bf16[2,128,1536]{2,1,0:T(8,128)(2,1)S(1)} %pad_maximum_fusion.5), channel_id=1, source_target_pairs={{2,0},{3,1},{4,2},{5,3},{6,4},{7,5},{8,6},{9,7},{10,8},{11,9},{12,... | collective-permute-start | bytes 2359304 | tf_op jit(solution)/shard_map/ppermute | solution.py:16
  99.6 19.0 %collective-permute-start.13 = (bf16[2,128,1536]{2,1,0:T(8,128)(2,1)S(1)}, bf16[2,128,1536]{2,1,0:T(8,128)(2,1)S(1)}, u32[]{:S(2)}, u32[]{:S(2)}) collective-permute-start(bf16[2,128,1536]{2,1,0:T(8,128)(2,1)S(1)} %pad_maximum_fusion.6), channel_id=1, source_target_pairs={{4,0},{5,1},{6,2},{7,3},{8,4},{9,5},{10,6},{11,7},{12,8},{13,9},{1... | collective-permute-start | bytes 2359304 | tf_op jit(solution)/shard_map/ppermute | solution.py:16
  101.8 48.4 %collective-permute-start.15 = (bf16[2,128,1536]{2,1,0:T(8,128)(2,1)S(1)}, bf16[2,128,1536]{2,1,0:T(8,128)(2,1)S(1)}, u32[]{:S(2)}, u32[]{:S(2)}) collective-permute-start(bf16[2,128,1536]{2,1,0:T(8,128)(2,1)S(1)} %pad_maximum_fusion.7), channel_id=1, source_target_pairs={{8,0},{9,1},{10,2},{11,3},{12,4},{13,5},{14,6},{15,7},{24,16},{25,... | collective-permute-start | bytes 2359304 | tf_op jit(solution)/shard_map/ppermute | solution.py:16
where the time goes:
time: 209 us; the launch traced here: 207 us
  waiting for transfers between devices  75.4 us (36%)
  starting transfers between devices  45.5 us (22%)
  matrix products  33.8 us (16%)
  local copies, waits for them, and re-layouts  25 us (12%)
  between operations  14.9 us (7%)
  loops' own time  8.01 us (4%)
  other arithmetic  4.77 us (2%)
    ppermute x16, waiting for transfers between devices, from_behind(): return lax.ppermute(block, axis, route)  75.4 us
    ppermute x16, starting transfers between devices, from_behind(): return lax.ppermute(block, axis, route)  45.5 us
    dot_general x12, matrix products, one_head(): lax.dot_general(head_queries, head_keys, (((1,), (1,)), ((), ())), prefer...  17.2 us
    dot_general x12, matrix products, one_head(): jnp.dot(weights, head_values, preferred_element_type=jnp.float32)  16.6 us
    unnamed x20, local copies, waits for them, and re-layouts  11 us
    another operation x1, loops' own time, attend_block(): per_head = lax.map(one_head, jnp.arange(HEADS, dtype=jnp.int32))  8.01 us
    dynamic_slice x12, local copies, waits for them, and re-layouts, attend_block(): per_head = lax.map(one_head, jnp.arange(HEADS, dtype=jnp.int32))  7.71 us
  transfers between devices with their start and end apart: 16, of which 5 were waited for; matrix products, arithmetic and copies ran while one was open for 6% of the time, Pallas kernels for 0%

commit v1 on v0

v1 whole, which is shorter than its diff:
```python
import functools
import math

import jax
import jax.numpy as jnp
from jax import lax
from jax.experimental import pallas as pl
from jax.experimental.pallas import tpu as pltpu
from jax.sharding import PartitionSpec as P

HD = 128
TILE = 128
STEP_HEADS = 2
LOG2_SCALE = math.log2(math.e) / math.sqrt(HD)


def attend_kernel(wide, tiles, carry_in, final, meta, *refs):
    refs = list(refs)
    q_ref = refs.pop(0)
    sources = []
    if wide:
        sources.append(((refs.pop(0),), (refs.pop(0),), None))
    for n, parts in enumerate(tiles):
        k_refs = [refs.pop(0) for _ in range(parts)]
        v_refs = [refs.pop(0) for _ in range(parts)]
        sources.append((k_refs, v_refs, n))
    if carry_in:
        acc_in, sum_in, max_in = refs.pop(0), refs.pop(0), refs.pop(0)
    rows = q_ref.shape[0]

    def load(some, cols):
        total = some[0][:, cols]
        for other in some[1:]:
            total = total + other[:, cols]
        return total

    def bias_of(n, count):
        if n is None:
            return jnp.zeros((1, count), jnp.float32)
        return jnp.full((1, count), jnp.where(meta[2 * n + 1] > 0, 0.0, -jnp.inf), jnp.float32)

    groups = [[s] for s in sources[:1]] if wide else []
    narrow = sources[1:] if wide else sources
    groups += [narrow[at : at + 2] for at in range(0, len(narrow), 2)]

    for head in range(STEP_HEADS):
        cols = slice(head * HD, (head + 1) * HD)
        query = q_ref[:, cols]
        scores, values = [], []
        for group in groups:
            key = [load(k, cols) for k, _, _ in group]
            value = [load(v, cols) for _, v, _ in group]
            key = key[0] if len(key) == 1 else jnp.concatenate(key, axis=0)
            value = value[0] if len(value) == 1 else jnp.concatenate(value, axis=0)
            part = lax.dot_general(
                query, key, (((1,), (1,)), ((), ())), preferred_element_type=jnp.float32
            )
            part = part * LOG2_SCALE
            if any(n is not None for _, _, n in group):
                bias = [bias_of(n, k[0].shape[0]) for k, _, n in group]
                part = part + (bias[0] if len(bias) == 1 else jnp.concatenate(bias, axis=1))
            scores.append(part)
            values.append(value)
        peak = functools.reduce(
            jnp.maximum, [jnp.max(part, axis=1, keepdims=True) for part in scores]
        )
        if carry_in:
            old = max_in[:, cols]
            peak = jnp.maximum(old, jnp.broadcast_to(peak, (rows, HD)))
            shrink = jnp.exp2(old - peak)
            acc = acc_in[:, cols] * shrink
            total = sum_in[:, cols] * shrink
        else:
            peak = jnp.broadcast_to(peak, (rows, HD))
            acc = total = None
        for part, value in zip(scores, values):
            count = part.shape[1]
            shift = peak if count == HD else jnp.concatenate([peak] * (count // HD), axis=1)
            weight = jnp.exp2(part - shift).astype(jnp.bfloat16)
            both = jnp.concatenate([value, jnp.ones_like(value)], axis=1)
            added = jnp.dot(weight, both, preferred_element_type=jnp.float32)
            acc = added[:, :HD] if acc is None else acc + added[:, :HD]
            total = added[:, HD:] if total is None else total + added[:, HD:]
        if final:
            refs[0][:, cols] = (acc / total).astype(jnp.bfloat16)
        else:
            refs[0][:, cols] = acc
            refs[1][:, cols] = total
            refs[2][:, cols] = peak


def attend(queries, own, tiles, carry, final):
    rows, width = queries.shape
    block = STEP_HEADS * HD
    meta = []
    for _, _, tile, usable in tiles:
        meta += [jnp.asarray(tile, jnp.int32), jnp.asarray(usable, jnp.int32)]
    meta = jnp.stack(meta) if meta else jnp.zeros((2,), jnp.int32)

    whole = pl.BlockSpec((rows, block), lambda step, meta: (0, step))
    operands, specs = [queries], [whole]
    keys_seen = 0
    if own is not None:
        operands += list(own)
        specs += [pl.BlockSpec((own[0].shape[0], block), lambda step, meta: (0, step))] * 2
        keys_seen += own[0].shape[0]
    for n, (keys, values, _, _) in enumerate(tiles):
        spec = pl.BlockSpec((TILE, block), functools.partial(lambda n, step, meta: (meta[2 * n], step), n))
        operands += list(keys) + list(values)
        specs += [spec] * (len(keys) + len(values))
        keys_seen += TILE
    if carry is not None:
        operands += list(carry)
        specs += [whole] * 3
    if final:
        out_shape = jax.ShapeDtypeStruct((rows, width), jnp.bfloat16)
        out_specs = whole
    else:
        out_shape = [jax.ShapeDtypeStruct((rows, width), jnp.float32)] * 3
        out_specs = [whole] * 3
    return pl.pallas_call(
        functools.partial(
            attend_kernel, own is not None, [len(t[0]) for t in tiles], carry is not None, final
        ),
        out_shape=out_shape,
        grid_spec=pltpu.PrefetchScalarGridSpec(
            num_scalar_prefetch=1,
            grid=(width // block,),
            in_specs=specs,
            out_specs=out_specs,
        ),
        compiler_params=pltpu.CompilerParams(vmem_limit_bytes=24 * 1024 * 1024),
        cost_estimate=pl.CostEstimate(
            flops=4 * rows * keys_seen * width,
            bytes_accessed=4 * keys_seen * width + 2 * rows * width,
            transcendentals=rows * keys_seen * (width // HD),
        ),
    )(meta, *operands)


def pick(array, tile):
    return lax.dynamic_slice_in_dim(array, tile * TILE, TILE, 0)


def send(array, route):
    return lax.ppermute(array, "frame", route)


def body_direct(queries, key_heads, value_heads, tile_lists):
    frames = lax.axis_size("frame")
    levels = frames.bit_length() - 1
    me = lax.axis_index("frame")
    lists = jnp.clip(lax.all_gather(tile_lists, "frame", tiled=True), 0, key_heads.shape[0] // TILE - 1)
    tiles = []
    for level in range(levels):
        for entry, distance in ((level, 1 << level), (levels + level, -(1 << level))):
            route = [(i, i + distance) for i in range(frames) if 0 <= i + distance < frames]
            wanted = lists[jnp.clip(me + distance, 0, frames - 1), entry]
            both = jnp.stack([pick(key_heads, wanted), pick(value_heads, wanted)])
            both = send(both, route)
            usable = (me - distance >= 0) & (me - distance < frames)
            tiles.append(([both[0]], [both[1]], 0, usable))
    return attend(queries, (key_heads, value_heads), tiles, None, True)


def body_planes(queries, key_heads, value_heads, tile_lists):
    frames = 16
    me = lax.axis_index("frame")
    spot = me % 4
    levels = 4
    every = range(frames)

    up = [(i, i + 4) for i in every if i + 4 < frames]
    down = [(i, i - 4) for i in every if i - 4 >= 0]
    across = [(i, i ^ 2) for i in every]
    beside = [(i, i ^ 1) for i in every]
    low_k = send(key_heads, up)
    high_k = send(key_heads, down)
    across_k = send(key_heads, across)
    low_v = send(value_heads, up)
    high_v = send(value_heads, down)
    across_v = send(value_heads, across)
    beside_k = send(key_heads, beside)
    beside_v = send(value_heads, beside)
    lists = jnp.clip(lax.all_gather(tile_lists, "frame", tiled=True), 0, key_heads.shape[0] // TILE - 1)

    def wanted(frame, entry):
        return lists[jnp.clip(frame, 0, frames - 1), entry]

    mine = lists[me]

    tile = wanted(me + 4, 3)
    far_low = send(
        jnp.stack([pick(low_k, tile), pick(low_v, tile)]), [(i, i + 4) for i in range(4, 12)]
    )
    tile = wanted(me - 4, levels + 3)
    far_high = send(
        jnp.stack([pick(high_k, tile), pick(high_v, tile)]), [(i, i - 4) for i in range(4, 12)]
    )
    right = spot >= 2
    tile = jnp.where(right, wanted(me - 2, 1), wanted(me + 2, levels + 1))
    two = send(
        jnp.stack(
            [
                jnp.where(right, pick(low_k, tile), pick(high_k, tile)),
                jnp.where(right, pick(low_v, tile), pick(high_v, tile)),
            ]
        ),
        across,
    )
    step = jnp.where(spot == 0, 1, jnp.where(spot == 3, -1, jnp.where(spot == 1, 3, -3)))
    entry = jnp.where((spot == 0) | (spot == 2), levels, 0)
    tile = wanted(me + step, entry)
    route = []
    for i in every:
        j = i + {0: 1, 3: -1, 1: 3, 2: -3}[i % 4]
        if 0 <= j < frames:
            route.append((i, j))
    one = send(jnp.stack([pick(across_k, tile), pick(across_v, tile)]), route)

    odd = spot % 2 == 1
    carry = attend(
        queries,
        (key_heads, value_heads),
        [([beside_k], [beside_v], jnp.where(odd, mine[0], mine[levels]), True)],
        None,
        False,
    )
    carry = attend(
        queries,
        None,
        [
            ([across_k], [across_v], jnp.where(right, mine[1], mine[levels + 1]), True),
            ([low_k], [low_v], mine[2], me >= 4),
            ([high_k], [high_v], mine[levels + 2], me + 4 < frames),
        ],
        carry,
        False,
    )
    two_there = jnp.where(right, me + 2 < frames, me - 2 >= 0)
    one_there = jnp.where(spot == 0, me >= 1, jnp.where(spot == 3, me + 1 < frames, True))
    return attend(
        queries,
        None,
        [
            ([two[0]], [two[1]], 0, two_there),
            ([one[0]], [one[1]], 0, one_there),
            ([far_low[0], far_high[0]], [far_low[1], far_high[1]], 0, True),
        ],
        carry,
        True,
    )


def solution(mesh):
    body = body_planes if mesh.shape["frame"] == 16 else body_direct
    in_specs = (
        P(("groups", "frame"), None),
        P(("groups", "frame"), None),
        P(("groups", "frame"), None),
        P("frame", None),
    )
    out_specs = P(("groups", "frame"), None)
    return jax.shard_map(body, mesh=mesh, in_specs=in_specs, out_specs=out_specs, check_vma=False)
```

time: 209 us -> 134 us (0.64)
  the two profiles are of different devices: /device:TPU:3 before, /device:TPU:24 now
where the time goes in v1:
time: 134 us; the launch traced here: 133 us
  waiting for transfers between devices  45.4 us (34%)
  blocking collectives  39.1 us (29%)
  starting transfers between devices  20.9 us (16%)
  Pallas kernels  18.1 us (14%)
  between operations  6.02 us (4%)
  local copies, waits for them, and re-layouts  3.04 us (2%)
    ppermute x12, waiting for transfers between devices, send(): return lax.ppermute(array, 'frame', route)  45.4 us
    all_gather x1, blocking collectives, body_planes(): lax.all_gather(tile_lists, 'frame', tiled=True)  39.1 us
    ppermute x12, starting transfers between devices, send(): return lax.ppermute(array, 'frame', route)  20.9 us
    pallas_call x3, Pallas kernels, attend(): pl.pallas_call(functools.partial(attend_kernel, own is not None, [len(t[0...  18.1 us
  transfers between devices with their start and end apart: 12, of which 3 were waited for; matrix products, arithmetic and copies ran while one was open for 3% of the time, Pallas kernels for 9%

profile of v1, /device:TPU:24, one launch (start us, length us, event | category | flops | bytes accessed | tf_op | source)
XLA Modules:
  0.0 133.2 jit_solution(17486979727054978236)
XLA Ops:
  0.0 1.3 collective-permute-start
  1.3 4.6 %collective-permute-start.1 = (bf16[256,1536]{1,0:T(8,128)(2,1)}, bf16[256,1536]{1,0:T(8,128)(2,1)S(1)}, u32[]{:S(2)}, u32[]{:S(2)}) collective-permute-start(bf16[256,1536]{1,0:T(8,128)(2,1)} %refs_1_.1), channel_id=1, source_target_pairs={{4,0},{5,1},{6,2},{7,3},{8,4},{9,5},{10,6},{11,7},{12,8},{13,9},{1... | collective-permute-start | bytes 2359304 | tf_op jit(solution)/shard_map/ppermute | solution.py:146
  5.9 0.1 collective-permute-start.10
  6.0 1.3 collective-permute-start.2
  7.3 4.6 %collective-permute-start.3 = (bf16[256,1536]{1,0:T(8,128)(2,1)}, bf16[256,1536]{1,0:T(8,128)(2,1)S(1)}, u32[]{:S(2)}, u32[]{:S(2)}) collective-permute-start(bf16[256,1536]{1,0:T(8,128)(2,1)} %refs_2_.1), channel_id=1, source_target_pairs={{4,0},{5,1},{6,2},{7,3},{8,4},{9,5},{10,6},{11,7},{12,8},{13,9},{1... | collective-permute-start | bytes 2359304 | tf_op jit(solution)/shard_map/ppermute | solution.py:146
  12.0 39.1 %all-gather = s32[16,1,8]{2,1,0:T(1,128)S(1)} all-gather(s32[1,1,8]{2,1,0:T(1,128)} %bitcast.52), channel_id=1, replica_groups=mesh['groups'=2,'frame'=16] {'frame'}, dimensions={0}, use_global_device_ids=true | all-gather | bytes 544 | tf_op jit(solution)/shard_map/all_gather | solution.py:185
  51.1 0.6 constant_dynamic-slice_fusion
  54.9 0.1 stack.75
  55.0 0.7 fusion.1
  58.2 1.3 %stack.94.meta = s32[6]{0:T(128)S(1)} concatenate(s32[1]{0:T(128)} %bitcast.27, s32[1]{0:T(128)} %constant.69.clone.1, s32[1]{0:T(128)} %bitcast.28, s32[1]{0:T(128)} %bitcast.29, s32[1]{0:T(128)} %bitcast.30, s32[1]{0:T(128)} %bitcast.31), dimensions={0} | concatenate | bytes 48 | tf_op jit(solution)/shard_map/stack | solution.py:98
  59.5 0.1 pad_add_fusion.meta
  59.6 0.3 collective-permute-start.11
  59.9 2.4 %collective-permute-start.5 = (bf16[256,1536]{1,0:T(8,128)(2,1)}, bf16[256,1536]{1,0:T(8,128)(2,1)S(1)}, u32[]{:S(2)}, u32[]{:S(2)}) collective-permute-start(bf16[256,1536]{1,0:T(8,128)(2,1)} %refs_1_.1), channel_id=1, source_target_pairs={{0,2},{1,3},{2,0},{3,1},{4,6},{5,7},{6,4},{7,5},{8,10},{9,11},{10,... | collective-permute-start | bytes 2359304 | tf_op jit(solution)/shard_map/ppermute | solution.py:146
  62.3 0.1 dynamic-slice_bitcast_fusion.1
  62.5 0.6 collective-permute-start.6
  63.1 0.1 dynamic-slice_bitcast_fusion
  63.2 0.1 pad_maximum_fusion.3
  63.3 0.7 collective-permute-start.9
  64.0 0.1 pad_maximum_fusion.2
  64.1 0.1 pad_maximum_fusion
  64.2 33.1 %collective-permute-done.6.refs_2_ = bf16[256,1536]{1,0:T(8,128)(2,1)S(1)} collective-permute-done((bf16[256,1536]{1,0:T(8,128)(2,1)S(1)}, bf16[256,1536]{1,0:T(8,128)(2,1)S(1)}, u32[]{:S(2)}, u32[]{:S(2)}) %collective-permute-start.6) | collective-permute-done | bytes 786464 | tf_op jit(solution)/shard_map/ppermute | solution.py:146
  97.3 1.3 collective-permute-start.8
  98.6 1.8 %collective-permute-start.4 = (bf16[2,128,1536]{2,1,0:T(8,128)(2,1)S(1)}, bf16[2,128,1536]{2,1,0:T(8,128)(2,1)S(1)}, u32[]{:S(2)}, u32[]{:S(2)}) collective-permute-start(bf16[2,128,1536]{2,1,0:T(8,128)(2,1)S(1)} %pad_maximum_fusion), channel_id=1, source_target_pairs={{0,2},{1,3},{2,0},{3,1},{4,6},{5,7},{6,4},{7,5},{8,10},{9,11},{10,... | collective-permute-start | bytes 2359304 | tf_op jit(solution)/shard_map/ppermute | solution.py:146
  100.5 0.1 pad_maximum_fusion.1
  100.6 1.9 %collective-permute-start.7 = (bf16[2,128,1536]{2,1,0:T(8,128)(2,1)S(1)}, bf16[2,128,1536]{2,1,0:T(8,128)(2,1)S(1)}, u32[]{:S(2)}, u32[]{:S(2)}) collective-permute-start(bf16[2,128,1536]{2,1,0:T(8,128)(2,1)S(1)} %pad_maximum_fusion.1), channel_id=1, source_target_pairs={{0,1},{1,4},{3,2},{4,5},{5,8},{6,3},{7,6},{8,9},{9,12},{10,7},{11,... | collective-permute-start | bytes 2359304 | tf_op jit(solution)/shard_map/ppermute | solution.py:146
  102.5 6.0 %shard_map.46 = (f32[256,1536]{1,0:T(8,128)S(1)}, f32[256,1536]{1,0:T(8,128)S(1)}, f32[256,1536]{1,0:T(8,128)S(1)}) custom-call(s32[2]{0:T(128)S(1)} %pad_add_fusion.meta, bf16[256,1536]{1,0:T(8,128)(2,1)S(1)} %copy-done, bf16[256,1536]{1,0:T(8,128)(2,1)S(1)} %copy-done.2, bf16[256,1536]{1,0:T(8,128)(2,1)S(1)} %copy-done.1, ...), custom_call_target="tpu_custom_call" | custom-call | flops 603979776 | bytes 3145728 | tf_op jit(solution)/shard_map/pallas_call | solution.py:121
  108.6 5.7 %shard_map.47 = (f32[256,1536]{1,0:T(8,128)S(1)}, f32[256,1536]{1,0:T(8,128)S(1)}, f32[256,1536]{1,0:T(8,128)S(1)}) custom-call(s32[6]{0:T(128)S(1)} %stack.94.meta, bf16[256,1536]{1,0:T(8,128)(2,1)S(1)} %copy-done, bf16[256,1536]{1,0:T(8,128)(2,1)S(1)} %collective-permute-done.5.refs_1_, bf16[256,1536]{1,0:T(8,128)(2,1)S(1)} %collective-permute-done.6.refs_2_, ...), custom_call_target="tpu_custom_call" | custom-call | flops 603979776 | bytes 3145728 | tf_op jit(solution)/shard_map/pallas_call | solution.py:121
  114.3 0.1 slice_bitcast_fusion
  114.3 5.3 %collective-permute-done.8 = bf16[2,128,1536]{2,1,0:T(8,128)(2,1)S(1)} collective-permute-done((bf16[2,128,1536]{2,1,0:T(8,128)(2,1)S(1)}, bf16[2,128,1536]{2,1,0:T(8,128)(2,1)S(1)}, u32[]{:S(2)}, u32[]{:S(2)}) %collective-permute-start.8) | collective-permute-done | bytes 786464 | tf_op jit(solution)/shard_map/ppermute | solution.py:146
  119.7 0.1 slice_bitcast_fusion.6
  119.8 7.0 %collective-permute-done.7 = bf16[2,128,1536]{2,1,0:T(8,128)(2,1)S(1)} collective-permute-done((bf16[2,128,1536]{2,1,0:T(8,128)(2,1)S(1)}, bf16[2,128,1536]{2,1,0:T(8,128)(2,1)S(1)}, u32[]{:S(2)}, u32[]{:S(2)}) %collective-permute-start.7) | collective-permute-done | bytes 786464 | tf_op jit(solution)/shard_map/ppermute | solution.py:146
  126.8 6.4 %shard_map.48 = bf16[256,1536]{1,0:T(8,128)(2,1)} custom-call(s32[6]{0:T(128)S(1)} %stack.76.meta, bf16[256,1536]{1,0:T(8,128)(2,1)S(1)} %copy-done, bf16[128,1536]{1,0:T(8,128)(2,1)S(1)} %get-tuple-element.30.refs_1_, bf16[128,1536]{1,0:T(8,128)(2,1)S(1)} %get-tuple-element.29.refs_2_, bf16[128,1536]{1,0:T(8,128)(2,1)S(1)} %get-tuple-element.28.refs_3_, ...), custom_call_target="tpu_custom_call" | custom-call | flops 603979776 | bytes 3145728 | tf_op jit(solution)/shard_map/pallas_call | solution.py:121
  (22 shorter events, 0.2 us)
Async XLA Ops:
  0.0 59.6 %collective-permute-start = (bf16[256,1536]{1,0:T(8,128)(2,1)}, bf16[256,1536]{1,0:T(8,128)(2,1)S(1)}, u32[]{:S(2)}, u32[]{:S(2)}) collective-permute-start(bf16[256,1536]{1,0:T(8,128)(2,1)} %refs_1_.1), channel_id=1, source_target_pairs={{0,4},{1,5},{2,6},{3,7},{4,8},{5,9},{6,10},{7,11},{8,12},{9,13},{1... | collective-permute-start | bytes 2359304 | tf_op jit(solution)/shard_map/ppermute | solution.py:146
  1.3 58.6 %collective-permute-start.1 = (bf16[256,1536]{1,0:T(8,128)(2,1)}, bf16[256,1536]{1,0:T(8,128)(2,1)S(1)}, u32[]{:S(2)}, u32[]{:S(2)}) collective-permute-start(bf16[256,1536]{1,0:T(8,128)(2,1)} %refs_1_.1), channel_id=1, source_target_pairs={{4,0},{5,1},{6,2},{7,3},{8,4},{9,5},{10,6},{11,7},{12,8},{13,9},{1... | collective-permute-start | bytes 2359304 | tf_op jit(solution)/shard_map/ppermute | solution.py:146
  5.9 94.7 %collective-permute-start.10 = (bf16[256,1536]{1,0:T(8,128)(2,1)}, bf16[256,1536]{1,0:T(8,128)(2,1)}, u32[]{:S(2)}, u32[]{:S(2)}) collective-permute-start(bf16[256,1536]{1,0:T(8,128)(2,1)} %refs_1_.1), channel_id=1, source_target_pairs={{0,1},{1,0},{2,3},{3,2},{4,5},{5,4},{6,7},{7,6},{8,9},{9,8},{10,11... | collective-permute-start | bytes 2359304 | tf_op jit(solution)/shard_map/ppermute | solution.py:146
  6.0 56.5 %collective-permute-start.2 = (bf16[256,1536]{1,0:T(8,128)(2,1)}, bf16[256,1536]{1,0:T(8,128)(2,1)S(1)}, u32[]{:S(2)}, u32[]{:S(2)}) collective-permute-start(bf16[256,1536]{1,0:T(8,128)(2,1)} %refs_2_.1), channel_id=1, source_target_pairs={{0,4},{1,5},{2,6},{3,7},{4,8},{5,9},{6,10},{7,11},{8,12},{9,13},{1... | collective-permute-start | bytes 2359304 | tf_op jit(solution)/shard_map/ppermute | solution.py:146
  7.3 55.8 %collective-permute-start.3 = (bf16[256,1536]{1,0:T(8,128)(2,1)}, bf16[256,1536]{1,0:T(8,128)(2,1)S(1)}, u32[]{:S(2)}, u32[]{:S(2)}) collective-permute-start(bf16[256,1536]{1,0:T(8,128)(2,1)} %refs_2_.1), channel_id=1, source_target_pairs={{4,0},{5,1},{6,2},{7,3},{8,4},{9,5},{10,6},{11,7},{12,8},{13,9},{1... | collective-permute-start | bytes 2359304 | tf_op jit(solution)/shard_map/ppermute | solution.py:146
  59.5 2.9 %copy-start.1 = (bf16[256,1536]{1,0:T(8,128)(2,1)S(1)}, bf16[256,1536]{1,0:T(8,128)(2,1)}, u32[]{:S(2)}) copy-start(bf16[256,1536]{1,0:T(8,128)(2,1)} %refs_2_.1) | copy-start | bytes 2359300
  59.6 42.9 %collective-permute-start.11 = (bf16[256,1536]{1,0:T(8,128)(2,1)}, bf16[256,1536]{1,0:T(8,128)(2,1)S(1)}, u32[]{:S(2)}, u32[]{:S(2)}) collective-permute-start(bf16[256,1536]{1,0:T(8,128)(2,1)} %refs_2_.1), channel_id=1, source_target_pairs={{0,1},{1,0},{2,3},{3,2},{4,5},{5,4},{6,7},{7,6},{8,9},{9,8},{10,11... | collective-permute-start | bytes 2359304 | tf_op jit(solution)/shard_map/ppermute | solution.py:146
  59.9 38.7 %collective-permute-start.5 = (bf16[256,1536]{1,0:T(8,128)(2,1)}, bf16[256,1536]{1,0:T(8,128)(2,1)S(1)}, u32[]{:S(2)}, u32[]{:S(2)}) collective-permute-start(bf16[256,1536]{1,0:T(8,128)(2,1)} %refs_1_.1), channel_id=1, source_target_pairs={{0,2},{1,3},{2,0},{3,1},{4,6},{5,7},{6,4},{7,5},{8,10},{9,11},{10,... | collective-permute-start | bytes 2359304 | tf_op jit(solution)/shard_map/ppermute | solution.py:146
  62.5 34.8 %collective-permute-start.6 = (bf16[256,1536]{1,0:T(8,128)(2,1)S(1)}, bf16[256,1536]{1,0:T(8,128)(2,1)S(1)}, u32[]{:S(2)}, u32[]{:S(2)}) collective-permute-start(bf16[256,1536]{1,0:T(8,128)(2,1)S(1)} %copy-done.1), channel_id=1, source_target_pairs={{0,2},{1,3},{2,0},{3,1},{4,6},{5,7},{6,4},{7,5},{8,10},{9,11},{10,... | collective-permute-start | bytes 2359304 | tf_op jit(solution)/shard_map/ppermute | solution.py:146
  63.3 51.0 %collective-permute-start.9 = (bf16[2,128,1536]{2,1,0:T(8,128)(2,1)S(1)}, bf16[2,128,1536]{2,1,0:T(8,128)(2,1)S(1)}, u32[]{:S(2)}, u32[]{:S(2)}) collective-permute-start(bf16[2,128,1536]{2,1,0:T(8,128)(2,1)S(1)} %pad_maximum_fusion.3), channel_id=1, source_target_pairs={{4,0},{5,1},{6,2},{7,3},{8,4},{9,5},{10,6},{11,7},{20,16},{21,17},... | collective-permute-start | bytes 2359304 | tf_op jit(solution)/shard_map/ppermute | solution.py:146
  64.2 38.4 %copy-start = (bf16[256,1536]{1,0:T(8,128)(2,1)S(1)}, bf16[256,1536]{1,0:T(8,128)(2,1)}, u32[]{:S(2)}) copy-start(bf16[256,1536]{1,0:T(8,128)(2,1)} %refs_0_.5) | copy-start | bytes 2359300
  64.2 38.4 %copy-start.2 = (bf16[256,1536]{1,0:T(8,128)(2,1)S(1)}, bf16[256,1536]{1,0:T(8,128)(2,1)}, u32[]{:S(2)}) copy-start(bf16[256,1536]{1,0:T(8,128)(2,1)} %refs_1_.1) | copy-start | bytes 2359300
  97.3 22.3 %collective-permute-start.8 = (bf16[2,128,1536]{2,1,0:T(8,128)(2,1)S(1)}, bf16[2,128,1536]{2,1,0:T(8,128)(2,1)S(1)}, u32[]{:S(2)}, u32[]{:S(2)}) collective-permute-start(bf16[2,128,1536]{2,1,0:T(8,128)(2,1)S(1)} %pad_maximum_fusion.2), channel_id=1, source_target_pairs={{4,8},{5,9},{6,10},{7,11},{8,12},{9,13},{10,14},{11,15},{20,24},{2... | collective-permute-start | bytes 2359304 | tf_op jit(solution)/shard_map/ppermute | solution.py:146
  98.6 21.0 %collective-permute-start.4 = (bf16[2,128,1536]{2,1,0:T(8,128)(2,1)S(1)}, bf16[2,128,1536]{2,1,0:T(8,128)(2,1)S(1)}, u32[]{:S(2)}, u32[]{:S(2)}) collective-permute-start(bf16[2,128,1536]{2,1,0:T(8,128)(2,1)S(1)} %pad_maximum_fusion), channel_id=1, source_target_pairs={{0,2},{1,3},{2,0},{3,1},{4,6},{5,7},{6,4},{7,5},{8,10},{9,11},{10,... | collective-permute-start | bytes 2359304 | tf_op jit(solution)/shard_map/ppermute | solution.py:146
  100.6 26.2 %collective-permute-start.7 = (bf16[2,128,1536]{2,1,0:T(8,128)(2,1)S(1)}, bf16[2,128,1536]{2,1,0:T(8,128)(2,1)S(1)}, u32[]{:S(2)}, u32[]{:S(2)}) collective-permute-start(bf16[2,128,1536]{2,1,0:T(8,128)(2,1)S(1)} %pad_maximum_fusion.1), channel_id=1, source_target_pairs={{0,1},{1,4},{3,2},{4,5},{5,8},{6,3},{7,6},{8,9},{9,12},{10,7},{11,... | collective-permute-start | bytes 2359304 | tf_op jit(solution)/shard_map/ppermute | solution.py:146

commit v2 on v0

v2 whole, which is shorter than its diff:
```python
import functools
import math

import jax
import jax.numpy as jnp
from jax import lax
from jax.experimental import pallas as pl
from jax.experimental.pallas import tpu as pltpu
from jax.sharding import PartitionSpec as P

HD = 128
TILE = 128
NOTE_ROWS = 16
LOG2_SCALE = math.log2(math.e) / math.sqrt(HD)
VMEM_LIMIT = 24 * 1024 * 1024


def attend_kernel(plan, heads, carry_in, final, meta, *refs):
    refs = list(refs)
    q_ref = refs.pop(0)
    sources = []
    for parts, usable in plan:
        k_refs = [refs.pop(0) for _ in range(parts)]
        v_refs = [refs.pop(0) for _ in range(parts)]
        bias = None
        if usable is not None:
            bias = jnp.where(usable(meta), 0.0, -jnp.inf).astype(jnp.float32)
        sources.append((k_refs, v_refs, bias))
    if carry_in:
        acc_in, sum_in, max_in = refs.pop(0), refs.pop(0), refs.pop(0)
    outs = refs[-1:] if final else refs[-3:]
    rows = q_ref.shape[0]

    def load(some, cols):
        total = some[0][:, cols]
        for other in some[1:]:
            total = total + other[:, cols]
        return total

    groups = [[s] for s in sources if s[0][0].shape[0] > TILE]
    narrow = [s for s in sources if s[0][0].shape[0] == TILE]
    groups += [narrow[at : at + 2] for at in range(0, len(narrow), 2)]

    for head in range(heads):
        cols = slice(head * HD, (head + 1) * HD)
        query = q_ref[:, cols]
        scores, values = [], []
        for group in groups:
            key = jnp.concatenate([load(k, cols) for k, _, _ in group], axis=0)
            values.append(jnp.concatenate([load(v, cols) for _, v, _ in group], axis=0))
            part = lax.dot_general(
                query, key, (((1,), (1,)), ((), ())), preferred_element_type=jnp.float32
            )
            pieces = []
            at = 0
            for k, _, bias in group:
                for _ in range(k[0].shape[0] // TILE):
                    piece = part[:, at : at + TILE] * LOG2_SCALE
                    pieces.append(piece if bias is None else piece + bias)
                    at += TILE
            scores.append(pieces)
        peak = functools.reduce(jnp.maximum, [piece for pieces in scores for piece in pieces])
        peak = jnp.broadcast_to(jnp.max(peak, axis=1, keepdims=True), (rows, HD))
        acc = total = None
        if carry_in:
            old = max_in[:, cols]
            peak = jnp.maximum(old, peak)
            shrink = jnp.exp2(old - peak)
            acc = acc_in[:, cols] * shrink
            total = sum_in[:, cols] * shrink
        for pieces, value in zip(scores, values):
            weight = [jnp.exp2(piece - peak).astype(jnp.bfloat16) for piece in pieces]
            both = jnp.concatenate([value, jnp.ones_like(value)], axis=1)
            added = jnp.dot(
                jnp.concatenate(weight, axis=1), both, preferred_element_type=jnp.float32
            )
            acc = added[:, :HD] if acc is None else acc + added[:, :HD]
            total = added[:, HD:] if total is None else total + added[:, HD:]
        if final:
            outs[0][:, cols] = (acc / total).astype(jnp.bfloat16)
        else:
            outs[0][:, cols] = acc
            outs[1][:, cols] = total
            outs[2][:, cols] = peak


def attend(queries, meta, sources, first, steps, heads, carry=None, final=False, into=None):
    rows, width = queries.shape
    block = heads * HD

    def spec(count, row, column):
        return pl.BlockSpec((count, block), lambda step, meta: (row(meta), column + step))

    def zero(meta):
        return 0

    operands, specs = [queries], [spec(rows, zero, first)]
    plan, keys_seen = [], 0
    for keys, values, usable in sources:
        for array, count, row, column in list(keys) + list(values):
            operands.append(array)
            specs.append(spec(count, row, column))
        keys_seen += keys[0][1]
        plan.append((len(keys), usable))
    if carry is not None:
        operands += list(carry)
        specs += [spec(rows, zero, 0)] * 3
    aliases = {}
    if final:
        out_shape = jax.ShapeDtypeStruct((rows, width), jnp.bfloat16)
        out_specs = spec(rows, zero, first)
        if into is not None:
            aliases = {len(operands) + 1: 0}
            operands.append(into)
            specs.append(pl.BlockSpec(memory_space=pl.ANY))
    else:
        out_shape = [jax.ShapeDtypeStruct((rows, steps * block), jnp.float32)] * 3
        out_specs = [spec(rows, zero, 0)] * 3
    done = steps * block
    return pl.pallas_call(
        functools.partial(attend_kernel, plan, heads, carry is not None, final),
        out_shape=out_shape,
        grid_spec=pltpu.PrefetchScalarGridSpec(
            num_scalar_prefetch=1, grid=(steps,), in_specs=specs, out_specs=out_specs
        ),
        input_output_aliases=aliases,
        compiler_params=pltpu.CompilerParams(vmem_limit_bytes=VMEM_LIMIT),
        cost_estimate=pl.CostEstimate(
            flops=4 * rows * keys_seen * done,
            bytes_accessed=4 * keys_seen * done + 2 * rows * done,
            transcendentals=rows * keys_seen * (done // HD),
        ),
    )(meta, *operands)


def pack_kernel(first, meta, k_ref, v_ref, out_ref, note, sems):
    rows = k_ref.shape[0]
    width = out_ref.shape[1]
    copies = [
        pltpu.make_async_copy(
            ref.at[:, pl.ds(first, width)], out_ref.at[pl.ds(n * rows, rows)], sems.at[n]
        )
        for n, ref in enumerate((k_ref, v_ref))
    ]
    for copy in copies:
        copy.start()
    lane = lax.broadcasted_iota(jnp.int32, note.shape, 1)
    row = jnp.zeros(note.shape, jnp.float32)
    for entry in range(8):
        row = jnp.where(lane == entry, meta[entry].astype(jnp.float32), row)
    note[...] = row.astype(jnp.bfloat16)
    last = pltpu.make_async_copy(note, out_ref.at[pl.ds(2 * rows, NOTE_ROWS)], sems.at[2])
    last.start()
    for copy in copies:
        copy.wait()
    last.wait()


def pack(meta, keys, values, first, width):
    rows = keys.shape[0]
    whole = pl.BlockSpec(memory_space=pl.ANY)
    return pl.pallas_call(
        functools.partial(pack_kernel, first),
        out_shape=jax.ShapeDtypeStruct((2 * rows + NOTE_ROWS, width), jnp.bfloat16),
        in_specs=[pl.BlockSpec(memory_space=pltpu.SMEM), whole, whole],
        out_specs=whole,
        scratch_shapes=[
            pltpu.VMEM((NOTE_ROWS, width), jnp.bfloat16),
            pltpu.SemaphoreType.DMA((3,)),
        ],
        compiler_params=pltpu.CompilerParams(vmem_limit_bytes=VMEM_LIMIT),
        cost_estimate=pl.CostEstimate(flops=0, bytes_accessed=8 * rows * width, transcendentals=0),
    )(meta, keys, values)


def choose_kernel(meta, list_ref, low, high, over, wants, far_up, far_down, two, one, notes, sems):
    rows = 2 * TILE
    spot = meta[8] % 4
    right = spot >= 2
    reads = [
        pltpu.make_async_copy(
            ref.at[pl.ds(2 * rows, NOTE_ROWS), pl.ds(0, HD)], notes.at[n], sems.at[n]
        )
        for n, ref in enumerate((low, high, over))
    ]
    for read in reads:
        read.start()
    for read in reads:
        read.wait()

    def entry(n, at):
        shape = notes.shape[1:]
        here = (lax.broadcasted_iota(jnp.int32, shape, 1) == at) & (
            lax.broadcasted_iota(jnp.int32, shape, 0) == 0
        )
        value = jnp.sum(jnp.where(here, notes[n].astype(jnp.float32), 0.0))
        return jnp.clip(value.astype(jnp.int32), 0, 1)

    up_tile = entry(1, 3)
    down_tile = entry(0, 7)
    two_tile = entry(2, jnp.where(right, 1, 5))
    one_tile = jnp.clip(list_ref[0, jnp.where(spot % 2 == 0, 4, 0)], 0, 1)
    wants[0] = up_tile
    wants[1] = down_tile
    wants[2] = two_tile
    wants[3] = one_tile
    copy_tiles(right, up_tile, down_tile, two_tile, one_tile, low, high, over, far_up, far_down, two, one, sems)


def choose_again_kernel(meta, wants, low, high, over, far_up, far_down, two, one, sems):
    right = meta[8] % 4 >= 2
    copy_tiles(right, wants[0], wants[1], wants[2], wants[3], low, high, over, far_up, far_down, two, one, sems)


def copy_tiles(right, up_tile, down_tile, two_tile, one_tile, low, high, over, far_up, far_down, two, one, sems):
    rows = 2 * TILE

    def copies(src, tile, dst, sem):
        start = pl.multiple_of(tile * TILE, TILE)
        return [
            pltpu.make_async_copy(
                src.at[pl.ds(n * rows + start, TILE)], dst.at[pl.ds(n * TILE, TILE)], sems.at[sem + n]
            )
            for n in (0, 1)
        ]

    always = copies(low, up_tile, far_up, 3) + copies(high, down_tile, far_down, 5) + copies(over, one_tile, one, 7)
    for copy in always:
        copy.start()

    @pl.when(right)
    def _():
        for copy in copies(low, two_tile, two, 9):
            copy.start()

    @pl.when(jnp.logical_not(right))
    def _():
        for copy in copies(high, two_tile, two, 9):
            copy.start()

    for copy in always + copies(low, two_tile, two, 9):
        copy.wait()


def choose(meta, lists, wants, low, high, over):
    width = low.shape[1]
    scalar = pl.BlockSpec(memory_space=pltpu.SMEM)
    whole = pl.BlockSpec(memory_space=pl.ANY)
    sent = jax.ShapeDtypeStruct((2 * TILE, width), jnp.bfloat16)
    again = wants is not None
    outs = ([] if again else [jax.ShapeDtypeStruct((4,), jnp.int32)]) + [sent] * 4
    return pl.pallas_call(
        choose_again_kernel if again else choose_kernel,
        out_shape=outs,
        in_specs=[scalar, scalar] + [whole] * 3,
        out_specs=([] if again else [scalar]) + [whole] * 4,
        scratch_shapes=([] if again else [pltpu.VMEM((3, NOTE_ROWS, HD), jnp.bfloat16)])
        + [pltpu.SemaphoreType.DMA((11,))],
        compiler_params=pltpu.CompilerParams(vmem_limit_bytes=VMEM_LIMIT),
        cost_estimate=pl.CostEstimate(flops=0, bytes_accessed=32 * TILE * width, transcendentals=0),
    )(meta, wants if again else lists, low, high, over)


def send(array, route):
    return lax.ppermute(array, "frame", route)


def fixed(block):
    return lambda meta: block


def body_direct(queries, key_heads, value_heads, tile_lists):
    frames = lax.axis_size("frame")
    levels = frames.bit_length() - 1
    rows, width = key_heads.shape
    me = lax.axis_index("frame")
    lists = jnp.clip(lax.all_gather(tile_lists, "frame", tiled=True), 0, rows // TILE - 1)
    meta = me.astype(jnp.int32).reshape(1)
    sources = [([(key_heads, rows, fixed(0), 0)], [(value_heads, rows, fixed(0), 0)], None)]
    for level in range(levels):
        for entry, distance in ((level, 1 << level), (levels + level, -(1 << level))):
            route = [(i, i + distance) for i in range(frames) if 0 <= i + distance < frames]
            start = lists[jnp.clip(me + distance, 0, frames - 1), entry] * TILE
            both = [lax.dynamic_slice_in_dim(a, start, TILE, 0) for a in (key_heads, value_heads)]
            both = send(jnp.concatenate(both, axis=0), route)

            def usable(meta, distance=distance):
                return (meta[0] >= distance) & (meta[0] - distance < frames)

            sources.append(([(both, TILE, fixed(0), 0)], [(both, TILE, fixed(1), 0)], usable))
    return attend(queries, meta, sources, 0, width // (2 * HD), 2, final=True)


def body_planes(queries, key_heads, value_heads, tile_lists):
    frames = 16
    rows, width = key_heads.shape
    half = width // 2
    heads = 3
    steps = half // (heads * HD)
    every = range(frames)
    meta = jnp.concatenate(
        [jnp.clip(tile_lists[0], 0, rows // TILE - 1), lax.axis_index("frame").astype(jnp.int32).reshape(1)]
    )
    up = [(i, i + 4) for i in every if i + 4 < frames]
    down = [(i, i - 4) for i in every if i - 4 >= 0]
    across = [(i, i ^ 2) for i in every]
    beside = [(i, i ^ 1) for i in every]
    far_up = [(i, i + 4) for i in range(4, 12)]
    far_down = [(i, i - 4) for i in range(4, 12)]
    off_chip = [(i, i + (1, 3, -3, -1)[i % 4]) for i in every]
    off_chip = [(i, j) for i, j in off_chip if 0 <= j < frames]
    back = [(j, i) for i, j in off_chip]

    def right(meta):
        return meta[8] % 4 >= 2

    def beside_tile(meta):
        return jnp.where(meta[8] % 2 == 1, meta[0], meta[4])

    def across_tile(meta):
        return jnp.where(right(meta), meta[1], meta[5])

    def two_there(meta):
        return jnp.where(right(meta), meta[8] + 2 < frames, meta[8] >= 2)

    def one_there(meta):
        return (meta[8] >= 1) & (meta[8] < frames - 1)

    def tile_of(array, tile, usable=None):
        return (
            [(array, TILE, tile, 0)],
            [(array, TILE, lambda meta: tile(meta) + 2, 0)],
            usable,
        )

    def pair_of(arrays, usable=None):
        return [(a, TILE, fixed(0), 0) for a in arrays], [(a, TILE, fixed(1), 0) for a in arrays], usable

    lists = send(tile_lists, back)
    packs = [pack(meta, key_heads, value_heads, n * half, half) for n in (0, 1)]
    wants = None
    carries, finals = [], []
    for n, packed in enumerate(packs):
        low = send(packed, up)
        high = send(packed, down)
        over = send(packed, across)
        next_to = send(packed, beside)
        if wants is None:
            wants, far_low, far_high, two, one = choose(meta, lists, None, low, high, over)
        else:
            far_low, far_high, two, one = choose(meta, None, wants, low, high, over)
        far_low = send(far_low, far_up)
        far_high = send(far_high, far_down)
        two = send(two, across)
        one = send(one, off_chip)
        carry = attend(
            queries,
            meta,
            [
                ([(key_heads, rows, fixed(0), n * steps)], [(value_heads, rows, fixed(0), n * steps)], None),
                tile_of(next_to, beside_tile),
            ],
            n * steps,
            steps,
            heads,
        )
        carry = attend(
            queries,
            meta,
            [
                tile_of(over, across_tile),
                tile_of(low, lambda meta: meta[2], lambda meta: meta[8] >= 4),
                tile_of(high, lambda meta: meta[6], lambda meta: meta[8] + 4 < frames),
            ],
            n * steps,
            steps,
            heads,
            carry,
        )
        carries.append(carry)
        finals.append([pair_of([two], two_there), pair_of([one], one_there), pair_of([far_low, far_high])])
    out = None
    for n in (0, 1):
        out = attend(queries, meta, finals[n], n * steps, steps, heads, carries[n], True, out)
    return out


def solution(mesh):
    body = body_planes if mesh.shape["frame"] == 16 else body_direct
    in_specs = (
        P(("groups", "frame"), None),
        P(("groups", "frame"), None),
        P(("groups", "frame"), None),
        P("frame", None),
    )
    out_specs = P(("groups", "frame"), None)
    return jax.shard_map(body, mesh=mesh, in_specs=in_specs, out_specs=out_specs, check_vma=False)
```

time: 209 us -> 91.2 us (0.44)
  the two profiles are of different devices: /device:TPU:3 before, /device:TPU:12 now
where the time goes in v2:
time: 91.2 us; the launch traced here: 89.9 us
  starting transfers between devices  35.9 us (39%)
  Pallas kernels  27.9 us (31%)
  waiting for transfers between devices  22.8 us (25%)
  local copies, waits for them, and re-layouts  2.94 us (3%)
    ppermute x17, starting transfers between devices, send(): return lax.ppermute(array, 'frame', route)  35.9 us
    ppermute x17, waiting for transfers between devices, send(): return lax.ppermute(array, 'frame', route)  22.8 us
    pallas_call x6, Pallas kernels, attend(): pl.pallas_call(functools.partial(attend_kernel, plan, heads, carry is not...  20.4 us
    pallas_call x2, Pallas kernels, choose(): pl.pallas_call(choose_again_kernel if again else choose_kernel, out_shape...  6.13 us
    unnamed x12, local copies, waits for them, and re-layouts  2.94 us
  transfers between devices with their start and end apart: 17, of which 4 were waited for; matrix products, arithmetic and copies ran while one was open for 0% of the time, Pallas kernels for 26%

profile of v2, /device:TPU:12, one launch (start us, length us, event | category | flops | bytes accessed | tf_op | source)
XLA Modules:
  0.0 89.9 jit_solution(7148330296444924177)
XLA Ops:
  0.0 0.7 copy-done.5
  0.7 0.1 pad_add_fusion.meta
  0.7 1.1 %copy-done.1 = bf16[256,1536]{1,0:T(8,128)(2,1)S(1)} copy-done((bf16[256,1536]{1,0:T(8,128)(2,1)S(1)}, bf16[256,1536]{1,0:T(8,128)(2,1)}, u32[]{:S(2)}) %copy-start.1) | copy-done | bytes 786456
  1.9 1.1 %copy-done.3 = bf16[256,1536]{1,0:T(8,128)(2,1)S(1)} copy-done((bf16[256,1536]{1,0:T(8,128)(2,1)S(1)}, bf16[256,1536]{1,0:T(8,128)(2,1)}, u32[]{:S(2)}) %copy-start.3) | copy-done | bytes 786456
  3.0 0.7 shard_map.46
  3.7 3.5 %collective-permute-start.1 = (bf16[528,768]{1,0:T(8,128)(2,1)S(1)}, bf16[528,768]{1,0:T(8,128)(2,1)S(1)}, u32[]{:S(2)}, u32[]{:S(2)}) collective-permute-start(bf16[528,768]{1,0:T(8,128)(2,1)S(1)} %shard_map.46), channel_id=1, source_target_pairs={{0,4},{1,5},{2,6},{3,7},{4,8},{5,9},{6,10},{7,11},{8,12},{9,13},{1... | collective-permute-start | bytes 2433032 | tf_op jit(solution)/shard_map/ppermute | solution.py:265
  7.2 2.4 %collective-permute-start.2 = (bf16[528,768]{1,0:T(8,128)(2,1)S(1)}, bf16[528,768]{1,0:T(8,128)(2,1)S(1)}, u32[]{:S(2)}, u32[]{:S(2)}) collective-permute-start(bf16[528,768]{1,0:T(8,128)(2,1)S(1)} %shard_map.46), channel_id=1, source_target_pairs={{4,0},{5,1},{6,2},{7,3},{8,4},{9,5},{10,6},{11,7},{12,8},{13,9},{1... | collective-permute-start | bytes 2433032 | tf_op jit(solution)/shard_map/ppermute | solution.py:265
  9.6 1.6 %collective-permute-start.3 = (bf16[528,768]{1,0:T(8,128)(2,1)S(1)}, bf16[528,768]{1,0:T(8,128)(2,1)S(1)}, u32[]{:S(2)}, u32[]{:S(2)}) collective-permute-start(bf16[528,768]{1,0:T(8,128)(2,1)S(1)} %shard_map.46), channel_id=1, source_target_pairs={{0,2},{1,3},{2,0},{3,1},{4,6},{5,7},{6,4},{7,5},{8,10},{9,11},{10,... | collective-permute-start | bytes 2433032 | tf_op jit(solution)/shard_map/ppermute | solution.py:265
  11.1 1.9 %collective-permute-start = (s32[1,8]{1,0:T(1,128)S(1)}, s32[1,8]{1,0:T(1,128)S(1)}, u32[]{:S(2)}, u32[]{:S(2)}) collective-permute-start(s32[1,8]{1,0:T(1,128)S(1)} %copy-done.5), channel_id=1, source_target_pairs={{1,0},{4,1},{2,3},{5,4},{8,5},{3,6},{6,7},{9,8},{12,9},{7,10},{10,... | collective-permute-start | bytes 104 | tf_op jit(solution)/shard_map/ppermute | solution.py:265
  13.1 0.7 shard_map.48
  13.7 12.9 %collective-permute-done.list_ref = s32[1,8]{1,0:T(1,128)S(1)} collective-permute-done((s32[1,8]{1,0:T(1,128)S(1)}, s32[1,8]{1,0:T(1,128)S(1)}, u32[]{:S(2)}, u32[]{:S(2)}) %collective-permute-start) | collective-permute-done | bytes 64 | tf_op jit(solution)/shard_map/ppermute | solution.py:265
  26.7 3.4 %collective-permute-start.4 = (bf16[528,768]{1,0:T(8,128)(2,1)S(1)}, bf16[528,768]{1,0:T(8,128)(2,1)S(1)}, u32[]{:S(2)}, u32[]{:S(2)}) collective-permute-start(bf16[528,768]{1,0:T(8,128)(2,1)S(1)} %shard_map.48), channel_id=1, source_target_pairs={{0,4},{1,5},{2,6},{3,7},{4,8},{5,9},{6,10},{7,11},{8,12},{9,13},{1... | collective-permute-start | bytes 2433032 | tf_op jit(solution)/shard_map/ppermute | solution.py:265
  30.1 2.5 %collective-permute-start.5 = (bf16[528,768]{1,0:T(8,128)(2,1)S(1)}, bf16[528,768]{1,0:T(8,128)(2,1)S(1)}, u32[]{:S(2)}, u32[]{:S(2)}) collective-permute-start(bf16[528,768]{1,0:T(8,128)(2,1)S(1)} %shard_map.48), channel_id=1, source_target_pairs={{4,0},{5,1},{6,2},{7,3},{8,4},{9,5},{10,6},{11,7},{12,8},{13,9},{1... | collective-permute-start | bytes 2433032 | tf_op jit(solution)/shard_map/ppermute | solution.py:265
  32.7 1.5 %collective-permute-start.11 = (bf16[528,768]{1,0:T(8,128)(2,1)S(1)}, bf16[528,768]{1,0:T(8,128)(2,1)S(1)}, u32[]{:S(2)}, u32[]{:S(2)}) collective-permute-start(bf16[528,768]{1,0:T(8,128)(2,1)S(1)} %shard_map.48), channel_id=1, source_target_pairs={{0,1},{1,0},{2,3},{3,2},{4,5},{5,4},{6,7},{7,6},{8,9},{9,8},{10,11... | collective-permute-start | bytes 2433032 | tf_op jit(solution)/shard_map/ppermute | solution.py:265
  34.2 3.4 %shard_map.47 = (s32[4]{0:T(128)S(1)}, bf16[256,768]{1,0:T(8,128)(2,1)S(1)}, bf16[256,768]{1,0:T(8,128)(2,1)S(1)}, bf16[256,768]{1,0:T(8,128)(2,1)S(1)}, bf16[256,768]{1,0:T(8,128)(2,1)S(1)}) custom-call(s32[9]{0:T(128)S(1)} %pad_add_fusion.meta, s32[1,8]{1,0:T(1,128)S(1)} %collective-permute-done.list_ref, ...), custom_call_target="tpu_custom_call" | custom-call | bytes 3145728 | tf_op jit(solution)/shard_map/pallas_call | solution.py:252
  37.6 1.7 %collective-permute-start.12 = (bf16[256,768]{1,0:T(8,128)(2,1)S(1)}, bf16[256,768]{1,0:T(8,128)(2,1)S(1)}, u32[]{:S(2)}, u32[]{:S(2)}) collective-permute-start(bf16[256,768]{1,0:T(8,128)(2,1)S(1)} %get-tuple-element.37), channel_id=1, source_target_pairs={{0,2},{1,3},{2,0},{3,1},{4,6},{5,7},{6,4},{7,5},{8,10},{9,11},{10,... | collective-permute-start | bytes 1179656 | tf_op jit(solution)/shard_map/ppermute | solution.py:265
  39.4 9.0 %collective-permute-done.4.low.refs_3_.refs_4_ = bf16[528,768]{1,0:T(8,128)(2,1)S(1)} collective-permute-done((bf16[528,768]{1,0:T(8,128)(2,1)S(1)}, bf16[528,768]{1,0:T(8,128)(2,1)S(1)}, u32[]{:S(2)}, u32[]{:S(2)}) %collective-permute-start.4) | collective-permute-done | bytes 811040 | tf_op jit(solution)/shard_map/ppermute | solution.py:265
  48.4 3.1 %collective-permute-start.13 = (bf16[256,768]{1,0:T(8,128)(2,1)S(1)}, bf16[256,768]{1,0:T(8,128)(2,1)S(1)}, u32[]{:S(2)}, u32[]{:S(2)}) collective-permute-start(bf16[256,768]{1,0:T(8,128)(2,1)S(1)} %get-tuple-element.38), channel_id=1, source_target_pairs={{0,1},{1,4},{3,2},{4,5},{5,8},{6,3},{7,6},{8,9},{9,12},{10,7},{11,... | collective-permute-start | bytes 1179656 | tf_op jit(solution)/shard_map/ppermute | solution.py:265
  51.5 0.6 collective-permute-done.5.high.refs_5_.refs_6_
  52.1 3.9 %collective-permute-start.14 = (bf16[256,768]{1,0:T(8,128)(2,1)S(1)}, bf16[256,768]{1,0:T(8,128)(2,1)S(1)}, u32[]{:S(2)}, u32[]{:S(2)}) collective-permute-start(bf16[256,768]{1,0:T(8,128)(2,1)S(1)} %get-tuple-element.39), channel_id=1, source_target_pairs={{4,8},{5,9},{6,10},{7,11},{8,12},{9,13},{10,14},{11,15},{20,24},{2... | collective-permute-start | bytes 1179656 | tf_op jit(solution)/shard_map/ppermute | solution.py:265
  56.0 1.9 %collective-permute-start.15 = (bf16[256,768]{1,0:T(8,128)(2,1)S(1)}, bf16[256,768]{1,0:T(8,128)(2,1)S(1)}, u32[]{:S(2)}, u32[]{:S(2)}) collective-permute-start(bf16[256,768]{1,0:T(8,128)(2,1)S(1)} %get-tuple-element.40), channel_id=1, source_target_pairs={{4,0},{5,1},{6,2},{7,3},{8,4},{9,5},{10,6},{11,7},{20,16},{21,17},... | collective-permute-start | bytes 1179656 | tf_op jit(solution)/shard_map/ppermute | solution.py:265
  58.0 2.7 %shard_map.49 = (bf16[256,768]{1,0:T(8,128)(2,1)S(1)}, bf16[256,768]{1,0:T(8,128)(2,1)S(1)}, bf16[256,768]{1,0:T(8,128)(2,1)S(1)}, bf16[256,768]{1,0:T(8,128)(2,1)S(1)}) custom-call(s32[9]{0:T(128)S(1)} %pad_add_fusion.meta, s32[4]{0:T(128)S(1)} %get-tuple-element.26.wants, bf16[528,768]{1,0:T(8,128)(2,1)S(1)} %collective-permute-done.4.low.refs_3_.refs_4_, ...), custom_call_target="tpu_custom_call" | custom-call | bytes 3145728 | tf_op jit(solution)/shard_map/pallas_call | solution.py:252
  60.7 1.9 %collective-permute-start.10 = (bf16[256,768]{1,0:T(8,128)(2,1)S(1)}, bf16[256,768]{1,0:T(8,128)(2,1)S(1)}, u32[]{:S(2)}, u32[]{:S(2)}) collective-permute-start(bf16[256,768]{1,0:T(8,128)(2,1)S(1)} %get-tuple-element.30), channel_id=1, source_target_pairs={{4,0},{5,1},{6,2},{7,3},{8,4},{9,5},{10,6},{11,7},{20,16},{21,17},... | collective-permute-start | bytes 1179656 | tf_op jit(solution)/shard_map/ppermute | solution.py:265
  62.7 2.1 %collective-permute-start.8 = (bf16[256,768]{1,0:T(8,128)(2,1)S(1)}, bf16[256,768]{1,0:T(8,128)(2,1)S(1)}, u32[]{:S(2)}, u32[]{:S(2)}) collective-permute-start(bf16[256,768]{1,0:T(8,128)(2,1)S(1)} %get-tuple-element.28), channel_id=1, source_target_pairs={{0,1},{1,4},{3,2},{4,5},{5,8},{6,3},{7,6},{8,9},{9,12},{10,7},{11,... | collective-permute-start | bytes 1179656 | tf_op jit(solution)/shard_map/ppermute | solution.py:265
  64.8 0.2 collective-permute-done.14.refs_5_.refs_7_
  65.0 4.4 %collective-permute-start.9 = (bf16[256,768]{1,0:T(8,128)(2,1)S(1)}, bf16[256,768]{1,0:T(8,128)(2,1)S(1)}, u32[]{:S(2)}, u32[]{:S(2)}) collective-permute-start(bf16[256,768]{1,0:T(8,128)(2,1)S(1)} %get-tuple-element.29), channel_id=1, source_target_pairs={{4,8},{5,9},{6,10},{7,11},{8,12},{9,13},{10,14},{11,15},{20,24},{2... | collective-permute-start | bytes 1179656 | tf_op jit(solution)/shard_map/ppermute | solution.py:265
  69.4 3.0 %shard_map.52 = (f32[256,768]{1,0:T(8,128)S(1)}, f32[256,768]{1,0:T(8,128)S(1)}, f32[256,768]{1,0:T(8,128)S(1)}) custom-call(s32[9]{0:T(128)S(1)} %pad_add_fusion.meta, bf16[256,1536]{1,0:T(8,128)(2,1)S(1)} %copy-done, bf16[256,1536]{1,0:T(8,128)(2,1)S(1)} %copy-done.2, bf16[256,1536]{1,0:T(8,128)(2,1)S(1)} %copy-done.4, ...), custom_call_target="tpu_custom_call" | custom-call | flops 301989888 | bytes 1572864 | tf_op jit(solution)/shard_map/pallas_call | solution.py:120
  72.4 3.0 %shard_map.50 = (f32[256,768]{1,0:T(8,128)S(1)}, f32[256,768]{1,0:T(8,128)S(1)}, f32[256,768]{1,0:T(8,128)S(1)}) custom-call(s32[9]{0:T(128)S(1)} %pad_add_fusion.meta, bf16[256,1536]{1,0:T(8,128)(2,1)S(1)} %copy-done, bf16[256,1536]{1,0:T(8,128)(2,1)S(1)} %copy-done.2, bf16[256,1536]{1,0:T(8,128)(2,1)S(1)} %copy-done.4, ...), custom_call_target="tpu_custom_call" | custom-call | flops 301989888 | bytes 1572864 | tf_op jit(solution)/shard_map/pallas_call | solution.py:120
  75.5 3.5 %shard_map.53 = (f32[256,768]{1,0:T(8,128)S(1)}, f32[256,768]{1,0:T(8,128)S(1)}, f32[256,768]{1,0:T(8,128)S(1)}) custom-call(s32[9]{0:T(128)S(1)} %pad_add_fusion.meta, bf16[256,1536]{1,0:T(8,128)(2,1)S(1)} %copy-done, bf16[528,768]{1,0:T(8,128)(2,1)S(1)} %collective-permute-done.3.over.refs_1_.refs_2_, ...), custom_call_target="tpu_custom_call" | custom-call | flops 301989888 | bytes 1572864 | tf_op jit(solution)/shard_map/pallas_call | solution.py:120
  79.0 3.5 %shard_map.51 = (f32[256,768]{1,0:T(8,128)S(1)}, f32[256,768]{1,0:T(8,128)S(1)}, f32[256,768]{1,0:T(8,128)S(1)}) custom-call(s32[9]{0:T(128)S(1)} %pad_add_fusion.meta, bf16[256,1536]{1,0:T(8,128)(2,1)S(1)} %copy-done, bf16[528,768]{1,0:T(8,128)(2,1)S(1)} %collective-permute-done.6.over.refs_1_.refs_2_, ...), custom_call_target="tpu_custom_call" | custom-call | flops 301989888 | bytes 1572864 | tf_op jit(solution)/shard_map/pallas_call | solution.py:120
  82.5 3.6 %shard_map.54.refs_12_ = bf16[256,1536]{1,0:T(8,128)(2,1)} custom-call(s32[9]{0:T(128)S(1)} %pad_add_fusion.meta, bf16[256,1536]{1,0:T(8,128)(2,1)S(1)} %copy-done, bf16[256,768]{1,0:T(8,128)(2,1)S(1)} %collective-permute-done.12.refs_1_.refs_2_, bf16[256,768]{1,0:T(8,128)(2,1)S(1)} %collective-permute-done.12.refs_1_.refs_2_, ...), custom_call_target="tpu_custom_call" | custom-call | flops 301989888 | bytes 1572864 | tf_op jit(solution)/shard_map/pallas_call | solution.py:120
  86.2 3.7 %shard_map.55 = bf16[256,1536]{1,0:T(8,128)(2,1)} custom-call(s32[9]{0:T(128)S(1)} %pad_add_fusion.meta, bf16[256,1536]{1,0:T(8,128)(2,1)S(1)} %copy-done, bf16[256,768]{1,0:T(8,128)(2,1)S(1)} %collective-permute-done.7.refs_1_.refs_2_, bf16[256,768]{1,0:T(8,128)(2,1)S(1)} %collective-permute-done.7.refs_1_.refs_2_, ...), custom_call_target="tpu_custom_call", output_to_operand_aliasing={{}: (13, {})} | custom-call | flops 301989888 | bytes 1572864 | tf_op jit(solution)/shard_map/pallas_call | solution.py:120
  (26 shorter events, 0.2 us)
Async XLA Ops:
  0.0 0.7 copy-start.5
  0.7 1.1 %copy-start.1 = (bf16[256,1536]{1,0:T(8,128)(2,1)S(1)}, bf16[256,1536]{1,0:T(8,128)(2,1)}, u32[]{:S(2)}) copy-start(bf16[256,1536]{1,0:T(8,128)(2,1)} %refs_1_.3) | copy-start | bytes 2359300
  1.9 1.1 %copy-start.3 = (bf16[256,1536]{1,0:T(8,128)(2,1)S(1)}, bf16[256,1536]{1,0:T(8,128)(2,1)}, u32[]{:S(2)}) copy-start(bf16[256,1536]{1,0:T(8,128)(2,1)} %refs_2_.3) | copy-start | bytes 2359300
  3.7 26.4 %collective-permute-start.1 = (bf16[528,768]{1,0:T(8,128)(2,1)S(1)}, bf16[528,768]{1,0:T(8,128)(2,1)S(1)}, u32[]{:S(2)}, u32[]{:S(2)}) collective-permute-start(bf16[528,768]{1,0:T(8,128)(2,1)S(1)} %shard_map.46), channel_id=1, source_target_pairs={{0,4},{1,5},{2,6},{3,7},{4,8},{5,9},{6,10},{7,11},{8,12},{9,13},{1... | collective-permute-start | bytes 2433032 | tf_op jit(solution)/shard_map/ppermute | solution.py:265
  7.2 25.4 %collective-permute-start.2 = (bf16[528,768]{1,0:T(8,128)(2,1)S(1)}, bf16[528,768]{1,0:T(8,128)(2,1)S(1)}, u32[]{:S(2)}, u32[]{:S(2)}) collective-permute-start(bf16[528,768]{1,0:T(8,128)(2,1)S(1)} %shard_map.46), channel_id=1, source_target_pairs={{4,0},{5,1},{6,2},{7,3},{8,4},{9,5},{10,6},{11,7},{12,8},{13,9},{1... | collective-permute-start | bytes 2433032 | tf_op jit(solution)/shard_map/ppermute | solution.py:265
  9.6 23.1 %collective-permute-start.3 = (bf16[528,768]{1,0:T(8,128)(2,1)S(1)}, bf16[528,768]{1,0:T(8,128)(2,1)S(1)}, u32[]{:S(2)}, u32[]{:S(2)}) collective-permute-start(bf16[528,768]{1,0:T(8,128)(2,1)S(1)} %shard_map.46), channel_id=1, source_target_pairs={{0,2},{1,3},{2,0},{3,1},{4,6},{5,7},{6,4},{7,5},{8,10},{9,11},{10,... | collective-permute-start | bytes 2433032 | tf_op jit(solution)/shard_map/ppermute | solution.py:265
  11.1 26.5 %collective-permute-start.16 = (bf16[528,768]{1,0:T(8,128)(2,1)S(1)}, bf16[528,768]{1,0:T(8,128)(2,1)S(1)}, u32[]{:S(2)}, u32[]{:S(2)}) collective-permute-start(bf16[528,768]{1,0:T(8,128)(2,1)S(1)} %shard_map.46), channel_id=1, source_target_pairs={{0,1},{1,0},{2,3},{3,2},{4,5},{5,4},{6,7},{7,6},{8,9},{9,8},{10,11... | collective-permute-start | bytes 2433032 | tf_op jit(solution)/shard_map/ppermute | solution.py:265
  11.1 15.5 %collective-permute-start = (s32[1,8]{1,0:T(1,128)S(1)}, s32[1,8]{1,0:T(1,128)S(1)}, u32[]{:S(2)}, u32[]{:S(2)}) collective-permute-start(s32[1,8]{1,0:T(1,128)S(1)} %copy-done.5), channel_id=1, source_target_pairs={{1,0},{4,1},{2,3},{5,4},{8,5},{3,6},{6,7},{9,8},{12,9},{7,10},{10,... | collective-permute-start | bytes 104 | tf_op jit(solution)/shard_map/ppermute | solution.py:265
  26.7 21.7 %collective-permute-start.4 = (bf16[528,768]{1,0:T(8,128)(2,1)S(1)}, bf16[528,768]{1,0:T(8,128)(2,1)S(1)}, u32[]{:S(2)}, u32[]{:S(2)}) collective-permute-start(bf16[528,768]{1,0:T(8,128)(2,1)S(1)} %shard_map.48), channel_id=1, source_target_pairs={{0,4},{1,5},{2,6},{3,7},{4,8},{5,9},{6,10},{7,11},{8,12},{9,13},{1... | collective-permute-start | bytes 2433032 | tf_op jit(solution)/shard_map/ppermute | solution.py:265
  30.1 22.0 %collective-permute-start.5 = (bf16[528,768]{1,0:T(8,128)(2,1)S(1)}, bf16[528,768]{1,0:T(8,128)(2,1)S(1)}, u32[]{:S(2)}, u32[]{:S(2)}) collective-permute-start(bf16[528,768]{1,0:T(8,128)(2,1)S(1)} %shard_map.48), channel_id=1, source_target_pairs={{4,0},{5,1},{6,2},{7,3},{8,4},{9,5},{10,6},{11,7},{12,8},{13,9},{1... | collective-permute-start | bytes 2433032 | tf_op jit(solution)/shard_map/ppermute | solution.py:265
  32.6 23.4 %collective-permute-start.6 = (bf16[528,768]{1,0:T(8,128)(2,1)S(1)}, bf16[528,768]{1,0:T(8,128)(2,1)S(1)}, u32[]{:S(2)}, u32[]{:S(2)}) collective-permute-start(bf16[528,768]{1,0:T(8,128)(2,1)S(1)} %shard_map.48), channel_id=1, source_target_pairs={{0,2},{1,3},{2,0},{3,1},{4,6},{5,7},{6,4},{7,5},{8,10},{9,11},{10,... | collective-permute-start | bytes 2433032 | tf_op jit(solution)/shard_map/ppermute | solution.py:265
  32.7 28.0 %collective-permute-start.11 = (bf16[528,768]{1,0:T(8,128)(2,1)S(1)}, bf16[528,768]{1,0:T(8,128)(2,1)S(1)}, u32[]{:S(2)}, u32[]{:S(2)}) collective-permute-start(bf16[528,768]{1,0:T(8,128)(2,1)S(1)} %shard_map.48), channel_id=1, source_target_pairs={{0,1},{1,0},{2,3},{3,2},{4,5},{5,4},{6,7},{7,6},{8,9},{9,8},{10,11... | collective-permute-start | bytes 2433032 | tf_op jit(solution)/shard_map/ppermute | solution.py:265
  37.6 25.0 %collective-permute-start.12 = (bf16[256,768]{1,0:T(8,128)(2,1)S(1)}, bf16[256,768]{1,0:T(8,128)(2,1)S(1)}, u32[]{:S(2)}, u32[]{:S(2)}) collective-permute-start(bf16[256,768]{1,0:T(8,128)(2,1)S(1)} %get-tuple-element.37), channel_id=1, source_target_pairs={{0,2},{1,3},{2,0},{3,1},{4,6},{5,7},{6,4},{7,5},{8,10},{9,11},{10,... | collective-permute-start | bytes 1179656 | tf_op jit(solution)/shard_map/ppermute | solution.py:265
  48.4 14.3 %collective-permute-start.13 = (bf16[256,768]{1,0:T(8,128)(2,1)S(1)}, bf16[256,768]{1,0:T(8,128)(2,1)S(1)}, u32[]{:S(2)}, u32[]{:S(2)}) collective-permute-start(bf16[256,768]{1,0:T(8,128)(2,1)S(1)} %get-tuple-element.38), channel_id=1, source_target_pairs={{0,1},{1,4},{3,2},{4,5},{5,8},{6,3},{7,6},{8,9},{9,12},{10,7},{11,... | collective-permute-start | bytes 1179656 | tf_op jit(solution)/shard_map/ppermute | solution.py:265
  52.1 12.8 %collective-permute-start.14 = (bf16[256,768]{1,0:T(8,128)(2,1)S(1)}, bf16[256,768]{1,0:T(8,128)(2,1)S(1)}, u32[]{:S(2)}, u32[]{:S(2)}) collective-permute-start(bf16[256,768]{1,0:T(8,128)(2,1)S(1)} %get-tuple-element.39), channel_id=1, source_target_pairs={{4,8},{5,9},{6,10},{7,11},{8,12},{9,13},{10,14},{11,15},{20,24},{2... | collective-permute-start | bytes 1179656 | tf_op jit(solution)/shard_map/ppermute | solution.py:265
  56.0 26.5 %collective-permute-start.15 = (bf16[256,768]{1,0:T(8,128)(2,1)S(1)}, bf16[256,768]{1,0:T(8,128)(2,1)S(1)}, u32[]{:S(2)}, u32[]{:S(2)}) collective-permute-start(bf16[256,768]{1,0:T(8,128)(2,1)S(1)} %get-tuple-element.40), channel_id=1, source_target_pairs={{4,0},{5,1},{6,2},{7,3},{8,4},{9,5},{10,6},{11,7},{20,16},{21,17},... | collective-permute-start | bytes 1179656 | tf_op jit(solution)/shard_map/ppermute | solution.py:265
  57.9 11.4 %copy-start = (bf16[256,1536]{1,0:T(8,128)(2,1)S(1)}, bf16[256,1536]{1,0:T(8,128)(2,1)}, u32[]{:S(2)}) copy-start(bf16[256,1536]{1,0:T(8,128)(2,1)} %refs_0_.11) | copy-start | bytes 2359300
  57.9 11.4 %copy-start.2 = (bf16[256,1536]{1,0:T(8,128)(2,1)S(1)}, bf16[256,1536]{1,0:T(8,128)(2,1)}, u32[]{:S(2)}) copy-start(bf16[256,1536]{1,0:T(8,128)(2,1)} %refs_1_.3) | copy-start | bytes 2359300
  57.9 11.4 %copy-start.4 = (bf16[256,1536]{1,0:T(8,128)(2,1)S(1)}, bf16[256,1536]{1,0:T(8,128)(2,1)}, u32[]{:S(2)}) copy-start(bf16[256,1536]{1,0:T(8,128)(2,1)} %refs_2_.3) | copy-start | bytes 2359300
  60.7 25.5 %collective-permute-start.10 = (bf16[256,768]{1,0:T(8,128)(2,1)S(1)}, bf16[256,768]{1,0:T(8,128)(2,1)S(1)}, u32[]{:S(2)}, u32[]{:S(2)}) collective-permute-start(bf16[256,768]{1,0:T(8,128)(2,1)S(1)} %get-tuple-element.30), channel_id=1, source_target_pairs={{4,0},{5,1},{6,2},{7,3},{8,4},{9,5},{10,6},{11,7},{20,16},{21,17},... | collective-permute-start | bytes 1179656 | tf_op jit(solution)/shard_map/ppermute | solution.py:265
  62.6 23.6 %collective-permute-start.7 = (bf16[256,768]{1,0:T(8,128)(2,1)S(1)}, bf16[256,768]{1,0:T(8,128)(2,1)S(1)}, u32[]{:S(2)}, u32[]{:S(2)}) collective-permute-start(bf16[256,768]{1,0:T(8,128)(2,1)S(1)} %get-tuple-element.27), channel_id=1, source_target_pairs={{0,2},{1,3},{2,0},{3,1},{4,6},{5,7},{6,4},{7,5},{8,10},{9,11},{10,... | collective-permute-start | bytes 1179656 | tf_op jit(solution)/shard_map/ppermute | solution.py:265
  62.7 23.5 %collective-permute-start.8 = (bf16[256,768]{1,0:T(8,128)(2,1)S(1)}, bf16[256,768]{1,0:T(8,128)(2,1)S(1)}, u32[]{:S(2)}, u32[]{:S(2)}) collective-permute-start(bf16[256,768]{1,0:T(8,128)(2,1)S(1)} %get-tuple-element.28), channel_id=1, source_target_pairs={{0,1},{1,4},{3,2},{4,5},{5,8},{6,3},{7,6},{8,9},{9,12},{10,7},{11,... | collective-permute-start | bytes 1179656 | tf_op jit(solution)/shard_map/ppermute | solution.py:265
  65.0 21.2 %collective-permute-start.9 = (bf16[256,768]{1,0:T(8,128)(2,1)S(1)}, bf16[256,768]{1,0:T(8,128)(2,1)S(1)}, u32[]{:S(2)}, u32[]{:S(2)}) collective-permute-start(bf16[256,768]{1,0:T(8,128)(2,1)S(1)} %get-tuple-element.29), channel_id=1, source_target_pairs={{4,8},{5,9},{6,10},{7,11},{8,12},{9,13},{10,14},{11,15},{20,24},{2... | collective-permute-start | bytes 1179656 | tf_op jit(solution)/shard_map/ppermute | solution.py:265

commit v3 on v2

--- a/solution.py
+++ b/solution.py
@@ -41,15 +41,16 @@
     narrow = [s for s in sources if s[0][0].shape[0] == TILE]
     groups += [narrow[at : at + 2] for at in range(0, len(narrow), 2)]
 
-    for head in range(heads):
-        cols = slice(head * HD, (head + 1) * HD)
-        query = q_ref[:, cols]
-        scores, values = [], []
+    def columns(head):
+        return slice(head * HD, (head + 1) * HD)
+
+    def scores_of(head):
+        cols = columns(head)
+        scores = []
         for group in groups:
             key = jnp.concatenate([load(k, cols) for k, _, _ in group], axis=0)
-            values.append(jnp.concatenate([load(v, cols) for _, v, _ in group], axis=0))
             part = lax.dot_general(
-                query, key, (((1,), (1,)), ((), ())), preferred_element_type=jnp.float32
+                q_ref[:, cols], key, (((1,), (1,)), ((), ())), preferred_element_type=jnp.float32
             )
             pieces = []
             at = 0
@@ -59,21 +60,30 @@
                     pieces.append(piece if bias is None else piece + bias)
                     at += TILE
             scores.append(pieces)
+        return scores
+
+    def weigh(head, scores):
         peak = functools.reduce(jnp.maximum, [piece for pieces in scores for piece in pieces])
         peak = jnp.broadcast_to(jnp.max(peak, axis=1, keepdims=True), (rows, HD))
+        if carry_in:
+            peak = jnp.maximum(max_in[:, columns(head)], peak)
+        weights = [
+            jnp.concatenate([jnp.exp2(piece - peak).astype(jnp.bfloat16) for piece in pieces], axis=1)
+            for pieces in scores
+        ]
+        return peak, weights
+
+    def add_up(head, peak, weights):
+        cols = columns(head)
         acc = total = None
         if carry_in:
-            old = max_in[:, cols]
-            peak = jnp.maximum(old, peak)
-            shrink = jnp.exp2(old - peak)
+            shrink = jnp.exp2(max_in[:, cols] - peak)
             acc = acc_in[:, cols] * shrink
             total = sum_in[:, cols] * shrink
-        for pieces, value in zip(scores, values):
-            weight = [jnp.exp2(piece - peak).astype(jnp.bfloat16) for piece in pieces]
+        for group, weight in zip(groups, weights):
+            value = jnp.concatenate([load(v, cols) for _, v, _ in group], axis=0)
             both = jnp.concatenate([value, jnp.ones_like(value)], axis=1)
-            added = jnp.dot(
-                jnp.concatenate(weight, axis=1), both, preferred_element_type=jnp.float32
-            )
+            added = jnp.dot(weight, both, preferred_element_type=jnp.float32)
             acc = added[:, :HD] if acc is None else acc + added[:, :HD]
             total = added[:, HD:] if total is None else total + added[:, HD:]
         if final:
@@ -83,8 +93,19 @@
             outs[1][:, cols] = total
             outs[2][:, cols] = peak
 
-
-def attend(queries, meta, sources, first, steps, heads, carry=None, final=False, into=None):
+    scores = scores_of(0)
+    last = None
+    for head in range(heads):
+        following = scores_of(head + 1) if head + 1 < heads else None
+        weighed = weigh(head, scores)
+        if last is not None:
+            add_up(*last)
+        last = (head, *weighed)
+        scores = following
+    add_up(*last)
+
+
+def attend(queries, meta, sources, first, steps, heads, carry=None, final=False, into=None, held=0):
     rows, width = queries.shape
     block = heads * HD
 
@@ -104,7 +125,7 @@
         plan.append((len(keys), usable))
     if carry is not None:
         operands += list(carry)
-        specs += [spec(rows, zero, 0)] * 3
+        specs += [spec(rows, zero, held)] * 3
     aliases = {}
     if final:
         out_shape = jax.ShapeDtypeStruct((rows, width), jnp.bfloat16)
@@ -133,7 +154,8 @@
     )(meta, *operands)
 
 
-def pack_kernel(first, meta, k_ref, v_ref, out_ref, note, sems):
+def pack_kernel(first, meta, k_ref, v_ref, *refs):
+    out_ref, note, sems = refs[-3:]
     rows = k_ref.shape[0]
     width = out_ref.shape[1]
     copies = [
@@ -156,13 +178,14 @@
     last.wait()
 
 
-def pack(meta, keys, values, first, width):
+def pack(meta, keys, values, first, width, after):
     rows = keys.shape[0]
     whole = pl.BlockSpec(memory_space=pl.ANY)
+    source = pl.BlockSpec(memory_space=pltpu.HBM)
     return pl.pallas_call(
         functools.partial(pack_kernel, first),
         out_shape=jax.ShapeDtypeStruct((2 * rows + NOTE_ROWS, width), jnp.bfloat16),
-        in_specs=[pl.BlockSpec(memory_space=pltpu.SMEM), whole, whole],
+        in_specs=[pl.BlockSpec(memory_space=pltpu.SMEM), source, source] + [whole] * len(after),
         out_specs=whole,
         scratch_shapes=[
             pltpu.VMEM((NOTE_ROWS, width), jnp.bfloat16),
@@ -170,50 +193,18 @@
         ],
         compiler_params=pltpu.CompilerParams(vmem_limit_bytes=VMEM_LIMIT),
         cost_estimate=pl.CostEstimate(flops=0, bytes_accessed=8 * rows * width, transcendentals=0),
-    )(meta, keys, values)
-
-
-def choose_kernel(meta, list_ref, low, high, over, wants, far_up, far_down, two, one, notes, sems):
+    )(meta, keys, values, *after)
+
+
+def choose_kernel(meta, far_list, one_list, own, low, high, over, *refs):
+    far, two, one, note, sems = refs[-5:]
     rows = 2 * TILE
-    spot = meta[8] % 4
+    spot, plane = meta[8] % 4, meta[8] // 4
     right = spot >= 2
-    reads = [
-        pltpu.make_async_copy(
-            ref.at[pl.ds(2 * rows, NOTE_ROWS), pl.ds(0, HD)], notes.at[n], sems.at[n]
-        )
-        for n, ref in enumerate((low, high, over))
-    ]
-    for read in reads:
-        read.start()
-    for read in reads:
-        read.wait()
-
-    def entry(n, at):
-        shape = notes.shape[1:]
-        here = (lax.broadcasted_iota(jnp.int32, shape, 1) == at) & (
-            lax.broadcasted_iota(jnp.int32, shape, 0) == 0
-        )
-        value = jnp.sum(jnp.where(here, notes[n].astype(jnp.float32), 0.0))
-        return jnp.clip(value.astype(jnp.int32), 0, 1)
-
-    up_tile = entry(1, 3)
-    down_tile = entry(0, 7)
-    two_tile = entry(2, jnp.where(right, 1, 5))
-    one_tile = jnp.clip(list_ref[0, jnp.where(spot % 2 == 0, 4, 0)], 0, 1)
-    wants[0] = up_tile
-    wants[1] = down_tile
-    wants[2] = two_tile
-    wants[3] = one_tile
-    copy_tiles(right, up_tile, down_tile, two_tile, one_tile, low, high, over, far_up, far_down, two, one, sems)
-
-
-def choose_again_kernel(meta, wants, low, high, over, far_up, far_down, two, one, sems):
-    right = meta[8] % 4 >= 2
-    copy_tiles(right, wants[0], wants[1], wants[2], wants[3], low, high, over, far_up, far_down, two, one, sems)
-
-
-def copy_tiles(right, up_tile, down_tile, two_tile, one_tile, low, high, over, far_up, far_down, two, one, sems):
-    rows = 2 * TILE
+    read = pltpu.make_async_copy(
+        over.at[pl.ds(2 * rows, NOTE_ROWS), pl.ds(0, HD)], note, sems.at[6]
+    )
+    read.start()
 
     def copies(src, tile, dst, sem):
         start = pl.multiple_of(tile * TILE, TILE)
@@ -224,41 +215,47 @@
             for n in (0, 1)
         ]
 
-    always = copies(low, up_tile, far_up, 3) + copies(high, down_tile, far_down, 5) + copies(over, one_tile, one, 7)
-    for copy in always:
+    def start_if(condition, *args):
+        @pl.when(condition)
+        def _():
+            for copy in copies(*args):
+                copy.start()
+
+    far_tile = jnp.clip(far_list[0, jnp.where(plane % 2 == 0, 3, 7)], 0, 1)
+    start_if((plane == 0) | (plane == 3), own, far_tile, far, 0)
+    start_if(plane == 1, high, far_tile, far, 0)
+    start_if(plane == 2, low, far_tile, far, 0)
+    one_tile = jnp.clip(one_list[0, jnp.where(spot % 2 == 0, 4, 0)], 0, 1)
+    for copy in copies(over, one_tile, one, 2):
         copy.start()
-
-    @pl.when(right)
-    def _():
-        for copy in copies(low, two_tile, two, 9):
-            copy.start()
-
-    @pl.when(jnp.logical_not(right))
-    def _():
-        for copy in copies(high, two_tile, two, 9):
-            copy.start()
-
-    for copy in always + copies(low, two_tile, two, 9):
+    read.wait()
+    here = (lax.broadcasted_iota(jnp.int32, note.shape, 1) == jnp.where(right, 1, 5)) & (
+        lax.broadcasted_iota(jnp.int32, note.shape, 0) == 0
+    )
+    two_tile = jnp.sum(jnp.where(here, note[...].astype(jnp.float32), 0.0))
+    two_tile = jnp.clip(two_tile.astype(jnp.int32), 0, 1)
+    start_if(right, low, two_tile, two, 4)
+    start_if(jnp.logical_not(right), high, two_tile, two, 4)
+    for copy in copies(own, far_tile, far, 0) + copies(over, one_tile, one, 2) + copies(low, two_tile, two, 4):
         copy.wait()
 
 
-def choose(meta, lists, wants, low, high, over):
+def choose(meta, far_list, one_list, own, low, high, over, after):
     width = low.shape[1]
     scalar = pl.BlockSpec(memory_space=pltpu.SMEM)
     whole = pl.BlockSpec(memory_space=pl.ANY)
-    sent = jax.ShapeDtypeStruct((2 * TILE, width), jnp.bfloat16)
-    again = wants is not None
-    outs = ([] if again else [jax.ShapeDtypeStruct((4,), jnp.int32)]) + [sent] * 4
     return pl.pallas_call(
-        choose_again_kernel if again else choose_kernel,
-        out_shape=outs,
-        in_specs=[scalar, scalar] + [whole] * 3,
-        out_specs=([] if again else [scalar]) + [whole] * 4,
-        scratch_shapes=([] if again else [pltpu.VMEM((3, NOTE_ROWS, HD), jnp.bfloat16)])
-        + [pltpu.SemaphoreType.DMA((11,))],
+        choose_kernel,
+        out_shape=[jax.ShapeDtypeStruct((2 * TILE, width), jnp.bfloat16)] * 3,
+        in_specs=[scalar] * 3 + [whole] * (4 + len(after)),
+        out_specs=[whole] * 3,
+        scratch_shapes=[
+            pltpu.VMEM((NOTE_ROWS, HD), jnp.bfloat16),
+            pltpu.SemaphoreType.DMA((7,)),
+        ],
         compiler_params=pltpu.CompilerParams(vmem_limit_bytes=VMEM_LIMIT),
-        cost_estimate=pl.CostEstimate(flops=0, bytes_accessed=32 * TILE * width, transcendentals=0),
-    )(meta, wants if again else lists, low, high, over)
+        cost_estimate=pl.CostEstimate(flops=0, bytes_accessed=24 * TILE * width, transcendentals=0),
+    )(meta, far_list, one_list, own, low, high, over, *after)
 
 
 def send(array, route):
@@ -305,11 +302,9 @@
     down = [(i, i - 4) for i in every if i - 4 >= 0]
     across = [(i, i ^ 2) for i in every]
     beside = [(i, i ^ 1) for i in every]
-    far_up = [(i, i + 4) for i in range(4, 12)]
-    far_down = [(i, i - 4) for i in range(4, 12)]
+    far = [(i, i + (8, -4, 4, -8)[i // 4]) for i in every]
     off_chip = [(i, i + (1, 3, -3, -1)[i % 4]) for i in every]
     off_chip = [(i, j) for i, j in off_chip if 0 <= j < frames]
-    back = [(j, i) for i, j in off_chip]
 
     def right(meta):
         return meta[8] % 4 >= 2
@@ -336,38 +331,33 @@
     def pair_of(arrays, usable=None):
         return [(a, TILE, fixed(0), 0) for a in arrays], [(a, TILE, fixed(1), 0) for a in arrays], usable
 
-    lists = send(tile_lists, back)
-    packs = [pack(meta, key_heads, value_heads, n * half, half) for n in (0, 1)]
-    wants = None
-    carries, finals = [], []
-    for n, packed in enumerate(packs):
+    def whole_of(n):
+        return [(key_heads, rows, fixed(0), n)], [(value_heads, rows, fixed(0), n)], None
+
+    def back(route):
+        return [(j, i) for i, j in route]
+
+    far_list = send(tile_lists, back(far))
+    one_list = send(tile_lists, back(off_chip))
+    first = pack(meta, key_heads, value_heads, 0, half, [far_list, one_list])
+    begun = attend(queries, meta, [whole_of(0)], 0, 2 * steps, heads)
+    second = pack(meta, key_heads, value_heads, half, half, [begun[0]])
+    after = []
+    middles, finals = [], []
+    for n, packed in enumerate((first, second)):
         low = send(packed, up)
         high = send(packed, down)
         over = send(packed, across)
         next_to = send(packed, beside)
-        if wants is None:
-            wants, far_low, far_high, two, one = choose(meta, lists, None, low, high, over)
-        else:
-            far_low, far_high, two, one = choose(meta, None, wants, low, high, over)
-        far_low = send(far_low, far_up)
-        far_high = send(far_high, far_down)
-        two = send(two, across)
-        one = send(one, off_chip)
-        carry = attend(
+        to_far, to_two, to_one = choose(meta, far_list, one_list, packed, low, high, over, after)
+        from_far = send(to_far, far)
+        two = send(to_two, across)
+        one = send(to_one, off_chip)
+        middle = attend(
             queries,
             meta,
             [
-                ([(key_heads, rows, fixed(0), n * steps)], [(value_heads, rows, fixed(0), n * steps)], None),
                 tile_of(next_to, beside_tile),
-            ],
-            n * steps,
-            steps,
-            heads,
-        )
-        carry = attend(
-            queries,
-            meta,
-            [
                 tile_of(over, across_tile),
                 tile_of(low, lambda meta: meta[2], lambda meta: meta[8] >= 4),
                 tile_of(high, lambda meta: meta[6], lambda meta: meta[8] + 4 < frames),
@@ -375,13 +365,15 @@
             n * steps,
             steps,
             heads,
-            carry,
+            begun,
+            held=n * steps,
         )
-        carries.append(carry)
-        finals.append([pair_of([two], two_there), pair_of([one], one_there), pair_of([far_low, far_high])])
+        after = [middle[0]]
+        middles.append(middle)
+        finals.append([pair_of([two], two_there), pair_of([one], one_there), pair_of([from_far])])
     out = None
     for n in (0, 1):
-        out = attend(queries, meta, finals[n], n * steps, steps, heads, carries[n], True, out)
+        out = attend(queries, meta, finals[n], n * steps, steps, heads, middles[n], True, out)
     return out
 
 

time: 91.2 us -> 87.3 us (0.957)
  the two profiles are of different devices: /device:TPU:12 before, /device:TPU:1 now
where the time goes in v3:
time: 87.3 us; the launch traced here: 87 us
  starting transfers between devices  31.8 us (36%)
  waiting for transfers between devices  30.1 us (34%)
  Pallas kernels  21.9 us (25%)
  local copies, waits for them, and re-layouts  2.27 us (3%)
    ppermute x16, starting transfers between devices, send(): return lax.ppermute(array, 'frame', route)  31.8 us
    ppermute x16, waiting for transfers between devices, send(): return lax.ppermute(array, 'frame', route)  30.1 us
    pallas_call x5, Pallas kernels, attend(): pl.pallas_call(functools.partial(attend_kernel, plan, heads, carry is not...  16 us
    pallas_call x2, Pallas kernels, choose(): pl.pallas_call(choose_kernel, out_shape=[jax.ShapeDtypeStruct((2 * TILE,...  4.63 us
    unnamed x6, local copies, waits for them, and re-layouts  2.27 us
  transfers between devices with their start and end apart: 16, of which 7 were waited for; matrix products, arithmetic and copies ran while one was open for 1% of the time, Pallas kernels for 21%

profile of v3, /device:TPU:1, one launch (start us, length us, event | category | flops | bytes accessed | tf_op | source)
XLA Modules:
  0.0 87.0 jit_solution(8729487514699917244)
XLA Ops:
  0.0 2.1 %collective-permute-start.1 = (s32[1,8]{1,0:T(1,128)}, s32[1,8]{1,0:T(1,128)S(1)}, u32[]{:S(2)}, u32[]{:S(2)}) collective-permute-start(s32[1,8]{1,0:T(1,128)} %param.7), channel_id=1, source_target_pairs={{1,0},{4,1},{2,3},{5,4},{8,5},{3,6},{6,7},{9,8},{12,9},{7,10},{10,... | collective-permute-start | bytes 104 | tf_op jit(solution)/shard_map/ppermute | solution.py:262
  2.1 2.8 %collective-permute-start = (s32[1,8]{1,0:T(1,128)}, s32[1,8]{1,0:T(1,128)S(1)}, u32[]{:S(2)}, u32[]{:S(2)}) collective-permute-start(s32[1,8]{1,0:T(1,128)} %param.7), channel_id=1, source_target_pairs={{8,0},{9,1},{10,2},{11,3},{0,4},{1,5},{2,6},{3,7},{12,8},{13,9},{1... | collective-permute-start | bytes 104 | tf_op jit(solution)/shard_map/ppermute | solution.py:262
  4.9 0.7 clamp_bitcast_fusion
  6.1 0.9 %collective-permute-done.refs_0_.far_list = s32[1,8]{1,0:T(1,128)S(1)} collective-permute-done((s32[1,8]{1,0:T(1,128)}, s32[1,8]{1,0:T(1,128)S(1)}, u32[]{:S(2)}, u32[]{:S(2)}) %collective-permute-start) | collective-permute-done | bytes 64 | tf_op jit(solution)/shard_map/ppermute | solution.py:262
  7.0 1.1 %copy-done.1 = bf16[256,1536]{1,0:T(8,128)(2,1)S(1)} copy-done((bf16[256,1536]{1,0:T(8,128)(2,1)S(1)}, bf16[256,1536]{1,0:T(8,128)(2,1)}, u32[]{:S(2)}) %copy-start.1) | copy-done | bytes 786456
  8.1 1.1 %copy-done.2 = bf16[256,1536]{1,0:T(8,128)(2,1)S(1)} copy-done((bf16[256,1536]{1,0:T(8,128)(2,1)S(1)}, bf16[256,1536]{1,0:T(8,128)(2,1)}, u32[]{:S(2)}) %copy-start.2) | copy-done | bytes 786456
  9.2 0.7 shard_map.48.own
  9.9 1.3 %collective-permute-start.8 = (bf16[528,768]{1,0:T(8,128)(2,1)S(1)}, bf16[528,768]{1,0:T(8,128)(2,1)S(1)}, u32[]{:S(2)}, u32[]{:S(2)}) collective-permute-start(bf16[528,768]{1,0:T(8,128)(2,1)S(1)} %shard_map.48.own), channel_id=1, source_target_pairs={{4,0},{5,1},{6,2},{7,3},{8,4},{9,5},{10,6},{11,7},{12,8},{13,9},{1... | collective-permute-start | bytes 2433032 | tf_op jit(solution)/shard_map/ppermute | solution.py:262
  11.2 4.0 %collective-permute-start.7 = (bf16[528,768]{1,0:T(8,128)(2,1)S(1)}, bf16[528,768]{1,0:T(8,128)(2,1)S(1)}, u32[]{:S(2)}, u32[]{:S(2)}) collective-permute-start(bf16[528,768]{1,0:T(8,128)(2,1)S(1)} %shard_map.48.own), channel_id=1, source_target_pairs={{0,4},{1,5},{2,6},{3,7},{4,8},{5,9},{6,10},{7,11},{8,12},{9,13},{1... | collective-permute-start | bytes 2433032 | tf_op jit(solution)/shard_map/ppermute | solution.py:262
  15.3 2.5 %collective-permute-start.6 = (bf16[528,768]{1,0:T(8,128)(2,1)S(1)}, bf16[528,768]{1,0:T(8,128)(2,1)S(1)}, u32[]{:S(2)}, u32[]{:S(2)}) collective-permute-start(bf16[528,768]{1,0:T(8,128)(2,1)S(1)} %shard_map.48.own), channel_id=1, source_target_pairs={{0,2},{1,3},{2,0},{3,1},{4,6},{5,7},{6,4},{7,5},{8,10},{9,11},{10,... | collective-permute-start | bytes 2433032 | tf_op jit(solution)/shard_map/ppermute | solution.py:262
  17.8 3.2 %shard_map.46 = (f32[256,1536]{1,0:T(8,128)S(1)}, f32[256,1536]{1,0:T(8,128)S(1)}, f32[256,1536]{1,0:T(8,128)S(1)}) custom-call(s32[9]{0:T(128)S(1)} %pad_add_fusion.meta, bf16[256,1536]{1,0:T(8,128)(2,1)S(1)} %copy-done, bf16[256,1536]{1,0:T(8,128)(2,1)S(1)} %copy-done.1, bf16[256,1536]{1,0:T(8,128)(2,1)S(1)} %copy-done.2), custom_call_target="tpu_custom_call" | custom-call | flops 402653184 | bytes 2359296 | tf_op jit(solution)/shard_map/pallas_call | solution.py:141
  21.0 0.7 shard_map.47.own
  21.8 1.3 %collective-permute-start.3 = (bf16[528,768]{1,0:T(8,128)(2,1)S(1)}, bf16[528,768]{1,0:T(8,128)(2,1)S(1)}, u32[]{:S(2)}, u32[]{:S(2)}) collective-permute-start(bf16[528,768]{1,0:T(8,128)(2,1)S(1)} %shard_map.47.own), channel_id=1, source_target_pairs={{4,0},{5,1},{6,2},{7,3},{8,4},{9,5},{10,6},{11,7},{12,8},{13,9},{1... | collective-permute-start | bytes 2433032 | tf_op jit(solution)/shard_map/ppermute | solution.py:262
  23.1 7.4 %collective-permute-done.8.refs_7_.refs_8_.high = bf16[528,768]{1,0:T(8,128)(2,1)S(1)} collective-permute-done((bf16[528,768]{1,0:T(8,128)(2,1)S(1)}, bf16[528,768]{1,0:T(8,128)(2,1)S(1)}, u32[]{:S(2)}, u32[]{:S(2)}) %collective-permute-start.8) | collective-permute-done | bytes 811040 | tf_op jit(solution)/shard_map/ppermute | solution.py:262
  30.5 3.2 %collective-permute-start.5 = (bf16[528,768]{1,0:T(8,128)(2,1)S(1)}, bf16[528,768]{1,0:T(8,128)(2,1)S(1)}, u32[]{:S(2)}, u32[]{:S(2)}) collective-permute-start(bf16[528,768]{1,0:T(8,128)(2,1)S(1)} %shard_map.48.own), channel_id=1, source_target_pairs={{0,1},{1,0},{2,3},{3,2},{4,5},{5,4},{6,7},{7,6},{8,9},{9,8},{10,11... | collective-permute-start | bytes 2433032 | tf_op jit(solution)/shard_map/ppermute | solution.py:262
  33.7 3.0 %collective-permute-start.2 = (bf16[528,768]{1,0:T(8,128)(2,1)S(1)}, bf16[528,768]{1,0:T(8,128)(2,1)S(1)}, u32[]{:S(2)}, u32[]{:S(2)}) collective-permute-start(bf16[528,768]{1,0:T(8,128)(2,1)S(1)} %shard_map.47.own), channel_id=1, source_target_pairs={{0,4},{1,5},{2,6},{3,7},{4,8},{5,9},{6,10},{7,11},{8,12},{9,13},{1... | collective-permute-start | bytes 2433032 | tf_op jit(solution)/shard_map/ppermute | solution.py:262
  36.7 1.3 %collective-permute-start.12 = (bf16[528,768]{1,0:T(8,128)(2,1)S(1)}, bf16[528,768]{1,0:T(8,128)(2,1)S(1)}, u32[]{:S(2)}, u32[]{:S(2)}) collective-permute-start(bf16[528,768]{1,0:T(8,128)(2,1)S(1)} %shard_map.47.own), channel_id=1, source_target_pairs={{0,1},{1,0},{2,3},{3,2},{4,5},{5,4},{6,7},{7,6},{8,9},{9,8},{10,11... | collective-permute-start | bytes 2433032 | tf_op jit(solution)/shard_map/ppermute | solution.py:262
  38.0 2.3 %shard_map.52 = (bf16[256,768]{1,0:T(8,128)(2,1)S(1)}, bf16[256,768]{1,0:T(8,128)(2,1)S(1)}, bf16[256,768]{1,0:T(8,128)(2,1)S(1)}) custom-call(s32[9]{0:T(128)S(1)} %pad_add_fusion.meta, s32[1,8]{1,0:T(1,128)S(1)} %collective-permute-done.refs_0_.far_list, s32[1,8]{1,0:T(1,128)S(1)} %collective-permute-done.1.refs_1_.one_list, ...), custom_call_target="tpu_custom_call" | custom-call | bytes 2359296 | tf_op jit(solution)/shard_map/pallas_call | solution.py:247
  40.3 12.6 %collective-permute-done.4.over.refs_3_.refs_4_ = bf16[528,768]{1,0:T(8,128)(2,1)S(1)} collective-permute-done((bf16[528,768]{1,0:T(8,128)(2,1)S(1)}, bf16[528,768]{1,0:T(8,128)(2,1)S(1)}, u32[]{:S(2)}, u32[]{:S(2)}) %collective-permute-start.4) | collective-permute-done | bytes 811040 | tf_op jit(solution)/shard_map/ppermute | solution.py:262
  52.9 1.6 %collective-permute-start.13 = (bf16[256,768]{1,0:T(8,128)(2,1)S(1)}, bf16[256,768]{1,0:T(8,128)(2,1)S(1)}, u32[]{:S(2)}, u32[]{:S(2)}) collective-permute-start(bf16[256,768]{1,0:T(8,128)(2,1)S(1)} %get-tuple-element.30), channel_id=1, source_target_pairs={{0,2},{1,3},{2,0},{3,1},{4,6},{5,7},{6,4},{7,5},{8,10},{9,11},{10,... | collective-permute-start | bytes 1179656 | tf_op jit(solution)/shard_map/ppermute | solution.py:262
  54.5 3.6 %collective-permute-start.14 = (bf16[256,768]{1,0:T(8,128)(2,1)S(1)}, bf16[256,768]{1,0:T(8,128)(2,1)S(1)}, u32[]{:S(2)}, u32[]{:S(2)}) collective-permute-start(bf16[256,768]{1,0:T(8,128)(2,1)S(1)} %get-tuple-element.31), channel_id=1, source_target_pairs={{0,1},{1,4},{3,2},{4,5},{5,8},{6,3},{7,6},{8,9},{9,12},{10,7},{11,... | collective-permute-start | bytes 1179656 | tf_op jit(solution)/shard_map/ppermute | solution.py:262
  58.6 3.3 %shard_map.49 = (f32[256,768]{1,0:T(8,128)S(1)}, f32[256,768]{1,0:T(8,128)S(1)}, f32[256,768]{1,0:T(8,128)S(1)}) custom-call(s32[9]{0:T(128)S(1)} %pad_add_fusion.meta, bf16[256,1536]{1,0:T(8,128)(2,1)S(1)} %copy-done, bf16[528,768]{1,0:T(8,128)(2,1)S(1)} %collective-permute-done.5.refs_1_.refs_2_, ...), custom_call_target="tpu_custom_call" | custom-call | flops 402653184 | bytes 1966080 | tf_op jit(solution)/shard_map/pallas_call | solution.py:141
  61.9 2.3 %shard_map.50 = (bf16[256,768]{1,0:T(8,128)(2,1)S(1)}, bf16[256,768]{1,0:T(8,128)(2,1)S(1)}, bf16[256,768]{1,0:T(8,128)(2,1)S(1)}) custom-call(s32[9]{0:T(128)S(1)} %pad_add_fusion.meta, s32[1,8]{1,0:T(1,128)S(1)} %collective-permute-done.refs_0_.far_list, s32[1,8]{1,0:T(1,128)S(1)} %collective-permute-done.1.refs_1_.one_list, ...), custom_call_target="tpu_custom_call" | custom-call | bytes 2359296 | tf_op jit(solution)/shard_map/pallas_call | solution.py:247
  64.2 0.8 collective-permute-start.9
  65.0 1.9 %collective-permute-start.10 = (bf16[256,768]{1,0:T(8,128)(2,1)S(1)}, bf16[256,768]{1,0:T(8,128)(2,1)S(1)}, u32[]{:S(2)}, u32[]{:S(2)}) collective-permute-start(bf16[256,768]{1,0:T(8,128)(2,1)S(1)} %get-tuple-element.25), channel_id=1, source_target_pairs={{0,1},{1,4},{3,2},{4,5},{5,8},{6,3},{7,6},{8,9},{9,12},{10,7},{11,... | collective-permute-start | bytes 1179656 | tf_op jit(solution)/shard_map/ppermute | solution.py:262
  67.0 1.9 %collective-permute-start.11 = (bf16[256,768]{1,0:T(8,128)(2,1)S(1)}, bf16[256,768]{1,0:T(8,128)(2,1)S(1)}, u32[]{:S(2)}, u32[]{:S(2)}) collective-permute-start(bf16[256,768]{1,0:T(8,128)(2,1)S(1)} %get-tuple-element.26), channel_id=1, source_target_pairs={{0,8},{1,9},{2,10},{3,11},{4,0},{5,1},{6,2},{7,3},{8,12},{9,13},{1... | collective-permute-start | bytes 1179656 | tf_op jit(solution)/shard_map/ppermute | solution.py:262
  68.8 3.3 %shard_map.51 = (f32[256,768]{1,0:T(8,128)S(1)}, f32[256,768]{1,0:T(8,128)S(1)}, f32[256,768]{1,0:T(8,128)S(1)}) custom-call(s32[9]{0:T(128)S(1)} %pad_add_fusion.meta, bf16[256,1536]{1,0:T(8,128)(2,1)S(1)} %copy-done, bf16[528,768]{1,0:T(8,128)(2,1)S(1)} %collective-permute-done.12.refs_1_.refs_2_, ...), custom_call_target="tpu_custom_call" | custom-call | flops 402653184 | bytes 1966080 | tf_op jit(solution)/shard_map/pallas_call | solution.py:141
  72.2 1.5 %collective-permute-done.15.refs_5_.refs_6_ = bf16[256,768]{1,0:T(8,128)(2,1)S(1)} collective-permute-done((bf16[256,768]{1,0:T(8,128)(2,1)S(1)}, bf16[256,768]{1,0:T(8,128)(2,1)S(1)}, u32[]{:S(2)}, u32[]{:S(2)}) %collective-permute-start.15) | collective-permute-done | bytes 393248 | tf_op jit(solution)/shard_map/ppermute | solution.py:262
  73.6 3.1 %shard_map.53.refs_10_ = bf16[256,1536]{1,0:T(8,128)(2,1)} custom-call(s32[9]{0:T(128)S(1)} %pad_add_fusion.meta, bf16[256,1536]{1,0:T(8,128)(2,1)S(1)} %copy-done, bf16[256,768]{1,0:T(8,128)(2,1)S(1)} %collective-permute-done.13.refs_1_.refs_2_, bf16[256,768]{1,0:T(8,128)(2,1)S(1)} %collective-permute-done.13.refs_1_.refs_2_, ...), custom_call_target="tpu_custom_call" | custom-call | flops 301989888 | bytes 1572864 | tf_op jit(solution)/shard_map/pallas_call | solution.py:141
  76.7 3.0 %collective-permute-done.10.refs_3_.refs_4_ = bf16[256,768]{1,0:T(8,128)(2,1)S(1)} collective-permute-done((bf16[256,768]{1,0:T(8,128)(2,1)S(1)}, bf16[256,768]{1,0:T(8,128)(2,1)S(1)}, u32[]{:S(2)}, u32[]{:S(2)}) %collective-permute-start.10) | collective-permute-done | bytes 393248 | tf_op jit(solution)/shard_map/ppermute | solution.py:262
  79.7 4.3 %collective-permute-done.11.refs_5_.refs_6_ = bf16[256,768]{1,0:T(8,128)(2,1)S(1)} collective-permute-done((bf16[256,768]{1,0:T(8,128)(2,1)S(1)}, bf16[256,768]{1,0:T(8,128)(2,1)S(1)}, u32[]{:S(2)}, u32[]{:S(2)}) %collective-permute-start.11) | collective-permute-done | bytes 393248 | tf_op jit(solution)/shard_map/ppermute | solution.py:262
  83.9 3.1 %shard_map.54 = bf16[256,1536]{1,0:T(8,128)(2,1)} custom-call(s32[9]{0:T(128)S(1)} %pad_add_fusion.meta, bf16[256,1536]{1,0:T(8,128)(2,1)S(1)} %copy-done, bf16[256,768]{1,0:T(8,128)(2,1)S(1)} %collective-permute-done.9.refs_1_.refs_2_, bf16[256,768]{1,0:T(8,128)(2,1)S(1)} %collective-permute-done.9.refs_1_.refs_2_, ...), custom_call_target="tpu_custom_call", output_to_operand_aliasing={{}: (11, {})} | custom-call | flops 301989888 | bytes 1572864 | tf_op jit(solution)/shard_map/pallas_call | solution.py:141
  (17 shorter events, 1.1 us)
Async XLA Ops:
  0.0 17.8 %copy-start = (bf16[256,1536]{1,0:T(8,128)(2,1)S(1)}, bf16[256,1536]{1,0:T(8,128)(2,1)}, u32[]{:S(2)}) copy-start(bf16[256,1536]{1,0:T(8,128)(2,1)} %refs_0_.9) | copy-start | bytes 2359300
  0.0 6.1 %collective-permute-start.1 = (s32[1,8]{1,0:T(1,128)}, s32[1,8]{1,0:T(1,128)S(1)}, u32[]{:S(2)}, u32[]{:S(2)}) collective-permute-start(s32[1,8]{1,0:T(1,128)} %param.7), channel_id=1, source_target_pairs={{1,0},{4,1},{2,3},{5,4},{8,5},{3,6},{6,7},{9,8},{12,9},{7,10},{10,... | collective-permute-start | bytes 104 | tf_op jit(solution)/shard_map/ppermute | solution.py:262
  2.1 4.9 %collective-permute-start = (s32[1,8]{1,0:T(1,128)}, s32[1,8]{1,0:T(1,128)S(1)}, u32[]{:S(2)}, u32[]{:S(2)}) collective-permute-start(s32[1,8]{1,0:T(1,128)} %param.7), channel_id=1, source_target_pairs={{8,0},{9,1},{10,2},{11,3},{0,4},{1,5},{2,6},{3,7},{12,8},{13,9},{1... | collective-permute-start | bytes 104 | tf_op jit(solution)/shard_map/ppermute | solution.py:262
  7.0 1.1 %copy-start.1 = (bf16[256,1536]{1,0:T(8,128)(2,1)S(1)}, bf16[256,1536]{1,0:T(8,128)(2,1)}, u32[]{:S(2)}) copy-start(bf16[256,1536]{1,0:T(8,128)(2,1)} %k_ref.3) | copy-start | bytes 2359300
  8.1 1.1 %copy-start.2 = (bf16[256,1536]{1,0:T(8,128)(2,1)S(1)}, bf16[256,1536]{1,0:T(8,128)(2,1)}, u32[]{:S(2)}) copy-start(bf16[256,1536]{1,0:T(8,128)(2,1)} %v_ref.3) | copy-start | bytes 2359300
  9.9 20.6 %collective-permute-start.8 = (bf16[528,768]{1,0:T(8,128)(2,1)S(1)}, bf16[528,768]{1,0:T(8,128)(2,1)S(1)}, u32[]{:S(2)}, u32[]{:S(2)}) collective-permute-start(bf16[528,768]{1,0:T(8,128)(2,1)S(1)} %shard_map.48.own), channel_id=1, source_target_pairs={{4,0},{5,1},{6,2},{7,3},{8,4},{9,5},{10,6},{11,7},{12,8},{13,9},{1... | collective-permute-start | bytes 2433032 | tf_op jit(solution)/shard_map/ppermute | solution.py:262
  11.2 22.5 %collective-permute-start.7 = (bf16[528,768]{1,0:T(8,128)(2,1)S(1)}, bf16[528,768]{1,0:T(8,128)(2,1)S(1)}, u32[]{:S(2)}, u32[]{:S(2)}) collective-permute-start(bf16[528,768]{1,0:T(8,128)(2,1)S(1)} %shard_map.48.own), channel_id=1, source_target_pairs={{0,4},{1,5},{2,6},{3,7},{4,8},{5,9},{6,10},{7,11},{8,12},{9,13},{1... | collective-permute-start | bytes 2433032 | tf_op jit(solution)/shard_map/ppermute | solution.py:262
  15.3 21.4 %collective-permute-start.6 = (bf16[528,768]{1,0:T(8,128)(2,1)S(1)}, bf16[528,768]{1,0:T(8,128)(2,1)S(1)}, u32[]{:S(2)}, u32[]{:S(2)}) collective-permute-start(bf16[528,768]{1,0:T(8,128)(2,1)S(1)} %shard_map.48.own), channel_id=1, source_target_pairs={{0,2},{1,3},{2,0},{3,1},{4,6},{5,7},{6,4},{7,5},{8,10},{9,11},{10,... | collective-permute-start | bytes 2433032 | tf_op jit(solution)/shard_map/ppermute | solution.py:262
  21.7 31.2 %collective-permute-start.4 = (bf16[528,768]{1,0:T(8,128)(2,1)S(1)}, bf16[528,768]{1,0:T(8,128)(2,1)S(1)}, u32[]{:S(2)}, u32[]{:S(2)}) collective-permute-start(bf16[528,768]{1,0:T(8,128)(2,1)S(1)} %shard_map.47.own), channel_id=1, source_target_pairs={{0,2},{1,3},{2,0},{3,1},{4,6},{5,7},{6,4},{7,5},{8,10},{9,11},{10,... | collective-permute-start | bytes 2433032 | tf_op jit(solution)/shard_map/ppermute | solution.py:262
  21.8 32.7 %collective-permute-start.3 = (bf16[528,768]{1,0:T(8,128)(2,1)S(1)}, bf16[528,768]{1,0:T(8,128)(2,1)S(1)}, u32[]{:S(2)}, u32[]{:S(2)}) collective-permute-start(bf16[528,768]{1,0:T(8,128)(2,1)S(1)} %shard_map.47.own), channel_id=1, source_target_pairs={{4,0},{5,1},{6,2},{7,3},{8,4},{9,5},{10,6},{11,7},{12,8},{13,9},{1... | collective-permute-start | bytes 2433032 | tf_op jit(solution)/shard_map/ppermute | solution.py:262
  30.5 27.6 %collective-permute-start.5 = (bf16[528,768]{1,0:T(8,128)(2,1)S(1)}, bf16[528,768]{1,0:T(8,128)(2,1)S(1)}, u32[]{:S(2)}, u32[]{:S(2)}) collective-permute-start(bf16[528,768]{1,0:T(8,128)(2,1)S(1)} %shard_map.48.own), channel_id=1, source_target_pairs={{0,1},{1,0},{2,3},{3,2},{4,5},{5,4},{6,7},{7,6},{8,9},{9,8},{10,11... | collective-permute-start | bytes 2433032 | tf_op jit(solution)/shard_map/ppermute | solution.py:262
  33.7 28.2 %collective-permute-start.2 = (bf16[528,768]{1,0:T(8,128)(2,1)S(1)}, bf16[528,768]{1,0:T(8,128)(2,1)S(1)}, u32[]{:S(2)}, u32[]{:S(2)}) collective-permute-start(bf16[528,768]{1,0:T(8,128)(2,1)S(1)} %shard_map.47.own), channel_id=1, source_target_pairs={{0,4},{1,5},{2,6},{3,7},{4,8},{5,9},{6,10},{7,11},{8,12},{9,13},{1... | collective-permute-start | bytes 2433032 | tf_op jit(solution)/shard_map/ppermute | solution.py:262
  36.7 28.3 %collective-permute-start.12 = (bf16[528,768]{1,0:T(8,128)(2,1)S(1)}, bf16[528,768]{1,0:T(8,128)(2,1)S(1)}, u32[]{:S(2)}, u32[]{:S(2)}) collective-permute-start(bf16[528,768]{1,0:T(8,128)(2,1)S(1)} %shard_map.47.own), channel_id=1, source_target_pairs={{0,1},{1,0},{2,3},{3,2},{4,5},{5,4},{6,7},{7,6},{8,9},{9,8},{10,11... | collective-permute-start | bytes 2433032 | tf_op jit(solution)/shard_map/ppermute | solution.py:262
  52.9 14.0 %collective-permute-start.13 = (bf16[256,768]{1,0:T(8,128)(2,1)S(1)}, bf16[256,768]{1,0:T(8,128)(2,1)S(1)}, u32[]{:S(2)}, u32[]{:S(2)}) collective-permute-start(bf16[256,768]{1,0:T(8,128)(2,1)S(1)} %get-tuple-element.30), channel_id=1, source_target_pairs={{0,2},{1,3},{2,0},{3,1},{4,6},{5,7},{6,4},{7,5},{8,10},{9,11},{10,... | collective-permute-start | bytes 1179656 | tf_op jit(solution)/shard_map/ppermute | solution.py:262
  54.5 17.7 %collective-permute-start.14 = (bf16[256,768]{1,0:T(8,128)(2,1)S(1)}, bf16[256,768]{1,0:T(8,128)(2,1)S(1)}, u32[]{:S(2)}, u32[]{:S(2)}) collective-permute-start(bf16[256,768]{1,0:T(8,128)(2,1)S(1)} %get-tuple-element.31), channel_id=1, source_target_pairs={{0,1},{1,4},{3,2},{4,5},{5,8},{6,3},{7,6},{8,9},{9,12},{10,7},{11,... | collective-permute-start | bytes 1179656 | tf_op jit(solution)/shard_map/ppermute | solution.py:262
  58.1 15.6 %collective-permute-start.15 = (bf16[256,768]{1,0:T(8,128)(2,1)S(1)}, bf16[256,768]{1,0:T(8,128)(2,1)S(1)}, u32[]{:S(2)}, u32[]{:S(2)}) collective-permute-start(bf16[256,768]{1,0:T(8,128)(2,1)S(1)} %get-tuple-element.32), channel_id=1, source_target_pairs={{0,8},{1,9},{2,10},{3,11},{4,0},{5,1},{6,2},{7,3},{8,12},{9,13},{1... | collective-permute-start | bytes 1179656 | tf_op jit(solution)/shard_map/ppermute | solution.py:262
  64.2 12.5 %collective-permute-start.9 = (bf16[256,768]{1,0:T(8,128)(2,1)S(1)}, bf16[256,768]{1,0:T(8,128)(2,1)S(1)}, u32[]{:S(2)}, u32[]{:S(2)}) collective-permute-start(bf16[256,768]{1,0:T(8,128)(2,1)S(1)} %get-tuple-element.24), channel_id=1, source_target_pairs={{0,2},{1,3},{2,0},{3,1},{4,6},{5,7},{6,4},{7,5},{8,10},{9,11},{10,... | collective-permute-start | bytes 1179656 | tf_op jit(solution)/shard_map/ppermute | solution.py:262
  65.0 14.6 %collective-permute-start.10 = (bf16[256,768]{1,0:T(8,128)(2,1)S(1)}, bf16[256,768]{1,0:T(8,128)(2,1)S(1)}, u32[]{:S(2)}, u32[]{:S(2)}) collective-permute-start(bf16[256,768]{1,0:T(8,128)(2,1)S(1)} %get-tuple-element.25), channel_id=1, source_target_pairs={{0,1},{1,4},{3,2},{4,5},{5,8},{6,3},{7,6},{8,9},{9,12},{10,7},{11,... | collective-permute-start | bytes 1179656 | tf_op jit(solution)/shard_map/ppermute | solution.py:262
  67.0 17.0 %collective-permute-start.11 = (bf16[256,768]{1,0:T(8,128)(2,1)S(1)}, bf16[256,768]{1,0:T(8,128)(2,1)S(1)}, u32[]{:S(2)}, u32[]{:S(2)}) collective-permute-start(bf16[256,768]{1,0:T(8,128)(2,1)S(1)} %get-tuple-element.26), channel_id=1, source_target_pairs={{0,8},{1,9},{2,10},{3,11},{4,0},{5,1},{6,2},{7,3},{8,12},{9,13},{1... | collective-permute-start | bytes 1179656 | tf_op jit(solution)/shard_map/ppermute | solution.py:262

commit v4 on v3

--- a/solution.py
+++ b/solution.py
@@ -140,6 +140,7 @@
     done = steps * block
     return pl.pallas_call(
         functools.partial(attend_kernel, plan, heads, carry is not None, final),
+        name="attend_last" if final else "attend_more" if carry is not None else "attend_own",
         out_shape=out_shape,
         grid_spec=pltpu.PrefetchScalarGridSpec(
             num_scalar_prefetch=1, grid=(steps,), in_specs=specs, out_specs=out_specs
@@ -154,108 +155,183 @@
     )(meta, *operands)
 
 
-def pack_kernel(first, meta, k_ref, v_ref, *refs):
-    out_ref, note, sems = refs[-3:]
-    rows = k_ref.shape[0]
-    width = out_ref.shape[1]
-    copies = [
+SCALAR = pl.BlockSpec(memory_space=pltpu.SMEM)
+WHOLE = pl.BlockSpec(memory_space=pl.ANY)
+
+
+def move(name, build, operands, specs, out_shape, out_specs, copies, moved, scratch=()):
+    return pl.pallas_call(
+        build,
+        name=name,
+        out_shape=out_shape,
+        in_specs=specs,
+        out_specs=out_specs,
+        scratch_shapes=[*scratch, pltpu.SemaphoreType.DMA((copies,))],
+        compiler_params=pltpu.CompilerParams(vmem_limit_bytes=VMEM_LIMIT),
+        cost_estimate=pl.CostEstimate(flops=0, bytes_accessed=moved, transcendentals=0),
+    )(*operands)
+
+
+def in_hbm(array):
+    return pltpu.with_memory_space_constraint(array, pltpu.HBM)
+
+
+def tile_copies(sources, tile, target, column, sems, at):
+    width = target.shape[1] if column is None else column[1]
+    to = 0 if column is None else column[0]
+    return [
         pltpu.make_async_copy(
-            ref.at[:, pl.ds(first, width)], out_ref.at[pl.ds(n * rows, rows)], sems.at[n]
+            ref.at[pl.ds(pl.multiple_of(row + tile * TILE, TILE), TILE), pl.ds(first, width)],
+            target.at[pl.ds(n * TILE, TILE), pl.ds(to, width)],
+            sems.at[at + n],
         )
-        for n, ref in enumerate((k_ref, v_ref))
+        for n, (ref, row, first) in enumerate(sources)
     ]
-    for copy in copies:
-        copy.start()
-    lane = lax.broadcasted_iota(jnp.int32, note.shape, 1)
-    row = jnp.zeros(note.shape, jnp.float32)
-    for entry in range(8):
-        row = jnp.where(lane == entry, meta[entry].astype(jnp.float32), row)
-    note[...] = row.astype(jnp.bfloat16)
-    last = pltpu.make_async_copy(note, out_ref.at[pl.ds(2 * rows, NOTE_ROWS)], sems.at[2])
-    last.start()
-    for copy in copies:
-        copy.wait()
-    last.wait()
-
-
-def pack(meta, keys, values, first, width, after):
+
+
+def start_if(condition, copies):
+    @pl.when(condition)
+    def _():
+        for copy in copies:
+            copy.start()
+
+
+def begin(tile_lists, me, beside_list, across_list, far_list, keys, values, width):
+    rows, all_width = keys.shape
+    tile_count = rows // TILE
+
+    def build(list_ref, me_ref, beside_ref, across_ref, far_ref, k_ref, v_ref, *refs):
+        meta, packed, to_beside, to_across, note, sems = refs
+        me = me_ref[0]
+        plane, right = me // 4, me % 4 >= 2
+
+        def tile_at(ref, entry):
+            return jnp.clip(ref[0, entry], 0, tile_count - 1)
+
+        copies = [
+            pltpu.make_async_copy(
+                ref.at[:, pl.ds(0, width)], packed.at[pl.ds(n * rows, rows)], sems.at[n]
+            )
+            for n, ref in enumerate((k_ref, v_ref))
+        ]
+        own = ((k_ref, 0, 0), (v_ref, 0, 0))
+        copies += tile_copies(own, tile_at(across_ref, jnp.where(right, 5, 1)), to_across, None, sems, 2)
+        copies += tile_copies(own, tile_at(beside_ref, jnp.where(me % 2 == 0, 0, 4)), to_beside, None, sems, 4)
+        for copy in copies:
+            copy.start()
+        lane = lax.broadcasted_iota(jnp.int32, note.shape, 1)
+        row = jnp.zeros(note.shape, jnp.float32)
+        for entry in range(8):
+            row = jnp.where(lane == entry, tile_at(beside_ref, entry).astype(jnp.float32), row)
+        note[...] = row.astype(jnp.bfloat16)
+        copies.append(
+            pltpu.make_async_copy(note, to_across.at[pl.ds(2 * TILE, NOTE_ROWS)], sems.at[6])
+        )
+        copies[-1].start()
+        for entry in range(8):
+            meta[entry] = tile_at(list_ref, entry)
+        meta[8] = me
+        meta[9] = tile_at(far_ref, jnp.where(plane % 2 == 0, 3, 7))
+        meta[10] = tile_at(across_ref, jnp.where(right, 1, 5))
+        for entry in range(11, 16):
+            meta[entry] = 0
+        for copy in copies:
+            copy.wait()
+
+    return move(
+        "begin",
+        build,
+        (tile_lists, me, beside_list, across_list, far_list, in_hbm(keys), in_hbm(values)),
+        [SCALAR] * 5 + [WHOLE] * 2,
+        [
+            jax.ShapeDtypeStruct((16,), jnp.int32),
+            jax.ShapeDtypeStruct((2 * rows, width), jnp.bfloat16),
+            jax.ShapeDtypeStruct((2 * TILE, all_width), jnp.bfloat16),
+            jax.ShapeDtypeStruct((2 * TILE + NOTE_ROWS, all_width), jnp.bfloat16),
+        ],
+        [SCALAR, WHOLE, WHOLE, WHOLE],
+        7,
+        24 * TILE * all_width,
+        [pltpu.VMEM((NOTE_ROWS, all_width), jnp.bfloat16)],
+    )
+
+
+def pack(keys, values, first, width, after):
     rows = keys.shape[0]
-    whole = pl.BlockSpec(memory_space=pl.ANY)
-    source = pl.BlockSpec(memory_space=pltpu.HBM)
-    return pl.pallas_call(
-        functools.partial(pack_kernel, first),
-        out_shape=jax.ShapeDtypeStruct((2 * rows + NOTE_ROWS, width), jnp.bfloat16),
-        in_specs=[pl.BlockSpec(memory_space=pltpu.SMEM), source, source] + [whole] * len(after),
-        out_specs=whole,
-        scratch_shapes=[
-            pltpu.VMEM((NOTE_ROWS, width), jnp.bfloat16),
-            pltpu.SemaphoreType.DMA((3,)),
-        ],
-        compiler_params=pltpu.CompilerParams(vmem_limit_bytes=VMEM_LIMIT),
-        cost_estimate=pl.CostEstimate(flops=0, bytes_accessed=8 * rows * width, transcendentals=0),
-    )(meta, keys, values, *after)
-
-
-def choose_kernel(meta, far_list, one_list, own, low, high, over, *refs):
-    far, two, one, note, sems = refs[-5:]
-    rows = 2 * TILE
-    spot, plane = meta[8] % 4, meta[8] // 4
-    right = spot >= 2
-    read = pltpu.make_async_copy(
-        over.at[pl.ds(2 * rows, NOTE_ROWS), pl.ds(0, HD)], note, sems.at[6]
+
+    def build(k_ref, v_ref, *refs):
+        out_ref, sems = refs[-2:]
+        copies = [
+            pltpu.make_async_copy(
+                ref.at[:, pl.ds(first, width)], out_ref.at[pl.ds(n * rows, rows)], sems.at[n]
+            )
+            for n, ref in enumerate((k_ref, v_ref))
+        ]
+        for copy in copies:
+            copy.start()
+        for copy in copies:
+            copy.wait()
+
+    return move(
+        "pack",
+        build,
+        (in_hbm(keys), in_hbm(values), *after),
+        [WHOLE] * (2 + len(after)),
+        jax.ShapeDtypeStruct((2 * rows, width), jnp.bfloat16),
+        WHOLE,
+        2,
+        8 * rows * width,
     )
-    read.start()
-
-    def copies(src, tile, dst, sem):
-        start = pl.multiple_of(tile * TILE, TILE)
-        return [
-            pltpu.make_async_copy(
-                src.at[pl.ds(n * rows + start, TILE)], dst.at[pl.ds(n * TILE, TILE)], sems.at[sem + n]
-            )
-            for n in (0, 1)
-        ]
-
-    def start_if(condition, *args):
-        @pl.when(condition)
-        def _():
-            for copy in copies(*args):
-                copy.start()
-
-    far_tile = jnp.clip(far_list[0, jnp.where(plane % 2 == 0, 3, 7)], 0, 1)
-    start_if((plane == 0) | (plane == 3), own, far_tile, far, 0)
-    start_if(plane == 1, high, far_tile, far, 0)
-    start_if(plane == 2, low, far_tile, far, 0)
-    one_tile = jnp.clip(one_list[0, jnp.where(spot % 2 == 0, 4, 0)], 0, 1)
-    for copy in copies(over, one_tile, one, 2):
-        copy.start()
-    read.wait()
-    here = (lax.broadcasted_iota(jnp.int32, note.shape, 1) == jnp.where(right, 1, 5)) & (
-        lax.broadcasted_iota(jnp.int32, note.shape, 0) == 0
+
+
+def choose(meta, over, keys, values, first, low, high, after):
+    rows, width = low.shape[0] // 2, low.shape[1]
+    tile_count = rows // TILE
+
+    def build(meta, over_ref, k_ref, v_ref, low, high, *refs):
+        to_two, to_one, to_far, note, sems = refs[-5:]
+        spot, plane = meta[8] % 4, meta[8] // 4
+        right = spot >= 2
+        read = pltpu.make_async_copy(
+            over_ref.at[pl.ds(2 * TILE, NOTE_ROWS), pl.ds(0, HD)], note, sems.at[6]
+        )
+        read.start()
+        own = ((k_ref, 0, first), (v_ref, 0, first))
+        below = ((low, 0, 0), (low, rows, 0))
+        above = ((high, 0, 0), (high, rows, 0))
+
+        def copies(source, tile, target, at):
+            return tile_copies(source, tile, target, None, sems, at)
+
+        start_if((plane == 0) | (plane == 3), copies(own, meta[9], to_far, 0))
+        start_if(plane == 1, copies(above, meta[9], to_far, 0))
+        start_if(plane == 2, copies(below, meta[9], to_far, 0))
+        start_if(right, copies(below, meta[10], to_two, 2))
+        start_if(jnp.logical_not(right), copies(above, meta[10], to_two, 2))
+        read.wait()
+        here = (lax.broadcasted_iota(jnp.int32, note.shape, 1) == jnp.where(spot % 2 == 0, 4, 0)) & (
+            lax.broadcasted_iota(jnp.int32, note.shape, 0) == 0
+        )
+        tile = jnp.sum(jnp.where(here, note[...].astype(jnp.float32), 0.0))
+        tile = jnp.clip(tile.astype(jnp.int32), 0, tile_count - 1)
+        start_if(spot == 0, copies(above, tile, to_one, 4))
+        start_if(spot == 3, copies(below, tile, to_one, 4))
+        start_if((spot == 1) | (spot == 2), copies(own, tile, to_one, 4))
+        for at, target in ((0, to_far), (2, to_two), (4, to_one)):
+            for copy in copies(own, 0, target, at):
+                copy.wait()
+
+    return move(
+        "choose",
+        build,
+        (meta, over, in_hbm(keys), in_hbm(values), low, high, *after),
+        [SCALAR] + [WHOLE] * (5 + len(after)),
+        [jax.ShapeDtypeStruct((2 * TILE, width), jnp.bfloat16)] * 3,
+        [WHOLE] * 3,
+        7,
+        24 * TILE * width,
+        [pltpu.VMEM((NOTE_ROWS, HD), jnp.bfloat16)],
     )
-    two_tile = jnp.sum(jnp.where(here, note[...].astype(jnp.float32), 0.0))
-    two_tile = jnp.clip(two_tile.astype(jnp.int32), 0, 1)
-    start_if(right, low, two_tile, two, 4)
-    start_if(jnp.logical_not(right), high, two_tile, two, 4)
-    for copy in copies(own, far_tile, far, 0) + copies(over, one_tile, one, 2) + copies(low, two_tile, two, 4):
-        copy.wait()
-
-
-def choose(meta, far_list, one_list, own, low, high, over, after):
-    width = low.shape[1]
-    scalar = pl.BlockSpec(memory_space=pltpu.SMEM)
-    whole = pl.BlockSpec(memory_space=pl.ANY)
-    return pl.pallas_call(
-        choose_kernel,
-        out_shape=[jax.ShapeDtypeStruct((2 * TILE, width), jnp.bfloat16)] * 3,
-        in_specs=[scalar] * 3 + [whole] * (4 + len(after)),
-        out_specs=[whole] * 3,
-        scratch_shapes=[
-            pltpu.VMEM((NOTE_ROWS, HD), jnp.bfloat16),
-            pltpu.SemaphoreType.DMA((7,)),
-        ],
-        compiler_params=pltpu.CompilerParams(vmem_limit_bytes=VMEM_LIMIT),
-        cost_estimate=pl.CostEstimate(flops=0, bytes_accessed=24 * TILE * width, transcendentals=0),
-    )(meta, far_list, one_list, own, low, high, over, *after)
 
 
 def send(array, route):
@@ -291,76 +367,67 @@
 def body_planes(queries, key_heads, value_heads, tile_lists):
     frames = 16
     rows, width = key_heads.shape
+    tile_count = rows // TILE
     half = width // 2
     heads = 3
     steps = half // (heads * HD)
     every = range(frames)
-    meta = jnp.concatenate(
-        [jnp.clip(tile_lists[0], 0, rows // TILE - 1), lax.axis_index("frame").astype(jnp.int32).reshape(1)]
-    )
     up = [(i, i + 4) for i in every if i + 4 < frames]
     down = [(i, i - 4) for i in every if i - 4 >= 0]
+    beside = [(i, i ^ 1) for i in every]
     across = [(i, i ^ 2) for i in every]
-    beside = [(i, i ^ 1) for i in every]
+    corner = [(i, i ^ 3) for i in every]
     far = [(i, i + (8, -4, 4, -8)[i // 4]) for i in every]
-    off_chip = [(i, i + (1, 3, -3, -1)[i % 4]) for i in every]
-    off_chip = [(i, j) for i, j in off_chip if 0 <= j < frames]
 
     def right(meta):
         return meta[8] % 4 >= 2
 
-    def beside_tile(meta):
-        return jnp.where(meta[8] % 2 == 1, meta[0], meta[4])
-
-    def across_tile(meta):
-        return jnp.where(right(meta), meta[1], meta[5])
-
     def two_there(meta):
         return jnp.where(right(meta), meta[8] + 2 < frames, meta[8] >= 2)
 
     def one_there(meta):
         return (meta[8] >= 1) & (meta[8] < frames - 1)
 
-    def tile_of(array, tile, usable=None):
-        return (
-            [(array, TILE, tile, 0)],
-            [(array, TILE, lambda meta: tile(meta) + 2, 0)],
-            usable,
-        )
-
-    def pair_of(arrays, usable=None):
-        return [(a, TILE, fixed(0), 0) for a in arrays], [(a, TILE, fixed(1), 0) for a in arrays], usable
-
-    def whole_of(n):
-        return [(key_heads, rows, fixed(0), n)], [(value_heads, rows, fixed(0), n)], None
-
-    def back(route):
-        return [(j, i) for i, j in route]
-
-    far_list = send(tile_lists, back(far))
-    one_list = send(tile_lists, back(off_chip))
-    first = pack(meta, key_heads, value_heads, 0, half, [far_list, one_list])
-    begun = attend(queries, meta, [whole_of(0)], 0, 2 * steps, heads)
-    second = pack(meta, key_heads, value_heads, half, half, [begun[0]])
+    def own_frame():
+        return [(key_heads, rows, fixed(0), 0)], [(value_heads, rows, fixed(0), 0)], None
+
+    def tile_of(array, tile, usable):
+        return [(array, TILE, tile, 0)], [(array, TILE, lambda meta: tile(meta) + tile_count, 0)], usable
+
+    def sent_tile(array, column=0, usable=None):
+        return [(array, TILE, fixed(0), column)], [(array, TILE, fixed(1), column)], usable
+
+    me = lax.axis_index("frame").astype(jnp.int32).reshape(1)
+    far_list = send(tile_lists, [(j, i) for i, j in far])
+    beside_list = send(tile_lists, beside)
+    across_list = send(tile_lists, across)
+    meta, first, to_beside, to_across = begin(
+        tile_lists, me, beside_list, across_list, far_list, key_heads, value_heads, half
+    )
+    over = send(to_across, across)
+    low = [send(first, up)]
+    high = [send(first, down)]
+    next_to = send(to_beside, beside)
+    begun = attend(queries, meta, [own_frame()], 0, 2 * steps, heads)
+    second = pack(key_heads, value_heads, half, half, [begun[0]])
+    low.append(send(second, up))
+    high.append(send(second, down))
+
     after = []
     middles, finals = [], []
-    for n, packed in enumerate((first, second)):
-        low = send(packed, up)
-        high = send(packed, down)
-        over = send(packed, across)
-        next_to = send(packed, beside)
-        to_far, to_two, to_one = choose(meta, far_list, one_list, packed, low, high, over, after)
-        from_far = send(to_far, far)
-        two = send(to_two, across)
-        one = send(to_one, off_chip)
+    for n in (0, 1):
+        sent = choose(meta, over, key_heads, value_heads, n * half, low[n], high[n], after)
+        two = send(sent[0], across)
+        one = send(sent[1], corner)
+        from_far = send(sent[2], far)
         middle = attend(
             queries,
             meta,
             [
-                tile_of(next_to, beside_tile),
-                tile_of(over, across_tile),
-                tile_of(low, lambda meta: meta[2], lambda meta: meta[8] >= 4),
-                tile_of(high, lambda meta: meta[6], lambda meta: meta[8] + 4 < frames),
+                sent_tile(next_to, n * steps),
+                sent_tile(over, n * steps),
+                tile_of(low[n], lambda meta: meta[2], lambda meta: meta[8] >= 4),
+                tile_of(high[n], lambda meta: meta[6], lambda meta: meta[8] + 4 < frames),
             ],
             n * steps,
             steps,
@@ -368,9 +435,9 @@
             begun,
             held=n * steps,
         )
-        after = [middle[0]]
+        after = [middle[0], two]
         middles.append(middle)
-        finals.append([pair_of([two], two_there), pair_of([one], one_there), pair_of([from_far])])
+        finals.append([sent_tile(two, 0, two_there), sent_tile(one, 0, one_there), sent_tile(from_far)])
     out = None
     for n in (0, 1):
         out = attend(queries, meta, finals[n], n * steps, steps, heads, middles[n], True, out)

time: 87.3 us -> 75.8 us (0.87)
  the two profiles are of different devices: /device:TPU:1 before, /device:TPU:9 now
where the time goes in v4:
time: 75.8 us; the launch traced here: 75.4 us
  starting transfers between devices  30.7 us (41%)
  Pallas kernels  24.5 us (32%)
  waiting for transfers between devices  18.2 us (24%)
  local copies, waits for them, and re-layouts  1.8 us (2%)
    ppermute x15, starting transfers between devices, send(): return lax.ppermute(array, 'frame', route)  30.7 us
    ppermute x15, waiting for transfers between devices, send(): return lax.ppermute(array, 'frame', route)  18.2 us
    pallas_call x5, Pallas kernels, attend(): pl.pallas_call(functools.partial(attend_kernel, plan, heads, carry is not...  14.9 us
    pallas_call x4, Pallas kernels, move(): pl.pallas_call(build, name=name, out_shape=out_shape, in_specs=specs, out...  9.6 us
    unnamed x8, local copies, waits for them, and re-layouts  1.8 us
  transfers between devices with their start and end apart: 15, of which 5 were waited for; matrix products, arithmetic and copies ran while one was open for 0% of the time, Pallas kernels for 25%

profile of v4, /device:TPU:9, one launch (start us, length us, event | category | flops | bytes accessed | tf_op | source)
XLA Modules:
  0.0 75.4 jit_solution(3259932926585354251)
XLA Ops:
  0.0 1.2 %collective-permute-start.1 = (s32[1,8]{1,0:T(1,128)}, s32[1,8]{1,0:T(1,128)S(1)}, u32[]{:S(2)}, u32[]{:S(2)}) collective-permute-start(s32[1,8]{1,0:T(1,128)} %list_ref.1), channel_id=1, source_target_pairs={{0,2},{1,3},{2,0},{3,1},{4,6},{5,7},{6,4},{7,5},{8,10},{9,11},{10,... | collective-permute-start | bytes 104 | tf_op jit(solution)/shard_map/ppermute | solution.py:338
  1.2 1.0 %collective-permute-start = (s32[1,8]{1,0:T(1,128)}, s32[1,8]{1,0:T(1,128)S(1)}, u32[]{:S(2)}, u32[]{:S(2)}) collective-permute-start(s32[1,8]{1,0:T(1,128)} %list_ref.1), channel_id=1, source_target_pairs={{0,1},{1,0},{2,3},{3,2},{4,5},{5,4},{6,7},{7,6},{8,9},{9,8},{10,11... | collective-permute-start | bytes 104 | tf_op jit(solution)/shard_map/ppermute | solution.py:338
  2.2 2.3 %collective-permute-start.2 = (s32[1,8]{1,0:T(1,128)}, s32[1,8]{1,0:T(1,128)S(1)}, u32[]{:S(2)}, u32[]{:S(2)}) collective-permute-start(s32[1,8]{1,0:T(1,128)} %list_ref.1), channel_id=1, source_target_pairs={{8,0},{9,1},{10,2},{11,3},{0,4},{1,5},{2,6},{3,7},{12,8},{13,9},{1... | collective-permute-start | bytes 104 | tf_op jit(solution)/shard_map/ppermute | solution.py:338
  4.5 0.0 collective-permute-done.1.across_ref
  4.5 0.0 collective-permute-done.beside_ref
  4.5 0.8 %collective-permute-done.2.far_ref = s32[1,8]{1,0:T(1,128)S(1)} collective-permute-done((s32[1,8]{1,0:T(1,128)}, s32[1,8]{1,0:T(1,128)S(1)}, u32[]{:S(2)}, u32[]{:S(2)}) %collective-permute-start.2) | collective-permute-done | bytes 64 | tf_op jit(solution)/shard_map/ppermute | solution.py:338
  5.3 0.7 copy-done.3
  6.0 2.8 %begin.1 = (s32[16]{0:T(128)S(1)}, bf16[512,768]{1,0:T(8,128)(2,1)S(1)}, bf16[256,1536]{1,0:T(8,128)(2,1)S(1)}, bf16[272,1536]{1,0:T(8,128)(2,1)S(1)}) custom-call(s32[1,8]{1,0:T(1,128)S(1)} %copy-done.3, s32[1]{0:T(128)} %bitcast.me_ref, s32[1,8]{1,0:T(1,128)S(1)} %collective-permute-done.beside_ref, s32[1,8]{1,0:T(1,128)S(1)} %collective-permute-done.1.across_ref, ...), custom_call_target="tpu_custom_call" | custom-call | bytes 4718592 | tf_op jit(solution)/shard_map/begin/pallas_call | solution.py:163
  8.9 2.3 %collective-permute-start.8 = (bf16[512,768]{1,0:T(8,128)(2,1)S(1)}, bf16[512,768]{1,0:T(8,128)(2,1)S(1)}, u32[]{:S(2)}, u32[]{:S(2)}) collective-permute-start(bf16[512,768]{1,0:T(8,128)(2,1)S(1)} %get-tuple-element.28), channel_id=1, source_target_pairs={{4,0},{5,1},{6,2},{7,3},{8,4},{9,5},{10,6},{11,7},{12,8},{13,9},{1... | collective-permute-start | bytes 2359304 | tf_op jit(solution)/shard_map/ppermute | solution.py:338
  11.2 0.3 collective-permute-start.3
  11.5 3.0 %collective-permute-start.7 = (bf16[512,768]{1,0:T(8,128)(2,1)S(1)}, bf16[512,768]{1,0:T(8,128)(2,1)S(1)}, u32[]{:S(2)}, u32[]{:S(2)}) collective-permute-start(bf16[512,768]{1,0:T(8,128)(2,1)S(1)} %get-tuple-element.28), channel_id=1, source_target_pairs={{0,4},{1,5},{2,6},{3,7},{4,8},{5,9},{6,10},{7,11},{8,12},{9,13},{1... | collective-permute-start | bytes 2359304 | tf_op jit(solution)/shard_map/ppermute | solution.py:338
  14.5 1.8 %collective-permute-start.6 = (bf16[256,1536]{1,0:T(8,128)(2,1)S(1)}, bf16[256,1536]{1,0:T(8,128)(2,1)S(1)}, u32[]{:S(2)}, u32[]{:S(2)}) collective-permute-start(bf16[256,1536]{1,0:T(8,128)(2,1)S(1)} %get-tuple-element.27), channel_id=1, source_target_pairs={{0,1},{1,0},{2,3},{3,2},{4,5},{5,4},{6,7},{7,6},{8,9},{9,8},{10,11... | collective-permute-start | bytes 2359304 | tf_op jit(solution)/shard_map/ppermute | solution.py:338
  16.3 1.1 %copy-done.2 = bf16[256,1536]{1,0:T(8,128)(2,1)S(1)} copy-done((bf16[256,1536]{1,0:T(8,128)(2,1)S(1)}, bf16[256,1536]{1,0:T(8,128)(2,1)}, u32[]{:S(2)}) %copy-start.2) | copy-done | bytes 786456
  17.4 3.2 %attend_own.1 = (f32[256,1536]{1,0:T(8,128)S(1)}, f32[256,1536]{1,0:T(8,128)S(1)}, f32[256,1536]{1,0:T(8,128)S(1)}) custom-call(s32[16]{0:T(128)S(1)} %get-tuple-element.24.meta, bf16[256,1536]{1,0:T(8,128)(2,1)S(1)} %copy-done, bf16[256,1536]{1,0:T(8,128)(2,1)S(1)} %copy-done.1, bf16[256,1536]{1,0:T(8,128)(2,1)S(1)} %copy-done.2), custom_call_target="tpu_custom_call" | custom-call | flops 402653184 | bytes 2359296 | tf_op jit(solution)/shard_map/attend_own/pallas_call | solution.py:141
  20.7 1.1 %pack.1 = bf16[512,768]{1,0:T(8,128)(2,1)S(1)} custom-call(bf16[256,1536]{1,0:T(8,128)(2,1)} %k_ref.7, bf16[256,1536]{1,0:T(8,128)(2,1)} %v_ref.7, f32[256,1536]{1,0:T(8,128)S(1)} %get-tuple-element.26.refs_0_.refs_9_), custom_call_target="tpu_custom_call" | custom-call | bytes 1572864 | tf_op jit(solution)/shard_map/pack/pallas_call | solution.py:163
  21.8 2.3 %collective-permute-start.5 = (bf16[512,768]{1,0:T(8,128)(2,1)S(1)}, bf16[512,768]{1,0:T(8,128)(2,1)S(1)}, u32[]{:S(2)}, u32[]{:S(2)}) collective-permute-start(bf16[512,768]{1,0:T(8,128)(2,1)S(1)} %pack.1), channel_id=1, source_target_pairs={{4,0},{5,1},{6,2},{7,3},{8,4},{9,5},{10,6},{11,7},{12,8},{13,9},{1... | collective-permute-start | bytes 2359304 | tf_op jit(solution)/shard_map/ppermute | solution.py:338
  24.1 4.8 %collective-permute-done.8.refs_7_.refs_8_.high = bf16[512,768]{1,0:T(8,128)(2,1)S(1)} collective-permute-done((bf16[512,768]{1,0:T(8,128)(2,1)S(1)}, bf16[512,768]{1,0:T(8,128)(2,1)S(1)}, u32[]{:S(2)}, u32[]{:S(2)}) %collective-permute-start.8) | collective-permute-done | bytes 786464 | tf_op jit(solution)/shard_map/ppermute | solution.py:338
  28.9 2.5 %collective-permute-start.4 = (bf16[512,768]{1,0:T(8,128)(2,1)S(1)}, bf16[512,768]{1,0:T(8,128)(2,1)S(1)}, u32[]{:S(2)}, u32[]{:S(2)}) collective-permute-start(bf16[512,768]{1,0:T(8,128)(2,1)S(1)} %pack.1), channel_id=1, source_target_pairs={{0,4},{1,5},{2,6},{3,7},{4,8},{5,9},{6,10},{7,11},{8,12},{9,13},{1... | collective-permute-start | bytes 2359304 | tf_op jit(solution)/shard_map/ppermute | solution.py:338
  31.4 2.8 %choose.2 = (bf16[256,768]{1,0:T(8,128)(2,1)S(1)}, bf16[256,768]{1,0:T(8,128)(2,1)S(1)}, bf16[256,768]{1,0:T(8,128)(2,1)S(1)}) custom-call(s32[16]{0:T(128)S(1)} %get-tuple-element.24.meta, bf16[272,1536]{1,0:T(8,128)(2,1)S(1)} %collective-permute-done.3.refs_3_.refs_4_.over_ref, bf16[256,1536]{1,0:T(8,128)(2,1)} %k_ref.7, bf16[256,1536]{1,0:T(8,128)(2,1)} %v_ref.7, ...), custom_call_target="tpu_custom_call" | custom-call | bytes 2359296 | tf_op jit(solution)/shard_map/choose/pallas_call | solution.py:163
  34.3 0.1 collective-permute-start.9
  34.3 4.9 %collective-permute-start.13 = (bf16[256,768]{1,0:T(8,128)(2,1)S(1)}, bf16[256,768]{1,0:T(8,128)(2,1)S(1)}, u32[]{:S(2)}, u32[]{:S(2)}) collective-permute-start(bf16[256,768]{1,0:T(8,128)(2,1)S(1)} %get-tuple-element.39), channel_id=1, source_target_pairs={{0,3},{1,2},{2,1},{3,0},{4,7},{5,6},{6,5},{7,4},{8,11},{9,10},{10,... | collective-permute-start | bytes 1179656 | tf_op jit(solution)/shard_map/ppermute | solution.py:338
  39.3 0.1 collective-permute-start.14
  39.3 2.8 %attend_more.2 = (f32[256,768]{1,0:T(8,128)S(1)}, f32[256,768]{1,0:T(8,128)S(1)}, f32[256,768]{1,0:T(8,128)S(1)}) custom-call(s32[16]{0:T(128)S(1)} %get-tuple-element.24.meta, bf16[256,1536]{1,0:T(8,128)(2,1)S(1)} %copy-done, bf16[256,1536]{1,0:T(8,128)(2,1)S(1)} %collective-permute-done.6.refs_1_.refs_2_, ...), custom_call_target="tpu_custom_call" | custom-call | flops 402653184 | bytes 1966080 | tf_op jit(solution)/shard_map/attend_more/pallas_call | solution.py:141
  42.1 3.7 %collective-permute-done.5.high.refs_7_.refs_8_ = bf16[512,768]{1,0:T(8,128)(2,1)S(1)} collective-permute-done((bf16[512,768]{1,0:T(8,128)(2,1)S(1)}, bf16[512,768]{1,0:T(8,128)(2,1)S(1)}, u32[]{:S(2)}, u32[]{:S(2)}) %collective-permute-start.5) | collective-permute-done | bytes 786464 | tf_op jit(solution)/shard_map/ppermute | solution.py:338
  45.8 0.9 %collective-permute-done.4.low.refs_5_.refs_6_ = bf16[512,768]{1,0:T(8,128)(2,1)S(1)} collective-permute-done((bf16[512,768]{1,0:T(8,128)(2,1)S(1)}, bf16[512,768]{1,0:T(8,128)(2,1)S(1)}, u32[]{:S(2)}, u32[]{:S(2)}) %collective-permute-start.4) | collective-permute-done | bytes 786464 | tf_op jit(solution)/shard_map/ppermute | solution.py:338
  46.7 2.8 %choose.3 = (bf16[256,768]{1,0:T(8,128)(2,1)S(1)}, bf16[256,768]{1,0:T(8,128)(2,1)S(1)}, bf16[256,768]{1,0:T(8,128)(2,1)S(1)}) custom-call(s32[16]{0:T(128)S(1)} %get-tuple-element.24.meta, bf16[272,1536]{1,0:T(8,128)(2,1)S(1)} %collective-permute-done.3.refs_3_.refs_4_.over_ref, bf16[256,1536]{1,0:T(8,128)(2,1)} %k_ref.7, bf16[256,1536]{1,0:T(8,128)(2,1)} %v_ref.7, ...), custom_call_target="tpu_custom_call" | custom-call | bytes 2359296 | tf_op jit(solution)/shard_map/choose/pallas_call | solution.py:163
  49.5 0.6 collective-permute-start.10
  50.1 8.4 %collective-permute-start.11 = (bf16[256,768]{1,0:T(8,128)(2,1)S(1)}, bf16[256,768]{1,0:T(8,128)(2,1)S(1)}, u32[]{:S(2)}, u32[]{:S(2)}) collective-permute-start(bf16[256,768]{1,0:T(8,128)(2,1)S(1)} %get-tuple-element.34), channel_id=1, source_target_pairs={{0,3},{1,2},{2,1},{3,0},{4,7},{5,6},{6,5},{7,4},{8,11},{9,10},{10,... | collective-permute-start | bytes 1179656 | tf_op jit(solution)/shard_map/ppermute | solution.py:338
  58.5 2.8 %attend_more.3 = (f32[256,768]{1,0:T(8,128)S(1)}, f32[256,768]{1,0:T(8,128)S(1)}, f32[256,768]{1,0:T(8,128)S(1)}) custom-call(s32[16]{0:T(128)S(1)} %get-tuple-element.24.meta, bf16[256,1536]{1,0:T(8,128)(2,1)S(1)} %copy-done, bf16[256,1536]{1,0:T(8,128)(2,1)S(1)} %collective-permute-done.6.refs_1_.refs_2_, ...), custom_call_target="tpu_custom_call" | custom-call | flops 402653184 | bytes 1966080 | tf_op jit(solution)/shard_map/attend_more/pallas_call | solution.py:141
  61.3 3.1 %attend_last.2.refs_10_ = bf16[256,1536]{1,0:T(8,128)(2,1)} custom-call(s32[16]{0:T(128)S(1)} %get-tuple-element.24.meta, bf16[256,1536]{1,0:T(8,128)(2,1)S(1)} %copy-done, bf16[256,768]{1,0:T(8,128)(2,1)S(1)} %collective-permute-done.9.refs_1_.refs_2_, bf16[256,768]{1,0:T(8,128)(2,1)S(1)} %collective-permute-done.9.refs_1_.refs_2_, ...), custom_call_target="tpu_custom_call" | custom-call | flops 301989888 | bytes 1572864 | tf_op jit(solution)/shard_map/attend_last/pallas_call | solution.py:141
  64.3 8.0 %collective-permute-done.11.refs_3_.refs_4_ = bf16[256,768]{1,0:T(8,128)(2,1)S(1)} collective-permute-done((bf16[256,768]{1,0:T(8,128)(2,1)S(1)}, bf16[256,768]{1,0:T(8,128)(2,1)S(1)}, u32[]{:S(2)}, u32[]{:S(2)}) %collective-permute-start.11) | collective-permute-done | bytes 393248 | tf_op jit(solution)/shard_map/ppermute | solution.py:338
  72.4 3.1 %attend_last.3 = bf16[256,1536]{1,0:T(8,128)(2,1)} custom-call(s32[16]{0:T(128)S(1)} %get-tuple-element.24.meta, bf16[256,1536]{1,0:T(8,128)(2,1)S(1)} %copy-done, bf16[256,768]{1,0:T(8,128)(2,1)S(1)} %collective-permute-done.10.refs_1_.refs_2_, bf16[256,768]{1,0:T(8,128)(2,1)S(1)} %collective-permute-done.10.refs_1_.refs_2_, ...), custom_call_target="tpu_custom_call", output_to_operand_aliasing={{}: (11, {})} | custom-call | flops 301989888 | bytes 1572864 | tf_op jit(solution)/shard_map/attend_last/pallas_call | solution.py:141
  (15 shorter events, 0.0 us)
Async XLA Ops:
  0.0 16.3 %copy-start.1 = (bf16[256,1536]{1,0:T(8,128)(2,1)S(1)}, bf16[256,1536]{1,0:T(8,128)(2,1)}, u32[]{:S(2)}) copy-start(bf16[256,1536]{1,0:T(8,128)(2,1)} %k_ref.7) | copy-start | bytes 2359300
  0.0 16.3 %copy-start = (bf16[256,1536]{1,0:T(8,128)(2,1)S(1)}, bf16[256,1536]{1,0:T(8,128)(2,1)}, u32[]{:S(2)}) copy-start(bf16[256,1536]{1,0:T(8,128)(2,1)} %refs_0_.9) | copy-start | bytes 2359300
  0.0 4.5 %collective-permute-start.1 = (s32[1,8]{1,0:T(1,128)}, s32[1,8]{1,0:T(1,128)S(1)}, u32[]{:S(2)}, u32[]{:S(2)}) collective-permute-start(s32[1,8]{1,0:T(1,128)} %list_ref.1), channel_id=1, source_target_pairs={{0,2},{1,3},{2,0},{3,1},{4,6},{5,7},{6,4},{7,5},{8,10},{9,11},{10,... | collective-permute-start | bytes 104 | tf_op jit(solution)/shard_map/ppermute | solution.py:338
  1.2 3.3 %collective-permute-start = (s32[1,8]{1,0:T(1,128)}, s32[1,8]{1,0:T(1,128)S(1)}, u32[]{:S(2)}, u32[]{:S(2)}) collective-permute-start(s32[1,8]{1,0:T(1,128)} %list_ref.1), channel_id=1, source_target_pairs={{0,1},{1,0},{2,3},{3,2},{4,5},{5,4},{6,7},{7,6},{8,9},{9,8},{10,11... | collective-permute-start | bytes 104 | tf_op jit(solution)/shard_map/ppermute | solution.py:338
  2.2 3.2 %collective-permute-start.2 = (s32[1,8]{1,0:T(1,128)}, s32[1,8]{1,0:T(1,128)S(1)}, u32[]{:S(2)}, u32[]{:S(2)}) collective-permute-start(s32[1,8]{1,0:T(1,128)} %list_ref.1), channel_id=1, source_target_pairs={{8,0},{9,1},{10,2},{11,3},{0,4},{1,5},{2,6},{3,7},{12,8},{13,9},{1... | collective-permute-start | bytes 104 | tf_op jit(solution)/shard_map/ppermute | solution.py:338
  5.3 0.7 copy-start.3
  8.9 20.1 %collective-permute-start.8 = (bf16[512,768]{1,0:T(8,128)(2,1)S(1)}, bf16[512,768]{1,0:T(8,128)(2,1)S(1)}, u32[]{:S(2)}, u32[]{:S(2)}) collective-permute-start(bf16[512,768]{1,0:T(8,128)(2,1)S(1)} %get-tuple-element.28), channel_id=1, source_target_pairs={{4,0},{5,1},{6,2},{7,3},{8,4},{9,5},{10,6},{11,7},{12,8},{13,9},{1... | collective-permute-start | bytes 2359304 | tf_op jit(solution)/shard_map/ppermute | solution.py:338
  11.2 20.2 %collective-permute-start.3 = (bf16[272,1536]{1,0:T(8,128)(2,1)S(1)}, bf16[272,1536]{1,0:T(8,128)(2,1)S(1)}, u32[]{:S(2)}, u32[]{:S(2)}) collective-permute-start(bf16[272,1536]{1,0:T(8,128)(2,1)S(1)} %get-tuple-element.25), channel_id=1, source_target_pairs={{0,2},{1,3},{2,0},{3,1},{4,6},{5,7},{6,4},{7,5},{8,10},{9,11},{10,... | collective-permute-start | bytes 2506760 | tf_op jit(solution)/shard_map/ppermute | solution.py:338
  11.5 19.9 %collective-permute-start.7 = (bf16[512,768]{1,0:T(8,128)(2,1)S(1)}, bf16[512,768]{1,0:T(8,128)(2,1)S(1)}, u32[]{:S(2)}, u32[]{:S(2)}) collective-permute-start(bf16[512,768]{1,0:T(8,128)(2,1)S(1)} %get-tuple-element.28), channel_id=1, source_target_pairs={{0,4},{1,5},{2,6},{3,7},{4,8},{5,9},{6,10},{7,11},{8,12},{9,13},{1... | collective-permute-start | bytes 2359304 | tf_op jit(solution)/shard_map/ppermute | solution.py:338
  14.5 24.8 %collective-permute-start.6 = (bf16[256,1536]{1,0:T(8,128)(2,1)S(1)}, bf16[256,1536]{1,0:T(8,128)(2,1)S(1)}, u32[]{:S(2)}, u32[]{:S(2)}) collective-permute-start(bf16[256,1536]{1,0:T(8,128)(2,1)S(1)} %get-tuple-element.27), channel_id=1, source_target_pairs={{0,1},{1,0},{2,3},{3,2},{4,5},{5,4},{6,7},{7,6},{8,9},{9,8},{10,11... | collective-permute-start | bytes 2359304 | tf_op jit(solution)/shard_map/ppermute | solution.py:338
  16.3 1.1 %copy-start.2 = (bf16[256,1536]{1,0:T(8,128)(2,1)S(1)}, bf16[256,1536]{1,0:T(8,128)(2,1)}, u32[]{:S(2)}) copy-start(bf16[256,1536]{1,0:T(8,128)(2,1)} %v_ref.7) | copy-start | bytes 2359300
  21.8 24.0 %collective-permute-start.5 = (bf16[512,768]{1,0:T(8,128)(2,1)S(1)}, bf16[512,768]{1,0:T(8,128)(2,1)S(1)}, u32[]{:S(2)}, u32[]{:S(2)}) collective-permute-start(bf16[512,768]{1,0:T(8,128)(2,1)S(1)} %pack.1), channel_id=1, source_target_pairs={{4,0},{5,1},{6,2},{7,3},{8,4},{9,5},{10,6},{11,7},{12,8},{13,9},{1... | collective-permute-start | bytes 2359304 | tf_op jit(solution)/shard_map/ppermute | solution.py:338
  28.9 17.7 %collective-permute-start.4 = (bf16[512,768]{1,0:T(8,128)(2,1)S(1)}, bf16[512,768]{1,0:T(8,128)(2,1)S(1)}, u32[]{:S(2)}, u32[]{:S(2)}) collective-permute-start(bf16[512,768]{1,0:T(8,128)(2,1)S(1)} %pack.1), channel_id=1, source_target_pairs={{0,4},{1,5},{2,6},{3,7},{4,8},{5,9},{6,10},{7,11},{8,12},{9,13},{1... | collective-permute-start | bytes 2359304 | tf_op jit(solution)/shard_map/ppermute | solution.py:338
  34.3 12.4 %collective-permute-start.9 = (bf16[256,768]{1,0:T(8,128)(2,1)S(1)}, bf16[256,768]{1,0:T(8,128)(2,1)S(1)}, u32[]{:S(2)}, u32[]{:S(2)}) collective-permute-start(bf16[256,768]{1,0:T(8,128)(2,1)S(1)} %get-tuple-element.32), channel_id=1, source_target_pairs={{0,2},{1,3},{2,0},{3,1},{4,6},{5,7},{6,4},{7,5},{8,10},{9,11},{10,... | collective-permute-start | bytes 1179656 | tf_op jit(solution)/shard_map/ppermute | solution.py:338
  34.3 26.9 %collective-permute-start.13 = (bf16[256,768]{1,0:T(8,128)(2,1)S(1)}, bf16[256,768]{1,0:T(8,128)(2,1)S(1)}, u32[]{:S(2)}, u32[]{:S(2)}) collective-permute-start(bf16[256,768]{1,0:T(8,128)(2,1)S(1)} %get-tuple-element.39), channel_id=1, source_target_pairs={{0,3},{1,2},{2,1},{3,0},{4,7},{5,6},{6,5},{7,4},{8,11},{9,10},{10,... | collective-permute-start | bytes 1179656 | tf_op jit(solution)/shard_map/ppermute | solution.py:338
  39.3 22.0 %collective-permute-start.14 = (bf16[256,768]{1,0:T(8,128)(2,1)S(1)}, bf16[256,768]{1,0:T(8,128)(2,1)S(1)}, u32[]{:S(2)}, u32[]{:S(2)}) collective-permute-start(bf16[256,768]{1,0:T(8,128)(2,1)S(1)} %get-tuple-element.40), channel_id=1, source_target_pairs={{0,8},{1,9},{2,10},{3,11},{4,0},{5,1},{6,2},{7,3},{8,12},{9,13},{1... | collective-permute-start | bytes 1179656 | tf_op jit(solution)/shard_map/ppermute | solution.py:338
  49.5 14.9 %collective-permute-start.10 = (bf16[256,768]{1,0:T(8,128)(2,1)S(1)}, bf16[256,768]{1,0:T(8,128)(2,1)S(1)}, u32[]{:S(2)}, u32[]{:S(2)}) collective-permute-start(bf16[256,768]{1,0:T(8,128)(2,1)S(1)} %get-tuple-element.33), channel_id=1, source_target_pairs={{0,2},{1,3},{2,0},{3,1},{4,6},{5,7},{6,4},{7,5},{8,10},{9,11},{10,... | collective-permute-start | bytes 1179656 | tf_op jit(solution)/shard_map/ppermute | solution.py:338
  50.1 22.3 %collective-permute-start.11 = (bf16[256,768]{1,0:T(8,128)(2,1)S(1)}, bf16[256,768]{1,0:T(8,128)(2,1)S(1)}, u32[]{:S(2)}, u32[]{:S(2)}) collective-permute-start(bf16[256,768]{1,0:T(8,128)(2,1)S(1)} %get-tuple-element.34), channel_id=1, source_target_pairs={{0,3},{1,2},{2,1},{3,0},{4,7},{5,6},{6,5},{7,4},{8,11},{9,10},{10,... | collective-permute-start | bytes 1179656 | tf_op jit(solution)/shard_map/ppermute | solution.py:338
  58.5 13.9 %collective-permute-start.12 = (bf16[256,768]{1,0:T(8,128)(2,1)S(1)}, bf16[256,768]{1,0:T(8,128)(2,1)S(1)}, u32[]{:S(2)}, u32[]{:S(2)}) collective-permute-start(bf16[256,768]{1,0:T(8,128)(2,1)S(1)} %get-tuple-element.35), channel_id=1, source_target_pairs={{0,8},{1,9},{2,10},{3,11},{4,0},{5,1},{6,2},{7,3},{8,12},{9,13},{1... | collective-permute-start | bytes 1179656 | tf_op jit(solution)/shard_map/ppermute | solution.py:338

commit v5 on v4

--- a/solution.py
+++ b/solution.py
@@ -196,77 +196,66 @@
             copy.start()
 
 
-def begin(tile_lists, me, beside_list, across_list, far_list, keys, values, width):
-    rows, all_width = keys.shape
+def tile_at(ref, entry, tile_count):
+    return jnp.clip(ref[0, entry], 0, tile_count - 1)
+
+
+def begin(me, beside_list, across_list, keys, values):
+    rows, width = keys.shape
     tile_count = rows // TILE
 
-    def build(list_ref, me_ref, beside_ref, across_ref, far_ref, k_ref, v_ref, *refs):
-        meta, packed, to_beside, to_across, note, sems = refs
+    def build(me_ref, beside_ref, across_ref, k_ref, v_ref, to_beside, to_across, note, sems):
         me = me_ref[0]
-        plane, right = me // 4, me % 4 >= 2
-
-        def tile_at(ref, entry):
-            return jnp.clip(ref[0, entry], 0, tile_count - 1)
-
-        copies = [
-            pltpu.make_async_copy(
-                ref.at[:, pl.ds(0, width)], packed.at[pl.ds(n * rows, rows)], sems.at[n]
-            )
-            for n, ref in enumerate((k_ref, v_ref))
-        ]
         own = ((k_ref, 0, 0), (v_ref, 0, 0))
-        copies += tile_copies(own, tile_at(across_ref, jnp.where(right, 5, 1)), to_across, None, sems, 2)
-        copies += tile_copies(own, tile_at(beside_ref, jnp.where(me % 2 == 0, 0, 4)), to_beside, None, sems, 4)
+        tile = tile_at(across_ref, jnp.where(me % 4 >= 2, 5, 1), tile_count)
+        copies = tile_copies(own, tile, to_across, None, sems, 0)
+        tile = tile_at(beside_ref, jnp.where(me % 2 == 0, 0, 4), tile_count)
+        copies += tile_copies(own, tile, to_beside, None, sems, 2)
         for copy in copies:
             copy.start()
         lane = lax.broadcasted_iota(jnp.int32, note.shape, 1)
         row = jnp.zeros(note.shape, jnp.float32)
         for entry in range(8):
-            row = jnp.where(lane == entry, tile_at(beside_ref, entry).astype(jnp.float32), row)
+            row = jnp.where(lane == entry, tile_at(beside_ref, entry, tile_count).astype(jnp.float32), row)
         note[...] = row.astype(jnp.bfloat16)
         copies.append(
-            pltpu.make_async_copy(note, to_across.at[pl.ds(2 * TILE, NOTE_ROWS)], sems.at[6])
+            pltpu.make_async_copy(note, to_across.at[pl.ds(2 * TILE, NOTE_ROWS)], sems.at[4])
         )
         copies[-1].start()
-        for entry in range(8):
-            meta[entry] = tile_at(list_ref, entry)
-        meta[8] = me
-        meta[9] = tile_at(far_ref, jnp.where(plane % 2 == 0, 3, 7))
-        meta[10] = tile_at(across_ref, jnp.where(right, 1, 5))
-        for entry in range(11, 16):
-            meta[entry] = 0
         for copy in copies:
             copy.wait()
 
     return move(
         "begin",
         build,
-        (tile_lists, me, beside_list, across_list, far_list, in_hbm(keys), in_hbm(values)),
-        [SCALAR] * 5 + [WHOLE] * 2,
+        (me, beside_list, across_list, in_hbm(keys), in_hbm(values)),
+        [SCALAR] * 3 + [WHOLE] * 2,
         [
-            jax.ShapeDtypeStruct((16,), jnp.int32),
-            jax.ShapeDtypeStruct((2 * rows, width), jnp.bfloat16),
-            jax.ShapeDtypeStruct((2 * TILE, all_width), jnp.bfloat16),
-            jax.ShapeDtypeStruct((2 * TILE + NOTE_ROWS, all_width), jnp.bfloat16),
+            jax.ShapeDtypeStruct((2 * TILE, width), jnp.bfloat16),
+            jax.ShapeDtypeStruct((2 * TILE + NOTE_ROWS, width), jnp.bfloat16),
         ],
-        [SCALAR, WHOLE, WHOLE, WHOLE],
-        7,
-        24 * TILE * all_width,
-        [pltpu.VMEM((NOTE_ROWS, all_width), jnp.bfloat16)],
+        [WHOLE, WHOLE],
+        5,
+        16 * TILE * width,
+        [pltpu.VMEM((NOTE_ROWS, width), jnp.bfloat16)],
     )
 
 
-def pack(keys, values, first, width, after):
+def pack_copies(k_ref, v_ref, first, packed, sems):
+    rows, width = k_ref.shape[0], packed.shape[1]
+    return [
+        pltpu.make_async_copy(
+            ref.at[:, pl.ds(first, width)], packed.at[pl.ds(n * rows, rows)], sems.at[n]
+        )
+        for n, ref in enumerate((k_ref, v_ref))
+    ]
+
+
+def pack(keys, values, width):
     rows = keys.shape[0]
 
-    def build(k_ref, v_ref, *refs):
-        out_ref, sems = refs[-2:]
-        copies = [
-            pltpu.make_async_copy(
-                ref.at[:, pl.ds(first, width)], out_ref.at[pl.ds(n * rows, rows)], sems.at[n]
-            )
-            for n, ref in enumerate((k_ref, v_ref))
-        ]
+    def build(k_ref, v_ref, packed, sems):
+        copies = pack_copies(k_ref, v_ref, 0, packed, sems)
         for copy in copies:
             copy.start()
         for copy in copies:
@@ -275,8 +264,8 @@
     return move(
         "pack",
         build,
-        (in_hbm(keys), in_hbm(values), *after),
-        [WHOLE] * (2 + len(after)),
+        (in_hbm(keys), in_hbm(values)),
+        [WHOLE] * 2,
         jax.ShapeDtypeStruct((2 * rows, width), jnp.bfloat16),
         WHOLE,
         2,
@@ -284,11 +273,44 @@
     )
 
 
-def choose(meta, over, keys, values, first, low, high, after):
+def pack_rest(tile_lists, me, across_list, keys, values, first, after):
+    rows = keys.shape[0]
+    width = keys.shape[1] - first
+    tile_count = rows // TILE
+
+    def build(list_ref, me_ref, across_ref, k_ref, v_ref, *refs):
+        packed, meta, sems = refs[-3:]
+        copies = pack_copies(k_ref, v_ref, first, packed, sems)
+        for copy in copies:
+            copy.start()
+        me = me_ref[0]
+        for entry in range(8):
+            meta[entry] = tile_at(list_ref, entry, tile_count)
+        meta[8] = me
+        meta[9] = tile_at(across_ref, jnp.where(me % 4 >= 2, 1, 5), tile_count)
+        for copy in copies:
+            copy.wait()
+
+    return move(
+        "pack_rest",
+        build,
+        (tile_lists, me, across_list, in_hbm(keys), in_hbm(values), *after),
+        [SCALAR] * 3 + [WHOLE] * (2 + len(after)),
+        [
+            jax.ShapeDtypeStruct((2 * rows, width), jnp.bfloat16),
+            jax.ShapeDtypeStruct((10,), jnp.int32),
+        ],
+        [WHOLE, SCALAR],
+        2,
+        8 * rows * width,
+    )
+
+
+def choose(meta, far_list, over, keys, values, first, low, high, after):
     rows, width = low.shape[0] // 2, low.shape[1]
     tile_count = rows // TILE
 
-    def build(meta, over_ref, k_ref, v_ref, low, high, *refs):
+    def build(meta, far_ref, over_ref, k_ref, v_ref, low, high, *refs):
         to_two, to_one, to_far, note, sems = refs[-5:]
         spot, plane = meta[8] % 4, meta[8] // 4
         right = spot >= 2
@@ -303,11 +325,12 @@
         def copies(source, tile, target, at):
             return tile_copies(source, tile, target, None, sems, at)
 
-        start_if((plane == 0) | (plane == 3), copies(own, meta[9], to_far, 0))
-        start_if(plane == 1, copies(above, meta[9], to_far, 0))
-        start_if(plane == 2, copies(below, meta[9], to_far, 0))
-        start_if(right, copies(below, meta[10], to_two, 2))
-        start_if(jnp.logical_not(right), copies(above, meta[10], to_two, 2))
+        tile = tile_at(far_ref, jnp.where(plane % 2 == 0, 3, 7), tile_count)
+        start_if((plane == 0) | (plane == 3), copies(own, tile, to_far, 0))
+        start_if(plane == 1, copies(above, tile, to_far, 0))
+        start_if(plane == 2, copies(below, tile, to_far, 0))
+        start_if(right, copies(below, meta[9], to_two, 2))
+        start_if(jnp.logical_not(right), copies(above, meta[9], to_two, 2))
         read.wait()
         here = (lax.broadcasted_iota(jnp.int32, note.shape, 1) == jnp.where(spot % 2 == 0, 4, 0)) & (
             lax.broadcasted_iota(jnp.int32, note.shape, 0) == 0
@@ -324,8 +347,8 @@
     return move(
         "choose",
         build,
-        (meta, over, in_hbm(keys), in_hbm(values), low, high, *after),
-        [SCALAR] + [WHOLE] * (5 + len(after)),
+        (meta, far_list, over, in_hbm(keys), in_hbm(values), low, high, *after),
+        [SCALAR] * 2 + [WHOLE] * (5 + len(after)),
         [jax.ShapeDtypeStruct((2 * TILE, width), jnp.bfloat16)] * 3,
         [WHOLE] * 3,
         7,
@@ -401,22 +424,21 @@
     far_list = send(tile_lists, [(j, i) for i, j in far])
     beside_list = send(tile_lists, beside)
     across_list = send(tile_lists, across)
-    meta, first, to_beside, to_across = begin(
-        tile_lists, me, beside_list, across_list, far_list, key_heads, value_heads, half
-    )
-    over = send(to_across, across)
+    first = pack(key_heads, value_heads, half)
     low = [send(first, up)]
     high = [send(first, down)]
+    to_beside, to_across = begin(me, beside_list, across_list, key_heads, value_heads)
+    over = send(to_across, across)
     next_to = send(to_beside, beside)
-    begun = attend(queries, meta, [own_frame()], 0, 2 * steps, heads)
-    second = pack(key_heads, value_heads, half, half, [begun[0]])
+    begun = attend(queries, me, [own_frame()], 0, 2 * steps, heads)
+    second, meta = pack_rest(tile_lists, me, across_list, key_heads, value_heads, half, [begun[0]])
     low.append(send(second, up))
     high.append(send(second, down))
 
     after = []
     middles, finals = [], []
     for n in (0, 1):
-        sent = choose(meta, over, key_heads, value_heads, n * half, low[n], high[n], after)
+        sent = choose(meta, far_list, over, key_heads, value_heads, n * half, low[n], high[n], after)
         two = send(sent[0], across)
         one = send(sent[1], corner)
         from_far = send(sent[2], far)
@@ -435,7 +457,7 @@
             begun,
             held=n * steps,
         )
-        after = [middle[0], two]
+        after = [middle[0]]
         middles.append(middle)
         finals.append([sent_tile(two, 0, two_there), sent_tile(one, 0, one_there), sent_tile(from_far)])
     out = None

time: 75.8 us -> 112 us (1.48)
  the two profiles are of different devices: /device:TPU:9 before, /device:TPU:12 now
where the time goes in v5:
time: 112 us; the launch traced here: 111 us
  Pallas kernels  48.2 us (43%)
  waiting for transfers between devices  32.6 us (29%)
  starting transfers between devices  30.4 us (27%)
    pallas_call x5, Pallas kernels, move(): pl.pallas_call(build, name=name, out_shape=out_shape, in_specs=specs, out...  33.9 us
    ppermute x15, waiting for transfers between devices, send(): return lax.ppermute(array, 'frame', route)  32.6 us
    ppermute x15, starting transfers between devices, send(): return lax.ppermute(array, 'frame', route)  30.4 us
    pallas_call x5, Pallas kernels, attend(): pl.pallas_call(functools.partial(attend_kernel, plan, heads, carry is not...  14.4 us
  transfers between devices with their start and end apart: 15, of which 7 were waited for; matrix products, arithmetic and copies ran while one was open for 0% of the time, Pallas kernels for 18%

profile of v5, /device:TPU:12, one launch (start us, length us, event | category | flops | bytes accessed | tf_op | source)
XLA Modules:
  0.0 111.4 jit_solution(10491812175420306091)
XLA Ops:
  0.0 24.9 %pack.1 = bf16[512,768]{1,0:T(8,128)(2,1)} custom-call(bf16[256,1536]{1,0:T(8,128)(2,1)} %k_ref.9, bf16[256,1536]{1,0:T(8,128)(2,1)} %v_ref.9), custom_call_target="tpu_custom_call" | custom-call | bytes 1572864 | tf_op jit(solution)/shard_map/pack/pallas_call | solution.py:163
  25.0 3.5 %collective-permute-start.7 = (bf16[512,768]{1,0:T(8,128)(2,1)}, bf16[512,768]{1,0:T(8,128)(2,1)S(1)}, u32[]{:S(2)}, u32[]{:S(2)}) collective-permute-start(bf16[512,768]{1,0:T(8,128)(2,1)} %pack.1), channel_id=1, source_target_pairs={{0,4},{1,5},{2,6},{3,7},{4,8},{5,9},{6,10},{7,11},{8,12},{9,13},{1... | collective-permute-start | bytes 2359304 | tf_op jit(solution)/shard_map/ppermute | solution.py:361
  28.5 1.6 %collective-permute-start = (s32[1,8]{1,0:T(1,128)S(1)}, s32[1,8]{1,0:T(1,128)S(1)}, u32[]{:S(2)}, u32[]{:S(2)}) collective-permute-start(s32[1,8]{1,0:T(1,128)S(1)} %copy-done.3), channel_id=1, source_target_pairs={{0,2},{1,3},{2,0},{3,1},{4,6},{5,7},{6,4},{7,5},{8,10},{9,11},{10,... | collective-permute-start | bytes 104 | tf_op jit(solution)/shard_map/ppermute | solution.py:361
  30.0 0.0 collective-permute-start.2
  30.0 2.0 %collective-permute-done.across_ref = s32[1,8]{1,0:T(1,128)S(1)} collective-permute-done((s32[1,8]{1,0:T(1,128)S(1)}, s32[1,8]{1,0:T(1,128)S(1)}, u32[]{:S(2)}, u32[]{:S(2)}) %collective-permute-start) | collective-permute-done | bytes 64 | tf_op jit(solution)/shard_map/ppermute | solution.py:361
  32.1 2.0 %begin.1 = (bf16[256,1536]{1,0:T(8,128)(2,1)S(1)}, bf16[272,1536]{1,0:T(8,128)(2,1)S(1)}) custom-call(s32[1]{0:T(128)} %bitcast.meta.me_ref, s32[1,8]{1,0:T(1,128)S(1)} %collective-permute-done.2.beside_ref, s32[1,8]{1,0:T(1,128)S(1)} %collective-permute-done.across_ref, bf16[256,1536]{1,0:T(8,128)(2,1)} %k_ref.9, bf16[256,1536]{1,0:T(8,128)(2,1)} %v_ref.9), custom_call_target="tpu_custom_call" | custom-call | bytes 3145728 | tf_op jit(solution)/shard_map/begin/pallas_call | solution.py:163
  34.1 1.6 %collective-permute-start.3 = (bf16[272,1536]{1,0:T(8,128)(2,1)S(1)}, bf16[272,1536]{1,0:T(8,128)(2,1)S(1)}, u32[]{:S(2)}, u32[]{:S(2)}) collective-permute-start(bf16[272,1536]{1,0:T(8,128)(2,1)S(1)} %get-tuple-element.26), channel_id=1, source_target_pairs={{0,2},{1,3},{2,0},{3,1},{4,6},{5,7},{6,4},{7,5},{8,10},{9,11},{10,... | collective-permute-start | bytes 2506760 | tf_op jit(solution)/shard_map/ppermute | solution.py:361
  35.7 2.3 %collective-permute-start.8 = (bf16[512,768]{1,0:T(8,128)(2,1)}, bf16[512,768]{1,0:T(8,128)(2,1)S(1)}, u32[]{:S(2)}, u32[]{:S(2)}) collective-permute-start(bf16[512,768]{1,0:T(8,128)(2,1)} %pack.1), channel_id=1, source_target_pairs={{4,0},{5,1},{6,2},{7,3},{8,4},{9,5},{10,6},{11,7},{12,8},{13,9},{1... | collective-permute-start | bytes 2359304 | tf_op jit(solution)/shard_map/ppermute | solution.py:361
  38.0 2.7 %collective-permute-start.1 = (s32[1,8]{1,0:T(1,128)S(1)}, s32[1,8]{1,0:T(1,128)S(1)}, u32[]{:S(2)}, u32[]{:S(2)}) collective-permute-start(s32[1,8]{1,0:T(1,128)S(1)} %copy-done.3), channel_id=1, source_target_pairs={{8,0},{9,1},{10,2},{11,3},{0,4},{1,5},{2,6},{3,7},{12,8},{13,9},{1... | collective-permute-start | bytes 104 | tf_op jit(solution)/shard_map/ppermute | solution.py:361
  40.7 0.0 collective-permute-start.6
  40.7 2.7 %attend_own.1 = (f32[256,1536]{1,0:T(8,128)S(1)}, f32[256,1536]{1,0:T(8,128)S(1)}, f32[256,1536]{1,0:T(8,128)S(1)}) custom-call(s32[1]{0:T(128)} %bitcast.meta.me_ref, bf16[256,1536]{1,0:T(8,128)(2,1)S(1)} %copy-done.2, bf16[256,1536]{1,0:T(8,128)(2,1)S(1)} %copy-done, bf16[256,1536]{1,0:T(8,128)(2,1)S(1)} %copy-done.1), custom_call_target="tpu_custom_call" | custom-call | flops 402653184 | bytes 2359296 | tf_op jit(solution)/shard_map/attend_own/pallas_call | solution.py:141
  43.4 2.3 %pack_rest.1 = (bf16[512,768]{1,0:T(8,128)(2,1)S(1)}, s32[10]{0:T(128)S(1)}) custom-call(s32[1,8]{1,0:T(1,128)S(1)} %copy-done.3, s32[1]{0:T(128)} %bitcast.meta.me_ref, s32[1,8]{1,0:T(1,128)S(1)} %collective-permute-done.across_ref, bf16[256,1536]{1,0:T(8,128)(2,1)} %k_ref.9, bf16[256,1536]{1,0:T(8,128)(2,1)} %v_ref.9, ...), custom_call_target="tpu_custom_call" | custom-call | bytes 1572864 | tf_op jit(solution)/shard_map/pack_rest/pallas_call | solution.py:163
  45.7 0.7 collective-permute-done.1.far_ref
  46.4 12.7 %collective-permute-start.4 = (bf16[512,768]{1,0:T(8,128)(2,1)S(1)}, bf16[512,768]{1,0:T(8,128)(2,1)S(1)}, u32[]{:S(2)}, u32[]{:S(2)}) collective-permute-start(bf16[512,768]{1,0:T(8,128)(2,1)S(1)} %get-tuple-element.27), channel_id=1, source_target_pairs={{0,4},{1,5},{2,6},{3,7},{4,8},{5,9},{6,10},{7,11},{8,12},{9,13},{1... | collective-permute-start | bytes 2359304 | tf_op jit(solution)/shard_map/ppermute | solution.py:361
  59.2 0.0 collective-permute-done.7.refs_5_.refs_6_.low
  59.2 1.9 %collective-permute-start.5 = (bf16[512,768]{1,0:T(8,128)(2,1)S(1)}, bf16[512,768]{1,0:T(8,128)(2,1)S(1)}, u32[]{:S(2)}, u32[]{:S(2)}) collective-permute-start(bf16[512,768]{1,0:T(8,128)(2,1)S(1)} %get-tuple-element.27), channel_id=1, source_target_pairs={{4,0},{5,1},{6,2},{7,3},{8,4},{9,5},{10,6},{11,7},{12,8},{13,9},{1... | collective-permute-start | bytes 2359304 | tf_op jit(solution)/shard_map/ppermute | solution.py:361
  61.1 2.3 %choose.3 = (bf16[256,768]{1,0:T(8,128)(2,1)S(1)}, bf16[256,768]{1,0:T(8,128)(2,1)S(1)}, bf16[256,768]{1,0:T(8,128)(2,1)S(1)}) custom-call(s32[10]{0:T(128)S(1)} %get-tuple-element.25.meta, s32[1,8]{1,0:T(1,128)S(1)} %collective-permute-done.1.far_ref, bf16[272,1536]{1,0:T(8,128)(2,1)S(1)} %collective-permute-done.3.refs_3_.refs_4_.over_ref, ...), custom_call_target="tpu_custom_call" | custom-call | bytes 2359296 | tf_op jit(solution)/shard_map/choose/pallas_call | solution.py:163
  63.5 1.7 %collective-permute-start.12 = (bf16[256,768]{1,0:T(8,128)(2,1)S(1)}, bf16[256,768]{1,0:T(8,128)(2,1)S(1)}, u32[]{:S(2)}, u32[]{:S(2)}) collective-permute-start(bf16[256,768]{1,0:T(8,128)(2,1)S(1)} %get-tuple-element.38), channel_id=1, source_target_pairs={{0,2},{1,3},{2,0},{3,1},{4,6},{5,7},{6,4},{7,5},{8,10},{9,11},{10,... | collective-permute-start | bytes 1179656 | tf_op jit(solution)/shard_map/ppermute | solution.py:361
  65.1 0.0 collective-permute-start.13
  65.2 2.8 %attend_more.2 = (f32[256,768]{1,0:T(8,128)S(1)}, f32[256,768]{1,0:T(8,128)S(1)}, f32[256,768]{1,0:T(8,128)S(1)}) custom-call(s32[10]{0:T(128)S(1)} %get-tuple-element.25.meta, bf16[256,1536]{1,0:T(8,128)(2,1)S(1)} %copy-done.2, bf16[256,1536]{1,0:T(8,128)(2,1)S(1)} %collective-permute-done.6.refs_1_.refs_2_, ...), custom_call_target="tpu_custom_call" | custom-call | flops 402653184 | bytes 1966080 | tf_op jit(solution)/shard_map/attend_more/pallas_call | solution.py:141
  67.9 14.0 %collective-permute-done.4.low.refs_5_.refs_6_ = bf16[512,768]{1,0:T(8,128)(2,1)S(1)} collective-permute-done((bf16[512,768]{1,0:T(8,128)(2,1)S(1)}, bf16[512,768]{1,0:T(8,128)(2,1)S(1)}, u32[]{:S(2)}, u32[]{:S(2)}) %collective-permute-start.4) | collective-permute-done | bytes 786464 | tf_op jit(solution)/shard_map/ppermute | solution.py:361
  82.0 4.1 %collective-permute-done.5.high.refs_7_.refs_8_ = bf16[512,768]{1,0:T(8,128)(2,1)S(1)} collective-permute-done((bf16[512,768]{1,0:T(8,128)(2,1)S(1)}, bf16[512,768]{1,0:T(8,128)(2,1)S(1)}, u32[]{:S(2)}, u32[]{:S(2)}) %collective-permute-start.5) | collective-permute-done | bytes 786464 | tf_op jit(solution)/shard_map/ppermute | solution.py:361
  86.1 2.3 %choose.2 = (bf16[256,768]{1,0:T(8,128)(2,1)S(1)}, bf16[256,768]{1,0:T(8,128)(2,1)S(1)}, bf16[256,768]{1,0:T(8,128)(2,1)S(1)}) custom-call(s32[10]{0:T(128)S(1)} %get-tuple-element.25.meta, s32[1,8]{1,0:T(1,128)S(1)} %collective-permute-done.1.far_ref, bf16[272,1536]{1,0:T(8,128)(2,1)S(1)} %collective-permute-done.3.refs_3_.refs_4_.over_ref, ...), custom_call_target="tpu_custom_call" | custom-call | bytes 2359296 | tf_op jit(solution)/shard_map/choose/pallas_call | solution.py:163
  88.4 0.1 collective-permute-start.10
  88.5 0.1 collective-permute-start.11
  88.6 2.3 %collective-permute-start.9 = (bf16[256,768]{1,0:T(8,128)(2,1)S(1)}, bf16[256,768]{1,0:T(8,128)(2,1)S(1)}, u32[]{:S(2)}, u32[]{:S(2)}) collective-permute-start(bf16[256,768]{1,0:T(8,128)(2,1)S(1)} %get-tuple-element.32), channel_id=1, source_target_pairs={{0,2},{1,3},{2,0},{3,1},{4,6},{5,7},{6,4},{7,5},{8,10},{9,11},{10,... | collective-permute-start | bytes 1179656 | tf_op jit(solution)/shard_map/ppermute | solution.py:361
  90.8 2.8 %attend_more.3 = (f32[256,768]{1,0:T(8,128)S(1)}, f32[256,768]{1,0:T(8,128)S(1)}, f32[256,768]{1,0:T(8,128)S(1)}) custom-call(s32[10]{0:T(128)S(1)} %get-tuple-element.25.meta, bf16[256,1536]{1,0:T(8,128)(2,1)S(1)} %copy-done.2, bf16[256,1536]{1,0:T(8,128)(2,1)S(1)} %collective-permute-done.6.refs_1_.refs_2_, ...), custom_call_target="tpu_custom_call" | custom-call | flops 402653184 | bytes 1966080 | tf_op jit(solution)/shard_map/attend_more/pallas_call | solution.py:141
  93.7 3.1 %attend_last.2.refs_10_ = bf16[256,1536]{1,0:T(8,128)(2,1)} custom-call(s32[10]{0:T(128)S(1)} %get-tuple-element.25.meta, bf16[256,1536]{1,0:T(8,128)(2,1)S(1)} %copy-done.2, bf16[256,768]{1,0:T(8,128)(2,1)S(1)} %collective-permute-done.12.refs_1_.refs_2_, bf16[256,768]{1,0:T(8,128)(2,1)S(1)} %collective-permute-done.12.refs_1_.refs_2_, ...), custom_call_target="tpu_custom_call" | custom-call | flops 301989888 | bytes 1572864 | tf_op jit(solution)/shard_map/attend_last/pallas_call | solution.py:141
  96.7 2.5 %collective-permute-done.10.refs_3_.refs_4_ = bf16[256,768]{1,0:T(8,128)(2,1)S(1)} collective-permute-done((bf16[256,768]{1,0:T(8,128)(2,1)S(1)}, bf16[256,768]{1,0:T(8,128)(2,1)S(1)}, u32[]{:S(2)}, u32[]{:S(2)}) %collective-permute-start.10) | collective-permute-done | bytes 393248 | tf_op jit(solution)/shard_map/ppermute | solution.py:361
  99.2 0.9 collective-permute-done.11.refs_5_.refs_6_
  100.1 8.2 %collective-permute-done.9.refs_1_.refs_2_ = bf16[256,768]{1,0:T(8,128)(2,1)S(1)} collective-permute-done((bf16[256,768]{1,0:T(8,128)(2,1)S(1)}, bf16[256,768]{1,0:T(8,128)(2,1)S(1)}, u32[]{:S(2)}, u32[]{:S(2)}) %collective-permute-start.9) | collective-permute-done | bytes 393248 | tf_op jit(solution)/shard_map/ppermute | solution.py:361
  108.3 3.1 %attend_last.3 = bf16[256,1536]{1,0:T(8,128)(2,1)} custom-call(s32[10]{0:T(128)S(1)} %get-tuple-element.25.meta, bf16[256,1536]{1,0:T(8,128)(2,1)S(1)} %copy-done.2, bf16[256,768]{1,0:T(8,128)(2,1)S(1)} %collective-permute-done.9.refs_1_.refs_2_, bf16[256,768]{1,0:T(8,128)(2,1)S(1)} %collective-permute-done.9.refs_1_.refs_2_, ...), custom_call_target="tpu_custom_call", output_to_operand_aliasing={{}: (11, {})} | custom-call | flops 301989888 | bytes 1572864 | tf_op jit(solution)/shard_map/attend_last/pallas_call | solution.py:141
  (16 shorter events, 0.0 us)
Async XLA Ops:
  0.0 40.7 %copy-start = (bf16[256,1536]{1,0:T(8,128)(2,1)S(1)}, bf16[256,1536]{1,0:T(8,128)(2,1)}, u32[]{:S(2)}) copy-start(bf16[256,1536]{1,0:T(8,128)(2,1)} %k_ref.9) | copy-start | bytes 2359300
  0.0 40.7 %copy-start.1 = (bf16[256,1536]{1,0:T(8,128)(2,1)S(1)}, bf16[256,1536]{1,0:T(8,128)(2,1)}, u32[]{:S(2)}) copy-start(bf16[256,1536]{1,0:T(8,128)(2,1)} %v_ref.9) | copy-start | bytes 2359300
  0.0 28.5 %copy-start.3 = (s32[1,8]{1,0:T(1,128)S(1)}, s32[1,8]{1,0:T(1,128)}, u32[]{:S(2)}) copy-start(s32[1,8]{1,0:T(1,128)} %list_ref.1) | copy-start | bytes 100
  0.0 40.7 %copy-start.2 = (bf16[256,1536]{1,0:T(8,128)(2,1)S(1)}, bf16[256,1536]{1,0:T(8,128)(2,1)}, u32[]{:S(2)}) copy-start(bf16[256,1536]{1,0:T(8,128)(2,1)} %refs_0_.9) | copy-start | bytes 2359300
  25.0 34.2 %collective-permute-start.7 = (bf16[512,768]{1,0:T(8,128)(2,1)}, bf16[512,768]{1,0:T(8,128)(2,1)S(1)}, u32[]{:S(2)}, u32[]{:S(2)}) collective-permute-start(bf16[512,768]{1,0:T(8,128)(2,1)} %pack.1), channel_id=1, source_target_pairs={{0,4},{1,5},{2,6},{3,7},{4,8},{5,9},{6,10},{7,11},{8,12},{9,13},{1... | collective-permute-start | bytes 2359304 | tf_op jit(solution)/shard_map/ppermute | solution.py:361
  28.5 3.6 %collective-permute-start = (s32[1,8]{1,0:T(1,128)S(1)}, s32[1,8]{1,0:T(1,128)S(1)}, u32[]{:S(2)}, u32[]{:S(2)}) collective-permute-start(s32[1,8]{1,0:T(1,128)S(1)} %copy-done.3), channel_id=1, source_target_pairs={{0,2},{1,3},{2,0},{3,1},{4,6},{5,7},{6,4},{7,5},{8,10},{9,11},{10,... | collective-permute-start | bytes 104 | tf_op jit(solution)/shard_map/ppermute | solution.py:361
  30.0 2.1 %collective-permute-start.2 = (s32[1,8]{1,0:T(1,128)S(1)}, s32[1,8]{1,0:T(1,128)S(1)}, u32[]{:S(2)}, u32[]{:S(2)}) collective-permute-start(s32[1,8]{1,0:T(1,128)S(1)} %copy-done.3), channel_id=1, source_target_pairs={{0,1},{1,0},{2,3},{3,2},{4,5},{5,4},{6,7},{7,6},{8,9},{9,8},{10,11... | collective-permute-start | bytes 104 | tf_op jit(solution)/shard_map/ppermute | solution.py:361
  34.1 27.0 %collective-permute-start.3 = (bf16[272,1536]{1,0:T(8,128)(2,1)S(1)}, bf16[272,1536]{1,0:T(8,128)(2,1)S(1)}, u32[]{:S(2)}, u32[]{:S(2)}) collective-permute-start(bf16[272,1536]{1,0:T(8,128)(2,1)S(1)} %get-tuple-element.26), channel_id=1, source_target_pairs={{0,2},{1,3},{2,0},{3,1},{4,6},{5,7},{6,4},{7,5},{8,10},{9,11},{10,... | collective-permute-start | bytes 2506760 | tf_op jit(solution)/shard_map/ppermute | solution.py:361
  35.7 25.4 %collective-permute-start.8 = (bf16[512,768]{1,0:T(8,128)(2,1)}, bf16[512,768]{1,0:T(8,128)(2,1)S(1)}, u32[]{:S(2)}, u32[]{:S(2)}) collective-permute-start(bf16[512,768]{1,0:T(8,128)(2,1)} %pack.1), channel_id=1, source_target_pairs={{4,0},{5,1},{6,2},{7,3},{8,4},{9,5},{10,6},{11,7},{12,8},{13,9},{1... | collective-permute-start | bytes 2359304 | tf_op jit(solution)/shard_map/ppermute | solution.py:361
  38.0 8.4 %collective-permute-start.1 = (s32[1,8]{1,0:T(1,128)S(1)}, s32[1,8]{1,0:T(1,128)S(1)}, u32[]{:S(2)}, u32[]{:S(2)}) collective-permute-start(s32[1,8]{1,0:T(1,128)S(1)} %copy-done.3), channel_id=1, source_target_pairs={{8,0},{9,1},{10,2},{11,3},{0,4},{1,5},{2,6},{3,7},{12,8},{13,9},{1... | collective-permute-start | bytes 104 | tf_op jit(solution)/shard_map/ppermute | solution.py:361
  40.7 24.4 %collective-permute-start.6 = (bf16[256,1536]{1,0:T(8,128)(2,1)S(1)}, bf16[256,1536]{1,0:T(8,128)(2,1)S(1)}, u32[]{:S(2)}, u32[]{:S(2)}) collective-permute-start(bf16[256,1536]{1,0:T(8,128)(2,1)S(1)} %get-tuple-element.28), channel_id=1, source_target_pairs={{0,1},{1,0},{2,3},{3,2},{4,5},{5,4},{6,7},{7,6},{8,9},{9,8},{10,11... | collective-permute-start | bytes 2359304 | tf_op jit(solution)/shard_map/ppermute | solution.py:361
  46.4 35.5 %collective-permute-start.4 = (bf16[512,768]{1,0:T(8,128)(2,1)S(1)}, bf16[512,768]{1,0:T(8,128)(2,1)S(1)}, u32[]{:S(2)}, u32[]{:S(2)}) collective-permute-start(bf16[512,768]{1,0:T(8,128)(2,1)S(1)} %get-tuple-element.27), channel_id=1, source_target_pairs={{0,4},{1,5},{2,6},{3,7},{4,8},{5,9},{6,10},{7,11},{8,12},{9,13},{1... | collective-permute-start | bytes 2359304 | tf_op jit(solution)/shard_map/ppermute | solution.py:361
  59.2 26.9 %collective-permute-start.5 = (bf16[512,768]{1,0:T(8,128)(2,1)S(1)}, bf16[512,768]{1,0:T(8,128)(2,1)S(1)}, u32[]{:S(2)}, u32[]{:S(2)}) collective-permute-start(bf16[512,768]{1,0:T(8,128)(2,1)S(1)} %get-tuple-element.27), channel_id=1, source_target_pairs={{4,0},{5,1},{6,2},{7,3},{8,4},{9,5},{10,6},{11,7},{12,8},{13,9},{1... | collective-permute-start | bytes 2359304 | tf_op jit(solution)/shard_map/ppermute | solution.py:361
  63.5 25.1 %collective-permute-start.12 = (bf16[256,768]{1,0:T(8,128)(2,1)S(1)}, bf16[256,768]{1,0:T(8,128)(2,1)S(1)}, u32[]{:S(2)}, u32[]{:S(2)}) collective-permute-start(bf16[256,768]{1,0:T(8,128)(2,1)S(1)} %get-tuple-element.38), channel_id=1, source_target_pairs={{0,2},{1,3},{2,0},{3,1},{4,6},{5,7},{6,4},{7,5},{8,10},{9,11},{10,... | collective-permute-start | bytes 1179656 | tf_op jit(solution)/shard_map/ppermute | solution.py:361
  65.1 28.5 %collective-permute-start.13 = (bf16[256,768]{1,0:T(8,128)(2,1)S(1)}, bf16[256,768]{1,0:T(8,128)(2,1)S(1)}, u32[]{:S(2)}, u32[]{:S(2)}) collective-permute-start(bf16[256,768]{1,0:T(8,128)(2,1)S(1)} %get-tuple-element.39), channel_id=1, source_target_pairs={{0,3},{1,2},{2,1},{3,0},{4,7},{5,6},{6,5},{7,4},{8,11},{9,10},{10,... | collective-permute-start | bytes 1179656 | tf_op jit(solution)/shard_map/ppermute | solution.py:361
  65.1 28.5 %collective-permute-start.14 = (bf16[256,768]{1,0:T(8,128)(2,1)S(1)}, bf16[256,768]{1,0:T(8,128)(2,1)S(1)}, u32[]{:S(2)}, u32[]{:S(2)}) collective-permute-start(bf16[256,768]{1,0:T(8,128)(2,1)S(1)} %get-tuple-element.40), channel_id=1, source_target_pairs={{0,8},{1,9},{2,10},{3,11},{4,0},{5,1},{6,2},{7,3},{8,12},{9,13},{1... | collective-permute-start | bytes 1179656 | tf_op jit(solution)/shard_map/ppermute | solution.py:361
  88.4 10.8 %collective-permute-start.10 = (bf16[256,768]{1,0:T(8,128)(2,1)S(1)}, bf16[256,768]{1,0:T(8,128)(2,1)S(1)}, u32[]{:S(2)}, u32[]{:S(2)}) collective-permute-start(bf16[256,768]{1,0:T(8,128)(2,1)S(1)} %get-tuple-element.33), channel_id=1, source_target_pairs={{0,3},{1,2},{2,1},{3,0},{4,7},{5,6},{6,5},{7,4},{8,11},{9,10},{10,... | collective-permute-start | bytes 1179656 | tf_op jit(solution)/shard_map/ppermute | solution.py:361
  88.5 11.6 %collective-permute-start.11 = (bf16[256,768]{1,0:T(8,128)(2,1)S(1)}, bf16[256,768]{1,0:T(8,128)(2,1)S(1)}, u32[]{:S(2)}, u32[]{:S(2)}) collective-permute-start(bf16[256,768]{1,0:T(8,128)(2,1)S(1)} %get-tuple-element.34), channel_id=1, source_target_pairs={{0,8},{1,9},{2,10},{3,11},{4,0},{5,1},{6,2},{7,3},{8,12},{9,13},{1... | collective-permute-start | bytes 1179656 | tf_op jit(solution)/shard_map/ppermute | solution.py:361
  88.6 19.8 %collective-permute-start.9 = (bf16[256,768]{1,0:T(8,128)(2,1)S(1)}, bf16[256,768]{1,0:T(8,128)(2,1)S(1)}, u32[]{:S(2)}, u32[]{:S(2)}) collective-permute-start(bf16[256,768]{1,0:T(8,128)(2,1)S(1)} %get-tuple-element.32), channel_id=1, source_target_pairs={{0,2},{1,3},{2,0},{3,1},{4,6},{5,7},{6,4},{7,5},{8,10},{9,11},{10,... | collective-permute-start | bytes 1179656 | tf_op jit(solution)/shard_map/ppermute | solution.py:361

commit v6 on v5

--- a/solution.py
+++ b/solution.py
@@ -251,11 +251,11 @@
     ]
 
 
-def pack(keys, values, width):
+def pack(keys, values, width, after):
     rows = keys.shape[0]
 
-    def build(k_ref, v_ref, packed, sems):
-        copies = pack_copies(k_ref, v_ref, 0, packed, sems)
+    def build(k_ref, v_ref, *refs):
+        copies = pack_copies(k_ref, v_ref, 0, *refs[-2:])
         for copy in copies:
             copy.start()
         for copy in copies:
@@ -264,8 +264,8 @@
     return move(
         "pack",
         build,
-        (in_hbm(keys), in_hbm(values)),
-        [WHOLE] * 2,
+        (in_hbm(keys), in_hbm(values), *after),
+        [WHOLE] * (2 + len(after)),
         jax.ShapeDtypeStruct((2 * rows, width), jnp.bfloat16),
         WHOLE,
         2,
@@ -424,7 +424,7 @@
     far_list = send(tile_lists, [(j, i) for i, j in far])
     beside_list = send(tile_lists, beside)
     across_list = send(tile_lists, across)
-    first = pack(key_heads, value_heads, half)
+    first = pack(key_heads, value_heads, half, [across_list, far_list])
     low = [send(first, up)]
     high = [send(first, down)]
     to_beside, to_across = begin(me, beside_list, across_list, key_heads, value_heads)

time: 112 us -> 104 us (0.929); the launches traced: 111 us -> 102 us
  starting transfers between devices: 30.4 us -> 21 us
    ppermute x15, starting transfers between devices: 30.4 us -> 21 us  [send(): return lax.ppermute(array, 'frame', route)]
  transfers between devices with their start and end apart: 15 -> 15, of which waited for: 7 -> 9; matrix products, arithmetic and copies ran while one was open for 0% -> 0% of each run, Pallas kernels for 18% -> 20%
where the time goes in v6:
time: 104 us; the launch traced here: 102 us
  Pallas kernels  48.2 us (46%)
  waiting for transfers between devices  32.5 us (31%)
  starting transfers between devices  21 us (20%)
    pallas_call x5, Pallas kernels, move(): pl.pallas_call(build, name=name, out_shape=out_shape, in_specs=specs, out...  33.9 us
    ppermute x15, waiting for transfers between devices, send(): return lax.ppermute(array, 'frame', route)  32.5 us
    ppermute x15, starting transfers between devices, send(): return lax.ppermute(array, 'frame', route)  21 us
    pallas_call x5, Pallas kernels, attend(): pl.pallas_call(functools.partial(attend_kernel, plan, heads, carry is not...  14.4 us
  transfers between devices with their start and end apart: 15, of which 9 were waited for; matrix products, arithmetic and copies ran while one was open for 0% of the time, Pallas kernels for 20%

profile of v6, /device:TPU:12, one launch (start us, length us, event | category | flops | bytes accessed | tf_op | source)
XLA Modules:
  0.0 101.9 jit_solution(802802477412724211)
XLA Ops:
  0.0 1.6 %collective-permute-start = (s32[1,8]{1,0:T(1,128)}, s32[1,8]{1,0:T(1,128)S(1)}, u32[]{:S(2)}, u32[]{:S(2)}) collective-permute-start(s32[1,8]{1,0:T(1,128)} %list_ref.1), channel_id=1, source_target_pairs={{0,2},{1,3},{2,0},{3,1},{4,6},{5,7},{6,4},{7,5},{8,10},{9,11},{10,... | collective-permute-start | bytes 104 | tf_op jit(solution)/shard_map/ppermute | solution.py:361
  1.6 2.6 %collective-permute-start.1 = (s32[1,8]{1,0:T(1,128)}, s32[1,8]{1,0:T(1,128)S(1)}, u32[]{:S(2)}, u32[]{:S(2)}) collective-permute-start(s32[1,8]{1,0:T(1,128)} %list_ref.1), channel_id=1, source_target_pairs={{8,0},{9,1},{10,2},{11,3},{0,4},{1,5},{2,6},{3,7},{12,8},{13,9},{1... | collective-permute-start | bytes 104 | tf_op jit(solution)/shard_map/ppermute | solution.py:361
  4.2 1.4 %collective-permute-done.1.refs_1_.far_ref = s32[1,8]{1,0:T(1,128)S(1)} collective-permute-done((s32[1,8]{1,0:T(1,128)}, s32[1,8]{1,0:T(1,128)S(1)}, u32[]{:S(2)}, u32[]{:S(2)}) %collective-permute-start.1) | collective-permute-done | bytes 64 | tf_op jit(solution)/shard_map/ppermute | solution.py:361
  5.6 24.9 %pack.1 = bf16[512,768]{1,0:T(8,128)(2,1)} custom-call(bf16[256,1536]{1,0:T(8,128)(2,1)} %k_ref.9, bf16[256,1536]{1,0:T(8,128)(2,1)} %v_ref.9, s32[1,8]{1,0:T(1,128)S(1)} %collective-permute-done.across_ref.refs_0_, s32[1,8]{1,0:T(1,128)S(1)} %collective-permute-done.1.refs_1_.far_ref), custom_call_target="tpu_custom_call" | custom-call | bytes 1572864 | tf_op jit(solution)/shard_map/pack/pallas_call | solution.py:163
  30.5 3.1 %collective-permute-start.7 = (bf16[512,768]{1,0:T(8,128)(2,1)}, bf16[512,768]{1,0:T(8,128)(2,1)S(1)}, u32[]{:S(2)}, u32[]{:S(2)}) collective-permute-start(bf16[512,768]{1,0:T(8,128)(2,1)} %pack.1), channel_id=1, source_target_pairs={{0,4},{1,5},{2,6},{3,7},{4,8},{5,9},{6,10},{7,11},{8,12},{9,13},{1... | collective-permute-start | bytes 2359304 | tf_op jit(solution)/shard_map/ppermute | solution.py:361
  33.7 0.1 collective-permute-start.2
  33.8 1.1 %collective-permute-done.2.beside_ref = s32[1,8]{1,0:T(1,128)S(1)} collective-permute-done((s32[1,8]{1,0:T(1,128)S(1)}, s32[1,8]{1,0:T(1,128)S(1)}, u32[]{:S(2)}, u32[]{:S(2)}) %collective-permute-start.2) | collective-permute-done | bytes 64 | tf_op jit(solution)/shard_map/ppermute | solution.py:361
  34.9 2.0 %begin.1 = (bf16[256,1536]{1,0:T(8,128)(2,1)S(1)}, bf16[272,1536]{1,0:T(8,128)(2,1)S(1)}) custom-call(s32[1]{0:T(128)} %bitcast.meta.me_ref, s32[1,8]{1,0:T(1,128)S(1)} %collective-permute-done.2.beside_ref, s32[1,8]{1,0:T(1,128)S(1)} %collective-permute-done.across_ref.refs_0_, bf16[256,1536]{1,0:T(8,128)(2,1)} %k_ref.9, bf16[256,1536]{1,0:T(8,128)(2,1)} %v_ref.9), custom_call_target="tpu_custom_call" | custom-call | bytes 3145728 | tf_op jit(solution)/shard_map/begin/pallas_call | solution.py:163
  36.9 0.6 collective-permute-start.3
  37.5 2.7 %collective-permute-start.8 = (bf16[512,768]{1,0:T(8,128)(2,1)}, bf16[512,768]{1,0:T(8,128)(2,1)S(1)}, u32[]{:S(2)}, u32[]{:S(2)}) collective-permute-start(bf16[512,768]{1,0:T(8,128)(2,1)} %pack.1), channel_id=1, source_target_pairs={{4,0},{5,1},{6,2},{7,3},{8,4},{9,5},{10,6},{11,7},{12,8},{13,9},{1... | collective-permute-start | bytes 2359304 | tf_op jit(solution)/shard_map/ppermute | solution.py:361
  40.2 0.1 collective-permute-start.6
  40.3 2.7 %attend_own.1 = (f32[256,1536]{1,0:T(8,128)S(1)}, f32[256,1536]{1,0:T(8,128)S(1)}, f32[256,1536]{1,0:T(8,128)S(1)}) custom-call(s32[1]{0:T(128)} %bitcast.meta.me_ref, bf16[256,1536]{1,0:T(8,128)(2,1)S(1)} %copy-done.2, bf16[256,1536]{1,0:T(8,128)(2,1)S(1)} %copy-done, bf16[256,1536]{1,0:T(8,128)(2,1)S(1)} %copy-done.1), custom_call_target="tpu_custom_call" | custom-call | flops 402653184 | bytes 2359296 | tf_op jit(solution)/shard_map/attend_own/pallas_call | solution.py:141
  43.0 2.3 %pack_rest.1 = (bf16[512,768]{1,0:T(8,128)(2,1)S(1)}, s32[10]{0:T(128)S(1)}) custom-call(s32[1,8]{1,0:T(1,128)S(1)} %copy-done.3, s32[1]{0:T(128)} %bitcast.meta.me_ref, s32[1,8]{1,0:T(1,128)S(1)} %collective-permute-done.across_ref.refs_0_, bf16[256,1536]{1,0:T(8,128)(2,1)} %k_ref.9, bf16[256,1536]{1,0:T(8,128)(2,1)} %v_ref.9, ...), custom_call_target="tpu_custom_call" | custom-call | bytes 1572864 | tf_op jit(solution)/shard_map/pack_rest/pallas_call | solution.py:163
  45.3 3.6 %collective-permute-start.4 = (bf16[512,768]{1,0:T(8,128)(2,1)S(1)}, bf16[512,768]{1,0:T(8,128)(2,1)S(1)}, u32[]{:S(2)}, u32[]{:S(2)}) collective-permute-start(bf16[512,768]{1,0:T(8,128)(2,1)S(1)} %get-tuple-element.27), channel_id=1, source_target_pairs={{0,4},{1,5},{2,6},{3,7},{4,8},{5,9},{6,10},{7,11},{8,12},{9,13},{1... | collective-permute-start | bytes 2359304 | tf_op jit(solution)/shard_map/ppermute | solution.py:361
  48.8 2.5 %collective-permute-done.7.refs_5_.refs_6_.low = bf16[512,768]{1,0:T(8,128)(2,1)S(1)} collective-permute-done((bf16[512,768]{1,0:T(8,128)(2,1)}, bf16[512,768]{1,0:T(8,128)(2,1)S(1)}, u32[]{:S(2)}, u32[]{:S(2)}) %collective-permute-start.7) | collective-permute-done | bytes 786464 | tf_op jit(solution)/shard_map/ppermute | solution.py:361
  51.3 1.9 %collective-permute-start.5 = (bf16[512,768]{1,0:T(8,128)(2,1)S(1)}, bf16[512,768]{1,0:T(8,128)(2,1)S(1)}, u32[]{:S(2)}, u32[]{:S(2)}) collective-permute-start(bf16[512,768]{1,0:T(8,128)(2,1)S(1)} %get-tuple-element.27), channel_id=1, source_target_pairs={{4,0},{5,1},{6,2},{7,3},{8,4},{9,5},{10,6},{11,7},{12,8},{13,9},{1... | collective-permute-start | bytes 2359304 | tf_op jit(solution)/shard_map/ppermute | solution.py:361
  53.2 7.2 %collective-permute-done.8.refs_7_.refs_8_.high = bf16[512,768]{1,0:T(8,128)(2,1)S(1)} collective-permute-done((bf16[512,768]{1,0:T(8,128)(2,1)}, bf16[512,768]{1,0:T(8,128)(2,1)S(1)}, u32[]{:S(2)}, u32[]{:S(2)}) %collective-permute-start.8) | collective-permute-done | bytes 786464 | tf_op jit(solution)/shard_map/ppermute | solution.py:361
  60.4 2.3 %choose.3 = (bf16[256,768]{1,0:T(8,128)(2,1)S(1)}, bf16[256,768]{1,0:T(8,128)(2,1)S(1)}, bf16[256,768]{1,0:T(8,128)(2,1)S(1)}) custom-call(s32[10]{0:T(128)S(1)} %get-tuple-element.25.meta, s32[1,8]{1,0:T(1,128)S(1)} %collective-permute-done.1.refs_1_.far_ref, bf16[272,1536]{1,0:T(8,128)(2,1)S(1)} %collective-permute-done.3.refs_3_.refs_4_.over_ref, ...), custom_call_target="tpu_custom_call" | custom-call | bytes 2359296 | tf_op jit(solution)/shard_map/choose/pallas_call | solution.py:163
  62.7 2.1 %collective-permute-start.12 = (bf16[256,768]{1,0:T(8,128)(2,1)S(1)}, bf16[256,768]{1,0:T(8,128)(2,1)S(1)}, u32[]{:S(2)}, u32[]{:S(2)}) collective-permute-start(bf16[256,768]{1,0:T(8,128)(2,1)S(1)} %get-tuple-element.38), channel_id=1, source_target_pairs={{0,2},{1,3},{2,0},{3,1},{4,6},{5,7},{6,4},{7,5},{8,10},{9,11},{10,... | collective-permute-start | bytes 1179656 | tf_op jit(solution)/shard_map/ppermute | solution.py:361
  64.8 2.8 %attend_more.2 = (f32[256,768]{1,0:T(8,128)S(1)}, f32[256,768]{1,0:T(8,128)S(1)}, f32[256,768]{1,0:T(8,128)S(1)}) custom-call(s32[10]{0:T(128)S(1)} %get-tuple-element.25.meta, bf16[256,1536]{1,0:T(8,128)(2,1)S(1)} %copy-done.2, bf16[256,1536]{1,0:T(8,128)(2,1)S(1)} %collective-permute-done.6.refs_1_.refs_2_, ...), custom_call_target="tpu_custom_call" | custom-call | flops 402653184 | bytes 1966080 | tf_op jit(solution)/shard_map/attend_more/pallas_call | solution.py:141
  67.6 0.1 collective-permute-done.4.low.refs_5_.refs_6_
  67.6 8.9 %collective-permute-done.5.high.refs_7_.refs_8_ = bf16[512,768]{1,0:T(8,128)(2,1)S(1)} collective-permute-done((bf16[512,768]{1,0:T(8,128)(2,1)S(1)}, bf16[512,768]{1,0:T(8,128)(2,1)S(1)}, u32[]{:S(2)}, u32[]{:S(2)}) %collective-permute-start.5) | collective-permute-done | bytes 786464 | tf_op jit(solution)/shard_map/ppermute | solution.py:361
  76.6 2.3 %choose.2 = (bf16[256,768]{1,0:T(8,128)(2,1)S(1)}, bf16[256,768]{1,0:T(8,128)(2,1)S(1)}, bf16[256,768]{1,0:T(8,128)(2,1)S(1)}) custom-call(s32[10]{0:T(128)S(1)} %get-tuple-element.25.meta, s32[1,8]{1,0:T(1,128)S(1)} %collective-permute-done.1.refs_1_.far_ref, bf16[272,1536]{1,0:T(8,128)(2,1)S(1)} %collective-permute-done.3.refs_3_.refs_4_.over_ref, ...), custom_call_target="tpu_custom_call" | custom-call | bytes 2359296 | tf_op jit(solution)/shard_map/choose/pallas_call | solution.py:163
  78.9 0.5 collective-permute-start.10
  79.4 0.2 collective-permute-start.11
  79.6 2.1 %collective-permute-start.9 = (bf16[256,768]{1,0:T(8,128)(2,1)S(1)}, bf16[256,768]{1,0:T(8,128)(2,1)S(1)}, u32[]{:S(2)}, u32[]{:S(2)}) collective-permute-start(bf16[256,768]{1,0:T(8,128)(2,1)S(1)} %get-tuple-element.32), channel_id=1, source_target_pairs={{0,2},{1,3},{2,0},{3,1},{4,6},{5,7},{6,4},{7,5},{8,10},{9,11},{10,... | collective-permute-start | bytes 1179656 | tf_op jit(solution)/shard_map/ppermute | solution.py:361
  81.6 2.8 %attend_more.3 = (f32[256,768]{1,0:T(8,128)S(1)}, f32[256,768]{1,0:T(8,128)S(1)}, f32[256,768]{1,0:T(8,128)S(1)}) custom-call(s32[10]{0:T(128)S(1)} %get-tuple-element.25.meta, bf16[256,1536]{1,0:T(8,128)(2,1)S(1)} %copy-done.2, bf16[256,1536]{1,0:T(8,128)(2,1)S(1)} %collective-permute-done.6.refs_1_.refs_2_, ...), custom_call_target="tpu_custom_call" | custom-call | flops 402653184 | bytes 1966080 | tf_op jit(solution)/shard_map/attend_more/pallas_call | solution.py:141
  84.5 2.7 %collective-permute-done.14.refs_5_.refs_6_ = bf16[256,768]{1,0:T(8,128)(2,1)S(1)} collective-permute-done((bf16[256,768]{1,0:T(8,128)(2,1)S(1)}, bf16[256,768]{1,0:T(8,128)(2,1)S(1)}, u32[]{:S(2)}, u32[]{:S(2)}) %collective-permute-start.14) | collective-permute-done | bytes 393248 | tf_op jit(solution)/shard_map/ppermute | solution.py:361
  87.1 3.1 %attend_last.2.refs_10_ = bf16[256,1536]{1,0:T(8,128)(2,1)} custom-call(s32[10]{0:T(128)S(1)} %get-tuple-element.25.meta, bf16[256,1536]{1,0:T(8,128)(2,1)S(1)} %copy-done.2, bf16[256,768]{1,0:T(8,128)(2,1)S(1)} %collective-permute-done.12.refs_1_.refs_2_, bf16[256,768]{1,0:T(8,128)(2,1)S(1)} %collective-permute-done.12.refs_1_.refs_2_, ...), custom_call_target="tpu_custom_call" | custom-call | flops 301989888 | bytes 1572864 | tf_op jit(solution)/shard_map/attend_last/pallas_call | solution.py:141
  90.2 4.4 %collective-permute-done.11.refs_5_.refs_6_ = bf16[256,768]{1,0:T(8,128)(2,1)S(1)} collective-permute-done((bf16[256,768]{1,0:T(8,128)(2,1)S(1)}, bf16[256,768]{1,0:T(8,128)(2,1)S(1)}, u32[]{:S(2)}, u32[]{:S(2)}) %collective-permute-start.11) | collective-permute-done | bytes 393248 | tf_op jit(solution)/shard_map/ppermute | solution.py:361
  94.6 4.2 %collective-permute-done.9.refs_1_.refs_2_ = bf16[256,768]{1,0:T(8,128)(2,1)S(1)} collective-permute-done((bf16[256,768]{1,0:T(8,128)(2,1)S(1)}, bf16[256,768]{1,0:T(8,128)(2,1)S(1)}, u32[]{:S(2)}, u32[]{:S(2)}) %collective-permute-start.9) | collective-permute-done | bytes 393248 | tf_op jit(solution)/shard_map/ppermute | solution.py:361
  98.8 3.1 %attend_last.3 = bf16[256,1536]{1,0:T(8,128)(2,1)} custom-call(s32[10]{0:T(128)S(1)} %get-tuple-element.25.meta, bf16[256,1536]{1,0:T(8,128)(2,1)S(1)} %copy-done.2, bf16[256,768]{1,0:T(8,128)(2,1)S(1)} %collective-permute-done.9.refs_1_.refs_2_, bf16[256,768]{1,0:T(8,128)(2,1)S(1)} %collective-permute-done.9.refs_1_.refs_2_, ...), custom_call_target="tpu_custom_call", output_to_operand_aliasing={{}: (11, {})} | custom-call | flops 301989888 | bytes 1572864 | tf_op jit(solution)/shard_map/attend_last/pallas_call | solution.py:141
  (16 shorter events, 0.0 us)
Async XLA Ops:
  0.0 33.7 %copy-start.3 = (s32[1,8]{1,0:T(1,128)S(1)}, s32[1,8]{1,0:T(1,128)}, u32[]{:S(2)}) copy-start(s32[1,8]{1,0:T(1,128)} %list_ref.1) | copy-start | bytes 100
  0.0 40.3 %copy-start = (bf16[256,1536]{1,0:T(8,128)(2,1)S(1)}, bf16[256,1536]{1,0:T(8,128)(2,1)}, u32[]{:S(2)}) copy-start(bf16[256,1536]{1,0:T(8,128)(2,1)} %k_ref.9) | copy-start | bytes 2359300
  0.0 40.3 %copy-start.1 = (bf16[256,1536]{1,0:T(8,128)(2,1)S(1)}, bf16[256,1536]{1,0:T(8,128)(2,1)}, u32[]{:S(2)}) copy-start(bf16[256,1536]{1,0:T(8,128)(2,1)} %v_ref.9) | copy-start | bytes 2359300
  0.0 40.3 %copy-start.2 = (bf16[256,1536]{1,0:T(8,128)(2,1)S(1)}, bf16[256,1536]{1,0:T(8,128)(2,1)}, u32[]{:S(2)}) copy-start(bf16[256,1536]{1,0:T(8,128)(2,1)} %refs_0_.9) | copy-start | bytes 2359300
  0.0 4.1 %collective-permute-start = (s32[1,8]{1,0:T(1,128)}, s32[1,8]{1,0:T(1,128)S(1)}, u32[]{:S(2)}, u32[]{:S(2)}) collective-permute-start(s32[1,8]{1,0:T(1,128)} %list_ref.1), channel_id=1, source_target_pairs={{0,2},{1,3},{2,0},{3,1},{4,6},{5,7},{6,4},{7,5},{8,10},{9,11},{10,... | collective-permute-start | bytes 104 | tf_op jit(solution)/shard_map/ppermute | solution.py:361
  1.6 4.0 %collective-permute-start.1 = (s32[1,8]{1,0:T(1,128)}, s32[1,8]{1,0:T(1,128)S(1)}, u32[]{:S(2)}, u32[]{:S(2)}) collective-permute-start(s32[1,8]{1,0:T(1,128)} %list_ref.1), channel_id=1, source_target_pairs={{8,0},{9,1},{10,2},{11,3},{0,4},{1,5},{2,6},{3,7},{12,8},{13,9},{1... | collective-permute-start | bytes 104 | tf_op jit(solution)/shard_map/ppermute | solution.py:361
  30.5 20.8 %collective-permute-start.7 = (bf16[512,768]{1,0:T(8,128)(2,1)}, bf16[512,768]{1,0:T(8,128)(2,1)S(1)}, u32[]{:S(2)}, u32[]{:S(2)}) collective-permute-start(bf16[512,768]{1,0:T(8,128)(2,1)} %pack.1), channel_id=1, source_target_pairs={{0,4},{1,5},{2,6},{3,7},{4,8},{5,9},{6,10},{7,11},{8,12},{9,13},{1... | collective-permute-start | bytes 2359304 | tf_op jit(solution)/shard_map/ppermute | solution.py:361
  33.7 1.2 %collective-permute-start.2 = (s32[1,8]{1,0:T(1,128)S(1)}, s32[1,8]{1,0:T(1,128)S(1)}, u32[]{:S(2)}, u32[]{:S(2)}) collective-permute-start(s32[1,8]{1,0:T(1,128)S(1)} %copy-done.3), channel_id=1, source_target_pairs={{0,1},{1,0},{2,3},{3,2},{4,5},{5,4},{6,7},{7,6},{8,9},{9,8},{10,11... | collective-permute-start | bytes 104 | tf_op jit(solution)/shard_map/ppermute | solution.py:361
  36.9 23.5 %collective-permute-start.3 = (bf16[272,1536]{1,0:T(8,128)(2,1)S(1)}, bf16[272,1536]{1,0:T(8,128)(2,1)S(1)}, u32[]{:S(2)}, u32[]{:S(2)}) collective-permute-start(bf16[272,1536]{1,0:T(8,128)(2,1)S(1)} %get-tuple-element.26), channel_id=1, source_target_pairs={{0,2},{1,3},{2,0},{3,1},{4,6},{5,7},{6,4},{7,5},{8,10},{9,11},{10,... | collective-permute-start | bytes 2506760 | tf_op jit(solution)/shard_map/ppermute | solution.py:361
  37.5 22.9 %collective-permute-start.8 = (bf16[512,768]{1,0:T(8,128)(2,1)}, bf16[512,768]{1,0:T(8,128)(2,1)S(1)}, u32[]{:S(2)}, u32[]{:S(2)}) collective-permute-start(bf16[512,768]{1,0:T(8,128)(2,1)} %pack.1), channel_id=1, source_target_pairs={{4,0},{5,1},{6,2},{7,3},{8,4},{9,5},{10,6},{11,7},{12,8},{13,9},{1... | collective-permute-start | bytes 2359304 | tf_op jit(solution)/shard_map/ppermute | solution.py:361
  40.2 24.6 %collective-permute-start.6 = (bf16[256,1536]{1,0:T(8,128)(2,1)S(1)}, bf16[256,1536]{1,0:T(8,128)(2,1)S(1)}, u32[]{:S(2)}, u32[]{:S(2)}) collective-permute-start(bf16[256,1536]{1,0:T(8,128)(2,1)S(1)} %get-tuple-element.28), channel_id=1, source_target_pairs={{0,1},{1,0},{2,3},{3,2},{4,5},{5,4},{6,7},{7,6},{8,9},{9,8},{10,11... | collective-permute-start | bytes 2359304 | tf_op jit(solution)/shard_map/ppermute | solution.py:361
  45.3 22.4 %collective-permute-start.4 = (bf16[512,768]{1,0:T(8,128)(2,1)S(1)}, bf16[512,768]{1,0:T(8,128)(2,1)S(1)}, u32[]{:S(2)}, u32[]{:S(2)}) collective-permute-start(bf16[512,768]{1,0:T(8,128)(2,1)S(1)} %get-tuple-element.27), channel_id=1, source_target_pairs={{0,4},{1,5},{2,6},{3,7},{4,8},{5,9},{6,10},{7,11},{8,12},{9,13},{1... | collective-permute-start | bytes 2359304 | tf_op jit(solution)/shard_map/ppermute | solution.py:361
  51.3 25.3 %collective-permute-start.5 = (bf16[512,768]{1,0:T(8,128)(2,1)S(1)}, bf16[512,768]{1,0:T(8,128)(2,1)S(1)}, u32[]{:S(2)}, u32[]{:S(2)}) collective-permute-start(bf16[512,768]{1,0:T(8,128)(2,1)S(1)} %get-tuple-element.27), channel_id=1, source_target_pairs={{4,0},{5,1},{6,2},{7,3},{8,4},{9,5},{10,6},{11,7},{12,8},{13,9},{1... | collective-permute-start | bytes 2359304 | tf_op jit(solution)/shard_map/ppermute | solution.py:361
  62.7 16.9 %collective-permute-start.12 = (bf16[256,768]{1,0:T(8,128)(2,1)S(1)}, bf16[256,768]{1,0:T(8,128)(2,1)S(1)}, u32[]{:S(2)}, u32[]{:S(2)}) collective-permute-start(bf16[256,768]{1,0:T(8,128)(2,1)S(1)} %get-tuple-element.38), channel_id=1, source_target_pairs={{0,2},{1,3},{2,0},{3,1},{4,6},{5,7},{6,4},{7,5},{8,10},{9,11},{10,... | collective-permute-start | bytes 1179656 | tf_op jit(solution)/shard_map/ppermute | solution.py:361
  64.8 19.7 %collective-permute-start.13 = (bf16[256,768]{1,0:T(8,128)(2,1)S(1)}, bf16[256,768]{1,0:T(8,128)(2,1)S(1)}, u32[]{:S(2)}, u32[]{:S(2)}) collective-permute-start(bf16[256,768]{1,0:T(8,128)(2,1)S(1)} %get-tuple-element.39), channel_id=1, source_target_pairs={{0,3},{1,2},{2,1},{3,0},{4,7},{5,6},{6,5},{7,4},{8,11},{9,10},{10,... | collective-permute-start | bytes 1179656 | tf_op jit(solution)/shard_map/ppermute | solution.py:361
  64.8 22.4 %collective-permute-start.14 = (bf16[256,768]{1,0:T(8,128)(2,1)S(1)}, bf16[256,768]{1,0:T(8,128)(2,1)S(1)}, u32[]{:S(2)}, u32[]{:S(2)}) collective-permute-start(bf16[256,768]{1,0:T(8,128)(2,1)S(1)} %get-tuple-element.40), channel_id=1, source_target_pairs={{0,8},{1,9},{2,10},{3,11},{4,0},{5,1},{6,2},{7,3},{8,12},{9,13},{1... | collective-permute-start | bytes 1179656 | tf_op jit(solution)/shard_map/ppermute | solution.py:361
  78.9 11.3 %collective-permute-start.10 = (bf16[256,768]{1,0:T(8,128)(2,1)S(1)}, bf16[256,768]{1,0:T(8,128)(2,1)S(1)}, u32[]{:S(2)}, u32[]{:S(2)}) collective-permute-start(bf16[256,768]{1,0:T(8,128)(2,1)S(1)} %get-tuple-element.33), channel_id=1, source_target_pairs={{0,3},{1,2},{2,1},{3,0},{4,7},{5,6},{6,5},{7,4},{8,11},{9,10},{10,... | collective-permute-start | bytes 1179656 | tf_op jit(solution)/shard_map/ppermute | solution.py:361
  79.4 15.2 %collective-permute-start.11 = (bf16[256,768]{1,0:T(8,128)(2,1)S(1)}, bf16[256,768]{1,0:T(8,128)(2,1)S(1)}, u32[]{:S(2)}, u32[]{:S(2)}) collective-permute-start(bf16[256,768]{1,0:T(8,128)(2,1)S(1)} %get-tuple-element.34), channel_id=1, source_target_pairs={{0,8},{1,9},{2,10},{3,11},{4,0},{5,1},{6,2},{7,3},{8,12},{9,13},{1... | collective-permute-start | bytes 1179656 | tf_op jit(solution)/shard_map/ppermute | solution.py:361
  79.6 19.2 %collective-permute-start.9 = (bf16[256,768]{1,0:T(8,128)(2,1)S(1)}, bf16[256,768]{1,0:T(8,128)(2,1)S(1)}, u32[]{:S(2)}, u32[]{:S(2)}) collective-permute-start(bf16[256,768]{1,0:T(8,128)(2,1)S(1)} %get-tuple-element.32), channel_id=1, source_target_pairs={{0,2},{1,3},{2,0},{3,1},{4,6},{5,7},{6,4},{7,5},{8,10},{9,11},{10,... | collective-permute-start | bytes 1179656 | tf_op jit(solution)/shard_map/ppermute | solution.py:361

commit v7 on v6

--- a/solution.py
+++ b/solution.py
@@ -231,8 +231,8 @@
         (me, beside_list, across_list, in_hbm(keys), in_hbm(values)),
         [SCALAR] * 3 + [WHOLE] * 2,
         [
-            jax.ShapeDtypeStruct((2 * TILE, width), jnp.bfloat16),
-            jax.ShapeDtypeStruct((2 * TILE + NOTE_ROWS, width), jnp.bfloat16),
+            pltpu.VMEM((2 * TILE, width), jnp.bfloat16),
+            pltpu.VMEM((2 * TILE + NOTE_ROWS, width), jnp.bfloat16),
         ],
         [WHOLE, WHOLE],
         5,
@@ -266,7 +266,7 @@
         build,
         (in_hbm(keys), in_hbm(values), *after),
         [WHOLE] * (2 + len(after)),
-        jax.ShapeDtypeStruct((2 * rows, width), jnp.bfloat16),
+        pltpu.VMEM((2 * rows, width), jnp.bfloat16),
         WHOLE,
         2,
         8 * rows * width,
@@ -297,7 +297,7 @@
         (tile_lists, me, across_list, in_hbm(keys), in_hbm(values), *after),
         [SCALAR] * 3 + [WHOLE] * (2 + len(after)),
         [
-            jax.ShapeDtypeStruct((2 * rows, width), jnp.bfloat16),
+            pltpu.VMEM((2 * rows, width), jnp.bfloat16),
             jax.ShapeDtypeStruct((10,), jnp.int32),
         ],
         [WHOLE, SCALAR],
@@ -349,7 +349,7 @@
         build,
         (meta, far_list, over, in_hbm(keys), in_hbm(values), low, high, *after),
         [SCALAR] * 2 + [WHOLE] * (5 + len(after)),
-        [jax.ShapeDtypeStruct((2 * TILE, width), jnp.bfloat16)] * 3,
+        [pltpu.VMEM((2 * TILE, width), jnp.bfloat16)] * 3,
         [WHOLE] * 3,
         7,
         24 * TILE * width,

time: 104 us -> 104 us (level)
  transfers between devices with their start and end apart: 15 -> 15, of which waited for: 9 -> 8; matrix products, arithmetic and copies ran while one was open for 0% -> 0% of each run, Pallas kernels for 20% -> 20%
where the time goes in v7:
time: 104 us; the launch traced here: 102 us
  Pallas kernels  48.2 us (46%)
  waiting for transfers between devices  32.2 us (31%)
  starting transfers between devices  21.2 us (20%)
    pallas_call x5, Pallas kernels, move(): pl.pallas_call(build, name=name, out_shape=out_shape, in_specs=specs, out...  33.8 us
    ppermute x15, waiting for transfers between devices, send(): return lax.ppermute(array, 'frame', route)  32.2 us
    ppermute x15, starting transfers between devices, send(): return lax.ppermute(array, 'frame', route)  21.2 us
    pallas_call x5, Pallas kernels, attend(): pl.pallas_call(functools.partial(attend_kernel, plan, heads, carry is not...  14.4 us
  transfers between devices with their start and end apart: 15, of which 8 were waited for; matrix products, arithmetic and copies ran while one was open for 0% of the time, Pallas kernels for 20%

profile of v7, /device:TPU:12, one launch (start us, length us, event | category | flops | bytes accessed | tf_op | source)
XLA Modules:
  0.0 101.8 jit_solution(802802477412724211)
XLA Ops:
  0.0 1.6 %collective-permute-start = (s32[1,8]{1,0:T(1,128)}, s32[1,8]{1,0:T(1,128)S(1)}, u32[]{:S(2)}, u32[]{:S(2)}) collective-permute-start(s32[1,8]{1,0:T(1,128)} %list_ref.1), channel_id=1, source_target_pairs={{0,2},{1,3},{2,0},{3,1},{4,6},{5,7},{6,4},{7,5},{8,10},{9,11},{10,... | collective-permute-start | bytes 104 | tf_op jit(solution)/shard_map/ppermute | solution.py:361
  1.6 2.6 %collective-permute-start.1 = (s32[1,8]{1,0:T(1,128)}, s32[1,8]{1,0:T(1,128)S(1)}, u32[]{:S(2)}, u32[]{:S(2)}) collective-permute-start(s32[1,8]{1,0:T(1,128)} %list_ref.1), channel_id=1, source_target_pairs={{8,0},{9,1},{10,2},{11,3},{0,4},{1,5},{2,6},{3,7},{12,8},{13,9},{1... | collective-permute-start | bytes 104 | tf_op jit(solution)/shard_map/ppermute | solution.py:361
  4.2 0.0 collective-permute-done.across_ref.refs_0_
  4.2 1.4 %collective-permute-done.1.refs_1_.far_ref = s32[1,8]{1,0:T(1,128)S(1)} collective-permute-done((s32[1,8]{1,0:T(1,128)}, s32[1,8]{1,0:T(1,128)S(1)}, u32[]{:S(2)}, u32[]{:S(2)}) %collective-permute-start.1) | collective-permute-done | bytes 64 | tf_op jit(solution)/shard_map/ppermute | solution.py:361
  5.6 24.9 %pack.1 = bf16[512,768]{1,0:T(8,128)(2,1)} custom-call(bf16[256,1536]{1,0:T(8,128)(2,1)} %k_ref.9, bf16[256,1536]{1,0:T(8,128)(2,1)} %v_ref.9, s32[1,8]{1,0:T(1,128)S(1)} %collective-permute-done.across_ref.refs_0_, s32[1,8]{1,0:T(1,128)S(1)} %collective-permute-done.1.refs_1_.far_ref), custom_call_target="tpu_custom_call" | custom-call | bytes 1572864 | tf_op jit(solution)/shard_map/pack/pallas_call | solution.py:163
  30.5 3.1 %collective-permute-start.7 = (bf16[512,768]{1,0:T(8,128)(2,1)}, bf16[512,768]{1,0:T(8,128)(2,1)S(1)}, u32[]{:S(2)}, u32[]{:S(2)}) collective-permute-start(bf16[512,768]{1,0:T(8,128)(2,1)} %pack.1), channel_id=1, source_target_pairs={{0,4},{1,5},{2,6},{3,7},{4,8},{5,9},{6,10},{7,11},{8,12},{9,13},{1... | collective-permute-start | bytes 2359304 | tf_op jit(solution)/shard_map/ppermute | solution.py:361
  33.7 0.1 collective-permute-start.2
  33.8 1.1 %collective-permute-done.2.beside_ref = s32[1,8]{1,0:T(1,128)S(1)} collective-permute-done((s32[1,8]{1,0:T(1,128)S(1)}, s32[1,8]{1,0:T(1,128)S(1)}, u32[]{:S(2)}, u32[]{:S(2)}) %collective-permute-start.2) | collective-permute-done | bytes 64 | tf_op jit(solution)/shard_map/ppermute | solution.py:361
  34.9 2.0 %begin.1 = (bf16[256,1536]{1,0:T(8,128)(2,1)S(1)}, bf16[272,1536]{1,0:T(8,128)(2,1)S(1)}) custom-call(s32[1]{0:T(128)} %bitcast.meta.me_ref, s32[1,8]{1,0:T(1,128)S(1)} %collective-permute-done.2.beside_ref, s32[1,8]{1,0:T(1,128)S(1)} %collective-permute-done.across_ref.refs_0_, bf16[256,1536]{1,0:T(8,128)(2,1)} %k_ref.9, bf16[256,1536]{1,0:T(8,128)(2,1)} %v_ref.9), custom_call_target="tpu_custom_call" | custom-call | bytes 3145728 | tf_op jit(solution)/shard_map/begin/pallas_call | solution.py:163
  36.8 0.7 collective-permute-start.3
  37.5 2.7 %collective-permute-start.8 = (bf16[512,768]{1,0:T(8,128)(2,1)}, bf16[512,768]{1,0:T(8,128)(2,1)S(1)}, u32[]{:S(2)}, u32[]{:S(2)}) collective-permute-start(bf16[512,768]{1,0:T(8,128)(2,1)} %pack.1), channel_id=1, source_target_pairs={{4,0},{5,1},{6,2},{7,3},{8,4},{9,5},{10,6},{11,7},{12,8},{13,9},{1... | collective-permute-start | bytes 2359304 | tf_op jit(solution)/shard_map/ppermute | solution.py:361
  40.3 0.1 collective-permute-start.6
  40.4 2.7 %attend_own.1 = (f32[256,1536]{1,0:T(8,128)S(1)}, f32[256,1536]{1,0:T(8,128)S(1)}, f32[256,1536]{1,0:T(8,128)S(1)}) custom-call(s32[1]{0:T(128)} %bitcast.meta.me_ref, bf16[256,1536]{1,0:T(8,128)(2,1)S(1)} %copy-done.2, bf16[256,1536]{1,0:T(8,128)(2,1)S(1)} %copy-done, bf16[256,1536]{1,0:T(8,128)(2,1)S(1)} %copy-done.1), custom_call_target="tpu_custom_call" | custom-call | flops 402653184 | bytes 2359296 | tf_op jit(solution)/shard_map/attend_own/pallas_call | solution.py:141
  43.1 2.3 %pack_rest.1 = (bf16[512,768]{1,0:T(8,128)(2,1)S(1)}, s32[10]{0:T(128)S(1)}) custom-call(s32[1,8]{1,0:T(1,128)S(1)} %copy-done.3, s32[1]{0:T(128)} %bitcast.meta.me_ref, s32[1,8]{1,0:T(1,128)S(1)} %collective-permute-done.across_ref.refs_0_, bf16[256,1536]{1,0:T(8,128)(2,1)} %k_ref.9, bf16[256,1536]{1,0:T(8,128)(2,1)} %v_ref.9, ...), custom_call_target="tpu_custom_call" | custom-call | bytes 1572864 | tf_op jit(solution)/shard_map/pack_rest/pallas_call | solution.py:163
  45.3 3.6 %collective-permute-start.4 = (bf16[512,768]{1,0:T(8,128)(2,1)S(1)}, bf16[512,768]{1,0:T(8,128)(2,1)S(1)}, u32[]{:S(2)}, u32[]{:S(2)}) collective-permute-start(bf16[512,768]{1,0:T(8,128)(2,1)S(1)} %get-tuple-element.27), channel_id=1, source_target_pairs={{0,4},{1,5},{2,6},{3,7},{4,8},{5,9},{6,10},{7,11},{8,12},{9,13},{1... | collective-permute-start | bytes 2359304 | tf_op jit(solution)/shard_map/ppermute | solution.py:361
  48.9 2.3 %collective-permute-done.7.refs_5_.refs_6_.low = bf16[512,768]{1,0:T(8,128)(2,1)S(1)} collective-permute-done((bf16[512,768]{1,0:T(8,128)(2,1)}, bf16[512,768]{1,0:T(8,128)(2,1)S(1)}, u32[]{:S(2)}, u32[]{:S(2)}) %collective-permute-start.7) | collective-permute-done | bytes 786464 | tf_op jit(solution)/shard_map/ppermute | solution.py:361
  51.2 1.9 %collective-permute-start.5 = (bf16[512,768]{1,0:T(8,128)(2,1)S(1)}, bf16[512,768]{1,0:T(8,128)(2,1)S(1)}, u32[]{:S(2)}, u32[]{:S(2)}) collective-permute-start(bf16[512,768]{1,0:T(8,128)(2,1)S(1)} %get-tuple-element.27), channel_id=1, source_target_pairs={{4,0},{5,1},{6,2},{7,3},{8,4},{9,5},{10,6},{11,7},{12,8},{13,9},{1... | collective-permute-start | bytes 2359304 | tf_op jit(solution)/shard_map/ppermute | solution.py:361
  53.1 7.3 %collective-permute-done.8.refs_7_.refs_8_.high = bf16[512,768]{1,0:T(8,128)(2,1)S(1)} collective-permute-done((bf16[512,768]{1,0:T(8,128)(2,1)}, bf16[512,768]{1,0:T(8,128)(2,1)S(1)}, u32[]{:S(2)}, u32[]{:S(2)}) %collective-permute-start.8) | collective-permute-done | bytes 786464 | tf_op jit(solution)/shard_map/ppermute | solution.py:361
  60.5 2.3 %choose.3 = (bf16[256,768]{1,0:T(8,128)(2,1)S(1)}, bf16[256,768]{1,0:T(8,128)(2,1)S(1)}, bf16[256,768]{1,0:T(8,128)(2,1)S(1)}) custom-call(s32[10]{0:T(128)S(1)} %get-tuple-element.25.meta, s32[1,8]{1,0:T(1,128)S(1)} %collective-permute-done.1.refs_1_.far_ref, bf16[272,1536]{1,0:T(8,128)(2,1)S(1)} %collective-permute-done.3.refs_3_.refs_4_.over_ref, ...), custom_call_target="tpu_custom_call" | custom-call | bytes 2359296 | tf_op jit(solution)/shard_map/choose/pallas_call | solution.py:163
  62.8 2.0 %collective-permute-start.12 = (bf16[256,768]{1,0:T(8,128)(2,1)S(1)}, bf16[256,768]{1,0:T(8,128)(2,1)S(1)}, u32[]{:S(2)}, u32[]{:S(2)}) collective-permute-start(bf16[256,768]{1,0:T(8,128)(2,1)S(1)} %get-tuple-element.38), channel_id=1, source_target_pairs={{0,2},{1,3},{2,0},{3,1},{4,6},{5,7},{6,4},{7,5},{8,10},{9,11},{10,... | collective-permute-start | bytes 1179656 | tf_op jit(solution)/shard_map/ppermute | solution.py:361
  64.8 2.8 %attend_more.2 = (f32[256,768]{1,0:T(8,128)S(1)}, f32[256,768]{1,0:T(8,128)S(1)}, f32[256,768]{1,0:T(8,128)S(1)}) custom-call(s32[10]{0:T(128)S(1)} %get-tuple-element.25.meta, bf16[256,1536]{1,0:T(8,128)(2,1)S(1)} %copy-done.2, bf16[256,1536]{1,0:T(8,128)(2,1)S(1)} %collective-permute-done.6.refs_1_.refs_2_, ...), custom_call_target="tpu_custom_call" | custom-call | flops 402653184 | bytes 1966080 | tf_op jit(solution)/shard_map/attend_more/pallas_call | solution.py:141
  67.7 8.9 %collective-permute-done.5.high.refs_7_.refs_8_ = bf16[512,768]{1,0:T(8,128)(2,1)S(1)} collective-permute-done((bf16[512,768]{1,0:T(8,128)(2,1)S(1)}, bf16[512,768]{1,0:T(8,128)(2,1)S(1)}, u32[]{:S(2)}, u32[]{:S(2)}) %collective-permute-start.5) | collective-permute-done | bytes 786464 | tf_op jit(solution)/shard_map/ppermute | solution.py:361
  76.5 2.3 %choose.2 = (bf16[256,768]{1,0:T(8,128)(2,1)S(1)}, bf16[256,768]{1,0:T(8,128)(2,1)S(1)}, bf16[256,768]{1,0:T(8,128)(2,1)S(1)}) custom-call(s32[10]{0:T(128)S(1)} %get-tuple-element.25.meta, s32[1,8]{1,0:T(1,128)S(1)} %collective-permute-done.1.refs_1_.far_ref, bf16[272,1536]{1,0:T(8,128)(2,1)S(1)} %collective-permute-done.3.refs_3_.refs_4_.over_ref, ...), custom_call_target="tpu_custom_call" | custom-call | bytes 2359296 | tf_op jit(solution)/shard_map/choose/pallas_call | solution.py:163
  78.8 0.6 collective-permute-start.10
  79.5 0.2 collective-permute-start.11
  79.7 2.0 %collective-permute-start.9 = (bf16[256,768]{1,0:T(8,128)(2,1)S(1)}, bf16[256,768]{1,0:T(8,128)(2,1)S(1)}, u32[]{:S(2)}, u32[]{:S(2)}) collective-permute-start(bf16[256,768]{1,0:T(8,128)(2,1)S(1)} %get-tuple-element.32), channel_id=1, source_target_pairs={{0,2},{1,3},{2,0},{3,1},{4,6},{5,7},{6,4},{7,5},{8,10},{9,11},{10,... | collective-permute-start | bytes 1179656 | tf_op jit(solution)/shard_map/ppermute | solution.py:361
  81.7 2.8 %attend_more.3 = (f32[256,768]{1,0:T(8,128)S(1)}, f32[256,768]{1,0:T(8,128)S(1)}, f32[256,768]{1,0:T(8,128)S(1)}) custom-call(s32[10]{0:T(128)S(1)} %get-tuple-element.25.meta, bf16[256,1536]{1,0:T(8,128)(2,1)S(1)} %copy-done.2, bf16[256,1536]{1,0:T(8,128)(2,1)S(1)} %collective-permute-done.6.refs_1_.refs_2_, ...), custom_call_target="tpu_custom_call" | custom-call | flops 402653184 | bytes 1966080 | tf_op jit(solution)/shard_map/attend_more/pallas_call | solution.py:141
  84.5 2.7 %collective-permute-done.14.refs_5_.refs_6_ = bf16[256,768]{1,0:T(8,128)(2,1)S(1)} collective-permute-done((bf16[256,768]{1,0:T(8,128)(2,1)S(1)}, bf16[256,768]{1,0:T(8,128)(2,1)S(1)}, u32[]{:S(2)}, u32[]{:S(2)}) %collective-permute-start.14) | collective-permute-done | bytes 393248 | tf_op jit(solution)/shard_map/ppermute | solution.py:361
  87.2 3.1 %attend_last.2.refs_10_ = bf16[256,1536]{1,0:T(8,128)(2,1)} custom-call(s32[10]{0:T(128)S(1)} %get-tuple-element.25.meta, bf16[256,1536]{1,0:T(8,128)(2,1)S(1)} %copy-done.2, bf16[256,768]{1,0:T(8,128)(2,1)S(1)} %collective-permute-done.12.refs_1_.refs_2_, bf16[256,768]{1,0:T(8,128)(2,1)S(1)} %collective-permute-done.12.refs_1_.refs_2_, ...), custom_call_target="tpu_custom_call" | custom-call | flops 301989888 | bytes 1572864 | tf_op jit(solution)/shard_map/attend_last/pallas_call | solution.py:141
  90.3 4.3 %collective-permute-done.11.refs_5_.refs_6_ = bf16[256,768]{1,0:T(8,128)(2,1)S(1)} collective-permute-done((bf16[256,768]{1,0:T(8,128)(2,1)S(1)}, bf16[256,768]{1,0:T(8,128)(2,1)S(1)}, u32[]{:S(2)}, u32[]{:S(2)}) %collective-permute-start.11) | collective-permute-done | bytes 393248 | tf_op jit(solution)/shard_map/ppermute | solution.py:361
  94.5 4.2 %collective-permute-done.9.refs_1_.refs_2_ = bf16[256,768]{1,0:T(8,128)(2,1)S(1)} collective-permute-done((bf16[256,768]{1,0:T(8,128)(2,1)S(1)}, bf16[256,768]{1,0:T(8,128)(2,1)S(1)}, u32[]{:S(2)}, u32[]{:S(2)}) %collective-permute-start.9) | collective-permute-done | bytes 393248 | tf_op jit(solution)/shard_map/ppermute | solution.py:361
  98.7 3.1 %attend_last.3 = bf16[256,1536]{1,0:T(8,128)(2,1)} custom-call(s32[10]{0:T(128)S(1)} %get-tuple-element.25.meta, bf16[256,1536]{1,0:T(8,128)(2,1)S(1)} %copy-done.2, bf16[256,768]{1,0:T(8,128)(2,1)S(1)} %collective-permute-done.9.refs_1_.refs_2_, bf16[256,768]{1,0:T(8,128)(2,1)S(1)} %collective-permute-done.9.refs_1_.refs_2_, ...), custom_call_target="tpu_custom_call", output_to_operand_aliasing={{}: (11, {})} | custom-call | flops 301989888 | bytes 1572864 | tf_op jit(solution)/shard_map/attend_last/pallas_call | solution.py:141
  (16 shorter events, 0.0 us)
Async XLA Ops:
  0.0 33.7 %copy-start.3 = (s32[1,8]{1,0:T(1,128)S(1)}, s32[1,8]{1,0:T(1,128)}, u32[]{:S(2)}) copy-start(s32[1,8]{1,0:T(1,128)} %list_ref.1) | copy-start | bytes 100
  0.0 40.3 %copy-start = (bf16[256,1536]{1,0:T(8,128)(2,1)S(1)}, bf16[256,1536]{1,0:T(8,128)(2,1)}, u32[]{:S(2)}) copy-start(bf16[256,1536]{1,0:T(8,128)(2,1)} %k_ref.9) | copy-start | bytes 2359300
  0.0 40.3 %copy-start.1 = (bf16[256,1536]{1,0:T(8,128)(2,1)S(1)}, bf16[256,1536]{1,0:T(8,128)(2,1)}, u32[]{:S(2)}) copy-start(bf16[256,1536]{1,0:T(8,128)(2,1)} %v_ref.9) | copy-start | bytes 2359300
  0.0 40.4 %copy-start.2 = (bf16[256,1536]{1,0:T(8,128)(2,1)S(1)}, bf16[256,1536]{1,0:T(8,128)(2,1)}, u32[]{:S(2)}) copy-start(bf16[256,1536]{1,0:T(8,128)(2,1)} %refs_0_.9) | copy-start | bytes 2359300
  0.0 4.1 %collective-permute-start = (s32[1,8]{1,0:T(1,128)}, s32[1,8]{1,0:T(1,128)S(1)}, u32[]{:S(2)}, u32[]{:S(2)}) collective-permute-start(s32[1,8]{1,0:T(1,128)} %list_ref.1), channel_id=1, source_target_pairs={{0,2},{1,3},{2,0},{3,1},{4,6},{5,7},{6,4},{7,5},{8,10},{9,11},{10,... | collective-permute-start | bytes 104 | tf_op jit(solution)/shard_map/ppermute | solution.py:361
  1.6 4.0 %collective-permute-start.1 = (s32[1,8]{1,0:T(1,128)}, s32[1,8]{1,0:T(1,128)S(1)}, u32[]{:S(2)}, u32[]{:S(2)}) collective-permute-start(s32[1,8]{1,0:T(1,128)} %list_ref.1), channel_id=1, source_target_pairs={{8,0},{9,1},{10,2},{11,3},{0,4},{1,5},{2,6},{3,7},{12,8},{13,9},{1... | collective-permute-start | bytes 104 | tf_op jit(solution)/shard_map/ppermute | solution.py:361
  30.5 20.7 %collective-permute-start.7 = (bf16[512,768]{1,0:T(8,128)(2,1)}, bf16[512,768]{1,0:T(8,128)(2,1)S(1)}, u32[]{:S(2)}, u32[]{:S(2)}) collective-permute-start(bf16[512,768]{1,0:T(8,128)(2,1)} %pack.1), channel_id=1, source_target_pairs={{0,4},{1,5},{2,6},{3,7},{4,8},{5,9},{6,10},{7,11},{8,12},{9,13},{1... | collective-permute-start | bytes 2359304 | tf_op jit(solution)/shard_map/ppermute | solution.py:361
  33.7 1.2 %collective-permute-start.2 = (s32[1,8]{1,0:T(1,128)S(1)}, s32[1,8]{1,0:T(1,128)S(1)}, u32[]{:S(2)}, u32[]{:S(2)}) collective-permute-start(s32[1,8]{1,0:T(1,128)S(1)} %copy-done.3), channel_id=1, source_target_pairs={{0,1},{1,0},{2,3},{3,2},{4,5},{5,4},{6,7},{7,6},{8,9},{9,8},{10,11... | collective-permute-start | bytes 104 | tf_op jit(solution)/shard_map/ppermute | solution.py:361
  36.8 23.6 %collective-permute-start.3 = (bf16[272,1536]{1,0:T(8,128)(2,1)S(1)}, bf16[272,1536]{1,0:T(8,128)(2,1)S(1)}, u32[]{:S(2)}, u32[]{:S(2)}) collective-permute-start(bf16[272,1536]{1,0:T(8,128)(2,1)S(1)} %get-tuple-element.26), channel_id=1, source_target_pairs={{0,2},{1,3},{2,0},{3,1},{4,6},{5,7},{6,4},{7,5},{8,10},{9,11},{10,... | collective-permute-start | bytes 2506760 | tf_op jit(solution)/shard_map/ppermute | solution.py:361
  37.5 22.9 %collective-permute-start.8 = (bf16[512,768]{1,0:T(8,128)(2,1)}, bf16[512,768]{1,0:T(8,128)(2,1)S(1)}, u32[]{:S(2)}, u32[]{:S(2)}) collective-permute-start(bf16[512,768]{1,0:T(8,128)(2,1)} %pack.1), channel_id=1, source_target_pairs={{4,0},{5,1},{6,2},{7,3},{8,4},{9,5},{10,6},{11,7},{12,8},{13,9},{1... | collective-permute-start | bytes 2359304 | tf_op jit(solution)/shard_map/ppermute | solution.py:361
  40.3 24.6 %collective-permute-start.6 = (bf16[256,1536]{1,0:T(8,128)(2,1)S(1)}, bf16[256,1536]{1,0:T(8,128)(2,1)S(1)}, u32[]{:S(2)}, u32[]{:S(2)}) collective-permute-start(bf16[256,1536]{1,0:T(8,128)(2,1)S(1)} %get-tuple-element.28), channel_id=1, source_target_pairs={{0,1},{1,0},{2,3},{3,2},{4,5},{5,4},{6,7},{7,6},{8,9},{9,8},{10,11... | collective-permute-start | bytes 2359304 | tf_op jit(solution)/shard_map/ppermute | solution.py:361
  45.3 22.3 %collective-permute-start.4 = (bf16[512,768]{1,0:T(8,128)(2,1)S(1)}, bf16[512,768]{1,0:T(8,128)(2,1)S(1)}, u32[]{:S(2)}, u32[]{:S(2)}) collective-permute-start(bf16[512,768]{1,0:T(8,128)(2,1)S(1)} %get-tuple-element.27), channel_id=1, source_target_pairs={{0,4},{1,5},{2,6},{3,7},{4,8},{5,9},{6,10},{7,11},{8,12},{9,13},{1... | collective-permute-start | bytes 2359304 | tf_op jit(solution)/shard_map/ppermute | solution.py:361
  51.2 25.3 %collective-permute-start.5 = (bf16[512,768]{1,0:T(8,128)(2,1)S(1)}, bf16[512,768]{1,0:T(8,128)(2,1)S(1)}, u32[]{:S(2)}, u32[]{:S(2)}) collective-permute-start(bf16[512,768]{1,0:T(8,128)(2,1)S(1)} %get-tuple-element.27), channel_id=1, source_target_pairs={{4,0},{5,1},{6,2},{7,3},{8,4},{9,5},{10,6},{11,7},{12,8},{13,9},{1... | collective-permute-start | bytes 2359304 | tf_op jit(solution)/shard_map/ppermute | solution.py:361
  62.8 16.9 %collective-permute-start.12 = (bf16[256,768]{1,0:T(8,128)(2,1)S(1)}, bf16[256,768]{1,0:T(8,128)(2,1)S(1)}, u32[]{:S(2)}, u32[]{:S(2)}) collective-permute-start(bf16[256,768]{1,0:T(8,128)(2,1)S(1)} %get-tuple-element.38), channel_id=1, source_target_pairs={{0,2},{1,3},{2,0},{3,1},{4,6},{5,7},{6,4},{7,5},{8,10},{9,11},{10,... | collective-permute-start | bytes 1179656 | tf_op jit(solution)/shard_map/ppermute | solution.py:361
  64.8 19.7 %collective-permute-start.13 = (bf16[256,768]{1,0:T(8,128)(2,1)S(1)}, bf16[256,768]{1,0:T(8,128)(2,1)S(1)}, u32[]{:S(2)}, u32[]{:S(2)}) collective-permute-start(bf16[256,768]{1,0:T(8,128)(2,1)S(1)} %get-tuple-element.39), channel_id=1, source_target_pairs={{0,3},{1,2},{2,1},{3,0},{4,7},{5,6},{6,5},{7,4},{8,11},{9,10},{10,... | collective-permute-start | bytes 1179656 | tf_op jit(solution)/shard_map/ppermute | solution.py:361
  64.8 22.4 %collective-permute-start.14 = (bf16[256,768]{1,0:T(8,128)(2,1)S(1)}, bf16[256,768]{1,0:T(8,128)(2,1)S(1)}, u32[]{:S(2)}, u32[]{:S(2)}) collective-permute-start(bf16[256,768]{1,0:T(8,128)(2,1)S(1)} %get-tuple-element.40), channel_id=1, source_target_pairs={{0,8},{1,9},{2,10},{3,11},{4,0},{5,1},{6,2},{7,3},{8,12},{9,13},{1... | collective-permute-start | bytes 1179656 | tf_op jit(solution)/shard_map/ppermute | solution.py:361
  78.8 11.4 %collective-permute-start.10 = (bf16[256,768]{1,0:T(8,128)(2,1)S(1)}, bf16[256,768]{1,0:T(8,128)(2,1)S(1)}, u32[]{:S(2)}, u32[]{:S(2)}) collective-permute-start(bf16[256,768]{1,0:T(8,128)(2,1)S(1)} %get-tuple-element.33), channel_id=1, source_target_pairs={{0,3},{1,2},{2,1},{3,0},{4,7},{5,6},{6,5},{7,4},{8,11},{9,10},{10,... | collective-permute-start | bytes 1179656 | tf_op jit(solution)/shard_map/ppermute | solution.py:361
  79.5 15.1 %collective-permute-start.11 = (bf16[256,768]{1,0:T(8,128)(2,1)S(1)}, bf16[256,768]{1,0:T(8,128)(2,1)S(1)}, u32[]{:S(2)}, u32[]{:S(2)}) collective-permute-start(bf16[256,768]{1,0:T(8,128)(2,1)S(1)} %get-tuple-element.34), channel_id=1, source_target_pairs={{0,8},{1,9},{2,10},{3,11},{4,0},{5,1},{6,2},{7,3},{8,12},{9,13},{1... | collective-permute-start | bytes 1179656 | tf_op jit(solution)/shard_map/ppermute | solution.py:361
  79.7 19.1 %collective-permute-start.9 = (bf16[256,768]{1,0:T(8,128)(2,1)S(1)}, bf16[256,768]{1,0:T(8,128)(2,1)S(1)}, u32[]{:S(2)}, u32[]{:S(2)}) collective-permute-start(bf16[256,768]{1,0:T(8,128)(2,1)S(1)} %get-tuple-element.32), channel_id=1, source_target_pairs={{0,2},{1,3},{2,0},{3,1},{4,6},{5,7},{6,4},{7,5},{8,10},{9,11},{10,... | collective-permute-start | bytes 1179656 | tf_op jit(solution)/shard_map/ppermute | solution.py:361

commit v8 on v4

--- a/solution.py
+++ b/solution.py
@@ -176,13 +176,11 @@
     return pltpu.with_memory_space_constraint(array, pltpu.HBM)
 
 
-def tile_copies(sources, tile, target, column, sems, at):
-    width = target.shape[1] if column is None else column[1]
-    to = 0 if column is None else column[0]
+def tile_copies(sources, tile, target, sems, at):
     return [
         pltpu.make_async_copy(
-            ref.at[pl.ds(pl.multiple_of(row + tile * TILE, TILE), TILE), pl.ds(first, width)],
-            target.at[pl.ds(n * TILE, TILE), pl.ds(to, width)],
+            ref.at[pl.ds(pl.multiple_of(row + tile * TILE, TILE), TILE), pl.ds(first, target.shape[1])],
+            target.at[pl.ds(n * TILE, TILE)],
             sems.at[at + n],
         )
         for n, (ref, row, first) in enumerate(sources)
@@ -196,63 +194,81 @@
             copy.start()
 
 
-def begin(tile_lists, me, beside_list, across_list, far_list, keys, values, width):
+def tile_at(ref, entry, tile_count):
+    return jnp.clip(ref[0, entry], 0, tile_count - 1)
+
+
+def write_note(note, ref, tile_count):
+    lane = lax.broadcasted_iota(jnp.int32, note.shape, 1)
+    row = jnp.zeros(note.shape, jnp.float32)
+    for entry in range(8):
+        row = jnp.where(lane == entry, tile_at(ref, entry, tile_count).astype(jnp.float32), row)
+    note[...] = row.astype(jnp.bfloat16)
+
+
+def read_note(note, entry, tile_count):
+    here = (lax.broadcasted_iota(jnp.int32, note.shape, 1) == entry) & (
+        lax.broadcasted_iota(jnp.int32, note.shape, 0) == 0
+    )
+    value = jnp.sum(jnp.where(here, note.astype(jnp.float32), 0.0))
+    return jnp.clip(value.astype(jnp.int32), 0, tile_count - 1)
+
+
+def begin(tile_lists, me, beside_list, across_list, keys, values, width):
     rows, all_width = keys.shape
     tile_count = rows // TILE
 
-    def build(list_ref, me_ref, beside_ref, across_ref, far_ref, k_ref, v_ref, *refs):
-        meta, packed, to_beside, to_across, note, sems = refs
+    def build(list_ref, me_ref, beside_ref, across_ref, k_ref, v_ref, *refs):
+        meta, packed, to_beside, to_across, own_note, beside_note, sems = refs
         me = me_ref[0]
-        plane, right = me // 4, me % 4 >= 2
-
-        def tile_at(ref, entry):
-            return jnp.clip(ref[0, entry], 0, tile_count - 1)
-
+        right = me % 4 >= 2
+        own = ((k_ref, 0, 0), (v_ref, 0, 0))
         copies = [
             pltpu.make_async_copy(
                 ref.at[:, pl.ds(0, width)], packed.at[pl.ds(n * rows, rows)], sems.at[n]
             )
             for n, ref in enumerate((k_ref, v_ref))
         ]
-        own = ((k_ref, 0, 0), (v_ref, 0, 0))
-        copies += tile_copies(own, tile_at(across_ref, jnp.where(right, 5, 1)), to_across, None, sems, 2)
-        copies += tile_copies(own, tile_at(beside_ref, jnp.where(me % 2 == 0, 0, 4)), to_beside, None, sems, 4)
+        tile = tile_at(across_ref, jnp.where(right, 5, 1), tile_count)
+        copies += tile_copies(own, tile, to_across, sems, 2)
+        tile = tile_at(beside_ref, jnp.where(me % 2 == 0, 0, 4), tile_count)
+        copies += tile_copies(own, tile, to_beside, sems, 4)
         for copy in copies:
             copy.start()
-        lane = lax.broadcasted_iota(jnp.int32, note.shape, 1)
-        row = jnp.zeros(note.shape, jnp.float32)
+        write_note(own_note, list_ref, tile_count)
+        write_note(beside_note, beside_ref, tile_count)
+        notes = [
+            pltpu.make_async_copy(
+                own_note, packed.at[pl.ds(2 * rows, NOTE_ROWS), pl.ds(0, HD)], sems.at[6]
+            ),
+            pltpu.make_async_copy(
+                beside_note, to_across.at[pl.ds(2 * TILE, NOTE_ROWS), pl.ds(0, HD)], sems.at[7]
+            ),
+        ]
+        for copy in notes:
+            copy.start()
         for entry in range(8):
-            row = jnp.where(lane == entry, tile_at(beside_ref, entry).astype(jnp.float32), row)
-        note[...] = row.astype(jnp.bfloat16)
-        copies.append(
-            pltpu.make_async_copy(note, to_across.at[pl.ds(2 * TILE, NOTE_ROWS)], sems.at[6])
-        )
-        copies[-1].start()
-        for entry in range(8):
-            meta[entry] = tile_at(list_ref, entry)
+            meta[entry] = tile_at(list_ref, entry, tile_count)
         meta[8] = me
-        meta[9] = tile_at(far_ref, jnp.where(plane % 2 == 0, 3, 7))
-        meta[10] = tile_at(across_ref, jnp.where(right, 1, 5))
-        for entry in range(11, 16):
-            meta[entry] = 0
-        for copy in copies:
+        meta[9] = tile_at(across_ref, jnp.where(right, 1, 5), tile_count)
+        for copy in copies + notes:
             copy.wait()
 
     return move(
         "begin",
         build,
-        (tile_lists, me, beside_list, across_list, far_list, in_hbm(keys), in_hbm(values)),
-        [SCALAR] * 5 + [WHOLE] * 2,
+        (tile_lists, me, beside_list, across_list, in_hbm(keys), in_hbm(values)),
+        [SCALAR] * 4 + [WHOLE] * 2,
         [
-            jax.ShapeDtypeStruct((16,), jnp.int32),
-            jax.ShapeDtypeStruct((2 * rows, width), jnp.bfloat16),
+            jax.ShapeDtypeStruct((10,), jnp.int32),
+            jax.ShapeDtypeStruct((2 * rows + NOTE_ROWS, width), jnp.bfloat16),
             jax.ShapeDtypeStruct((2 * TILE, all_width), jnp.bfloat16),
             jax.ShapeDtypeStruct((2 * TILE + NOTE_ROWS, all_width), jnp.bfloat16),
         ],
         [SCALAR, WHOLE, WHOLE, WHOLE],
-        7,
+        8,
         24 * TILE * all_width,
-        [pltpu.VMEM((NOTE_ROWS, all_width), jnp.bfloat16)],
+        [pltpu.VMEM((NOTE_ROWS, HD), jnp.bfloat16)] * 2,
     )
 
 
@@ -284,53 +300,70 @@
     )
 
 
-def choose(meta, over, keys, values, first, low, high, after):
-    rows, width = low.shape[0] // 2, low.shape[1]
+def choose(meta, wants, over, keys, values, first, outer, inner, after):
+    rows, width = keys.shape[0], outer.shape[1]
     tile_count = rows // TILE
-
-    def build(meta, over_ref, k_ref, v_ref, low, high, *refs):
-        to_two, to_one, to_far, note, sems = refs[-5:]
+    again = wants is not None
+
+    def build(meta, *refs):
+        if again:
+            wants, k_ref, v_ref, outer, inner = refs[:5]
+        else:
+            over_ref, k_ref, v_ref, outer, inner = refs[:5]
+            wants, notes = refs[-7], refs[-2]
+        to_two, to_one, to_outer, to_inner = refs[-5:-1] if again else refs[-6:-2]
+        sems = refs[-1]
         spot, plane = meta[8] % 4, meta[8] // 4
-        right = spot >= 2
-        read = pltpu.make_async_copy(
-            over_ref.at[pl.ds(2 * TILE, NOTE_ROWS), pl.ds(0, HD)], note, sems.at[6]
-        )
-        read.start()
+        right, odd = spot >= 2, plane % 2 == 1
         own = ((k_ref, 0, first), (v_ref, 0, first))
-        below = ((low, 0, 0), (low, rows, 0))
-        above = ((high, 0, 0), (high, rows, 0))
-
-        def copies(source, tile, target, at):
-            return tile_copies(source, tile, target, None, sems, at)
-
-        start_if((plane == 0) | (plane == 3), copies(own, meta[9], to_far, 0))
-        start_if(plane == 1, copies(above, meta[9], to_far, 0))
-        start_if(plane == 2, copies(below, meta[9], to_far, 0))
-        start_if(right, copies(below, meta[10], to_two, 2))
-        start_if(jnp.logical_not(right), copies(above, meta[10], to_two, 2))
-        read.wait()
-        here = (lax.broadcasted_iota(jnp.int32, note.shape, 1) == jnp.where(spot % 2 == 0, 4, 0)) & (
-            lax.broadcasted_iota(jnp.int32, note.shape, 0) == 0
-        )
-        tile = jnp.sum(jnp.where(here, note[...].astype(jnp.float32), 0.0))
-        tile = jnp.clip(tile.astype(jnp.int32), 0, tile_count - 1)
-        start_if(spot == 0, copies(above, tile, to_one, 4))
-        start_if(spot == 3, copies(below, tile, to_one, 4))
-        start_if((spot == 1) | (spot == 2), copies(own, tile, to_one, 4))
-        for at, target in ((0, to_far), (2, to_two), (4, to_one)):
-            for copy in copies(own, 0, target, at):
+        from_outer = ((outer, 0, 0), (outer, rows, 0))
+        from_inner = ((inner, 0, 0), (inner, rows, 0))
+        if not again:
+            reads = [
+                pltpu.make_async_copy(
+                    ref.at[pl.ds(at, NOTE_ROWS), pl.ds(0, HD)], notes.at[n], sems.at[8 + n]
+                )
+                for n, (ref, at) in enumerate(((over_ref, 2 * TILE), (outer, 2 * rows), (inner, 2 * rows)))
+            ]
+            for read in reads:
+                read.start()
+        start_if(right == odd, tile_copies(from_outer, meta[9], to_two, sems, 0))
+        start_if(right != odd, tile_copies(from_inner, meta[9], to_two, sems, 0))
+        if not again:
+            for read in reads:
+                read.wait()
+            wants[0] = read_note(notes[0], jnp.where(spot % 2 == 0, 4, 0), tile_count)
+            wants[1] = read_note(notes[1], jnp.where(plane == 1, 7, 3), tile_count)
+            wants[2] = read_note(notes[2], jnp.where(plane == 1, 3, 7), tile_count)
+        near_outer = ((spot == 0) & jnp.logical_not(odd)) | ((spot == 3) & odd)
+        near_inner = ((spot == 0) & odd) | ((spot == 3) & jnp.logical_not(odd))
+        start_if(near_outer, tile_copies(from_outer, wants[0], to_one, sems, 2))
+        start_if(near_inner, tile_copies(from_inner, wants[0], to_one, sems, 2))
+        start_if((spot == 1) | (spot == 2), tile_copies(own, wants[0], to_one, sems, 2))
+        for copy in tile_copies(from_inner, wants[1], to_outer, sems, 4):
+            copy.start()
+        for copy in tile_copies(from_outer, wants[2], to_inner, sems, 6):
+            copy.start()
+        for n, target in enumerate((to_two, to_one, to_outer, to_inner)):
+            for copy in tile_copies(from_outer, 0, target, sems, 2 * n):
                 copy.wait()
 
+    sent = [jax.ShapeDtypeStruct((2 * TILE, width), jnp.bfloat16)] * 4
+    if again:
+        operands, specs = (meta, wants), [SCALAR, SCALAR]
+    else:
+        operands, specs = (meta, over), [SCALAR, WHOLE]
+        sent = [jax.ShapeDtypeStruct((3,), jnp.int32)] + sent
     return move(
-        "choose",
+        "choose_again" if again else "choose",
         build,
-        (meta, over, in_hbm(keys), in_hbm(values), low, high, *after),
-        [SCALAR] + [WHOLE] * (5 + len(after)),
-        [jax.ShapeDtypeStruct((2 * TILE, width), jnp.bfloat16)] * 3,
-        [WHOLE] * 3,
-        7,
-        24 * TILE * width,
-        [pltpu.VMEM((NOTE_ROWS, HD), jnp.bfloat16)],
+        (*operands, in_hbm(keys), in_hbm(values), outer, inner, *after),
+        specs + [WHOLE] * (4 + len(after)),
+        sent,
+        [SCALAR] * (not again) + [WHOLE] * 4,
+        11,
+        32 * TILE * width,
+        [] if again else [pltpu.VMEM((3, NOTE_ROWS, HD), jnp.bfloat16)],
     )
 
 
@@ -372,12 +405,12 @@
     heads = 3
     steps = half // (heads * HD)
     every = range(frames)
-    up = [(i, i + 4) for i in every if i + 4 < frames]
-    down = [(i, i - 4) for i in every if i - 4 >= 0]
     beside = [(i, i ^ 1) for i in every]
     across = [(i, i ^ 2) for i in every]
     corner = [(i, i ^ 3) for i in every]
-    far = [(i, i + (8, -4, 4, -8)[i // 4]) for i in every]
+    outer = [(i, i ^ 4) for i in every]
+    inner = [(i, i ^ 12) for i in every if i // 4 in (1, 2)]
+    outward = [(i, i ^ 4) for i in every if i // 4 in (1, 2)]
 
     def right(meta):
         return meta[8] % 4 >= 2
@@ -388,46 +421,54 @@
     def one_there(meta):
         return (meta[8] >= 1) & (meta[8] < frames - 1)
 
+    def outer_tile(meta):
+        return jnp.where(meta[8] // 4 % 2 == 1, meta[2], meta[6])
+
+    def inner_tile(meta):
+        return jnp.where(meta[8] // 4 % 2 == 1, meta[6], meta[2])
+
+    def inner_there(meta):
+        return (meta[8] >= 4) & (meta[8] < frames - 4)
+
     def own_frame():
         return [(key_heads, rows, fixed(0), 0)], [(value_heads, rows, fixed(0), 0)], None
 
-    def tile_of(array, tile, usable):
+    def tile_of(array, tile, usable=None):
         return [(array, TILE, tile, 0)], [(array, TILE, lambda meta: tile(meta) + tile_count, 0)], usable
 
-    def sent_tile(array, column=0, usable=None):
-        return [(array, TILE, fixed(0), column)], [(array, TILE, fixed(1), column)], usable
+    def sent_tile(arrays, column=0, usable=None):
+        return [(a, TILE, fixed(0), column) for a in arrays], [(a, TILE, fixed(1), column) for a in arrays], usable
 
     me = lax.axis_index("frame").astype(jnp.int32).reshape(1)
-    far_list = send(tile_lists, [(j, i) for i, j in far])
     beside_list = send(tile_lists, beside)
     across_list = send(tile_lists, across)
     meta, first, to_beside, to_across = begin(
-        tile_lists, me, beside_list, across_list, far_list, key_heads, value_heads, half
+        tile_lists, me, beside_list, across_list, key_heads, value_heads, half
     )
     over = send(to_across, across)
-    low = [send(first, up)]
-    high = [send(first, down)]
     next_to = send(to_beside, beside)
     begun = attend(queries, meta, [own_frame()], 0, 2 * steps, heads)
     second = pack(key_heads, value_heads, half, half, [begun[0]])
-    low.append(send(second, up))
-    high.append(send(second, down))
-
-    after = []
+
+    after, wants = [], None
     middles, finals = [], []
-    for n in (0, 1):
-        sent = choose(meta, over, key_heads, value_heads, n * half, low[n], high[n], after)
+    for n, packed in enumerate((first, second)):
+        from_outer = send(packed, outer)
+        from_inner = send(packed, inner)
+        sent = choose(meta, wants, over, key_heads, value_heads, n * half, from_outer, from_inner, after)
+        if wants is None:
+            wants, *sent = sent
         two = send(sent[0], across)
         one = send(sent[1], corner)
-        from_far = send(sent[2], far)
+        far = [send(sent[2], outward), send(sent[3], inner)]
         middle = attend(
             queries,
             meta,
             [
-                sent_tile(next_to, n * steps),
-                sent_tile(over, n * steps),
-                tile_of(low[n], lambda meta: meta[2], lambda meta: meta[8] >= 4),
-                tile_of(high[n], lambda meta: meta[6], lambda meta: meta[8] + 4 < frames),
+                sent_tile([next_to], n * steps),
+                sent_tile([over], n * steps),
+                tile_of(from_outer, outer_tile),
+                tile_of(from_inner, inner_tile, inner_there),
             ],
             n * steps,
             steps,
@@ -435,9 +476,9 @@
             begun,
             held=n * steps,
         )
-        after = [middle[0], two]
+        after = [middle[0]]
         middles.append(middle)
-        finals.append([sent_tile(two, 0, two_there), sent_tile(one, 0, one_there), sent_tile(from_far)])
+        finals.append([sent_tile([two], 0, two_there), sent_tile([one], 0, one_there), sent_tile(far)])
     out = None
     for n in (0, 1):
         out = attend(queries, meta, finals[n], n * steps, steps, heads, middles[n], True, out)

time: 75.8 us -> 75.8 us (level)
  the two profiles are of different devices: /device:TPU:9 before, /device:TPU:12 now
where the time goes in v8:
time: 75.8 us; the launch traced here: 74.5 us
  waiting for transfers between devices  26.6 us (35%)
  Pallas kernels  25.7 us (34%)
  starting transfers between devices  20.2 us (27%)
  local copies, waits for them, and re-layouts  1.8 us (2%)
    ppermute x16, waiting for transfers between devices, send(): return lax.ppermute(array, 'frame', route)  26.6 us
    ppermute x16, starting transfers between devices, send(): return lax.ppermute(array, 'frame', route)  20.2 us
    pallas_call x5, Pallas kernels, attend(): pl.pallas_call(functools.partial(attend_kernel, plan, heads, carry is not...  15.5 us
    pallas_call x4, Pallas kernels, move(): pl.pallas_call(build, name=name, out_shape=out_shape, in_specs=specs, out...  10.2 us
    unnamed x10, local copies, waits for them, and re-layouts  1.8 us
  transfers between devices with their start and end apart: 16, of which 6 were waited for; matrix products, arithmetic and copies ran while one was open for 0% of the time, Pallas kernels for 26%

profile of v8, /device:TPU:12, one launch (start us, length us, event | category | flops | bytes accessed | tf_op | source)
XLA Modules:
  0.0 74.5 jit_solution(4122052843241392856)
XLA Ops:
  0.0 0.0 collective-permute-start
  0.0 1.6 %collective-permute-start.1 = (s32[1,8]{1,0:T(1,128)}, s32[1,8]{1,0:T(1,128)S(1)}, u32[]{:S(2)}, u32[]{:S(2)}) collective-permute-start(s32[1,8]{1,0:T(1,128)} %list_ref.1), channel_id=1, source_target_pairs={{0,2},{1,3},{2,0},{3,1},{4,6},{5,7},{6,4},{7,5},{8,10},{9,11},{10,... | collective-permute-start | bytes 104 | tf_op jit(solution)/shard_map/ppermute | solution.py:371
  1.6 2.2 %collective-permute-done.1.across_ref = s32[1,8]{1,0:T(1,128)S(1)} collective-permute-done((s32[1,8]{1,0:T(1,128)}, s32[1,8]{1,0:T(1,128)S(1)}, u32[]{:S(2)}, u32[]{:S(2)}) %collective-permute-start.1) | collective-permute-done | bytes 64 | tf_op jit(solution)/shard_map/ppermute | solution.py:371
  3.8 0.7 copy-done.4
  4.4 2.9 %begin.1 = (s32[10]{0:T(128)S(1)}, bf16[528,768]{1,0:T(8,128)(2,1)S(1)}, bf16[256,1536]{1,0:T(8,128)(2,1)S(1)}, bf16[272,1536]{1,0:T(8,128)(2,1)S(1)}) custom-call(s32[1,8]{1,0:T(1,128)S(1)} %copy-done.4, s32[1]{0:T(128)} %bitcast.me_ref, s32[1,8]{1,0:T(1,128)S(1)} %collective-permute-done.beside_ref, s32[1,8]{1,0:T(1,128)S(1)} %collective-permute-done.1.across_ref, ...), custom_call_target="tpu_custom_call" | custom-call | bytes 4718592 | tf_op jit(solution)/shard_map/begin/pallas_call | solution.py:163
  7.3 3.6 %collective-permute-start.4 = (bf16[528,768]{1,0:T(8,128)(2,1)S(1)}, bf16[528,768]{1,0:T(8,128)(2,1)S(1)}, u32[]{:S(2)}, u32[]{:S(2)}) collective-permute-start(bf16[528,768]{1,0:T(8,128)(2,1)S(1)} %get-tuple-element.29), channel_id=1, source_target_pairs={{4,8},{5,9},{6,10},{7,11},{8,4},{9,5},{10,6},{11,7},{20,24},{21,25... | collective-permute-start | bytes 2433032 | tf_op jit(solution)/shard_map/ppermute | solution.py:371
  10.8 1.5 %collective-permute-start.2 = (bf16[272,1536]{1,0:T(8,128)(2,1)S(1)}, bf16[272,1536]{1,0:T(8,128)(2,1)S(1)}, u32[]{:S(2)}, u32[]{:S(2)}) collective-permute-start(bf16[272,1536]{1,0:T(8,128)(2,1)S(1)} %get-tuple-element.28), channel_id=1, source_target_pairs={{0,2},{1,3},{2,0},{3,1},{4,6},{5,7},{6,4},{7,5},{8,10},{9,11},{10,... | collective-permute-start | bytes 2506760 | tf_op jit(solution)/shard_map/ppermute | solution.py:371
  12.4 0.0 copy-start.2
  12.4 1.1 %copy-done.2 = bf16[256,1536]{1,0:T(8,128)(2,1)S(1)} copy-done((bf16[256,1536]{1,0:T(8,128)(2,1)S(1)}, bf16[256,1536]{1,0:T(8,128)(2,1)}, u32[]{:S(2)}) %copy-start.2) | copy-done | bytes 786456
  13.5 3.2 %attend_own.1 = (f32[256,1536]{1,0:T(8,128)S(1)}, f32[256,1536]{1,0:T(8,128)S(1)}, f32[256,1536]{1,0:T(8,128)S(1)}) custom-call(s32[10]{0:T(128)S(1)} %get-tuple-element.27.meta, bf16[256,1536]{1,0:T(8,128)(2,1)S(1)} %copy-done.2, bf16[256,1536]{1,0:T(8,128)(2,1)S(1)} %copy-done, bf16[256,1536]{1,0:T(8,128)(2,1)S(1)} %copy-done.1), custom_call_target="tpu_custom_call" | custom-call | flops 402653184 | bytes 2359296 | tf_op jit(solution)/shard_map/attend_own/pallas_call | solution.py:141
  16.7 1.1 %pack.1 = bf16[512,768]{1,0:T(8,128)(2,1)S(1)} custom-call(bf16[256,1536]{1,0:T(8,128)(2,1)} %refs_1_.5, bf16[256,1536]{1,0:T(8,128)(2,1)} %refs_2_.5, f32[256,1536]{1,0:T(8,128)S(1)} %get-tuple-element.31.refs_0_.refs_9_), custom_call_target="tpu_custom_call" | custom-call | bytes 1572864 | tf_op jit(solution)/shard_map/pack/pallas_call | solution.py:163
  17.9 0.0 copy-start.3
  17.9 2.5 %collective-permute-start.6 = (bf16[512,768]{1,0:T(8,128)(2,1)S(1)}, bf16[512,768]{1,0:T(8,128)(2,1)S(1)}, u32[]{:S(2)}, u32[]{:S(2)}) collective-permute-start(bf16[512,768]{1,0:T(8,128)(2,1)S(1)} %pack.1), channel_id=1, source_target_pairs={{4,8},{5,9},{6,10},{7,11},{8,4},{9,5},{10,6},{11,7},{20,24},{21,25... | collective-permute-start | bytes 2359304 | tf_op jit(solution)/shard_map/ppermute | solution.py:371
  20.3 9.8 %collective-permute-done.4.refs_4_.refs_7_.refs_8_ = bf16[528,768]{1,0:T(8,128)(2,1)S(1)} collective-permute-done((bf16[528,768]{1,0:T(8,128)(2,1)S(1)}, bf16[528,768]{1,0:T(8,128)(2,1)S(1)}, u32[]{:S(2)}, u32[]{:S(2)}) %collective-permute-start.4) | collective-permute-done | bytes 811040 | tf_op jit(solution)/shard_map/ppermute | solution.py:371
  30.2 2.5 %collective-permute-done.3.refs_3_.refs_5_.refs_6_ = bf16[528,768]{1,0:T(8,128)(2,1)S(1)} collective-permute-done((bf16[528,768]{1,0:T(8,128)(2,1)S(1)}, bf16[528,768]{1,0:T(8,128)(2,1)S(1)}, u32[]{:S(2)}, u32[]{:S(2)}) %collective-permute-start.3) | collective-permute-done | bytes 811040 | tf_op jit(solution)/shard_map/ppermute | solution.py:371
  32.7 0.0 collective-permute-done.2.refs_0_.refs_3_.refs_4_
  32.7 3.5 %choose.1 = (s32[3]{0:T(128)S(1)}, bf16[256,768]{1,0:T(8,128)(2,1)S(1)}, bf16[256,768]{1,0:T(8,128)(2,1)S(1)}, bf16[256,768]{1,0:T(8,128)(2,1)S(1)}, bf16[256,768]{1,0:T(8,128)(2,1)S(1)}) custom-call(s32[10]{0:T(128)S(1)} %get-tuple-element.27.meta, bf16[272,1536]{1,0:T(8,128)(2,1)S(1)} %collective-permute-done.2.refs_0_.refs_3_.refs_4_, ...), custom_call_target="tpu_custom_call" | custom-call | bytes 3145728 | tf_op jit(solution)/shard_map/choose/pallas_call | solution.py:163
  36.2 0.1 collective-permute-start.12
  36.2 0.1 collective-permute-start.13
  36.3 2.3 %collective-permute-start.14 = (bf16[256,768]{1,0:T(8,128)(2,1)S(1)}, bf16[256,768]{1,0:T(8,128)(2,1)S(1)}, u32[]{:S(2)}, u32[]{:S(2)}) collective-permute-start(bf16[256,768]{1,0:T(8,128)(2,1)S(1)} %get-tuple-element.45), channel_id=1, source_target_pairs={{4,0},{5,1},{6,2},{7,3},{8,12},{9,13},{10,14},{11,15},{20,16},{21,... | collective-permute-start | bytes 1179656 | tf_op jit(solution)/shard_map/ppermute | solution.py:371
  38.6 6.7 %collective-permute-done.6.refs_4_.refs_7_.refs_8_ = bf16[512,768]{1,0:T(8,128)(2,1)S(1)} collective-permute-done((bf16[512,768]{1,0:T(8,128)(2,1)S(1)}, bf16[512,768]{1,0:T(8,128)(2,1)S(1)}, u32[]{:S(2)}, u32[]{:S(2)}) %collective-permute-start.6) | collective-permute-done | bytes 786464 | tf_op jit(solution)/shard_map/ppermute | solution.py:371
  45.3 3.5 %collective-permute-start.15 = (bf16[256,768]{1,0:T(8,128)(2,1)S(1)}, bf16[256,768]{1,0:T(8,128)(2,1)S(1)}, u32[]{:S(2)}, u32[]{:S(2)}) collective-permute-start(bf16[256,768]{1,0:T(8,128)(2,1)S(1)} %get-tuple-element.46), channel_id=1, source_target_pairs={{4,8},{5,9},{6,10},{7,11},{8,4},{9,5},{10,6},{11,7},{20,24},{21,25... | collective-permute-start | bytes 1179656 | tf_op jit(solution)/shard_map/ppermute | solution.py:371
  48.8 3.1 %attend_more.2 = (f32[256,768]{1,0:T(8,128)S(1)}, f32[256,768]{1,0:T(8,128)S(1)}, f32[256,768]{1,0:T(8,128)S(1)}) custom-call(s32[10]{0:T(128)S(1)} %get-tuple-element.27.meta, bf16[256,1536]{1,0:T(8,128)(2,1)S(1)} %copy-done.3, bf16[256,1536]{1,0:T(8,128)(2,1)S(1)} %collective-permute-done.7.refs_1_.refs_2_, ...), custom_call_target="tpu_custom_call" | custom-call | flops 402653184 | bytes 1966080 | tf_op jit(solution)/shard_map/attend_more/pallas_call | solution.py:141
  51.9 2.7 %choose_again.1 = (bf16[256,768]{1,0:T(8,128)(2,1)S(1)}, bf16[256,768]{1,0:T(8,128)(2,1)S(1)}, bf16[256,768]{1,0:T(8,128)(2,1)S(1)}, bf16[256,768]{1,0:T(8,128)(2,1)S(1)}) custom-call(s32[10]{0:T(128)S(1)} %get-tuple-element.27.meta, s32[3]{0:T(128)S(1)} %get-tuple-element.30.refs_0_, bf16[256,1536]{1,0:T(8,128)(2,1)} %refs_1_.5, bf16[256,1536]{1,0:T(8,128)(2,1)} %refs_2_.5, ...), custom_call_target="tpu_custom_call" | custom-call | bytes 3145728 | tf_op jit(solution)/shard_map/choose_again/pallas_call | solution.py:163
  54.7 1.1 %collective-permute-start.8 = (bf16[256,768]{1,0:T(8,128)(2,1)S(1)}, bf16[256,768]{1,0:T(8,128)(2,1)S(1)}, u32[]{:S(2)}, u32[]{:S(2)}) collective-permute-start(bf16[256,768]{1,0:T(8,128)(2,1)S(1)} %get-tuple-element.36), channel_id=1, source_target_pairs={{0,2},{1,3},{2,0},{3,1},{4,6},{5,7},{6,4},{7,5},{8,10},{9,11},{10,... | collective-permute-start | bytes 1179656 | tf_op jit(solution)/shard_map/ppermute | solution.py:371
  55.8 1.3 %collective-permute-start.10 = (bf16[256,768]{1,0:T(8,128)(2,1)S(1)}, bf16[256,768]{1,0:T(8,128)(2,1)S(1)}, u32[]{:S(2)}, u32[]{:S(2)}) collective-permute-start(bf16[256,768]{1,0:T(8,128)(2,1)S(1)} %get-tuple-element.38), channel_id=1, source_target_pairs={{4,0},{5,1},{6,2},{7,3},{8,12},{9,13},{10,14},{11,15},{20,16},{21,... | collective-permute-start | bytes 1179656 | tf_op jit(solution)/shard_map/ppermute | solution.py:371
  57.1 2.8 %collective-permute-start.11 = (bf16[256,768]{1,0:T(8,128)(2,1)S(1)}, bf16[256,768]{1,0:T(8,128)(2,1)S(1)}, u32[]{:S(2)}, u32[]{:S(2)}) collective-permute-start(bf16[256,768]{1,0:T(8,128)(2,1)S(1)} %get-tuple-element.39), channel_id=1, source_target_pairs={{4,8},{5,9},{6,10},{7,11},{8,4},{9,5},{10,6},{11,7},{20,24},{21,25... | collective-permute-start | bytes 1179656 | tf_op jit(solution)/shard_map/ppermute | solution.py:371
  59.9 2.9 %attend_more.3 = (f32[256,768]{1,0:T(8,128)S(1)}, f32[256,768]{1,0:T(8,128)S(1)}, f32[256,768]{1,0:T(8,128)S(1)}) custom-call(s32[10]{0:T(128)S(1)} %get-tuple-element.27.meta, bf16[256,1536]{1,0:T(8,128)(2,1)S(1)} %copy-done.3, bf16[256,1536]{1,0:T(8,128)(2,1)S(1)} %collective-permute-done.7.refs_1_.refs_2_, ...), custom_call_target="tpu_custom_call" | custom-call | flops 402653184 | bytes 1966080 | tf_op jit(solution)/shard_map/attend_more/pallas_call | solution.py:141
  62.9 3.1 %attend_last.2.refs_12_ = bf16[256,1536]{1,0:T(8,128)(2,1)} custom-call(s32[10]{0:T(128)S(1)} %get-tuple-element.27.meta, bf16[256,1536]{1,0:T(8,128)(2,1)S(1)} %copy-done.3, bf16[256,768]{1,0:T(8,128)(2,1)S(1)} %collective-permute-done.12.refs_1_.refs_2_, bf16[256,768]{1,0:T(8,128)(2,1)S(1)} %collective-permute-done.12.refs_1_.refs_2_, ...), custom_call_target="tpu_custom_call" | custom-call | flops 301989888 | bytes 1572864 | tf_op jit(solution)/shard_map/attend_last/pallas_call | solution.py:141
  66.0 0.8 %collective-permute-done.8.refs_1_.refs_2_ = bf16[256,768]{1,0:T(8,128)(2,1)S(1)} collective-permute-done((bf16[256,768]{1,0:T(8,128)(2,1)S(1)}, bf16[256,768]{1,0:T(8,128)(2,1)S(1)}, u32[]{:S(2)}, u32[]{:S(2)}) %collective-permute-start.8) | collective-permute-done | bytes 393248 | tf_op jit(solution)/shard_map/ppermute | solution.py:371
  66.8 4.6 %collective-permute-done.9.refs_3_.refs_4_ = bf16[256,768]{1,0:T(8,128)(2,1)S(1)} collective-permute-done((bf16[256,768]{1,0:T(8,128)(2,1)S(1)}, bf16[256,768]{1,0:T(8,128)(2,1)S(1)}, u32[]{:S(2)}, u32[]{:S(2)}) %collective-permute-start.9) | collective-permute-done | bytes 393248 | tf_op jit(solution)/shard_map/ppermute | solution.py:371
  71.4 3.1 %attend_last.3 = bf16[256,1536]{1,0:T(8,128)(2,1)} custom-call(s32[10]{0:T(128)S(1)} %get-tuple-element.27.meta, bf16[256,1536]{1,0:T(8,128)(2,1)S(1)} %copy-done.3, bf16[256,768]{1,0:T(8,128)(2,1)S(1)} %collective-permute-done.8.refs_1_.refs_2_, bf16[256,768]{1,0:T(8,128)(2,1)S(1)} %collective-permute-done.8.refs_1_.refs_2_, ...), custom_call_target="tpu_custom_call", output_to_operand_aliasing={{}: (13, {})} | custom-call | flops 301989888 | bytes 1572864 | tf_op jit(solution)/shard_map/attend_last/pallas_call | solution.py:141
  (19 shorter events, 0.0 us)
Async XLA Ops:
  0.0 12.3 %copy-start.1 = (bf16[256,1536]{1,0:T(8,128)(2,1)S(1)}, bf16[256,1536]{1,0:T(8,128)(2,1)}, u32[]{:S(2)}) copy-start(bf16[256,1536]{1,0:T(8,128)(2,1)} %refs_2_.5) | copy-start | bytes 2359300
  0.0 12.4 %copy-start = (bf16[256,1536]{1,0:T(8,128)(2,1)S(1)}, bf16[256,1536]{1,0:T(8,128)(2,1)}, u32[]{:S(2)}) copy-start(bf16[256,1536]{1,0:T(8,128)(2,1)} %refs_1_.5) | copy-start | bytes 2359300
  0.0 1.6 %collective-permute-start = (s32[1,8]{1,0:T(1,128)}, s32[1,8]{1,0:T(1,128)S(1)}, u32[]{:S(2)}, u32[]{:S(2)}) collective-permute-start(s32[1,8]{1,0:T(1,128)} %list_ref.1), channel_id=1, source_target_pairs={{0,1},{1,0},{2,3},{3,2},{4,5},{5,4},{6,7},{7,6},{8,9},{9,8},{10,11... | collective-permute-start | bytes 104 | tf_op jit(solution)/shard_map/ppermute | solution.py:371
  0.0 3.7 %collective-permute-start.1 = (s32[1,8]{1,0:T(1,128)}, s32[1,8]{1,0:T(1,128)S(1)}, u32[]{:S(2)}, u32[]{:S(2)}) collective-permute-start(s32[1,8]{1,0:T(1,128)} %list_ref.1), channel_id=1, source_target_pairs={{0,2},{1,3},{2,0},{3,1},{4,6},{5,7},{6,4},{7,5},{8,10},{9,11},{10,... | collective-permute-start | bytes 104 | tf_op jit(solution)/shard_map/ppermute | solution.py:371
  3.8 0.7 copy-start.4
  7.3 22.9 %collective-permute-start.4 = (bf16[528,768]{1,0:T(8,128)(2,1)S(1)}, bf16[528,768]{1,0:T(8,128)(2,1)S(1)}, u32[]{:S(2)}, u32[]{:S(2)}) collective-permute-start(bf16[528,768]{1,0:T(8,128)(2,1)S(1)} %get-tuple-element.29), channel_id=1, source_target_pairs={{4,8},{5,9},{6,10},{7,11},{8,4},{9,5},{10,6},{11,7},{20,24},{21,25... | collective-permute-start | bytes 2433032 | tf_op jit(solution)/shard_map/ppermute | solution.py:371
  10.8 21.9 %collective-permute-start.2 = (bf16[272,1536]{1,0:T(8,128)(2,1)S(1)}, bf16[272,1536]{1,0:T(8,128)(2,1)S(1)}, u32[]{:S(2)}, u32[]{:S(2)}) collective-permute-start(bf16[272,1536]{1,0:T(8,128)(2,1)S(1)} %get-tuple-element.28), channel_id=1, source_target_pairs={{0,2},{1,3},{2,0},{3,1},{4,6},{5,7},{6,4},{7,5},{8,10},{9,11},{10,... | collective-permute-start | bytes 2506760 | tf_op jit(solution)/shard_map/ppermute | solution.py:371
  12.3 20.3 %collective-permute-start.3 = (bf16[528,768]{1,0:T(8,128)(2,1)S(1)}, bf16[528,768]{1,0:T(8,128)(2,1)S(1)}, u32[]{:S(2)}, u32[]{:S(2)}) collective-permute-start(bf16[528,768]{1,0:T(8,128)(2,1)S(1)} %get-tuple-element.29), channel_id=1, source_target_pairs={{0,4},{1,5},{2,6},{3,7},{4,0},{5,1},{6,2},{7,3},{8,12},{9,13},{10,... | collective-permute-start | bytes 2433032 | tf_op jit(solution)/shard_map/ppermute | solution.py:371
  12.3 24.0 %collective-permute-start.7 = (bf16[256,1536]{1,0:T(8,128)(2,1)S(1)}, bf16[256,1536]{1,0:T(8,128)(2,1)S(1)}, u32[]{:S(2)}, u32[]{:S(2)}) collective-permute-start(bf16[256,1536]{1,0:T(8,128)(2,1)S(1)} %get-tuple-element.32), channel_id=1, source_target_pairs={{0,1},{1,0},{2,3},{3,2},{4,5},{5,4},{6,7},{7,6},{8,9},{9,8},{10,11... | collective-permute-start | bytes 2359304 | tf_op jit(solution)/shard_map/ppermute | solution.py:371
  12.4 1.1 %copy-start.2 = (bf16[256,1536]{1,0:T(8,128)(2,1)S(1)}, bf16[256,1536]{1,0:T(8,128)(2,1)}, u32[]{:S(2)}) copy-start(bf16[256,1536]{1,0:T(8,128)(2,1)} %refs_0_.9) | copy-start | bytes 2359300
  17.9 30.9 %copy-start.3 = (bf16[256,1536]{1,0:T(8,128)(2,1)S(1)}, bf16[256,1536]{1,0:T(8,128)(2,1)}, u32[]{:S(2)}) copy-start(bf16[256,1536]{1,0:T(8,128)(2,1)} %refs_0_.9) | copy-start | bytes 2359300
  17.9 27.4 %collective-permute-start.6 = (bf16[512,768]{1,0:T(8,128)(2,1)S(1)}, bf16[512,768]{1,0:T(8,128)(2,1)S(1)}, u32[]{:S(2)}, u32[]{:S(2)}) collective-permute-start(bf16[512,768]{1,0:T(8,128)(2,1)S(1)} %pack.1), channel_id=1, source_target_pairs={{4,8},{5,9},{6,10},{7,11},{8,4},{9,5},{10,6},{11,7},{20,24},{21,25... | collective-permute-start | bytes 2359304 | tf_op jit(solution)/shard_map/ppermute | solution.py:371
  30.2 21.7 %collective-permute-start.5 = (bf16[512,768]{1,0:T(8,128)(2,1)S(1)}, bf16[512,768]{1,0:T(8,128)(2,1)S(1)}, u32[]{:S(2)}, u32[]{:S(2)}) collective-permute-start(bf16[512,768]{1,0:T(8,128)(2,1)S(1)} %pack.1), channel_id=1, source_target_pairs={{0,4},{1,5},{2,6},{3,7},{4,0},{5,1},{6,2},{7,3},{8,12},{9,13},{10,... | collective-permute-start | bytes 2359304 | tf_op jit(solution)/shard_map/ppermute | solution.py:371
  36.2 19.6 %collective-permute-start.12 = (bf16[256,768]{1,0:T(8,128)(2,1)S(1)}, bf16[256,768]{1,0:T(8,128)(2,1)S(1)}, u32[]{:S(2)}, u32[]{:S(2)}) collective-permute-start(bf16[256,768]{1,0:T(8,128)(2,1)S(1)} %get-tuple-element.43), channel_id=1, source_target_pairs={{0,2},{1,3},{2,0},{3,1},{4,6},{5,7},{6,4},{7,5},{8,10},{9,11},{10,... | collective-permute-start | bytes 1179656 | tf_op jit(solution)/shard_map/ppermute | solution.py:371
  36.2 19.5 %collective-permute-start.13 = (bf16[256,768]{1,0:T(8,128)(2,1)S(1)}, bf16[256,768]{1,0:T(8,128)(2,1)S(1)}, u32[]{:S(2)}, u32[]{:S(2)}) collective-permute-start(bf16[256,768]{1,0:T(8,128)(2,1)S(1)} %get-tuple-element.44), channel_id=1, source_target_pairs={{0,3},{1,2},{2,1},{3,0},{4,7},{5,6},{6,5},{7,4},{8,11},{9,10},{10,... | collective-permute-start | bytes 1179656 | tf_op jit(solution)/shard_map/ppermute | solution.py:371
  36.3 20.8 %collective-permute-start.14 = (bf16[256,768]{1,0:T(8,128)(2,1)S(1)}, bf16[256,768]{1,0:T(8,128)(2,1)S(1)}, u32[]{:S(2)}, u32[]{:S(2)}) collective-permute-start(bf16[256,768]{1,0:T(8,128)(2,1)S(1)} %get-tuple-element.45), channel_id=1, source_target_pairs={{4,0},{5,1},{6,2},{7,3},{8,12},{9,13},{10,14},{11,15},{20,16},{21,... | collective-permute-start | bytes 1179656 | tf_op jit(solution)/shard_map/ppermute | solution.py:371
  45.3 17.6 %collective-permute-start.15 = (bf16[256,768]{1,0:T(8,128)(2,1)S(1)}, bf16[256,768]{1,0:T(8,128)(2,1)S(1)}, u32[]{:S(2)}, u32[]{:S(2)}) collective-permute-start(bf16[256,768]{1,0:T(8,128)(2,1)S(1)} %get-tuple-element.46), channel_id=1, source_target_pairs={{4,8},{5,9},{6,10},{7,11},{8,4},{9,5},{10,6},{11,7},{20,24},{21,25... | collective-permute-start | bytes 1179656 | tf_op jit(solution)/shard_map/ppermute | solution.py:371
  54.7 12.1 %collective-permute-start.8 = (bf16[256,768]{1,0:T(8,128)(2,1)S(1)}, bf16[256,768]{1,0:T(8,128)(2,1)S(1)}, u32[]{:S(2)}, u32[]{:S(2)}) collective-permute-start(bf16[256,768]{1,0:T(8,128)(2,1)S(1)} %get-tuple-element.36), channel_id=1, source_target_pairs={{0,2},{1,3},{2,0},{3,1},{4,6},{5,7},{6,4},{7,5},{8,10},{9,11},{10,... | collective-permute-start | bytes 1179656 | tf_op jit(solution)/shard_map/ppermute | solution.py:371
  55.8 15.6 %collective-permute-start.9 = (bf16[256,768]{1,0:T(8,128)(2,1)S(1)}, bf16[256,768]{1,0:T(8,128)(2,1)S(1)}, u32[]{:S(2)}, u32[]{:S(2)}) collective-permute-start(bf16[256,768]{1,0:T(8,128)(2,1)S(1)} %get-tuple-element.37), channel_id=1, source_target_pairs={{0,3},{1,2},{2,1},{3,0},{4,7},{5,6},{6,5},{7,4},{8,11},{9,10},{10,... | collective-permute-start | bytes 1179656 | tf_op jit(solution)/shard_map/ppermute | solution.py:371
  55.8 15.6 %collective-permute-start.10 = (bf16[256,768]{1,0:T(8,128)(2,1)S(1)}, bf16[256,768]{1,0:T(8,128)(2,1)S(1)}, u32[]{:S(2)}, u32[]{:S(2)}) collective-permute-start(bf16[256,768]{1,0:T(8,128)(2,1)S(1)} %get-tuple-element.38), channel_id=1, source_target_pairs={{4,0},{5,1},{6,2},{7,3},{8,12},{9,13},{10,14},{11,15},{20,16},{21,... | collective-permute-start | bytes 1179656 | tf_op jit(solution)/shard_map/ppermute | solution.py:371
  57.1 14.3 %collective-permute-start.11 = (bf16[256,768]{1,0:T(8,128)(2,1)S(1)}, bf16[256,768]{1,0:T(8,128)(2,1)S(1)}, u32[]{:S(2)}, u32[]{:S(2)}) collective-permute-start(bf16[256,768]{1,0:T(8,128)(2,1)S(1)} %get-tuple-element.39), channel_id=1, source_target_pairs={{4,8},{5,9},{6,10},{7,11},{8,4},{9,5},{10,6},{11,7},{20,24},{21,25... | collective-permute-start | bytes 1179656 | tf_op jit(solution)/shard_map/ppermute | solution.py:371

commit v9 on v8

--- a/solution.py
+++ b/solution.py
@@ -214,79 +214,107 @@
     return jnp.clip(value.astype(jnp.int32), 0, tile_count - 1)
 
 
-def begin(tile_lists, me, beside_list, across_list, keys, values, width):
+def part_copies(k_ref, v_ref, first, width, target, sems, at):
+    rows = k_ref.shape[0]
+    return [
+        pltpu.make_async_copy(
+            ref.at[:, pl.ds(first, width)], target.at[pl.ds(n * rows, rows)], sems.at[at + n]
+        )
+        for n, ref in enumerate((k_ref, v_ref))
+    ]
+
+
+def begin(tile_lists, me, across_list, keys, values, width):
     rows, all_width = keys.shape
     tile_count = rows // TILE
 
-    def build(list_ref, me_ref, beside_ref, across_ref, k_ref, v_ref, *refs):
-        meta, packed, to_beside, to_across, own_note, beside_note, sems = refs
+    def build(me_ref, across_ref, list_hbm, k_ref, v_ref, meta, packed, to_across, list_ref, note, sems):
+        read = pltpu.make_async_copy(list_hbm, list_ref, sems.at[5])
+        read.start()
         me = me_ref[0]
         right = me % 4 >= 2
-        own = ((k_ref, 0, 0), (v_ref, 0, 0))
-        copies = [
-            pltpu.make_async_copy(
-                ref.at[:, pl.ds(0, width)], packed.at[pl.ds(n * rows, rows)], sems.at[n]
-            )
-            for n, ref in enumerate((k_ref, v_ref))
-        ]
+        copies = part_copies(k_ref, v_ref, 0, width, packed, sems, 0)
         tile = tile_at(across_ref, jnp.where(right, 5, 1), tile_count)
-        copies += tile_copies(own, tile, to_across, sems, 2)
-        tile = tile_at(beside_ref, jnp.where(me % 2 == 0, 0, 4), tile_count)
-        copies += tile_copies(own, tile, to_beside, sems, 4)
+        copies += tile_copies(((k_ref, 0, 0), (v_ref, 0, 0)), tile, to_across, sems, 2)
         for copy in copies:
             copy.start()
-        write_note(own_note, list_ref, tile_count)
-        write_note(beside_note, beside_ref, tile_count)
-        notes = [
-            pltpu.make_async_copy(
-                own_note, packed.at[pl.ds(2 * rows, NOTE_ROWS), pl.ds(0, HD)], sems.at[6]
-            ),
-            pltpu.make_async_copy(
-                beside_note, to_across.at[pl.ds(2 * TILE, NOTE_ROWS), pl.ds(0, HD)], sems.at[7]
-            ),
-        ]
-        for copy in notes:
-            copy.start()
+        read.wait()
+        write_note(note, list_ref, tile_count)
+        last = pltpu.make_async_copy(
+            note, packed.at[pl.ds(2 * rows, NOTE_ROWS), pl.ds(0, HD)], sems.at[4]
+        )
+        last.start()
         for entry in range(8):
             meta[entry] = tile_at(list_ref, entry, tile_count)
         meta[8] = me
         meta[9] = tile_at(across_ref, jnp.where(right, 1, 5), tile_count)
-        for copy in copies + notes:
+        for copy in copies + [last]:
             copy.wait()
 
     return move(
         "begin",
         build,
-        (tile_lists, me, beside_list, across_list, in_hbm(keys), in_hbm(values)),
-        [SCALAR] * 4 + [WHOLE] * 2,
+        (me, across_list, in_hbm(tile_lists), in_hbm(keys), in_hbm(values)),
+        [SCALAR] * 2 + [WHOLE] * 3,
         [
             jax.ShapeDtypeStruct((10,), jnp.int32),
             jax.ShapeDtypeStruct((2 * rows + NOTE_ROWS, width), jnp.bfloat16),
             jax.ShapeDtypeStruct((2 * TILE, all_width), jnp.bfloat16),
-            jax.ShapeDtypeStruct((2 * TILE + NOTE_ROWS, all_width), jnp.bfloat16),
         ],
-        [SCALAR, WHOLE, WHOLE, WHOLE],
-        8,
-        24 * TILE * all_width,
-        [pltpu.VMEM((NOTE_ROWS, HD), jnp.bfloat16)] * 2,
+        [SCALAR, WHOLE, WHOLE],
+        6,
+        8 * rows * width + 8 * TILE * all_width,
+        [pltpu.SMEM(tile_lists.shape, jnp.int32), pltpu.VMEM((NOTE_ROWS, HD), jnp.bfloat16)],
     )
 
 
-def pack(keys, values, first, width, after):
-    rows = keys.shape[0]
-
-    def build(k_ref, v_ref, *refs):
-        out_ref, sems = refs[-2:]
-        copies = [
-            pltpu.make_async_copy(
-                ref.at[:, pl.ds(first, width)], out_ref.at[pl.ds(n * rows, rows)], sems.at[n]
-            )
-            for n, ref in enumerate((k_ref, v_ref))
-        ]
+def choose_near(meta, beside_list, corner_list, keys, values):
+    rows, width = keys.shape
+    tile_count = rows // TILE
+
+    def build(meta, beside_ref, corner_ref, k_ref, v_ref, wanted, to_beside, to_corner, sems):
+        even = meta[8] % 2 == 0
+        own = ((k_ref, 0, 0), (v_ref, 0, 0))
+        copies = tile_copies(own, tile_at(beside_ref, jnp.where(even, 0, 4), tile_count), to_beside, sems, 0)
+        wanted[0] = tile_at(corner_ref, jnp.where(even, 4, 0), tile_count)
+        copies += tile_copies(own, wanted[0], to_corner, sems, 2)
         for copy in copies:
             copy.start()
         for copy in copies:
             copy.wait()
+
+    tile = jax.ShapeDtypeStruct((2 * TILE, width), jnp.bfloat16)
+    return move(
+        "choose_near",
+        build,
+        (meta, beside_list, corner_list, in_hbm(keys), in_hbm(values)),
+        [SCALAR] * 3 + [WHOLE] * 2,
+        [jax.ShapeDtypeStruct((1,), jnp.int32), tile, tile],
+        [SCALAR, WHOLE, WHOLE],
+        4,
+        16 * TILE * width,
+    )
+
+
+def pack(keys, values, first, width, after):
+    rows = keys.shape[0]
+
+    def build(k_ref, v_ref, *refs):
+        out_ref, stage, sems = refs[-3:]
+        reads = part_copies(k_ref, v_ref, first, width, stage, sems, 0)
+        writes = [
+            pltpu.make_async_copy(
+                stage.at[pl.ds(n * rows, rows)], out_ref.at[pl.ds(n * rows, rows)], sems.at[2 + n]
+            )
+            for n in (0, 1)
+        ]
+        for read in reads:
+            read.start()
+        for read, write in zip(reads, writes):
+            read.wait()
+            write.start()
+        for write in writes:
+            write.wait()
 
     return move(
         "pack",
@@ -295,75 +323,68 @@
         [WHOLE] * (2 + len(after)),
         jax.ShapeDtypeStruct((2 * rows, width), jnp.bfloat16),
         WHOLE,
-        2,
+        4,
         8 * rows * width,
+        [pltpu.VMEM((2 * rows, width), jnp.bfloat16)],
     )
 
 
-def choose(meta, wants, over, keys, values, first, outer, inner, after):
-    rows, width = keys.shape[0], outer.shape[1]
+def choose(meta, corner_tile, wants, outer, inner, after):
+    rows, width = outer.shape[0] // 2 // TILE * TILE, outer.shape[1]
     tile_count = rows // TILE
     again = wants is not None
 
-    def build(meta, *refs):
+    def build(meta, corner_ref, *refs):
         if again:
-            wants, k_ref, v_ref, outer, inner = refs[:5]
+            wants, outer, inner = refs[:3]
+            to_two, to_one, to_outer, to_inner = refs[-5:-1]
         else:
-            over_ref, k_ref, v_ref, outer, inner = refs[:5]
-            wants, notes = refs[-7], refs[-2]
-        to_two, to_one, to_outer, to_inner = refs[-5:-1] if again else refs[-6:-2]
+            outer, inner, wants = refs[:2] + refs[-7:-6]
+            to_two, to_one, to_outer, to_inner, notes = refs[-6:-1]
         sems = refs[-1]
         spot, plane = meta[8] % 4, meta[8] // 4
         right, odd = spot >= 2, plane % 2 == 1
-        own = ((k_ref, 0, first), (v_ref, 0, first))
         from_outer = ((outer, 0, 0), (outer, rows, 0))
         from_inner = ((inner, 0, 0), (inner, rows, 0))
         if not again:
             reads = [
                 pltpu.make_async_copy(
-                    ref.at[pl.ds(at, NOTE_ROWS), pl.ds(0, HD)], notes.at[n], sems.at[8 + n]
+                    ref.at[pl.ds(2 * rows, NOTE_ROWS), pl.ds(0, HD)], notes.at[n], sems.at[8 + n]
                 )
-                for n, (ref, at) in enumerate(((over_ref, 2 * TILE), (outer, 2 * rows), (inner, 2 * rows)))
+                for n, ref in enumerate((outer, inner))
             ]
             for read in reads:
                 read.start()
-        start_if(right == odd, tile_copies(from_outer, meta[9], to_two, sems, 0))
-        start_if(right != odd, tile_copies(from_inner, meta[9], to_two, sems, 0))
+        for source, here in ((from_outer, right == odd), (from_inner, right != odd)):
+            start_if(
+                here,
+                tile_copies(source, meta[9], to_two, sems, 0)
+                + tile_copies(source, corner_ref[0], to_one, sems, 2),
+            )
         if not again:
             for read in reads:
                 read.wait()
-            wants[0] = read_note(notes[0], jnp.where(spot % 2 == 0, 4, 0), tile_count)
-            wants[1] = read_note(notes[1], jnp.where(plane == 1, 7, 3), tile_count)
-            wants[2] = read_note(notes[2], jnp.where(plane == 1, 3, 7), tile_count)
-        near_outer = ((spot == 0) & jnp.logical_not(odd)) | ((spot == 3) & odd)
-        near_inner = ((spot == 0) & odd) | ((spot == 3) & jnp.logical_not(odd))
-        start_if(near_outer, tile_copies(from_outer, wants[0], to_one, sems, 2))
-        start_if(near_inner, tile_copies(from_inner, wants[0], to_one, sems, 2))
-        start_if((spot == 1) | (spot == 2), tile_copies(own, wants[0], to_one, sems, 2))
-        for copy in tile_copies(from_inner, wants[1], to_outer, sems, 4):
-            copy.start()
-        for copy in tile_copies(from_outer, wants[2], to_inner, sems, 6):
+            wants[0] = read_note(notes[0], jnp.where(plane == 1, 7, 3), tile_count)
+            wants[1] = read_note(notes[1], jnp.where(plane == 1, 3, 7), tile_count)
+        copies = tile_copies(from_inner, wants[0], to_outer, sems, 4)
+        copies += tile_copies(from_outer, wants[1], to_inner, sems, 6)
+        for copy in copies:
             copy.start()
         for n, target in enumerate((to_two, to_one, to_outer, to_inner)):
             for copy in tile_copies(from_outer, 0, target, sems, 2 * n):
                 copy.wait()
 
     sent = [jax.ShapeDtypeStruct((2 * TILE, width), jnp.bfloat16)] * 4
-    if again:
-        operands, specs = (meta, wants), [SCALAR, SCALAR]
-    else:
-        operands, specs = (meta, over), [SCALAR, WHOLE]
-        sent = [jax.ShapeDtypeStruct((3,), jnp.int32)] + sent
     return move(
         "choose_again" if again else "choose",
         build,
-        (*operands, in_hbm(keys), in_hbm(values), outer, inner, *after),
-        specs + [WHOLE] * (4 + len(after)),
-        sent,
+        (meta, corner_tile, *([wants] if again else []), outer, inner, *after),
+        [SCALAR] * (2 + again) + [WHOLE] * (2 + len(after)),
+        ([] if again else [jax.ShapeDtypeStruct((2,), jnp.int32)]) + sent,
         [SCALAR] * (not again) + [WHOLE] * 4,
-        11,
+        10,
         32 * TILE * width,
-        [] if again else [pltpu.VMEM((3, NOTE_ROWS, HD), jnp.bfloat16)],
+        [] if again else [pltpu.VMEM((2, NOTE_ROWS, HD), jnp.bfloat16)],
     )
 
 
@@ -401,13 +422,14 @@
     frames = 16
     rows, width = key_heads.shape
     tile_count = rows // TILE
-    half = width // 2
-    heads = 3
-    steps = half // (heads * HD)
+    heads = 4
+    block = heads * HD
+    parts = ((0, 2), (2, 1))
     every = range(frames)
     beside = [(i, i ^ 1) for i in every]
     across = [(i, i ^ 2) for i in every]
-    corner = [(i, i ^ 3) for i in every]
+    corner_in = [(i, i ^ 3) for i in every if i % 4 in (1, 2)]
+    corner_out = [(i, i ^ 3) for i in every if i % 4 in (0, 3)]
     outer = [(i, i ^ 4) for i in every]
     inner = [(i, i ^ 12) for i in every if i // 4 in (1, 2)]
     outward = [(i, i ^ 4) for i in every if i // 4 in (1, 2)]
@@ -436,52 +458,64 @@
     def tile_of(array, tile, usable=None):
         return [(array, TILE, tile, 0)], [(array, TILE, lambda meta: tile(meta) + tile_count, 0)], usable
 
-    def sent_tile(arrays, column=0, usable=None):
-        return [(a, TILE, fixed(0), column) for a in arrays], [(a, TILE, fixed(1), column) for a in arrays], usable
+    def sent_tile(arrays, usable=None):
+        return (
+            [(a, TILE, fixed(0), column) for a, column in arrays],
+            [(a, TILE, fixed(1), column) for a, column in arrays],
+            usable,
+        )
 
     me = lax.axis_index("frame").astype(jnp.int32).reshape(1)
+    across_list = send(tile_lists, across)
     beside_list = send(tile_lists, beside)
-    across_list = send(tile_lists, across)
-    meta, first, to_beside, to_across = begin(
-        tile_lists, me, beside_list, across_list, key_heads, value_heads, half
-    )
+    corner_list = send(across_list, beside)
+    first_width = parts[0][1] * block
+    meta, first, to_across = begin(tile_lists, me, across_list, key_heads, value_heads, first_width)
     over = send(to_across, across)
+    corner_tile, to_beside, to_corner = choose_near(meta, beside_list, corner_list, key_heads, value_heads)
     next_to = send(to_beside, beside)
-    begun = attend(queries, meta, [own_frame()], 0, 2 * steps, heads)
-    second = pack(key_heads, value_heads, half, half, [begun[0]])
-
-    after, wants = [], None
+    one_in = send(to_corner, corner_in)
+    begun = attend(queries, corner_tile, [own_frame()], 0, width // block, heads)
+    second = pack(key_heads, value_heads, first_width, width - first_width, [begun[0]])
+
+    after, wants = [over, next_to, one_in], None
     middles, finals = [], []
-    for n, packed in enumerate((first, second)):
+    for (at, steps), packed in zip(parts, (first, second)):
         from_outer = send(packed, outer)
         from_inner = send(packed, inner)
-        sent = choose(meta, wants, over, key_heads, value_heads, n * half, from_outer, from_inner, after)
+        sent = choose(meta, corner_tile, wants, from_outer, from_inner, after)
         if wants is None:
             wants, *sent = sent
         two = send(sent[0], across)
-        one = send(sent[1], corner)
+        one = send(sent[1], corner_out)
         far = [send(sent[2], outward), send(sent[3], inner)]
         middle = attend(
             queries,
             meta,
             [
-                sent_tile([next_to], n * steps),
-                sent_tile([over], n * steps),
+                sent_tile([(next_to, at)]),
+                sent_tile([(over, at)]),
                 tile_of(from_outer, outer_tile),
                 tile_of(from_inner, inner_tile, inner_there),
             ],
-            n * steps,
+            at,
             steps,
             heads,
             begun,
-            held=n * steps,
+            held=at,
         )
         after = [middle[0]]
         middles.append(middle)
-        finals.append([sent_tile([two], 0, two_there), sent_tile([one], 0, one_there), sent_tile(far)])
+        finals.append(
+            [
+                sent_tile([(two, 0)], two_there),
+                sent_tile([(one_in, at), (one, 0)], one_there),
+                sent_tile([(a, 0) for a in far]),
+            ]
+        )
     out = None
-    for n in (0, 1):
-        out = attend(queries, meta, finals[n], n * steps, steps, heads, middles[n], True, out)
+    for (at, steps), sources, middle in zip(parts, finals, middles):
+        out = attend(queries, meta, sources, at, steps, heads, middle, True, out)
     return out
 
 

time: 75.8 us -> 71.4 us (0.942)
  waiting for transfers between devices: 26.6 us -> 14 us
  starting transfers between devices: 20.2 us -> 30.7 us
  local copies, waits for them, and re-layouts: 1.8 us -> 0.01 us
    ppermute x16 -> x18, waiting for transfers between devices: 26.6 us -> 14 us  [send(): return lax.ppermute(array, 'frame', route)]
    ppermute x16 -> x18, starting transfers between devices: 20.2 us -> 30.7 us  [send(): return lax.ppermute(array, 'frame', route)]
    unnamed x10 -> x8, local copies, waits for them, and re-layouts: 1.8 us -> 0.01 us
    pallas_call x5, Pallas kernels: 15.5 us -> 13.8 us  [attend(): pl.pallas_call(functools.partial(attend_kernel, plan, heads, carry is not...]
    pallas_call x4 -> x5, Pallas kernels: 10.2 us -> 11.2 us  [move(): pl.pallas_call(build, name=name, out_shape=out_shape, in_specs=specs, out...]
  transfers between devices with their start and end apart: 16 -> 18, of which waited for: 6 -> 8; matrix products, arithmetic and copies ran while one was open for 0% -> 0% of each run, Pallas kernels for 26% -> 29%
where the time goes in v9:
time: 71.4 us; the launch traced here: 70 us
  starting transfers between devices  30.7 us (43%)
  Pallas kernels  25 us (35%)
  waiting for transfers between devices  14 us (20%)
    ppermute x18, starting transfers between devices, send(): return lax.ppermute(array, 'frame', route)  30.7 us
    ppermute x18, waiting for transfers between devices, send(): return lax.ppermute(array, 'frame', route)  14 us
    pallas_call x5, Pallas kernels, attend(): pl.pallas_call(functools.partial(attend_kernel, plan, heads, carry is not...  13.8 us
    pallas_call x5, Pallas kernels, move(): pl.pallas_call(build, name=name, out_shape=out_shape, in_specs=specs, out...  11.2 us
  transfers between devices with their start and end apart: 18, of which 8 were waited for; matrix products, arithmetic and copies ran while one was open for 0% of the time, Pallas kernels for 29%

profile of v9, /device:TPU:12, one launch (start us, length us, event | category | flops | bytes accessed | tf_op | source)
XLA Modules:
  0.0 70.0 jit_solution(2811314514156195511)
XLA Ops:
  0.0 1.5 %collective-permute-start = (s32[1,8]{1,0:T(1,128)}, s32[1,8]{1,0:T(1,128)S(1)}, u32[]{:S(2)}, u32[]{:S(2)}) collective-permute-start(s32[1,8]{1,0:T(1,128)} %list_hbm.1), channel_id=1, source_target_pairs={{0,2},{1,3},{2,0},{3,1},{4,6},{5,7},{6,4},{7,5},{8,10},{9,11},{10,... | collective-permute-start | bytes 104 | tf_op jit(solution)/shard_map/ppermute | solution.py:392
  1.5 2.2 %collective-permute-done.across_ref = s32[1,8]{1,0:T(1,128)S(1)} collective-permute-done((s32[1,8]{1,0:T(1,128)}, s32[1,8]{1,0:T(1,128)S(1)}, u32[]{:S(2)}, u32[]{:S(2)}) %collective-permute-start) | collective-permute-done | bytes 64 | tf_op jit(solution)/shard_map/ppermute | solution.py:392
  3.7 2.8 %begin.1 = (s32[10]{0:T(128)S(1)}, bf16[528,1024]{1,0:T(8,128)(2,1)S(1)}, bf16[256,1536]{1,0:T(8,128)(2,1)S(1)}) custom-call(s32[1]{0:T(128)} %bitcast.me_ref, s32[1,8]{1,0:T(1,128)S(1)} %collective-permute-done.across_ref, s32[1,8]{1,0:T(1,128)} %list_hbm.1, bf16[256,1536]{1,0:T(8,128)(2,1)} %k_ref.5, bf16[256,1536]{1,0:T(8,128)(2,1)} %v_ref.5), custom_call_target="tpu_custom_call" | custom-call | bytes 3670016 | tf_op jit(solution)/shard_map/begin/pallas_call | solution.py:163
  6.5 1.6 %collective-permute-start.5 = (bf16[256,1536]{1,0:T(8,128)(2,1)S(1)}, bf16[256,1536]{1,0:T(8,128)(2,1)S(1)}, u32[]{:S(2)}, u32[]{:S(2)}) collective-permute-start(bf16[256,1536]{1,0:T(8,128)(2,1)S(1)} %get-tuple-element.32), channel_id=1, source_target_pairs={{0,2},{1,3},{2,0},{3,1},{4,6},{5,7},{6,4},{7,5},{8,10},{9,11},{10,... | collective-permute-start | bytes 2359304 | tf_op jit(solution)/shard_map/ppermute | solution.py:392
  8.0 0.4 collective-permute-start.3
  8.5 4.6 %collective-permute-start.4 = (bf16[528,1024]{1,0:T(8,128)(2,1)S(1)}, bf16[528,1024]{1,0:T(8,128)(2,1)S(1)}, u32[]{:S(2)}, u32[]{:S(2)}) collective-permute-start(bf16[528,1024]{1,0:T(8,128)(2,1)S(1)} %get-tuple-element.31), channel_id=1, source_target_pairs={{4,8},{5,9},{6,10},{7,11},{8,4},{9,5},{10,6},{11,7},{20,24},{21,25... | collective-permute-start | bytes 3244040 | tf_op jit(solution)/shard_map/ppermute | solution.py:392
  13.2 0.5 collective-permute-start.2
  13.7 0.6 collective-permute-done.1.beside_ref
  14.3 0.2 collective-permute-done.2.corner_ref
  14.5 2.5 %choose_near.1 = (s32[1]{0:T(128)}, bf16[256,1536]{1,0:T(8,128)(2,1)S(1)}, bf16[256,1536]{1,0:T(8,128)(2,1)S(1)}) custom-call(s32[10]{0:T(128)S(1)} %get-tuple-element.29.meta, s32[1,8]{1,0:T(1,128)S(1)} %collective-permute-done.1.beside_ref, s32[1,8]{1,0:T(1,128)S(1)} %collective-permute-done.2.corner_ref, bf16[256,1536]{1,0:T(8,128)(2,1)} %k_ref.5, ...), custom_call_target="tpu_custom_call" | custom-call | bytes 3145728 | tf_op jit(solution)/shard_map/choose_near/pallas_call | solution.py:163
  17.0 0.4 collective-permute-start.6
  17.3 0.7 collective-permute-start.7
  18.1 2.9 %attend_own.1 = (f32[256,1536]{1,0:T(8,128)S(1)}, f32[256,1536]{1,0:T(8,128)S(1)}, f32[256,1536]{1,0:T(8,128)S(1)}) custom-call(s32[1]{0:T(128)} %get-tuple-element.30.corner_ref.meta, bf16[256,1536]{1,0:T(8,128)(2,1)S(1)} %copy-done, bf16[256,1536]{1,0:T(8,128)(2,1)S(1)} %copy-done.1, bf16[256,1536]{1,0:T(8,128)(2,1)S(1)} %copy-done.2), custom_call_target="tpu_custom_call" | custom-call | flops 402653184 | bytes 2359296 | tf_op jit(solution)/shard_map/attend_own/pallas_call | solution.py:141
  21.0 1.1 %pack.1 = bf16[512,512]{1,0:T(8,128)(2,1)S(1)} custom-call(bf16[256,1536]{1,0:T(8,128)(2,1)} %k_ref.5, bf16[256,1536]{1,0:T(8,128)(2,1)} %v_ref.5, f32[256,1536]{1,0:T(8,128)S(1)} %get-tuple-element.36.refs_0_.refs_9_), custom_call_target="tpu_custom_call" | custom-call | bytes 1048576 | tf_op jit(solution)/shard_map/pack/pallas_call | solution.py:163
  22.1 3.9 %collective-permute-done.5.refs_2_.refs_3_.refs_4_ = bf16[256,1536]{1,0:T(8,128)(2,1)S(1)} collective-permute-done((bf16[256,1536]{1,0:T(8,128)(2,1)S(1)}, bf16[256,1536]{1,0:T(8,128)(2,1)S(1)}, u32[]{:S(2)}, u32[]{:S(2)}) %collective-permute-start.5) | collective-permute-done | bytes 786464 | tf_op jit(solution)/shard_map/ppermute | solution.py:392
  26.0 0.4 collective-permute-start.8
  26.5 4.6 %collective-permute-start.9 = (bf16[512,512]{1,0:T(8,128)(2,1)S(1)}, bf16[512,512]{1,0:T(8,128)(2,1)S(1)}, u32[]{:S(2)}, u32[]{:S(2)}) collective-permute-start(bf16[512,512]{1,0:T(8,128)(2,1)S(1)} %pack.1), channel_id=1, source_target_pairs={{4,8},{5,9},{6,10},{7,11},{8,4},{9,5},{10,6},{11,7},{20,24},{21,25... | collective-permute-start | bytes 1572872 | tf_op jit(solution)/shard_map/ppermute | solution.py:392
  31.1 3.7 %collective-permute-done.3.refs_0_.refs_5_.refs_6_ = bf16[528,1024]{1,0:T(8,128)(2,1)S(1)} collective-permute-done((bf16[528,1024]{1,0:T(8,128)(2,1)S(1)}, bf16[528,1024]{1,0:T(8,128)(2,1)S(1)}, u32[]{:S(2)}, u32[]{:S(2)}) %collective-permute-start.3) | collective-permute-done | bytes 1081376 | tf_op jit(solution)/shard_map/ppermute | solution.py:392
  34.8 3.0 %collective-permute-done.4.refs_1_.refs_7_.refs_8_ = bf16[528,1024]{1,0:T(8,128)(2,1)S(1)} collective-permute-done((bf16[528,1024]{1,0:T(8,128)(2,1)S(1)}, bf16[528,1024]{1,0:T(8,128)(2,1)S(1)}, u32[]{:S(2)}, u32[]{:S(2)}) %collective-permute-start.4) | collective-permute-done | bytes 1081376 | tf_op jit(solution)/shard_map/ppermute | solution.py:392
  37.8 2.2 %choose.1 = (s32[2]{0:T(128)S(1)}, bf16[256,1024]{1,0:T(8,128)(2,1)S(1)}, bf16[256,1024]{1,0:T(8,128)(2,1)S(1)}, bf16[256,1024]{1,0:T(8,128)(2,1)S(1)}, bf16[256,1024]{1,0:T(8,128)(2,1)S(1)}) custom-call(s32[10]{0:T(128)S(1)} %get-tuple-element.29.meta, s32[1]{0:T(128)} %get-tuple-element.30.corner_ref.meta, ...), custom_call_target="tpu_custom_call" | custom-call | bytes 4194304 | tf_op jit(solution)/shard_map/choose/pallas_call | solution.py:163
  40.0 0.6 collective-permute-start.14
  40.6 1.9 %collective-permute-start.15 = (bf16[256,1024]{1,0:T(8,128)(2,1)S(1)}, bf16[256,1024]{1,0:T(8,128)(2,1)S(1)}, u32[]{:S(2)}, u32[]{:S(2)}) collective-permute-start(bf16[256,1024]{1,0:T(8,128)(2,1)S(1)} %get-tuple-element.48), channel_id=1, source_target_pairs={{0,3},{3,0},{4,7},{7,4},{8,11},{11,8},{12,15},{15,12},{16,19},{19,... | collective-permute-start | bytes 1572872 | tf_op jit(solution)/shard_map/ppermute | solution.py:392
  42.6 1.3 %collective-permute-start.16 = (bf16[256,1024]{1,0:T(8,128)(2,1)S(1)}, bf16[256,1024]{1,0:T(8,128)(2,1)S(1)}, u32[]{:S(2)}, u32[]{:S(2)}) collective-permute-start(bf16[256,1024]{1,0:T(8,128)(2,1)S(1)} %get-tuple-element.49), channel_id=1, source_target_pairs={{4,0},{5,1},{6,2},{7,3},{8,12},{9,13},{10,14},{11,15},{20,16},{21,... | collective-permute-start | bytes 1572872 | tf_op jit(solution)/shard_map/ppermute | solution.py:392
  44.0 4.6 %collective-permute-start.17 = (bf16[256,1024]{1,0:T(8,128)(2,1)S(1)}, bf16[256,1024]{1,0:T(8,128)(2,1)S(1)}, u32[]{:S(2)}, u32[]{:S(2)}) collective-permute-start(bf16[256,1024]{1,0:T(8,128)(2,1)S(1)} %get-tuple-element.50), channel_id=1, source_target_pairs={{4,8},{5,9},{6,10},{7,11},{8,4},{9,5},{10,6},{11,7},{20,24},{21,25... | collective-permute-start | bytes 1572872 | tf_op jit(solution)/shard_map/ppermute | solution.py:392
  48.6 3.5 %attend_more.2 = (f32[256,1024]{1,0:T(8,128)S(1)}, f32[256,1024]{1,0:T(8,128)S(1)}, f32[256,1024]{1,0:T(8,128)S(1)}) custom-call(s32[10]{0:T(128)S(1)} %get-tuple-element.29.meta, bf16[256,1536]{1,0:T(8,128)(2,1)S(1)} %copy-done, bf16[256,1536]{1,0:T(8,128)(2,1)S(1)} %collective-permute-done.6.refs_3_.refs_1_.refs_2_, ...), custom_call_target="tpu_custom_call" | custom-call | flops 536870912 | bytes 2621440 | tf_op jit(solution)/shard_map/attend_more/pallas_call | solution.py:141
  52.1 2.7 %choose_again.1 = (bf16[256,512]{1,0:T(8,128)(2,1)S(1)}, bf16[256,512]{1,0:T(8,128)(2,1)S(1)}, bf16[256,512]{1,0:T(8,128)(2,1)S(1)}, bf16[256,512]{1,0:T(8,128)(2,1)S(1)}) custom-call(s32[10]{0:T(128)S(1)} %get-tuple-element.29.meta, s32[1]{0:T(128)} %get-tuple-element.30.corner_ref.meta, s32[2]{0:T(128)S(1)} %get-tuple-element.35.refs_0_, ...), custom_call_target="tpu_custom_call" | custom-call | bytes 2097152 | tf_op jit(solution)/shard_map/choose_again/pallas_call | solution.py:163
  54.9 2.6 %collective-permute-start.11 = (bf16[256,512]{1,0:T(8,128)(2,1)S(1)}, bf16[256,512]{1,0:T(8,128)(2,1)S(1)}, u32[]{:S(2)}, u32[]{:S(2)}) collective-permute-start(bf16[256,512]{1,0:T(8,128)(2,1)S(1)} %get-tuple-element.41), channel_id=1, source_target_pairs={{0,3},{3,0},{4,7},{7,4},{8,11},{11,8},{12,15},{15,12},{16,19},{19,... | collective-permute-start | bytes 786440 | tf_op jit(solution)/shard_map/ppermute | solution.py:392
  57.5 1.3 %collective-permute-start.12 = (bf16[256,512]{1,0:T(8,128)(2,1)S(1)}, bf16[256,512]{1,0:T(8,128)(2,1)S(1)}, u32[]{:S(2)}, u32[]{:S(2)}) collective-permute-start(bf16[256,512]{1,0:T(8,128)(2,1)S(1)} %get-tuple-element.42), channel_id=1, source_target_pairs={{4,0},{5,1},{6,2},{7,3},{8,12},{9,13},{10,14},{11,15},{20,16},{21,... | collective-permute-start | bytes 786440 | tf_op jit(solution)/shard_map/ppermute | solution.py:392
  58.8 3.5 %collective-permute-start.13 = (bf16[256,512]{1,0:T(8,128)(2,1)S(1)}, bf16[256,512]{1,0:T(8,128)(2,1)S(1)}, u32[]{:S(2)}, u32[]{:S(2)}) collective-permute-start(bf16[256,512]{1,0:T(8,128)(2,1)S(1)} %get-tuple-element.43), channel_id=1, source_target_pairs={{4,8},{5,9},{6,10},{7,11},{8,4},{9,5},{10,6},{11,7},{20,24},{21,25... | collective-permute-start | bytes 786440 | tf_op jit(solution)/shard_map/ppermute | solution.py:392
  62.4 1.6 %attend_more.3 = (f32[256,512]{1,0:T(8,128)S(1)}, f32[256,512]{1,0:T(8,128)S(1)}, f32[256,512]{1,0:T(8,128)S(1)}) custom-call(s32[10]{0:T(128)S(1)} %get-tuple-element.29.meta, bf16[256,1536]{1,0:T(8,128)(2,1)S(1)} %copy-done, bf16[256,1536]{1,0:T(8,128)(2,1)S(1)} %collective-permute-done.6.refs_3_.refs_1_.refs_2_, ...), custom_call_target="tpu_custom_call" | custom-call | flops 268435456 | bytes 1310720 | tf_op jit(solution)/shard_map/attend_more/pallas_call | solution.py:141
  64.0 3.5 %attend_last.2.refs_14_ = bf16[256,1536]{1,0:T(8,128)(2,1)} custom-call(s32[10]{0:T(128)S(1)} %get-tuple-element.29.meta, bf16[256,1536]{1,0:T(8,128)(2,1)S(1)} %copy-done, bf16[256,1024]{1,0:T(8,128)(2,1)S(1)} %collective-permute-done.14.refs_1_.refs_2_, bf16[256,1024]{1,0:T(8,128)(2,1)S(1)} %collective-permute-done.14.refs_1_.refs_2_, ...), custom_call_target="tpu_custom_call" | custom-call | flops 402653184 | bytes 2097152 | tf_op jit(solution)/shard_map/attend_last/pallas_call | solution.py:141
  67.8 2.2 %attend_last.3 = bf16[256,1536]{1,0:T(8,128)(2,1)} custom-call(s32[10]{0:T(128)S(1)} %get-tuple-element.29.meta, bf16[256,1536]{1,0:T(8,128)(2,1)S(1)} %copy-done, bf16[256,512]{1,0:T(8,128)(2,1)S(1)} %collective-permute-done.10.refs_1_.refs_2_, bf16[256,512]{1,0:T(8,128)(2,1)S(1)} %collective-permute-done.10.refs_1_.refs_2_, ...), custom_call_target="tpu_custom_call", output_to_operand_aliasing={{}: (15, {})} | custom-call | flops 201326592 | bytes 1048576 | tf_op jit(solution)/shard_map/attend_last/pallas_call | solution.py:141
  (22 shorter events, 0.5 us)
Async XLA Ops:
  0.0 13.1 %copy-start.3 = (s32[1,8]{1,0:T(1,128)S(1)}, s32[1,8]{1,0:T(1,128)}, u32[]{:S(2)}) copy-start(s32[1,8]{1,0:T(1,128)} %list_hbm.1) | copy-start | bytes 100
  0.0 3.7 %collective-permute-start = (s32[1,8]{1,0:T(1,128)}, s32[1,8]{1,0:T(1,128)S(1)}, u32[]{:S(2)}, u32[]{:S(2)}) collective-permute-start(s32[1,8]{1,0:T(1,128)} %list_hbm.1), channel_id=1, source_target_pairs={{0,2},{1,3},{2,0},{3,1},{4,6},{5,7},{6,4},{7,5},{8,10},{9,11},{10,... | collective-permute-start | bytes 104 | tf_op jit(solution)/shard_map/ppermute | solution.py:392
  3.7 14.4 %copy-start = (bf16[256,1536]{1,0:T(8,128)(2,1)S(1)}, bf16[256,1536]{1,0:T(8,128)(2,1)}, u32[]{:S(2)}) copy-start(bf16[256,1536]{1,0:T(8,128)(2,1)} %refs_0_.9) | copy-start | bytes 2359300
  3.7 14.4 %copy-start.1 = (bf16[256,1536]{1,0:T(8,128)(2,1)S(1)}, bf16[256,1536]{1,0:T(8,128)(2,1)}, u32[]{:S(2)}) copy-start(bf16[256,1536]{1,0:T(8,128)(2,1)} %k_ref.5) | copy-start | bytes 2359300
  3.7 14.4 %copy-start.2 = (bf16[256,1536]{1,0:T(8,128)(2,1)S(1)}, bf16[256,1536]{1,0:T(8,128)(2,1)}, u32[]{:S(2)}) copy-start(bf16[256,1536]{1,0:T(8,128)(2,1)} %v_ref.5) | copy-start | bytes 2359300
  6.5 19.6 %collective-permute-start.5 = (bf16[256,1536]{1,0:T(8,128)(2,1)S(1)}, bf16[256,1536]{1,0:T(8,128)(2,1)S(1)}, u32[]{:S(2)}, u32[]{:S(2)}) collective-permute-start(bf16[256,1536]{1,0:T(8,128)(2,1)S(1)} %get-tuple-element.32), channel_id=1, source_target_pairs={{0,2},{1,3},{2,0},{3,1},{4,6},{5,7},{6,4},{7,5},{8,10},{9,11},{10,... | collective-permute-start | bytes 2359304 | tf_op jit(solution)/shard_map/ppermute | solution.py:392
  8.0 26.8 %collective-permute-start.3 = (bf16[528,1024]{1,0:T(8,128)(2,1)S(1)}, bf16[528,1024]{1,0:T(8,128)(2,1)S(1)}, u32[]{:S(2)}, u32[]{:S(2)}) collective-permute-start(bf16[528,1024]{1,0:T(8,128)(2,1)S(1)} %get-tuple-element.31), channel_id=1, source_target_pairs={{0,4},{1,5},{2,6},{3,7},{4,0},{5,1},{6,2},{7,3},{8,12},{9,13},{10,... | collective-permute-start | bytes 3244040 | tf_op jit(solution)/shard_map/ppermute | solution.py:392
  8.5 29.4 %collective-permute-start.4 = (bf16[528,1024]{1,0:T(8,128)(2,1)S(1)}, bf16[528,1024]{1,0:T(8,128)(2,1)S(1)}, u32[]{:S(2)}, u32[]{:S(2)}) collective-permute-start(bf16[528,1024]{1,0:T(8,128)(2,1)S(1)} %get-tuple-element.31), channel_id=1, source_target_pairs={{4,8},{5,9},{6,10},{7,11},{8,4},{9,5},{10,6},{11,7},{20,24},{21,25... | collective-permute-start | bytes 3244040 | tf_op jit(solution)/shard_map/ppermute | solution.py:392
  13.1 1.2 %collective-permute-start.1 = (s32[1,8]{1,0:T(1,128)S(1)}, s32[1,8]{1,0:T(1,128)S(1)}, u32[]{:S(2)}, u32[]{:S(2)}) collective-permute-start(s32[1,8]{1,0:T(1,128)S(1)} %copy-done.3), channel_id=1, source_target_pairs={{0,1},{1,0},{2,3},{3,2},{4,5},{5,4},{6,7},{7,6},{8,9},{9,8},{10,11... | collective-permute-start | bytes 104 | tf_op jit(solution)/shard_map/ppermute | solution.py:392
  13.2 1.3 %collective-permute-start.2 = (s32[1,8]{1,0:T(1,128)S(1)}, s32[1,8]{1,0:T(1,128)S(1)}, u32[]{:S(2)}, u32[]{:S(2)}) collective-permute-start(s32[1,8]{1,0:T(1,128)S(1)} %collective-permute-done.across_ref), channel_id=1, source_target_pairs={{0,1},{1,0},{2,3},{3,2},{4,5},{5,4},{6,7},{7,6},{8,9},{9,8},{10,11... | collective-permute-start | bytes 104 | tf_op jit(solution)/shard_map/ppermute | solution.py:392
  17.0 9.5 %collective-permute-start.6 = (bf16[256,1536]{1,0:T(8,128)(2,1)S(1)}, bf16[256,1536]{1,0:T(8,128)(2,1)S(1)}, u32[]{:S(2)}, u32[]{:S(2)}) collective-permute-start(bf16[256,1536]{1,0:T(8,128)(2,1)S(1)} %get-tuple-element.33), channel_id=1, source_target_pairs={{0,1},{1,0},{2,3},{3,2},{4,5},{5,4},{6,7},{7,6},{8,9},{9,8},{10,11... | collective-permute-start | bytes 2359304 | tf_op jit(solution)/shard_map/ppermute | solution.py:392
  17.3 13.8 %collective-permute-start.7 = (bf16[256,1536]{1,0:T(8,128)(2,1)S(1)}, bf16[256,1536]{1,0:T(8,128)(2,1)S(1)}, u32[]{:S(2)}, u32[]{:S(2)}) collective-permute-start(bf16[256,1536]{1,0:T(8,128)(2,1)S(1)} %get-tuple-element.34), channel_id=1, source_target_pairs={{1,2},{2,1},{5,6},{6,5},{9,10},{10,9},{13,14},{14,13},{17,18},{18,... | collective-permute-start | bytes 2359304 | tf_op jit(solution)/shard_map/ppermute | solution.py:392
  26.0 18.0 %collective-permute-start.8 = (bf16[512,512]{1,0:T(8,128)(2,1)S(1)}, bf16[512,512]{1,0:T(8,128)(2,1)S(1)}, u32[]{:S(2)}, u32[]{:S(2)}) collective-permute-start(bf16[512,512]{1,0:T(8,128)(2,1)S(1)} %pack.1), channel_id=1, source_target_pairs={{0,4},{1,5},{2,6},{3,7},{4,0},{5,1},{6,2},{7,3},{8,12},{9,13},{10,... | collective-permute-start | bytes 1572872 | tf_op jit(solution)/shard_map/ppermute | solution.py:392
  26.5 25.6 %collective-permute-start.9 = (bf16[512,512]{1,0:T(8,128)(2,1)S(1)}, bf16[512,512]{1,0:T(8,128)(2,1)S(1)}, u32[]{:S(2)}, u32[]{:S(2)}) collective-permute-start(bf16[512,512]{1,0:T(8,128)(2,1)S(1)} %pack.1), channel_id=1, source_target_pairs={{4,8},{5,9},{6,10},{7,11},{8,4},{9,5},{10,6},{11,7},{20,24},{21,25... | collective-permute-start | bytes 1572872 | tf_op jit(solution)/shard_map/ppermute | solution.py:392
  40.0 14.8 %collective-permute-start.14 = (bf16[256,1024]{1,0:T(8,128)(2,1)S(1)}, bf16[256,1024]{1,0:T(8,128)(2,1)S(1)}, u32[]{:S(2)}, u32[]{:S(2)}) collective-permute-start(bf16[256,1024]{1,0:T(8,128)(2,1)S(1)} %get-tuple-element.47), channel_id=1, source_target_pairs={{0,2},{1,3},{2,0},{3,1},{4,6},{5,7},{6,4},{7,5},{8,10},{9,11},{10,... | collective-permute-start | bytes 1572872 | tf_op jit(solution)/shard_map/ppermute | solution.py:392
  40.6 16.8 %collective-permute-start.15 = (bf16[256,1024]{1,0:T(8,128)(2,1)S(1)}, bf16[256,1024]{1,0:T(8,128)(2,1)S(1)}, u32[]{:S(2)}, u32[]{:S(2)}) collective-permute-start(bf16[256,1024]{1,0:T(8,128)(2,1)S(1)} %get-tuple-element.48), channel_id=1, source_target_pairs={{0,3},{3,0},{4,7},{7,4},{8,11},{11,8},{12,15},{15,12},{16,19},{19,... | collective-permute-start | bytes 1572872 | tf_op jit(solution)/shard_map/ppermute | solution.py:392
  42.6 16.2 %collective-permute-start.16 = (bf16[256,1024]{1,0:T(8,128)(2,1)S(1)}, bf16[256,1024]{1,0:T(8,128)(2,1)S(1)}, u32[]{:S(2)}, u32[]{:S(2)}) collective-permute-start(bf16[256,1024]{1,0:T(8,128)(2,1)S(1)} %get-tuple-element.49), channel_id=1, source_target_pairs={{4,0},{5,1},{6,2},{7,3},{8,12},{9,13},{10,14},{11,15},{20,16},{21,... | collective-permute-start | bytes 1572872 | tf_op jit(solution)/shard_map/ppermute | solution.py:392
  44.0 20.0 %collective-permute-start.17 = (bf16[256,1024]{1,0:T(8,128)(2,1)S(1)}, bf16[256,1024]{1,0:T(8,128)(2,1)S(1)}, u32[]{:S(2)}, u32[]{:S(2)}) collective-permute-start(bf16[256,1024]{1,0:T(8,128)(2,1)S(1)} %get-tuple-element.50), channel_id=1, source_target_pairs={{4,8},{5,9},{6,10},{7,11},{8,4},{9,5},{10,6},{11,7},{20,24},{21,25... | collective-permute-start | bytes 1572872 | tf_op jit(solution)/shard_map/ppermute | solution.py:392
  54.8 12.8 %collective-permute-start.10 = (bf16[256,512]{1,0:T(8,128)(2,1)S(1)}, bf16[256,512]{1,0:T(8,128)(2,1)S(1)}, u32[]{:S(2)}, u32[]{:S(2)}) collective-permute-start(bf16[256,512]{1,0:T(8,128)(2,1)S(1)} %get-tuple-element.40), channel_id=1, source_target_pairs={{0,2},{1,3},{2,0},{3,1},{4,6},{5,7},{6,4},{7,5},{8,10},{9,11},{10,... | collective-permute-start | bytes 786440 | tf_op jit(solution)/shard_map/ppermute | solution.py:392
  54.9 12.7 %collective-permute-start.11 = (bf16[256,512]{1,0:T(8,128)(2,1)S(1)}, bf16[256,512]{1,0:T(8,128)(2,1)S(1)}, u32[]{:S(2)}, u32[]{:S(2)}) collective-permute-start(bf16[256,512]{1,0:T(8,128)(2,1)S(1)} %get-tuple-element.41), channel_id=1, source_target_pairs={{0,3},{3,0},{4,7},{7,4},{8,11},{11,8},{12,15},{15,12},{16,19},{19,... | collective-permute-start | bytes 786440 | tf_op jit(solution)/shard_map/ppermute | solution.py:392
  57.5 10.1 %collective-permute-start.12 = (bf16[256,512]{1,0:T(8,128)(2,1)S(1)}, bf16[256,512]{1,0:T(8,128)(2,1)S(1)}, u32[]{:S(2)}, u32[]{:S(2)}) collective-permute-start(bf16[256,512]{1,0:T(8,128)(2,1)S(1)} %get-tuple-element.42), channel_id=1, source_target_pairs={{4,0},{5,1},{6,2},{7,3},{8,12},{9,13},{10,14},{11,15},{20,16},{21,... | collective-permute-start | bytes 786440 | tf_op jit(solution)/shard_map/ppermute | solution.py:392
  58.8 9.0 %collective-permute-start.13 = (bf16[256,512]{1,0:T(8,128)(2,1)S(1)}, bf16[256,512]{1,0:T(8,128)(2,1)S(1)}, u32[]{:S(2)}, u32[]{:S(2)}) collective-permute-start(bf16[256,512]{1,0:T(8,128)(2,1)S(1)} %get-tuple-element.43), channel_id=1, source_target_pairs={{4,8},{5,9},{6,10},{7,11},{8,4},{9,5},{10,6},{11,7},{20,24},{21,25... | collective-permute-start | bytes 786440 | tf_op jit(solution)/shard_map/ppermute | solution.py:392

commit v10 on v9

--- a/solution.py
+++ b/solution.py
@@ -187,6 +187,12 @@
     ]
 
 
+def zero_copies(zeros, target, sems, at):
+    return [
+        pltpu.make_async_copy(zeros, target.at[pl.ds(n * TILE, TILE)], sems.at[at + n]) for n in (0, 1)
+    ]
+
+
 def start_if(condition, copies):
     @pl.when(condition)
     def _():
@@ -272,15 +278,19 @@
     rows, width = keys.shape
     tile_count = rows // TILE
 
-    def build(meta, beside_ref, corner_ref, k_ref, v_ref, wanted, to_beside, to_corner, sems):
+    def build(meta, beside_ref, corner_ref, k_ref, v_ref, wanted, to_beside, to_corner, zeros, sems):
         even = meta[8] % 2 == 0
         own = ((k_ref, 0, 0), (v_ref, 0, 0))
         copies = tile_copies(own, tile_at(beside_ref, jnp.where(even, 0, 4), tile_count), to_beside, sems, 0)
-        wanted[0] = tile_at(corner_ref, jnp.where(even, 4, 0), tile_count)
-        copies += tile_copies(own, wanted[0], to_corner, sems, 2)
         for copy in copies:
             copy.start()
-        for copy in copies:
+        wanted[0] = tile_at(corner_ref, jnp.where(even, 4, 0), tile_count)
+        inside = (meta[8] % 4 == 1) | (meta[8] % 4 == 2)
+        start_if(inside, tile_copies(own, wanted[0], to_corner, sems, 2))
+        zeros[...] = jnp.zeros_like(zeros)
+        blank = zero_copies(zeros, to_corner, sems, 2)
+        start_if(jnp.logical_not(inside), blank)
+        for copy in copies + blank:
             copy.wait()
 
     tile = jax.ShapeDtypeStruct((2 * TILE, width), jnp.bfloat16)
@@ -293,6 +303,7 @@
         [SCALAR, WHOLE, WHOLE],
         4,
         16 * TILE * width,
+        [pltpu.VMEM((TILE, width), jnp.bfloat16)],
     )
 
 
@@ -337,11 +348,11 @@
     def build(meta, corner_ref, *refs):
         if again:
             wants, outer, inner = refs[:3]
-            to_two, to_one, to_outer, to_inner = refs[-5:-1]
+            to_two, to_one, to_outer, to_inner = refs[-6:-2]
         else:
-            outer, inner, wants = refs[:2] + refs[-7:-6]
-            to_two, to_one, to_outer, to_inner, notes = refs[-6:-1]
-        sems = refs[-1]
+            outer, inner, wants = refs[:2] + refs[-8:-7]
+            to_two, to_one, to_outer, to_inner, notes = refs[-7:-2]
+        zeros, sems = refs[-2:]
         spot, plane = meta[8] % 4, meta[8] // 4
         right, odd = spot >= 2, plane % 2 == 1
         from_outer = ((outer, 0, 0), (outer, rows, 0))
@@ -355,21 +366,27 @@
             ]
             for read in reads:
                 read.start()
+        edge = (spot == 0) | (spot == 3)
         for source, here in ((from_outer, right == odd), (from_inner, right != odd)):
-            start_if(
-                here,
-                tile_copies(source, meta[9], to_two, sems, 0)
-                + tile_copies(source, corner_ref[0], to_one, sems, 2),
-            )
+            start_if(here, tile_copies(source, meta[9], to_two, sems, 0))
+            start_if(here & edge, tile_copies(source, corner_ref[0], to_one, sems, 2))
+        zeros[...] = jnp.zeros_like(zeros)
+        start_if(jnp.logical_not(edge), zero_copies(zeros, to_one, sems, 2))
+        between = (plane == 1) | (plane == 2)
+        start_if(
+            jnp.logical_not(between),
+            zero_copies(zeros, to_outer, sems, 4) + zero_copies(zeros, to_inner, sems, 6),
+        )
         if not again:
             for read in reads:
                 read.wait()
             wants[0] = read_note(notes[0], jnp.where(plane == 1, 7, 3), tile_count)
             wants[1] = read_note(notes[1], jnp.where(plane == 1, 3, 7), tile_count)
-        copies = tile_copies(from_inner, wants[0], to_outer, sems, 4)
-        copies += tile_copies(from_outer, wants[1], to_inner, sems, 6)
-        for copy in copies:
-            copy.start()
+        start_if(
+            between,
+            tile_copies(from_inner, wants[0], to_outer, sems, 4)
+            + tile_copies(from_outer, wants[1], to_inner, sems, 6),
+        )
         for n, target in enumerate((to_two, to_one, to_outer, to_inner)):
             for copy in tile_copies(from_outer, 0, target, sems, 2 * n):
                 copy.wait()
@@ -384,7 +401,8 @@
         [SCALAR] * (not again) + [WHOLE] * 4,
         10,
         32 * TILE * width,
-        [] if again else [pltpu.VMEM((2, NOTE_ROWS, HD), jnp.bfloat16)],
+        ([] if again else [pltpu.VMEM((2, NOTE_ROWS, HD), jnp.bfloat16)])
+        + [pltpu.VMEM((TILE, width), jnp.bfloat16)],
     )
 
 
@@ -428,11 +446,10 @@
     every = range(frames)
     beside = [(i, i ^ 1) for i in every]
     across = [(i, i ^ 2) for i in every]
-    corner_in = [(i, i ^ 3) for i in every if i % 4 in (1, 2)]
-    corner_out = [(i, i ^ 3) for i in every if i % 4 in (0, 3)]
+    corner_in = [(i, i ^ 3 if i % 4 in (1, 2) else i) for i in every]
+    corner_out = [(i, i ^ 3 if i % 4 in (0, 3) else i) for i in every]
     outer = [(i, i ^ 4) for i in every]
-    inner = [(i, i ^ 12) for i in every if i // 4 in (1, 2)]
-    outward = [(i, i ^ 4) for i in every if i // 4 in (1, 2)]
+    inner = [(i, i ^ 12 if i // 4 in (1, 2) else i) for i in every]
 
     def right(meta):
         return meta[8] % 4 >= 2
@@ -475,10 +492,11 @@
     corner_tile, to_beside, to_corner = choose_near(meta, beside_list, corner_list, key_heads, value_heads)
     next_to = send(to_beside, beside)
     one_in = send(to_corner, corner_in)
-    begun = attend(queries, corner_tile, [own_frame()], 0, width // block, heads)
-    second = pack(key_heads, value_heads, first_width, width - first_width, [begun[0]])
-
-    after, wants = [over, next_to, one_in], None
+    second = pack(key_heads, value_heads, first_width, width - first_width, [to_beside])
+    near = [own_frame(), sent_tile([(next_to, 0)]), sent_tile([(over, 0)])]
+    begun = attend(queries, meta, near, 0, width // block, heads)
+
+    after, wants = [begun[0], one_in], None
     middles, finals = [], []
     for (at, steps), packed in zip(parts, (first, second)):
         from_outer = send(packed, outer)
@@ -488,13 +506,11 @@
             wants, *sent = sent
         two = send(sent[0], across)
         one = send(sent[1], corner_out)
-        far = [send(sent[2], outward), send(sent[3], inner)]
+        far = [send(sent[2], outer), send(sent[3], inner)]
         middle = attend(
             queries,
             meta,
             [
-                sent_tile([(next_to, at)]),
-                sent_tile([(over, at)]),
                 tile_of(from_outer, outer_tile),
                 tile_of(from_inner, inner_tile, inner_there),
             ],

time: 71.4 us -> 70.5 us (0.987); the launches traced: 70 us -> 70.2 us
  waiting for transfers between devices: 14 us -> 22.4 us
  starting transfers between devices: 30.7 us -> 22.7 us
    ppermute x18, waiting for transfers between devices: 14 us -> 22.4 us  [send(): return lax.ppermute(array, 'frame', route)]
    ppermute x18, starting transfers between devices: 30.7 us -> 22.7 us  [send(): return lax.ppermute(array, 'frame', route)]
  transfers between devices with their start and end apart: 18 -> 18, of which waited for: 8 -> 9; matrix products, arithmetic and copies ran while one was open for 0% -> 0% of each run, Pallas kernels for 29% -> 28%
where the time goes in v10:
time: 70.5 us; the launch traced here: 70.2 us
  Pallas kernels  24.7 us (35%)
  starting transfers between devices  22.7 us (32%)
  waiting for transfers between devices  22.4 us (32%)
    ppermute x18, starting transfers between devices, send(): return lax.ppermute(array, 'frame', route)  22.7 us
    ppermute x18, waiting for transfers between devices, send(): return lax.ppermute(array, 'frame', route)  22.4 us
    pallas_call x5, Pallas kernels, attend(): pl.pallas_call(functools.partial(attend_kernel, plan, heads, carry is not...  13.9 us
    pallas_call x5, Pallas kernels, move(): pl.pallas_call(build, name=name, out_shape=out_shape, in_specs=specs, out...  10.9 us
  transfers between devices with their start and end apart: 18, of which 9 were waited for; matrix products, arithmetic and copies ran while one was open for 0% of the time, Pallas kernels for 28%

profile of v10, /device:TPU:12, one launch (start us, length us, event | category | flops | bytes accessed | tf_op | source)
XLA Modules:
  0.0 70.2 jit_solution(17490463441089362180)
XLA Ops:
  0.0 1.5 %collective-permute-start = (s32[1,8]{1,0:T(1,128)}, s32[1,8]{1,0:T(1,128)S(1)}, u32[]{:S(2)}, u32[]{:S(2)}) collective-permute-start(s32[1,8]{1,0:T(1,128)} %list_hbm.1), channel_id=1, source_target_pairs={{0,2},{1,3},{2,0},{3,1},{4,6},{5,7},{6,4},{7,5},{8,10},{9,11},{10,... | collective-permute-start | bytes 104 | tf_op jit(solution)/shard_map/ppermute | solution.py:410
  1.5 2.2 %collective-permute-done.across_ref = s32[1,8]{1,0:T(1,128)S(1)} collective-permute-done((s32[1,8]{1,0:T(1,128)}, s32[1,8]{1,0:T(1,128)S(1)}, u32[]{:S(2)}, u32[]{:S(2)}) %collective-permute-start) | collective-permute-done | bytes 64 | tf_op jit(solution)/shard_map/ppermute | solution.py:410
  3.7 2.6 %begin.1 = (s32[10]{0:T(128)S(1)}, bf16[528,1024]{1,0:T(8,128)(2,1)S(1)}, bf16[256,1536]{1,0:T(8,128)(2,1)S(1)}) custom-call(s32[1]{0:T(128)} %bitcast.me_ref, s32[1,8]{1,0:T(1,128)S(1)} %collective-permute-done.across_ref, s32[1,8]{1,0:T(1,128)} %list_hbm.1, bf16[256,1536]{1,0:T(8,128)(2,1)} %k_ref.5, bf16[256,1536]{1,0:T(8,128)(2,1)} %v_ref.5), custom_call_target="tpu_custom_call" | custom-call | bytes 3670016 | tf_op jit(solution)/shard_map/begin/pallas_call | solution.py:163
  6.3 1.6 %collective-permute-start.6 = (bf16[256,1536]{1,0:T(8,128)(2,1)S(1)}, bf16[256,1536]{1,0:T(8,128)(2,1)S(1)}, u32[]{:S(2)}, u32[]{:S(2)}) collective-permute-start(bf16[256,1536]{1,0:T(8,128)(2,1)S(1)} %get-tuple-element.33), channel_id=1, source_target_pairs={{0,2},{1,3},{2,0},{3,1},{4,6},{5,7},{6,4},{7,5},{8,10},{9,11},{10,... | collective-permute-start | bytes 2359304 | tf_op jit(solution)/shard_map/ppermute | solution.py:410
  7.9 3.4 %collective-permute-start.4 = (bf16[528,1024]{1,0:T(8,128)(2,1)S(1)}, bf16[528,1024]{1,0:T(8,128)(2,1)S(1)}, u32[]{:S(2)}, u32[]{:S(2)}) collective-permute-start(bf16[528,1024]{1,0:T(8,128)(2,1)S(1)} %get-tuple-element.31), channel_id=1, source_target_pairs={{0,0},{1,1},{2,2},{3,3},{4,8},{5,9},{6,10},{7,11},{8,4},{9,5},{10,... | collective-permute-start | bytes 3244040 | tf_op jit(solution)/shard_map/ppermute | solution.py:410
  11.5 0.5 collective-permute-start.2
  12.0 0.6 collective-permute-done.1.beside_ref
  12.6 0.2 collective-permute-done.2.corner_ref
  12.8 2.2 %choose_near.1 = (s32[1]{0:T(128)}, bf16[256,1536]{1,0:T(8,128)(2,1)S(1)}, bf16[256,1536]{1,0:T(8,128)(2,1)S(1)}) custom-call(s32[10]{0:T(128)S(1)} %get-tuple-element.29.meta, s32[1,8]{1,0:T(1,128)S(1)} %collective-permute-done.1.beside_ref, s32[1,8]{1,0:T(1,128)S(1)} %collective-permute-done.2.corner_ref, bf16[256,1536]{1,0:T(8,128)(2,1)} %k_ref.5, ...), custom_call_target="tpu_custom_call" | custom-call | bytes 3145728 | tf_op jit(solution)/shard_map/choose_near/pallas_call | solution.py:163
  15.1 0.7 collective-permute-start.5
  15.8 0.8 %collective-permute-start.7 = (bf16[256,1536]{1,0:T(8,128)(2,1)S(1)}, bf16[256,1536]{1,0:T(8,128)(2,1)S(1)}, u32[]{:S(2)}, u32[]{:S(2)}) collective-permute-start(bf16[256,1536]{1,0:T(8,128)(2,1)S(1)} %get-tuple-element.35), channel_id=1, source_target_pairs={{0,0},{1,2},{2,1},{3,3},{4,4},{5,6},{6,5},{7,7},{8,8},{9,10},{10,9... | collective-permute-start | bytes 2359304 | tf_op jit(solution)/shard_map/ppermute | solution.py:410
  16.6 1.1 %pack.1 = bf16[512,512]{1,0:T(8,128)(2,1)S(1)} custom-call(bf16[256,1536]{1,0:T(8,128)(2,1)} %k_ref.5, bf16[256,1536]{1,0:T(8,128)(2,1)} %v_ref.5, bf16[256,1536]{1,0:T(8,128)(2,1)S(1)} %get-tuple-element.32.refs_0_), custom_call_target="tpu_custom_call" | custom-call | bytes 1048576 | tf_op jit(solution)/shard_map/pack/pallas_call | solution.py:163
  17.7 8.2 %collective-permute-done.6.refs_5_.refs_6_ = bf16[256,1536]{1,0:T(8,128)(2,1)S(1)} collective-permute-done((bf16[256,1536]{1,0:T(8,128)(2,1)S(1)}, bf16[256,1536]{1,0:T(8,128)(2,1)S(1)}, u32[]{:S(2)}, u32[]{:S(2)}) %collective-permute-start.6) | collective-permute-done | bytes 786464 | tf_op jit(solution)/shard_map/ppermute | solution.py:410
  25.9 3.4 %collective-permute-start.9 = (bf16[512,512]{1,0:T(8,128)(2,1)S(1)}, bf16[512,512]{1,0:T(8,128)(2,1)S(1)}, u32[]{:S(2)}, u32[]{:S(2)}) collective-permute-start(bf16[512,512]{1,0:T(8,128)(2,1)S(1)} %pack.1), channel_id=1, source_target_pairs={{0,0},{1,1},{2,2},{3,3},{4,8},{5,9},{6,10},{7,11},{8,4},{9,5},{10,... | collective-permute-start | bytes 1572872 | tf_op jit(solution)/shard_map/ppermute | solution.py:410
  29.5 4.1 %attend_own.1 = (f32[256,1536]{1,0:T(8,128)S(1)}, f32[256,1536]{1,0:T(8,128)S(1)}, f32[256,1536]{1,0:T(8,128)S(1)}) custom-call(s32[10]{0:T(128)S(1)} %get-tuple-element.29.meta, bf16[256,1536]{1,0:T(8,128)(2,1)S(1)} %copy-done, bf16[256,1536]{1,0:T(8,128)(2,1)S(1)} %copy-done.1, bf16[256,1536]{1,0:T(8,128)(2,1)S(1)} %copy-done.2, ...), custom_call_target="tpu_custom_call" | custom-call | flops 805306368 | bytes 3932160 | tf_op jit(solution)/shard_map/attend_own/pallas_call | solution.py:141
  33.6 3.0 %collective-permute-done.4.refs_1_.refs_3_.refs_4_ = bf16[528,1024]{1,0:T(8,128)(2,1)S(1)} collective-permute-done((bf16[528,1024]{1,0:T(8,128)(2,1)S(1)}, bf16[528,1024]{1,0:T(8,128)(2,1)S(1)}, u32[]{:S(2)}, u32[]{:S(2)}) %collective-permute-start.4) | collective-permute-done | bytes 1081376 | tf_op jit(solution)/shard_map/ppermute | solution.py:410
  36.6 1.6 %collective-permute-done.3.refs_0_.refs_1_.refs_2_ = bf16[528,1024]{1,0:T(8,128)(2,1)S(1)} collective-permute-done((bf16[528,1024]{1,0:T(8,128)(2,1)S(1)}, bf16[528,1024]{1,0:T(8,128)(2,1)S(1)}, u32[]{:S(2)}, u32[]{:S(2)}) %collective-permute-start.3) | collective-permute-done | bytes 1081376 | tf_op jit(solution)/shard_map/ppermute | solution.py:410
  38.2 2.2 %choose.1 = (s32[2]{0:T(128)S(1)}, bf16[256,1024]{1,0:T(8,128)(2,1)S(1)}, bf16[256,1024]{1,0:T(8,128)(2,1)S(1)}, bf16[256,1024]{1,0:T(8,128)(2,1)S(1)}, bf16[256,1024]{1,0:T(8,128)(2,1)S(1)}) custom-call(s32[10]{0:T(128)S(1)} %get-tuple-element.29.meta, s32[1]{0:T(128)} %get-tuple-element.30.corner_ref, ...), custom_call_target="tpu_custom_call" | custom-call | bytes 4194304 | tf_op jit(solution)/shard_map/choose/pallas_call | solution.py:163
  40.4 0.6 collective-permute-start.14
  41.0 1.9 %collective-permute-start.15 = (bf16[256,1024]{1,0:T(8,128)(2,1)S(1)}, bf16[256,1024]{1,0:T(8,128)(2,1)S(1)}, u32[]{:S(2)}, u32[]{:S(2)}) collective-permute-start(bf16[256,1024]{1,0:T(8,128)(2,1)S(1)} %get-tuple-element.48), channel_id=1, source_target_pairs={{0,3},{1,1},{2,2},{3,0},{4,7},{5,5},{6,6},{7,4},{8,11},{9,9},{10,1... | collective-permute-start | bytes 1572872 | tf_op jit(solution)/shard_map/ppermute | solution.py:410
  43.0 2.1 %collective-permute-done.9.refs_2_.refs_3_.refs_4_ = bf16[512,512]{1,0:T(8,128)(2,1)S(1)} collective-permute-done((bf16[512,512]{1,0:T(8,128)(2,1)S(1)}, bf16[512,512]{1,0:T(8,128)(2,1)S(1)}, u32[]{:S(2)}, u32[]{:S(2)}) %collective-permute-start.9) | collective-permute-done | bytes 524320 | tf_op jit(solution)/shard_map/ppermute | solution.py:410
  45.1 3.5 %collective-permute-start.17 = (bf16[256,1024]{1,0:T(8,128)(2,1)S(1)}, bf16[256,1024]{1,0:T(8,128)(2,1)S(1)}, u32[]{:S(2)}, u32[]{:S(2)}) collective-permute-start(bf16[256,1024]{1,0:T(8,128)(2,1)S(1)} %get-tuple-element.50), channel_id=1, source_target_pairs={{0,0},{1,1},{2,2},{3,3},{4,8},{5,9},{6,10},{7,11},{8,4},{9,5},{10,... | collective-permute-start | bytes 1572872 | tf_op jit(solution)/shard_map/ppermute | solution.py:410
  48.7 2.7 %attend_more.2 = (f32[256,1024]{1,0:T(8,128)S(1)}, f32[256,1024]{1,0:T(8,128)S(1)}, f32[256,1024]{1,0:T(8,128)S(1)}) custom-call(s32[10]{0:T(128)S(1)} %get-tuple-element.29.meta, bf16[256,1536]{1,0:T(8,128)(2,1)S(1)} %copy-done, bf16[528,1024]{1,0:T(8,128)(2,1)S(1)} %collective-permute-done.3.refs_0_.refs_1_.refs_2_, ...), custom_call_target="tpu_custom_call" | custom-call | flops 268435456 | bytes 1572864 | tf_op jit(solution)/shard_map/attend_more/pallas_call | solution.py:141
  51.4 2.7 %choose_again.1 = (bf16[256,512]{1,0:T(8,128)(2,1)S(1)}, bf16[256,512]{1,0:T(8,128)(2,1)S(1)}, bf16[256,512]{1,0:T(8,128)(2,1)S(1)}, bf16[256,512]{1,0:T(8,128)(2,1)S(1)}) custom-call(s32[10]{0:T(128)S(1)} %get-tuple-element.29.meta, s32[1]{0:T(128)} %get-tuple-element.30.corner_ref, s32[2]{0:T(128)S(1)} %get-tuple-element.36.refs_0_, ...), custom_call_target="tpu_custom_call" | custom-call | bytes 2097152 | tf_op jit(solution)/shard_map/choose_again/pallas_call | solution.py:163
  54.1 0.6 collective-permute-start.10
  54.7 1.9 %collective-permute-start.11 = (bf16[256,512]{1,0:T(8,128)(2,1)S(1)}, bf16[256,512]{1,0:T(8,128)(2,1)S(1)}, u32[]{:S(2)}, u32[]{:S(2)}) collective-permute-start(bf16[256,512]{1,0:T(8,128)(2,1)S(1)} %get-tuple-element.41), channel_id=1, source_target_pairs={{0,3},{1,1},{2,2},{3,0},{4,7},{5,5},{6,6},{7,4},{8,11},{9,9},{10,1... | collective-permute-start | bytes 786440 | tf_op jit(solution)/shard_map/ppermute | solution.py:410
  56.7 2.9 %collective-permute-done.16.refs_7_.refs_9_ = bf16[256,1024]{1,0:T(8,128)(2,1)S(1)} collective-permute-done((bf16[256,1024]{1,0:T(8,128)(2,1)S(1)}, bf16[256,1024]{1,0:T(8,128)(2,1)S(1)}, u32[]{:S(2)}, u32[]{:S(2)}) %collective-permute-start.16) | collective-permute-done | bytes 524320 | tf_op jit(solution)/shard_map/ppermute | solution.py:410
  59.7 1.9 %collective-permute-start.13 = (bf16[256,512]{1,0:T(8,128)(2,1)S(1)}, bf16[256,512]{1,0:T(8,128)(2,1)S(1)}, u32[]{:S(2)}, u32[]{:S(2)}) collective-permute-start(bf16[256,512]{1,0:T(8,128)(2,1)S(1)} %get-tuple-element.43), channel_id=1, source_target_pairs={{0,0},{1,1},{2,2},{3,3},{4,8},{5,9},{6,10},{7,11},{8,4},{9,5},{10,... | collective-permute-start | bytes 786440 | tf_op jit(solution)/shard_map/ppermute | solution.py:410
  61.6 1.2 %attend_more.3 = (f32[256,512]{1,0:T(8,128)S(1)}, f32[256,512]{1,0:T(8,128)S(1)}, f32[256,512]{1,0:T(8,128)S(1)}) custom-call(s32[10]{0:T(128)S(1)} %get-tuple-element.29.meta, bf16[256,1536]{1,0:T(8,128)(2,1)S(1)} %copy-done, bf16[512,512]{1,0:T(8,128)(2,1)S(1)} %collective-permute-done.8.refs_1_.refs_2_, ...), custom_call_target="tpu_custom_call" | custom-call | flops 134217728 | bytes 786432 | tf_op jit(solution)/shard_map/attend_more/pallas_call | solution.py:141
  62.8 3.5 %attend_last.2.refs_14_ = bf16[256,1536]{1,0:T(8,128)(2,1)} custom-call(s32[10]{0:T(128)S(1)} %get-tuple-element.29.meta, bf16[256,1536]{1,0:T(8,128)(2,1)S(1)} %copy-done, bf16[256,1024]{1,0:T(8,128)(2,1)S(1)} %collective-permute-done.14.refs_1_.refs_2_, bf16[256,1024]{1,0:T(8,128)(2,1)S(1)} %collective-permute-done.14.refs_1_.refs_2_, ...), custom_call_target="tpu_custom_call" | custom-call | flops 402653184 | bytes 2097152 | tf_op jit(solution)/shard_map/attend_last/pallas_call | solution.py:141
  66.4 1.5 %collective-permute-done.13.refs_8_.refs_10_ = bf16[256,512]{1,0:T(8,128)(2,1)S(1)} collective-permute-done((bf16[256,512]{1,0:T(8,128)(2,1)S(1)}, bf16[256,512]{1,0:T(8,128)(2,1)S(1)}, u32[]{:S(2)}, u32[]{:S(2)}) %collective-permute-start.13) | collective-permute-done | bytes 262176 | tf_op jit(solution)/shard_map/ppermute | solution.py:410
  67.9 2.3 %attend_last.3 = bf16[256,1536]{1,0:T(8,128)(2,1)} custom-call(s32[10]{0:T(128)S(1)} %get-tuple-element.29.meta, bf16[256,1536]{1,0:T(8,128)(2,1)S(1)} %copy-done, bf16[256,512]{1,0:T(8,128)(2,1)S(1)} %collective-permute-done.10.refs_1_.refs_2_, bf16[256,512]{1,0:T(8,128)(2,1)S(1)} %collective-permute-done.10.refs_1_.refs_2_, ...), custom_call_target="tpu_custom_call", output_to_operand_aliasing={{}: (15, {})} | custom-call | flops 201326592 | bytes 1048576 | tf_op jit(solution)/shard_map/attend_last/pallas_call | solution.py:141
  (22 shorter events, 0.4 us)
Async XLA Ops:
  0.0 11.4 %copy-start.3 = (s32[1,8]{1,0:T(1,128)S(1)}, s32[1,8]{1,0:T(1,128)}, u32[]{:S(2)}) copy-start(s32[1,8]{1,0:T(1,128)} %list_hbm.1) | copy-start | bytes 100
  0.0 3.7 %collective-permute-start = (s32[1,8]{1,0:T(1,128)}, s32[1,8]{1,0:T(1,128)S(1)}, u32[]{:S(2)}, u32[]{:S(2)}) collective-permute-start(s32[1,8]{1,0:T(1,128)} %list_hbm.1), channel_id=1, source_target_pairs={{0,2},{1,3},{2,0},{3,1},{4,6},{5,7},{6,4},{7,5},{8,10},{9,11},{10,... | collective-permute-start | bytes 104 | tf_op jit(solution)/shard_map/ppermute | solution.py:410
  6.3 19.6 %collective-permute-start.6 = (bf16[256,1536]{1,0:T(8,128)(2,1)S(1)}, bf16[256,1536]{1,0:T(8,128)(2,1)S(1)}, u32[]{:S(2)}, u32[]{:S(2)}) collective-permute-start(bf16[256,1536]{1,0:T(8,128)(2,1)S(1)} %get-tuple-element.33), channel_id=1, source_target_pairs={{0,2},{1,3},{2,0},{3,1},{4,6},{5,7},{6,4},{7,5},{8,10},{9,11},{10,... | collective-permute-start | bytes 2359304 | tf_op jit(solution)/shard_map/ppermute | solution.py:410
  7.9 28.7 %collective-permute-start.4 = (bf16[528,1024]{1,0:T(8,128)(2,1)S(1)}, bf16[528,1024]{1,0:T(8,128)(2,1)S(1)}, u32[]{:S(2)}, u32[]{:S(2)}) collective-permute-start(bf16[528,1024]{1,0:T(8,128)(2,1)S(1)} %get-tuple-element.31), channel_id=1, source_target_pairs={{0,0},{1,1},{2,2},{3,3},{4,8},{5,9},{6,10},{7,11},{8,4},{9,5},{10,... | collective-permute-start | bytes 3244040 | tf_op jit(solution)/shard_map/ppermute | solution.py:410
  11.3 26.9 %collective-permute-start.3 = (bf16[528,1024]{1,0:T(8,128)(2,1)S(1)}, bf16[528,1024]{1,0:T(8,128)(2,1)S(1)}, u32[]{:S(2)}, u32[]{:S(2)}) collective-permute-start(bf16[528,1024]{1,0:T(8,128)(2,1)S(1)} %get-tuple-element.31), channel_id=1, source_target_pairs={{0,4},{1,5},{2,6},{3,7},{4,0},{5,1},{6,2},{7,3},{8,12},{9,13},{10,... | collective-permute-start | bytes 3244040 | tf_op jit(solution)/shard_map/ppermute | solution.py:410
  11.4 1.2 %collective-permute-start.1 = (s32[1,8]{1,0:T(1,128)S(1)}, s32[1,8]{1,0:T(1,128)S(1)}, u32[]{:S(2)}, u32[]{:S(2)}) collective-permute-start(s32[1,8]{1,0:T(1,128)S(1)} %copy-done.3), channel_id=1, source_target_pairs={{0,1},{1,0},{2,3},{3,2},{4,5},{5,4},{6,7},{7,6},{8,9},{9,8},{10,11... | collective-permute-start | bytes 104 | tf_op jit(solution)/shard_map/ppermute | solution.py:410
  11.5 1.3 %collective-permute-start.2 = (s32[1,8]{1,0:T(1,128)S(1)}, s32[1,8]{1,0:T(1,128)S(1)}, u32[]{:S(2)}, u32[]{:S(2)}) collective-permute-start(s32[1,8]{1,0:T(1,128)S(1)} %collective-permute-done.across_ref), channel_id=1, source_target_pairs={{0,1},{1,0},{2,3},{3,2},{4,5},{5,4},{6,7},{7,6},{8,9},{9,8},{10,11... | collective-permute-start | bytes 104 | tf_op jit(solution)/shard_map/ppermute | solution.py:410
  15.1 14.4 %copy-start = (bf16[256,1536]{1,0:T(8,128)(2,1)S(1)}, bf16[256,1536]{1,0:T(8,128)(2,1)}, u32[]{:S(2)}) copy-start(bf16[256,1536]{1,0:T(8,128)(2,1)} %refs_0_.9) | copy-start | bytes 2359300
  15.1 14.4 %copy-start.1 = (bf16[256,1536]{1,0:T(8,128)(2,1)S(1)}, bf16[256,1536]{1,0:T(8,128)(2,1)}, u32[]{:S(2)}) copy-start(bf16[256,1536]{1,0:T(8,128)(2,1)} %k_ref.5) | copy-start | bytes 2359300
  15.1 14.4 %copy-start.2 = (bf16[256,1536]{1,0:T(8,128)(2,1)S(1)}, bf16[256,1536]{1,0:T(8,128)(2,1)}, u32[]{:S(2)}) copy-start(bf16[256,1536]{1,0:T(8,128)(2,1)} %v_ref.5) | copy-start | bytes 2359300
  15.1 14.2 %collective-permute-start.5 = (bf16[256,1536]{1,0:T(8,128)(2,1)S(1)}, bf16[256,1536]{1,0:T(8,128)(2,1)S(1)}, u32[]{:S(2)}, u32[]{:S(2)}) collective-permute-start(bf16[256,1536]{1,0:T(8,128)(2,1)S(1)} %get-tuple-element.32.refs_0_), channel_id=1, source_target_pairs={{0,1},{1,0},{2,3},{3,2},{4,5},{5,4},{6,7},{7,6},{8,9},{9,8},{10,11... | collective-permute-start | bytes 2359304 | tf_op jit(solution)/shard_map/ppermute | solution.py:410
  15.8 17.8 %collective-permute-start.7 = (bf16[256,1536]{1,0:T(8,128)(2,1)S(1)}, bf16[256,1536]{1,0:T(8,128)(2,1)S(1)}, u32[]{:S(2)}, u32[]{:S(2)}) collective-permute-start(bf16[256,1536]{1,0:T(8,128)(2,1)S(1)} %get-tuple-element.35), channel_id=1, source_target_pairs={{0,0},{1,2},{2,1},{3,3},{4,4},{5,6},{6,5},{7,7},{8,8},{9,10},{10,9... | collective-permute-start | bytes 2359304 | tf_op jit(solution)/shard_map/ppermute | solution.py:410
  25.9 19.3 %collective-permute-start.9 = (bf16[512,512]{1,0:T(8,128)(2,1)S(1)}, bf16[512,512]{1,0:T(8,128)(2,1)S(1)}, u32[]{:S(2)}, u32[]{:S(2)}) collective-permute-start(bf16[512,512]{1,0:T(8,128)(2,1)S(1)} %pack.1), channel_id=1, source_target_pairs={{0,0},{1,1},{2,2},{3,3},{4,8},{5,9},{6,10},{7,11},{8,4},{9,5},{10,... | collective-permute-start | bytes 1572872 | tf_op jit(solution)/shard_map/ppermute | solution.py:410
  29.3 22.1 %collective-permute-start.8 = (bf16[512,512]{1,0:T(8,128)(2,1)S(1)}, bf16[512,512]{1,0:T(8,128)(2,1)S(1)}, u32[]{:S(2)}, u32[]{:S(2)}) collective-permute-start(bf16[512,512]{1,0:T(8,128)(2,1)S(1)} %pack.1), channel_id=1, source_target_pairs={{0,4},{1,5},{2,6},{3,7},{4,0},{5,1},{6,2},{7,3},{8,12},{9,13},{10,... | collective-permute-start | bytes 1572872 | tf_op jit(solution)/shard_map/ppermute | solution.py:410
  40.4 14.3 %collective-permute-start.14 = (bf16[256,1024]{1,0:T(8,128)(2,1)S(1)}, bf16[256,1024]{1,0:T(8,128)(2,1)S(1)}, u32[]{:S(2)}, u32[]{:S(2)}) collective-permute-start(bf16[256,1024]{1,0:T(8,128)(2,1)S(1)} %get-tuple-element.47), channel_id=1, source_target_pairs={{0,2},{1,3},{2,0},{3,1},{4,6},{5,7},{6,4},{7,5},{8,10},{9,11},{10,... | collective-permute-start | bytes 1572872 | tf_op jit(solution)/shard_map/ppermute | solution.py:410
  41.0 15.6 %collective-permute-start.15 = (bf16[256,1024]{1,0:T(8,128)(2,1)S(1)}, bf16[256,1024]{1,0:T(8,128)(2,1)S(1)}, u32[]{:S(2)}, u32[]{:S(2)}) collective-permute-start(bf16[256,1024]{1,0:T(8,128)(2,1)S(1)} %get-tuple-element.48), channel_id=1, source_target_pairs={{0,3},{1,1},{2,2},{3,0},{4,7},{5,5},{6,6},{7,4},{8,11},{9,9},{10,1... | collective-permute-start | bytes 1572872 | tf_op jit(solution)/shard_map/ppermute | solution.py:410
  43.0 16.7 %collective-permute-start.16 = (bf16[256,1024]{1,0:T(8,128)(2,1)S(1)}, bf16[256,1024]{1,0:T(8,128)(2,1)S(1)}, u32[]{:S(2)}, u32[]{:S(2)}) collective-permute-start(bf16[256,1024]{1,0:T(8,128)(2,1)S(1)} %get-tuple-element.49), channel_id=1, source_target_pairs={{0,4},{1,5},{2,6},{3,7},{4,0},{5,1},{6,2},{7,3},{8,12},{9,13},{10,... | collective-permute-start | bytes 1572872 | tf_op jit(solution)/shard_map/ppermute | solution.py:410
  45.1 17.7 %collective-permute-start.17 = (bf16[256,1024]{1,0:T(8,128)(2,1)S(1)}, bf16[256,1024]{1,0:T(8,128)(2,1)S(1)}, u32[]{:S(2)}, u32[]{:S(2)}) collective-permute-start(bf16[256,1024]{1,0:T(8,128)(2,1)S(1)} %get-tuple-element.50), channel_id=1, source_target_pairs={{0,0},{1,1},{2,2},{3,3},{4,8},{5,9},{6,10},{7,11},{8,4},{9,5},{10,... | collective-permute-start | bytes 1572872 | tf_op jit(solution)/shard_map/ppermute | solution.py:410
  54.1 12.3 %collective-permute-start.10 = (bf16[256,512]{1,0:T(8,128)(2,1)S(1)}, bf16[256,512]{1,0:T(8,128)(2,1)S(1)}, u32[]{:S(2)}, u32[]{:S(2)}) collective-permute-start(bf16[256,512]{1,0:T(8,128)(2,1)S(1)} %get-tuple-element.40), channel_id=1, source_target_pairs={{0,2},{1,3},{2,0},{3,1},{4,6},{5,7},{6,4},{7,5},{8,10},{9,11},{10,... | collective-permute-start | bytes 786440 | tf_op jit(solution)/shard_map/ppermute | solution.py:410
  54.7 11.7 %collective-permute-start.11 = (bf16[256,512]{1,0:T(8,128)(2,1)S(1)}, bf16[256,512]{1,0:T(8,128)(2,1)S(1)}, u32[]{:S(2)}, u32[]{:S(2)}) collective-permute-start(bf16[256,512]{1,0:T(8,128)(2,1)S(1)} %get-tuple-element.41), channel_id=1, source_target_pairs={{0,3},{1,1},{2,2},{3,0},{4,7},{5,5},{6,6},{7,4},{8,11},{9,9},{10,1... | collective-permute-start | bytes 786440 | tf_op jit(solution)/shard_map/ppermute | solution.py:410
  56.7 9.7 %collective-permute-start.12 = (bf16[256,512]{1,0:T(8,128)(2,1)S(1)}, bf16[256,512]{1,0:T(8,128)(2,1)S(1)}, u32[]{:S(2)}, u32[]{:S(2)}) collective-permute-start(bf16[256,512]{1,0:T(8,128)(2,1)S(1)} %get-tuple-element.42), channel_id=1, source_target_pairs={{0,4},{1,5},{2,6},{3,7},{4,0},{5,1},{6,2},{7,3},{8,12},{9,13},{10,... | collective-permute-start | bytes 786440 | tf_op jit(solution)/shard_map/ppermute | solution.py:410
  59.7 8.3 %collective-permute-start.13 = (bf16[256,512]{1,0:T(8,128)(2,1)S(1)}, bf16[256,512]{1,0:T(8,128)(2,1)S(1)}, u32[]{:S(2)}, u32[]{:S(2)}) collective-permute-start(bf16[256,512]{1,0:T(8,128)(2,1)S(1)} %get-tuple-element.43), channel_id=1, source_target_pairs={{0,0},{1,1},{2,2},{3,3},{4,8},{5,9},{6,10},{7,11},{8,4},{9,5},{10,... | collective-permute-start | bytes 786440 | tf_op jit(solution)/shard_map/ppermute | solution.py:410

commit v11 on v10

--- a/solution.py
+++ b/solution.py
@@ -274,11 +274,12 @@
     )
 
 
-def choose_near(meta, beside_list, corner_list, keys, values):
+def choose_near(meta, beside_list, corner_list, keys, values, after):
     rows, width = keys.shape
     tile_count = rows // TILE
 
-    def build(meta, beside_ref, corner_ref, k_ref, v_ref, wanted, to_beside, to_corner, zeros, sems):
+    def build(meta, beside_ref, corner_ref, k_ref, v_ref, *refs):
+        wanted, to_beside, to_corner, zeros, sems = refs[-5:]
         even = meta[8] % 2 == 0
         own = ((k_ref, 0, 0), (v_ref, 0, 0))
         copies = tile_copies(own, tile_at(beside_ref, jnp.where(even, 0, 4), tile_count), to_beside, sems, 0)
@@ -297,8 +298,8 @@
     return move(
         "choose_near",
         build,
-        (meta, beside_list, corner_list, in_hbm(keys), in_hbm(values)),
-        [SCALAR] * 3 + [WHOLE] * 2,
+        (meta, beside_list, corner_list, in_hbm(keys), in_hbm(values), *after),
+        [SCALAR] * 3 + [WHOLE] * (2 + len(after)),
         [jax.ShapeDtypeStruct((1,), jnp.int32), tile, tile],
         [SCALAR, WHOLE, WHOLE],
         4,
@@ -340,69 +341,94 @@
     )
 
 
-def choose(meta, corner_tile, wants, outer, inner, after):
-    rows, width = outer.shape[0] // 2 // TILE * TILE, outer.shape[1]
-    tile_count = rows // TILE
-    again = wants is not None
-
-    def build(meta, corner_ref, *refs):
-        if again:
-            wants, outer, inner = refs[:3]
-            to_two, to_one, to_outer, to_inner = refs[-6:-2]
-        else:
-            outer, inner, wants = refs[:2] + refs[-8:-7]
-            to_two, to_one, to_outer, to_inner, notes = refs[-7:-2]
-        zeros, sems = refs[-2:]
+def halves_of(ref):
+    rows = ref.shape[0] // 2 // TILE * TILE
+    return (ref, 0, 0), (ref, rows, 0)
+
+
+def start_far(plane, wants, outer, inner, to_outer, to_inner, zeros, sems, at):
+    between = (plane == 1) | (plane == 2)
+    start_if(
+        between,
+        tile_copies(halves_of(inner), wants[0], to_outer, sems, at)
+        + tile_copies(halves_of(outer), wants[1], to_inner, sems, at + 2),
+    )
+    start_if(
+        jnp.logical_not(between),
+        zero_copies(zeros, to_outer, sems, at) + zero_copies(zeros, to_inner, sems, at + 2),
+    )
+
+
+def choose(meta, corner_tile, outer, inner, after, wants=None):
+    width = outer.shape[1]
+    count = 2 if wants is None else 4
+
+    def build(meta, corner_ref, outer, inner, *refs):
+        targets, zeros, sems = refs[-count - 2 : -2], refs[-2], refs[-1]
         spot, plane = meta[8] % 4, meta[8] // 4
         right, odd = spot >= 2, plane % 2 == 1
-        from_outer = ((outer, 0, 0), (outer, rows, 0))
-        from_inner = ((inner, 0, 0), (inner, rows, 0))
-        if not again:
-            reads = [
-                pltpu.make_async_copy(
-                    ref.at[pl.ds(2 * rows, NOTE_ROWS), pl.ds(0, HD)], notes.at[n], sems.at[8 + n]
-                )
-                for n, ref in enumerate((outer, inner))
-            ]
-            for read in reads:
-                read.start()
         edge = (spot == 0) | (spot == 3)
-        for source, here in ((from_outer, right == odd), (from_inner, right != odd)):
-            start_if(here, tile_copies(source, meta[9], to_two, sems, 0))
-            start_if(here & edge, tile_copies(source, corner_ref[0], to_one, sems, 2))
+        for source, here in ((outer, right == odd), (inner, right != odd)):
+            start_if(here, tile_copies(halves_of(source), meta[9], targets[0], sems, 0))
+            start_if(here & edge, tile_copies(halves_of(source), corner_ref[0], targets[1], sems, 2))
         zeros[...] = jnp.zeros_like(zeros)
-        start_if(jnp.logical_not(edge), zero_copies(zeros, to_one, sems, 2))
-        between = (plane == 1) | (plane == 2)
-        start_if(
-            jnp.logical_not(between),
-            zero_copies(zeros, to_outer, sems, 4) + zero_copies(zeros, to_inner, sems, 6),
-        )
-        if not again:
-            for read in reads:
-                read.wait()
-            wants[0] = read_note(notes[0], jnp.where(plane == 1, 7, 3), tile_count)
-            wants[1] = read_note(notes[1], jnp.where(plane == 1, 3, 7), tile_count)
-        start_if(
-            between,
-            tile_copies(from_inner, wants[0], to_outer, sems, 4)
-            + tile_copies(from_outer, wants[1], to_inner, sems, 6),
-        )
-        for n, target in enumerate((to_two, to_one, to_outer, to_inner)):
-            for copy in tile_copies(from_outer, 0, target, sems, 2 * n):
+        start_if(jnp.logical_not(edge), zero_copies(zeros, targets[1], sems, 2))
+        if count == 4:
+            start_far(plane, refs[0], outer, inner, *targets[2:], zeros, sems, 4)
+        for n, target in enumerate(targets):
+            for copy in zero_copies(zeros, target, sems, 2 * n):
                 copy.wait()
 
-    sent = [jax.ShapeDtypeStruct((2 * TILE, width), jnp.bfloat16)] * 4
+    extra = [] if wants is None else [wants]
     return move(
-        "choose_again" if again else "choose",
+        "choose",
         build,
-        (meta, corner_tile, *([wants] if again else []), outer, inner, *after),
-        [SCALAR] * (2 + again) + [WHOLE] * (2 + len(after)),
-        ([] if again else [jax.ShapeDtypeStruct((2,), jnp.int32)]) + sent,
-        [SCALAR] * (not again) + [WHOLE] * 4,
-        10,
-        32 * TILE * width,
-        ([] if again else [pltpu.VMEM((2, NOTE_ROWS, HD), jnp.bfloat16)])
-        + [pltpu.VMEM((TILE, width), jnp.bfloat16)],
+        (meta, corner_tile, outer, inner, *extra, *after),
+        [SCALAR] * 2 + [WHOLE] * 2 + [SCALAR] * len(extra) + [WHOLE] * len(after),
+        [jax.ShapeDtypeStruct((2 * TILE, width), jnp.bfloat16)] * count,
+        [WHOLE] * count,
+        2 * count,
+        8 * count * TILE * width,
+        [pltpu.VMEM((TILE, width), jnp.bfloat16)],
+    )
+
+
+def choose_far(meta, outer, inner, after):
+    width = outer.shape[1]
+    rows = outer.shape[0] - NOTE_ROWS
+    tile_count = rows // 2 // TILE
+
+    def build(meta, outer, inner, *refs):
+        wants, to_outer, to_inner, zeros, notes, sems = refs[-6:]
+        reads = [
+            pltpu.make_async_copy(
+                ref.at[pl.ds(rows, NOTE_ROWS), pl.ds(0, HD)], notes.at[n], sems.at[4 + n]
+            )
+            for n, ref in enumerate((outer, inner))
+        ]
+        for read in reads:
+            read.start()
+        plane = meta[8] // 4
+        zeros[...] = jnp.zeros_like(zeros)
+        for read in reads:
+            read.wait()
+        wants[0] = read_note(notes[0], jnp.where(plane == 1, 7, 3), tile_count)
+        wants[1] = read_note(notes[1], jnp.where(plane == 1, 3, 7), tile_count)
+        start_far(plane, wants, outer, inner, to_outer, to_inner, zeros, sems, 0)
+        for copy in zero_copies(zeros, to_outer, sems, 0) + zero_copies(zeros, to_inner, sems, 2):
+            copy.wait()
+
+    sent = [jax.ShapeDtypeStruct((2 * TILE, width), jnp.bfloat16)] * 2
+    return move(
+        "choose_far",
+        build,
+        (meta, outer, inner, *after),
+        [SCALAR] + [WHOLE] * (2 + len(after)),
+        [jax.ShapeDtypeStruct((2,), jnp.int32)] + sent,
+        [SCALAR] + [WHOLE] * 2,
+        6,
+        16 * TILE * width,
+        [pltpu.VMEM((TILE, width), jnp.bfloat16), pltpu.VMEM((2, NOTE_ROWS, HD), jnp.bfloat16)],
     )
 
 
@@ -440,9 +466,9 @@
     frames = 16
     rows, width = key_heads.shape
     tile_count = rows // TILE
-    heads = 4
+    heads = 3
     block = heads * HD
-    parts = ((0, 2), (2, 1))
+    parts = ((0, 2), (2, 2))
     every = range(frames)
     beside = [(i, i ^ 1) for i in every]
     across = [(i, i ^ 2) for i in every]
@@ -489,37 +515,32 @@
     first_width = parts[0][1] * block
     meta, first, to_across = begin(tile_lists, me, across_list, key_heads, value_heads, first_width)
     over = send(to_across, across)
-    corner_tile, to_beside, to_corner = choose_near(meta, beside_list, corner_list, key_heads, value_heads)
+    begun = attend(queries, meta, [own_frame()], 0, width // block, heads)
+    second = pack(key_heads, value_heads, first_width, width - first_width, [begun[0]])
+    corner_tile, to_beside, to_corner = choose_near(
+        meta, beside_list, corner_list, key_heads, value_heads, [over, second]
+    )
     next_to = send(to_beside, beside)
     one_in = send(to_corner, corner_in)
-    second = pack(key_heads, value_heads, first_width, width - first_width, [to_beside])
-    near = [own_frame(), sent_tile([(next_to, 0)]), sent_tile([(over, 0)])]
-    begun = attend(queries, meta, near, 0, width // block, heads)
-
-    after, wants = [begun[0], one_in], None
+
+    after, wants = [], None
     middles, finals = [], []
     for (at, steps), packed in zip(parts, (first, second)):
         from_outer = send(packed, outer)
         from_inner = send(packed, inner)
-        sent = choose(meta, corner_tile, wants, from_outer, from_inner, after)
+        to_two, to_one, *to_far = choose(meta, corner_tile, from_outer, from_inner, after, wants)
+        z_tiles = [
+            tile_of(from_outer, outer_tile),
+            tile_of(from_inner, inner_tile, inner_there),
+            sent_tile([(over, at)]),
+            sent_tile([(next_to, at)]),
+        ]
+        two = send(to_two, across)
+        one = send(to_one, corner_out)
+        middle = attend(queries, meta, z_tiles, at, steps, heads, begun, held=at)
         if wants is None:
-            wants, *sent = sent
-        two = send(sent[0], across)
-        one = send(sent[1], corner_out)
-        far = [send(sent[2], outer), send(sent[3], inner)]
-        middle = attend(
-            queries,
-            meta,
-            [
-                tile_of(from_outer, outer_tile),
-                tile_of(from_inner, inner_tile, inner_there),
-            ],
-            at,
-            steps,
-            heads,
-            begun,
-            held=at,
-        )
+            wants, *to_far = choose_far(meta, from_outer, from_inner, [middle[0], one_in])
+        far = [send(to_far[0], outer), send(to_far[1], inner)]
         after = [middle[0]]
         middles.append(middle)
         finals.append(

time: 70.5 us -> 74.3 us (1.054)
  waiting for transfers between devices: 22.4 us -> 10.2 us
  starting transfers between devices: 22.7 us -> 32.5 us
  Pallas kernels: 24.7 us -> 29.9 us
  local copies, waits for them, and re-layouts: 0.02 us -> 1.14 us
    ppermute x18, waiting for transfers between devices: 22.4 us -> 10.2 us  [send(): return lax.ppermute(array, 'frame', route)]
    ppermute x18, starting transfers between devices: 22.7 us -> 32.5 us  [send(): return lax.ppermute(array, 'frame', route)]
    pallas_call x5 -> x6, Pallas kernels: 10.9 us -> 14.2 us  [move(): pl.pallas_call(build, name=name, out_shape=out_shape, in_specs=specs, out...]
    pallas_call x5, Pallas kernels: 13.9 us -> 15.7 us  [attend(): pl.pallas_call(functools.partial(attend_kernel, plan, heads, carry is not...]
    unnamed x8, local copies, waits for them, and re-layouts: 0.02 us -> 1.14 us
  transfers between devices with their start and end apart: 18 -> 18, of which waited for: 9 -> 4; matrix products, arithmetic and copies ran while one was open for 0% -> 0% of each run, Pallas kernels for 28% -> 33%
where the time goes in v11:
time: 74.3 us; the launch traced here: 73.9 us
  starting transfers between devices  32.5 us (44%)
  Pallas kernels  29.9 us (40%)
  waiting for transfers between devices  10.2 us (14%)
  local copies, waits for them, and re-layouts  1.14 us (2%)
    ppermute x18, starting transfers between devices, send(): return lax.ppermute(array, 'frame', route)  32.5 us
    pallas_call x5, Pallas kernels, attend(): pl.pallas_call(functools.partial(attend_kernel, plan, heads, carry is not...  15.7 us
    pallas_call x6, Pallas kernels, move(): pl.pallas_call(build, name=name, out_shape=out_shape, in_specs=specs, out...  14.2 us
    ppermute x18, waiting for transfers between devices, send(): return lax.ppermute(array, 'frame', route)  10.2 us
  transfers between devices with their start and end apart: 18, of which 4 were waited for; matrix products, arithmetic and copies ran while one was open for 0% of the time, Pallas kernels for 33%

profile of v11, /device:TPU:12, one launch (start us, length us, event | category | flops | bytes accessed | tf_op | source)
XLA Modules:
  0.0 73.9 jit_solution(9757436210178309135)
XLA Ops:
  0.0 1.6 %collective-permute-start = (s32[1,8]{1,0:T(1,128)}, s32[1,8]{1,0:T(1,128)S(1)}, u32[]{:S(2)}, u32[]{:S(2)}) collective-permute-start(s32[1,8]{1,0:T(1,128)} %list_hbm.1), channel_id=1, source_target_pairs={{0,2},{1,3},{2,0},{3,1},{4,6},{5,7},{6,4},{7,5},{8,10},{9,11},{10,... | collective-permute-start | bytes 104 | tf_op jit(solution)/shard_map/ppermute | solution.py:436
  1.6 2.2 %collective-permute-done.across_ref = s32[1,8]{1,0:T(1,128)S(1)} collective-permute-done((s32[1,8]{1,0:T(1,128)}, s32[1,8]{1,0:T(1,128)S(1)}, u32[]{:S(2)}, u32[]{:S(2)}) %collective-permute-start) | collective-permute-done | bytes 64 | tf_op jit(solution)/shard_map/ppermute | solution.py:436
  3.8 2.5 %begin.1 = (s32[10]{0:T(128)S(1)}, bf16[528,768]{1,0:T(8,128)(2,1)S(1)}, bf16[256,1536]{1,0:T(8,128)(2,1)S(1)}) custom-call(s32[1]{0:T(128)} %bitcast.me_ref, s32[1,8]{1,0:T(1,128)S(1)} %collective-permute-done.across_ref, s32[1,8]{1,0:T(1,128)} %list_hbm.1, bf16[256,1536]{1,0:T(8,128)(2,1)} %k_ref.5, bf16[256,1536]{1,0:T(8,128)(2,1)} %v_ref.5), custom_call_target="tpu_custom_call" | custom-call | bytes 3145728 | tf_op jit(solution)/shard_map/begin/pallas_call | solution.py:163
  6.3 1.6 %collective-permute-start.3 = (bf16[256,1536]{1,0:T(8,128)(2,1)S(1)}, bf16[256,1536]{1,0:T(8,128)(2,1)S(1)}, u32[]{:S(2)}, u32[]{:S(2)}) collective-permute-start(bf16[256,1536]{1,0:T(8,128)(2,1)S(1)} %get-tuple-element.30), channel_id=1, source_target_pairs={{0,2},{1,3},{2,0},{3,1},{4,6},{5,7},{6,4},{7,5},{8,10},{9,11},{10,... | collective-permute-start | bytes 2359304 | tf_op jit(solution)/shard_map/ppermute | solution.py:436
  7.9 0.4 collective-permute-start.6
  8.3 4.6 %collective-permute-start.7 = (bf16[528,768]{1,0:T(8,128)(2,1)S(1)}, bf16[528,768]{1,0:T(8,128)(2,1)S(1)}, u32[]{:S(2)}, u32[]{:S(2)}) collective-permute-start(bf16[528,768]{1,0:T(8,128)(2,1)S(1)} %get-tuple-element.33), channel_id=1, source_target_pairs={{0,0},{1,1},{2,2},{3,3},{4,8},{5,9},{6,10},{7,11},{8,4},{9,5},{10,... | collective-permute-start | bytes 2433032 | tf_op jit(solution)/shard_map/ppermute | solution.py:436
  13.0 1.1 %copy-done.2 = bf16[256,1536]{1,0:T(8,128)(2,1)S(1)} copy-done((bf16[256,1536]{1,0:T(8,128)(2,1)S(1)}, bf16[256,1536]{1,0:T(8,128)(2,1)}, u32[]{:S(2)}) %copy-start.2) | copy-done | bytes 786456
  14.1 3.2 %attend_own.1 = (f32[256,1536]{1,0:T(8,128)S(1)}, f32[256,1536]{1,0:T(8,128)S(1)}, f32[256,1536]{1,0:T(8,128)S(1)}) custom-call(s32[10]{0:T(128)S(1)} %get-tuple-element.29.meta, bf16[256,1536]{1,0:T(8,128)(2,1)S(1)} %copy-done, bf16[256,1536]{1,0:T(8,128)(2,1)S(1)} %copy-done.1, bf16[256,1536]{1,0:T(8,128)(2,1)S(1)} %copy-done.2), custom_call_target="tpu_custom_call" | custom-call | flops 402653184 | bytes 2359296 | tf_op jit(solution)/shard_map/attend_own/pallas_call | solution.py:141
  17.3 1.4 %pack.1.refs_1_ = bf16[512,768]{1,0:T(8,128)(2,1)S(1)} custom-call(bf16[256,1536]{1,0:T(8,128)(2,1)} %k_ref.5, bf16[256,1536]{1,0:T(8,128)(2,1)} %v_ref.5, f32[256,1536]{1,0:T(8,128)S(1)} %get-tuple-element.31.refs_0_.refs_9_), custom_call_target="tpu_custom_call" | custom-call | bytes 1572864 | tf_op jit(solution)/shard_map/pack/pallas_call | solution.py:163
  18.7 0.3 collective-permute-start.2
  19.0 0.9 %collective-permute-done.2.corner_ref = s32[1,8]{1,0:T(1,128)S(1)} collective-permute-done((s32[1,8]{1,0:T(1,128)S(1)}, s32[1,8]{1,0:T(1,128)S(1)}, u32[]{:S(2)}, u32[]{:S(2)}) %collective-permute-start.2) | collective-permute-done | bytes 64 | tf_op jit(solution)/shard_map/ppermute | solution.py:436
  19.9 4.6 %collective-permute-done.3.refs_0_.refs_5_.refs_6_ = bf16[256,1536]{1,0:T(8,128)(2,1)S(1)} collective-permute-done((bf16[256,1536]{1,0:T(8,128)(2,1)S(1)}, bf16[256,1536]{1,0:T(8,128)(2,1)S(1)}, u32[]{:S(2)}, u32[]{:S(2)}) %collective-permute-start.3) | collective-permute-done | bytes 786464 | tf_op jit(solution)/shard_map/ppermute | solution.py:436
  24.5 2.2 %choose_near.1 = (s32[1]{0:T(128)}, bf16[256,1536]{1,0:T(8,128)(2,1)S(1)}, bf16[256,1536]{1,0:T(8,128)(2,1)S(1)}) custom-call(s32[10]{0:T(128)S(1)} %get-tuple-element.29.meta, s32[1,8]{1,0:T(1,128)S(1)} %collective-permute-done.1.beside_ref, s32[1,8]{1,0:T(1,128)S(1)} %collective-permute-done.2.corner_ref, bf16[256,1536]{1,0:T(8,128)(2,1)} %k_ref.5, ...), custom_call_target="tpu_custom_call" | custom-call | bytes 3145728 | tf_op jit(solution)/shard_map/choose_near/pallas_call | solution.py:163
  26.8 0.7 collective-permute-start.9
  27.5 0.5 collective-permute-start.4
  28.1 4.6 %collective-permute-start.5 = (bf16[512,768]{1,0:T(8,128)(2,1)S(1)}, bf16[512,768]{1,0:T(8,128)(2,1)S(1)}, u32[]{:S(2)}, u32[]{:S(2)}) collective-permute-start(bf16[512,768]{1,0:T(8,128)(2,1)S(1)} %pack.1.refs_1_), channel_id=1, source_target_pairs={{0,0},{1,1},{2,2},{3,3},{4,8},{5,9},{6,10},{7,11},{8,4},{9,5},{10,... | collective-permute-start | bytes 2359304 | tf_op jit(solution)/shard_map/ppermute | solution.py:436
  32.7 2.3 %choose.3 = (bf16[256,768]{1,0:T(8,128)(2,1)S(1)}, bf16[256,768]{1,0:T(8,128)(2,1)S(1)}) custom-call(s32[10]{0:T(128)S(1)} %get-tuple-element.29.meta, s32[1]{0:T(128)} %get-tuple-element.32.corner_ref, bf16[528,768]{1,0:T(8,128)(2,1)S(1)} %collective-permute-done.6.refs_1_.refs_2_.outer, bf16[528,768]{1,0:T(8,128)(2,1)S(1)} %collective-permute-done.7.refs_3_.refs_4_.inner), custom_call_target="tpu_custom_call" | custom-call | bytes 1572864 | tf_op jit(solution)/shard_map/choose/pallas_call | solution.py:163
  35.0 3.4 %collective-permute-start.14 = (bf16[256,768]{1,0:T(8,128)(2,1)S(1)}, bf16[256,768]{1,0:T(8,128)(2,1)S(1)}, u32[]{:S(2)}, u32[]{:S(2)}) collective-permute-start(bf16[256,768]{1,0:T(8,128)(2,1)S(1)} %get-tuple-element.47), channel_id=1, source_target_pairs={{0,2},{1,3},{2,0},{3,1},{4,6},{5,7},{6,4},{7,5},{8,10},{9,11},{10,... | collective-permute-start | bytes 1179656 | tf_op jit(solution)/shard_map/ppermute | solution.py:436
  38.4 2.5 %collective-permute-start.15 = (bf16[256,768]{1,0:T(8,128)(2,1)S(1)}, bf16[256,768]{1,0:T(8,128)(2,1)S(1)}, u32[]{:S(2)}, u32[]{:S(2)}) collective-permute-start(bf16[256,768]{1,0:T(8,128)(2,1)S(1)} %get-tuple-element.48), channel_id=1, source_target_pairs={{0,3},{1,1},{2,2},{3,0},{4,7},{5,5},{6,6},{7,4},{8,11},{9,9},{10,1... | collective-permute-start | bytes 1179656 | tf_op jit(solution)/shard_map/ppermute | solution.py:436
  40.8 3.1 %attend_more.2 = (f32[256,768]{1,0:T(8,128)S(1)}, f32[256,768]{1,0:T(8,128)S(1)}, f32[256,768]{1,0:T(8,128)S(1)}) custom-call(s32[10]{0:T(128)S(1)} %get-tuple-element.29.meta, bf16[256,1536]{1,0:T(8,128)(2,1)S(1)} %copy-done, bf16[528,768]{1,0:T(8,128)(2,1)S(1)} %collective-permute-done.6.refs_1_.refs_2_.outer, ...), custom_call_target="tpu_custom_call" | custom-call | flops 402653184 | bytes 1966080 | tf_op jit(solution)/shard_map/attend_more/pallas_call | solution.py:141
  44.0 2.4 %choose_far.1 = (s32[2]{0:T(128)S(1)}, bf16[256,768]{1,0:T(8,128)(2,1)S(1)}, bf16[256,768]{1,0:T(8,128)(2,1)S(1)}) custom-call(s32[10]{0:T(128)S(1)} %get-tuple-element.29.meta, bf16[528,768]{1,0:T(8,128)(2,1)S(1)} %collective-permute-done.6.refs_1_.refs_2_.outer, bf16[528,768]{1,0:T(8,128)(2,1)S(1)} %collective-permute-done.7.refs_3_.refs_4_.inner, ...), custom_call_target="tpu_custom_call" | custom-call | bytes 1572864 | tf_op jit(solution)/shard_map/choose_far/pallas_call | solution.py:163
  46.3 0.1 collective-permute-start.16
  46.4 2.9 %collective-permute-start.17 = (bf16[256,768]{1,0:T(8,128)(2,1)S(1)}, bf16[256,768]{1,0:T(8,128)(2,1)S(1)}, u32[]{:S(2)}, u32[]{:S(2)}) collective-permute-start(bf16[256,768]{1,0:T(8,128)(2,1)S(1)} %get-tuple-element.50), channel_id=1, source_target_pairs={{0,0},{1,1},{2,2},{3,3},{4,8},{5,9},{6,10},{7,11},{8,4},{9,5},{10,... | collective-permute-start | bytes 1179656 | tf_op jit(solution)/shard_map/ppermute | solution.py:436
  49.3 3.4 %choose.2 = (bf16[256,768]{1,0:T(8,128)(2,1)S(1)}, bf16[256,768]{1,0:T(8,128)(2,1)S(1)}, bf16[256,768]{1,0:T(8,128)(2,1)S(1)}, bf16[256,768]{1,0:T(8,128)(2,1)S(1)}) custom-call(s32[10]{0:T(128)S(1)} %get-tuple-element.29.meta, s32[1]{0:T(128)} %get-tuple-element.32.corner_ref, bf16[512,768]{1,0:T(8,128)(2,1)S(1)} %collective-permute-done.4.outer.refs_1_.refs_2_, ...), custom_call_target="tpu_custom_call" | custom-call | bytes 3145728 | tf_op jit(solution)/shard_map/choose/pallas_call | solution.py:163
  52.7 4.2 %collective-permute-start.10 = (bf16[256,768]{1,0:T(8,128)(2,1)S(1)}, bf16[256,768]{1,0:T(8,128)(2,1)S(1)}, u32[]{:S(2)}, u32[]{:S(2)}) collective-permute-start(bf16[256,768]{1,0:T(8,128)(2,1)S(1)} %get-tuple-element.40), channel_id=1, source_target_pairs={{0,2},{1,3},{2,0},{3,1},{4,6},{5,7},{6,4},{7,5},{8,10},{9,11},{10,... | collective-permute-start | bytes 1179656 | tf_op jit(solution)/shard_map/ppermute | solution.py:436
  56.9 1.9 %collective-permute-start.11 = (bf16[256,768]{1,0:T(8,128)(2,1)S(1)}, bf16[256,768]{1,0:T(8,128)(2,1)S(1)}, u32[]{:S(2)}, u32[]{:S(2)}) collective-permute-start(bf16[256,768]{1,0:T(8,128)(2,1)S(1)} %get-tuple-element.41), channel_id=1, source_target_pairs={{0,3},{1,1},{2,2},{3,0},{4,7},{5,5},{6,6},{7,4},{8,11},{9,9},{10,1... | collective-permute-start | bytes 1179656 | tf_op jit(solution)/shard_map/ppermute | solution.py:436
  58.8 0.1 collective-permute-start.12
  58.9 3.1 %collective-permute-start.13 = (bf16[256,768]{1,0:T(8,128)(2,1)S(1)}, bf16[256,768]{1,0:T(8,128)(2,1)S(1)}, u32[]{:S(2)}, u32[]{:S(2)}) collective-permute-start(bf16[256,768]{1,0:T(8,128)(2,1)S(1)} %get-tuple-element.43), channel_id=1, source_target_pairs={{0,0},{1,1},{2,2},{3,3},{4,8},{5,9},{6,10},{7,11},{8,4},{9,5},{10,... | collective-permute-start | bytes 1179656 | tf_op jit(solution)/shard_map/ppermute | solution.py:436
  62.1 2.9 %attend_more.3 = (f32[256,768]{1,0:T(8,128)S(1)}, f32[256,768]{1,0:T(8,128)S(1)}, f32[256,768]{1,0:T(8,128)S(1)}) custom-call(s32[10]{0:T(128)S(1)} %get-tuple-element.29.meta, bf16[256,1536]{1,0:T(8,128)(2,1)S(1)} %copy-done, bf16[512,768]{1,0:T(8,128)(2,1)S(1)} %collective-permute-done.4.outer.refs_1_.refs_2_, ...), custom_call_target="tpu_custom_call" | custom-call | flops 402653184 | bytes 1966080 | tf_op jit(solution)/shard_map/attend_more/pallas_call | solution.py:141
  65.0 3.2 %attend_last.2.refs_14_ = bf16[256,1536]{1,0:T(8,128)(2,1)} custom-call(s32[10]{0:T(128)S(1)} %get-tuple-element.29.meta, bf16[256,1536]{1,0:T(8,128)(2,1)S(1)} %copy-done, bf16[256,768]{1,0:T(8,128)(2,1)S(1)} %collective-permute-done.14.refs_1_.refs_2_, bf16[256,768]{1,0:T(8,128)(2,1)S(1)} %collective-permute-done.14.refs_1_.refs_2_, ...), custom_call_target="tpu_custom_call" | custom-call | flops 301989888 | bytes 1572864 | tf_op jit(solution)/shard_map/attend_last/pallas_call | solution.py:141
  68.2 2.4 %collective-permute-done.11.refs_4_.refs_6_ = bf16[256,768]{1,0:T(8,128)(2,1)S(1)} collective-permute-done((bf16[256,768]{1,0:T(8,128)(2,1)S(1)}, bf16[256,768]{1,0:T(8,128)(2,1)S(1)}, u32[]{:S(2)}, u32[]{:S(2)}) %collective-permute-start.11) | collective-permute-done | bytes 393248 | tf_op jit(solution)/shard_map/ppermute | solution.py:436
  70.7 3.2 %attend_last.3 = bf16[256,1536]{1,0:T(8,128)(2,1)} custom-call(s32[10]{0:T(128)S(1)} %get-tuple-element.29.meta, bf16[256,1536]{1,0:T(8,128)(2,1)S(1)} %copy-done, bf16[256,768]{1,0:T(8,128)(2,1)S(1)} %collective-permute-done.10.refs_1_.refs_2_, bf16[256,768]{1,0:T(8,128)(2,1)S(1)} %collective-permute-done.10.refs_1_.refs_2_, ...), custom_call_target="tpu_custom_call", output_to_operand_aliasing={{}: (15, {})} | custom-call | flops 301989888 | bytes 1572864 | tf_op jit(solution)/shard_map/attend_last/pallas_call | solution.py:141
  (23 shorter events, 0.1 us)
Async XLA Ops:
  0.0 8.3 %copy-start.3 = (s32[1,8]{1,0:T(1,128)S(1)}, s32[1,8]{1,0:T(1,128)}, u32[]{:S(2)}) copy-start(s32[1,8]{1,0:T(1,128)} %list_hbm.1) | copy-start | bytes 100
  0.0 12.9 %copy-start.1 = (bf16[256,1536]{1,0:T(8,128)(2,1)S(1)}, bf16[256,1536]{1,0:T(8,128)(2,1)}, u32[]{:S(2)}) copy-start(bf16[256,1536]{1,0:T(8,128)(2,1)} %k_ref.5) | copy-start | bytes 2359300
  0.0 12.9 %copy-start = (bf16[256,1536]{1,0:T(8,128)(2,1)S(1)}, bf16[256,1536]{1,0:T(8,128)(2,1)}, u32[]{:S(2)}) copy-start(bf16[256,1536]{1,0:T(8,128)(2,1)} %refs_0_.9) | copy-start | bytes 2359300
  0.0 3.7 %collective-permute-start = (s32[1,8]{1,0:T(1,128)}, s32[1,8]{1,0:T(1,128)S(1)}, u32[]{:S(2)}, u32[]{:S(2)}) collective-permute-start(s32[1,8]{1,0:T(1,128)} %list_hbm.1), channel_id=1, source_target_pairs={{0,2},{1,3},{2,0},{3,1},{4,6},{5,7},{6,4},{7,5},{8,10},{9,11},{10,... | collective-permute-start | bytes 104 | tf_op jit(solution)/shard_map/ppermute | solution.py:436
  6.3 18.2 %collective-permute-start.3 = (bf16[256,1536]{1,0:T(8,128)(2,1)S(1)}, bf16[256,1536]{1,0:T(8,128)(2,1)S(1)}, u32[]{:S(2)}, u32[]{:S(2)}) collective-permute-start(bf16[256,1536]{1,0:T(8,128)(2,1)S(1)} %get-tuple-element.30), channel_id=1, source_target_pairs={{0,2},{1,3},{2,0},{3,1},{4,6},{5,7},{6,4},{7,5},{8,10},{9,11},{10,... | collective-permute-start | bytes 2359304 | tf_op jit(solution)/shard_map/ppermute | solution.py:436
  7.9 20.2 %collective-permute-start.6 = (bf16[528,768]{1,0:T(8,128)(2,1)S(1)}, bf16[528,768]{1,0:T(8,128)(2,1)S(1)}, u32[]{:S(2)}, u32[]{:S(2)}) collective-permute-start(bf16[528,768]{1,0:T(8,128)(2,1)S(1)} %get-tuple-element.33), channel_id=1, source_target_pairs={{0,4},{1,5},{2,6},{3,7},{4,0},{5,1},{6,2},{7,3},{8,12},{9,13},{10,... | collective-permute-start | bytes 2433032 | tf_op jit(solution)/shard_map/ppermute | solution.py:436
  8.3 10.7 %collective-permute-start.1 = (s32[1,8]{1,0:T(1,128)S(1)}, s32[1,8]{1,0:T(1,128)S(1)}, u32[]{:S(2)}, u32[]{:S(2)}) collective-permute-start(s32[1,8]{1,0:T(1,128)S(1)} %copy-done.3), channel_id=1, source_target_pairs={{0,1},{1,0},{2,3},{3,2},{4,5},{5,4},{6,7},{7,6},{8,9},{9,8},{10,11... | collective-permute-start | bytes 104 | tf_op jit(solution)/shard_map/ppermute | solution.py:436
  8.3 24.4 %collective-permute-start.7 = (bf16[528,768]{1,0:T(8,128)(2,1)S(1)}, bf16[528,768]{1,0:T(8,128)(2,1)S(1)}, u32[]{:S(2)}, u32[]{:S(2)}) collective-permute-start(bf16[528,768]{1,0:T(8,128)(2,1)S(1)} %get-tuple-element.33), channel_id=1, source_target_pairs={{0,0},{1,1},{2,2},{3,3},{4,8},{5,9},{6,10},{7,11},{8,4},{9,5},{10,... | collective-permute-start | bytes 2433032 | tf_op jit(solution)/shard_map/ppermute | solution.py:436
  12.9 1.1 %copy-start.2 = (bf16[256,1536]{1,0:T(8,128)(2,1)S(1)}, bf16[256,1536]{1,0:T(8,128)(2,1)}, u32[]{:S(2)}) copy-start(bf16[256,1536]{1,0:T(8,128)(2,1)} %v_ref.5) | copy-start | bytes 2359300
  18.7 1.2 %collective-permute-start.2 = (s32[1,8]{1,0:T(1,128)S(1)}, s32[1,8]{1,0:T(1,128)S(1)}, u32[]{:S(2)}, u32[]{:S(2)}) collective-permute-start(s32[1,8]{1,0:T(1,128)S(1)} %collective-permute-done.across_ref), channel_id=1, source_target_pairs={{0,1},{1,0},{2,3},{3,2},{4,5},{5,4},{6,7},{7,6},{8,9},{9,8},{10,11... | collective-permute-start | bytes 104 | tf_op jit(solution)/shard_map/ppermute | solution.py:436
  26.7 11.6 %collective-permute-start.8 = (bf16[256,1536]{1,0:T(8,128)(2,1)S(1)}, bf16[256,1536]{1,0:T(8,128)(2,1)S(1)}, u32[]{:S(2)}, u32[]{:S(2)}) collective-permute-start(bf16[256,1536]{1,0:T(8,128)(2,1)S(1)} %get-tuple-element.34), channel_id=1, source_target_pairs={{0,1},{1,0},{2,3},{3,2},{4,5},{5,4},{6,7},{7,6},{8,9},{9,8},{10,11... | collective-permute-start | bytes 2359304 | tf_op jit(solution)/shard_map/ppermute | solution.py:436
  26.8 17.2 %collective-permute-start.9 = (bf16[256,1536]{1,0:T(8,128)(2,1)S(1)}, bf16[256,1536]{1,0:T(8,128)(2,1)S(1)}, u32[]{:S(2)}, u32[]{:S(2)}) collective-permute-start(bf16[256,1536]{1,0:T(8,128)(2,1)S(1)} %get-tuple-element.38), channel_id=1, source_target_pairs={{0,0},{1,2},{2,1},{3,3},{4,4},{5,6},{6,5},{7,7},{8,8},{9,10},{10,9... | collective-permute-start | bytes 2359304 | tf_op jit(solution)/shard_map/ppermute | solution.py:436
  27.5 18.9 %collective-permute-start.4 = (bf16[512,768]{1,0:T(8,128)(2,1)S(1)}, bf16[512,768]{1,0:T(8,128)(2,1)S(1)}, u32[]{:S(2)}, u32[]{:S(2)}) collective-permute-start(bf16[512,768]{1,0:T(8,128)(2,1)S(1)} %pack.1.refs_1_), channel_id=1, source_target_pairs={{0,4},{1,5},{2,6},{3,7},{4,0},{5,1},{6,2},{7,3},{8,12},{9,13},{10,... | collective-permute-start | bytes 2359304 | tf_op jit(solution)/shard_map/ppermute | solution.py:436
  28.1 21.2 %collective-permute-start.5 = (bf16[512,768]{1,0:T(8,128)(2,1)S(1)}, bf16[512,768]{1,0:T(8,128)(2,1)S(1)}, u32[]{:S(2)}, u32[]{:S(2)}) collective-permute-start(bf16[512,768]{1,0:T(8,128)(2,1)S(1)} %pack.1.refs_1_), channel_id=1, source_target_pairs={{0,0},{1,1},{2,2},{3,3},{4,8},{5,9},{6,10},{7,11},{8,4},{9,5},{10,... | collective-permute-start | bytes 2359304 | tf_op jit(solution)/shard_map/ppermute | solution.py:436
  35.0 21.9 %collective-permute-start.14 = (bf16[256,768]{1,0:T(8,128)(2,1)S(1)}, bf16[256,768]{1,0:T(8,128)(2,1)S(1)}, u32[]{:S(2)}, u32[]{:S(2)}) collective-permute-start(bf16[256,768]{1,0:T(8,128)(2,1)S(1)} %get-tuple-element.47), channel_id=1, source_target_pairs={{0,2},{1,3},{2,0},{3,1},{4,6},{5,7},{6,4},{7,5},{8,10},{9,11},{10,... | collective-permute-start | bytes 1179656 | tf_op jit(solution)/shard_map/ppermute | solution.py:436
  38.4 20.5 %collective-permute-start.15 = (bf16[256,768]{1,0:T(8,128)(2,1)S(1)}, bf16[256,768]{1,0:T(8,128)(2,1)S(1)}, u32[]{:S(2)}, u32[]{:S(2)}) collective-permute-start(bf16[256,768]{1,0:T(8,128)(2,1)S(1)} %get-tuple-element.48), channel_id=1, source_target_pairs={{0,3},{1,1},{2,2},{3,0},{4,7},{5,5},{6,6},{7,4},{8,11},{9,9},{10,1... | collective-permute-start | bytes 1179656 | tf_op jit(solution)/shard_map/ppermute | solution.py:436
  46.3 12.6 %collective-permute-start.16 = (bf16[256,768]{1,0:T(8,128)(2,1)S(1)}, bf16[256,768]{1,0:T(8,128)(2,1)S(1)}, u32[]{:S(2)}, u32[]{:S(2)}) collective-permute-start(bf16[256,768]{1,0:T(8,128)(2,1)S(1)} %get-tuple-element.49), channel_id=1, source_target_pairs={{0,4},{1,5},{2,6},{3,7},{4,0},{5,1},{6,2},{7,3},{8,12},{9,13},{10,... | collective-permute-start | bytes 1179656 | tf_op jit(solution)/shard_map/ppermute | solution.py:436
  46.4 18.6 %collective-permute-start.17 = (bf16[256,768]{1,0:T(8,128)(2,1)S(1)}, bf16[256,768]{1,0:T(8,128)(2,1)S(1)}, u32[]{:S(2)}, u32[]{:S(2)}) collective-permute-start(bf16[256,768]{1,0:T(8,128)(2,1)S(1)} %get-tuple-element.50), channel_id=1, source_target_pairs={{0,0},{1,1},{2,2},{3,3},{4,8},{5,9},{6,10},{7,11},{8,4},{9,5},{10,... | collective-permute-start | bytes 1179656 | tf_op jit(solution)/shard_map/ppermute | solution.py:436
  52.7 15.5 %collective-permute-start.10 = (bf16[256,768]{1,0:T(8,128)(2,1)S(1)}, bf16[256,768]{1,0:T(8,128)(2,1)S(1)}, u32[]{:S(2)}, u32[]{:S(2)}) collective-permute-start(bf16[256,768]{1,0:T(8,128)(2,1)S(1)} %get-tuple-element.40), channel_id=1, source_target_pairs={{0,2},{1,3},{2,0},{3,1},{4,6},{5,7},{6,4},{7,5},{8,10},{9,11},{10,... | collective-permute-start | bytes 1179656 | tf_op jit(solution)/shard_map/ppermute | solution.py:436
  56.9 13.8 %collective-permute-start.11 = (bf16[256,768]{1,0:T(8,128)(2,1)S(1)}, bf16[256,768]{1,0:T(8,128)(2,1)S(1)}, u32[]{:S(2)}, u32[]{:S(2)}) collective-permute-start(bf16[256,768]{1,0:T(8,128)(2,1)S(1)} %get-tuple-element.41), channel_id=1, source_target_pairs={{0,3},{1,1},{2,2},{3,0},{4,7},{5,5},{6,6},{7,4},{8,11},{9,9},{10,1... | collective-permute-start | bytes 1179656 | tf_op jit(solution)/shard_map/ppermute | solution.py:436
  58.8 11.8 %collective-permute-start.12 = (bf16[256,768]{1,0:T(8,128)(2,1)S(1)}, bf16[256,768]{1,0:T(8,128)(2,1)S(1)}, u32[]{:S(2)}, u32[]{:S(2)}) collective-permute-start(bf16[256,768]{1,0:T(8,128)(2,1)S(1)} %get-tuple-element.42), channel_id=1, source_target_pairs={{0,4},{1,5},{2,6},{3,7},{4,0},{5,1},{6,2},{7,3},{8,12},{9,13},{10,... | collective-permute-start | bytes 1179656 | tf_op jit(solution)/shard_map/ppermute | solution.py:436
  58.9 11.8 %collective-permute-start.13 = (bf16[256,768]{1,0:T(8,128)(2,1)S(1)}, bf16[256,768]{1,0:T(8,128)(2,1)S(1)}, u32[]{:S(2)}, u32[]{:S(2)}) collective-permute-start(bf16[256,768]{1,0:T(8,128)(2,1)S(1)} %get-tuple-element.43), channel_id=1, source_target_pairs={{0,0},{1,1},{2,2},{3,3},{4,8},{5,9},{6,10},{7,11},{8,4},{9,5},{10,... | collective-permute-start | bytes 1179656 | tf_op jit(solution)/shard_map/ppermute | solution.py:436

commit v12 on v10

--- a/solution.py
+++ b/solution.py
@@ -10,7 +10,6 @@
 
 HD = 128
 TILE = 128
-NOTE_ROWS = 16
 LOG2_SCALE = math.log2(math.e) / math.sqrt(HD)
 VMEM_LIMIT = 24 * 1024 * 1024
 
@@ -204,22 +203,6 @@
     return jnp.clip(ref[0, entry], 0, tile_count - 1)
 
 
-def write_note(note, ref, tile_count):
-    lane = lax.broadcasted_iota(jnp.int32, note.shape, 1)
-    row = jnp.zeros(note.shape, jnp.float32)
-    for entry in range(8):
-        row = jnp.where(lane == entry, tile_at(ref, entry, tile_count).astype(jnp.float32), row)
-    note[...] = row.astype(jnp.bfloat16)
-
-
-def read_note(note, entry, tile_count):
-    here = (lax.broadcasted_iota(jnp.int32, note.shape, 1) == entry) & (
-        lax.broadcasted_iota(jnp.int32, note.shape, 0) == 0
-    )
-    value = jnp.sum(jnp.where(here, note.astype(jnp.float32), 0.0))
-    return jnp.clip(value.astype(jnp.int32), 0, tile_count - 1)
-
-
 def part_copies(k_ref, v_ref, first, width, target, sems, at):
     rows = k_ref.shape[0]
     return [
@@ -234,8 +217,8 @@
     rows, all_width = keys.shape
     tile_count = rows // TILE
 
-    def build(me_ref, across_ref, list_hbm, k_ref, v_ref, meta, packed, to_across, list_ref, note, sems):
-        read = pltpu.make_async_copy(list_hbm, list_ref, sems.at[5])
+    def build(me_ref, across_ref, list_hbm, k_ref, v_ref, meta, packed, to_across, list_ref, sems):
+        read = pltpu.make_async_copy(list_hbm, list_ref, sems.at[4])
         read.start()
         me = me_ref[0]
         right = me % 4 >= 2
@@ -245,16 +228,11 @@
         for copy in copies:
             copy.start()
         read.wait()
-        write_note(note, list_ref, tile_count)
-        last = pltpu.make_async_copy(
-            note, packed.at[pl.ds(2 * rows, NOTE_ROWS), pl.ds(0, HD)], sems.at[4]
-        )
-        last.start()
         for entry in range(8):
             meta[entry] = tile_at(list_ref, entry, tile_count)
         meta[8] = me
         meta[9] = tile_at(across_ref, jnp.where(right, 1, 5), tile_count)
-        for copy in copies + [last]:
+        for copy in copies:
             copy.wait()
 
     return move(
@@ -264,24 +242,25 @@
         [SCALAR] * 2 + [WHOLE] * 3,
         [
             jax.ShapeDtypeStruct((10,), jnp.int32),
-            jax.ShapeDtypeStruct((2 * rows + NOTE_ROWS, width), jnp.bfloat16),
+            jax.ShapeDtypeStruct((2 * rows, width), jnp.bfloat16),
             jax.ShapeDtypeStruct((2 * TILE, all_width), jnp.bfloat16),
         ],
         [SCALAR, WHOLE, WHOLE],
-        6,
+        5,
         8 * rows * width + 8 * TILE * all_width,
-        [pltpu.SMEM(tile_lists.shape, jnp.int32), pltpu.VMEM((NOTE_ROWS, HD), jnp.bfloat16)],
+        [pltpu.SMEM(tile_lists.shape, jnp.int32)],
     )
 
 
-def choose_near(meta, beside_list, corner_list, keys, values):
+def choose_near(meta, tile_lists, beside_list, corner_list, keys, values):
     rows, width = keys.shape
     tile_count = rows // TILE
 
-    def build(meta, beside_ref, corner_ref, k_ref, v_ref, wanted, to_beside, to_corner, zeros, sems):
+    def build(meta, list_hbm, beside_ref, corner_ref, k_ref, v_ref, wanted, listing, to_beside, to_corner, zeros, sems):
         even = meta[8] % 2 == 0
         own = ((k_ref, 0, 0), (v_ref, 0, 0))
         copies = tile_copies(own, tile_at(beside_ref, jnp.where(even, 0, 4), tile_count), to_beside, sems, 0)
+        copies.append(pltpu.make_async_copy(list_hbm, listing, sems.at[4]))
         for copy in copies:
             copy.start()
         wanted[0] = tile_at(corner_ref, jnp.where(even, 4, 0), tile_count)
@@ -297,11 +276,16 @@
     return move(
         "choose_near",
         build,
-        (meta, beside_list, corner_list, in_hbm(keys), in_hbm(values)),
-        [SCALAR] * 3 + [WHOLE] * 2,
-        [jax.ShapeDtypeStruct((1,), jnp.int32), tile, tile],
-        [SCALAR, WHOLE, WHOLE],
-        4,
+        (meta, in_hbm(tile_lists), beside_list, corner_list, in_hbm(keys), in_hbm(values)),
+        [SCALAR, WHOLE] + [SCALAR] * 2 + [WHOLE] * 2,
+        [
+            jax.ShapeDtypeStruct((1,), jnp.int32),
+            jax.ShapeDtypeStruct(tile_lists.shape, jnp.int32),
+            tile,
+            tile,
+        ],
+        [SCALAR, WHOLE, WHOLE, WHOLE],
+        5,
         16 * TILE * width,
         [pltpu.VMEM((TILE, width), jnp.bfloat16)],
     )
@@ -340,69 +324,41 @@
     )
 
 
-def choose(meta, corner_tile, wants, outer, inner, after):
-    rows, width = outer.shape[0] // 2 // TILE * TILE, outer.shape[1]
+def choose(meta, corner_tile, far_list, keys, values, first, outer, inner, after):
+    rows, width = keys.shape[0], outer.shape[1]
     tile_count = rows // TILE
-    again = wants is not None
-
-    def build(meta, corner_ref, *refs):
-        if again:
-            wants, outer, inner = refs[:3]
-            to_two, to_one, to_outer, to_inner = refs[-6:-2]
-        else:
-            outer, inner, wants = refs[:2] + refs[-8:-7]
-            to_two, to_one, to_outer, to_inner, notes = refs[-7:-2]
-        zeros, sems = refs[-2:]
+
+    def build(meta, corner_ref, far_ref, k_ref, v_ref, outer, inner, *refs):
+        to_two, to_one, to_far, zeros, sems = refs[-5:]
         spot, plane = meta[8] % 4, meta[8] // 4
         right, odd = spot >= 2, plane % 2 == 1
+        edge = (spot == 0) | (spot == 3)
+        between = (plane == 1) | (plane == 2)
+        own = ((k_ref, 0, first), (v_ref, 0, first))
         from_outer = ((outer, 0, 0), (outer, rows, 0))
         from_inner = ((inner, 0, 0), (inner, rows, 0))
-        if not again:
-            reads = [
-                pltpu.make_async_copy(
-                    ref.at[pl.ds(2 * rows, NOTE_ROWS), pl.ds(0, HD)], notes.at[n], sems.at[8 + n]
-                )
-                for n, ref in enumerate((outer, inner))
-            ]
-            for read in reads:
-                read.start()
-        edge = (spot == 0) | (spot == 3)
         for source, here in ((from_outer, right == odd), (from_inner, right != odd)):
             start_if(here, tile_copies(source, meta[9], to_two, sems, 0))
             start_if(here & edge, tile_copies(source, corner_ref[0], to_one, sems, 2))
+        tile = tile_at(far_ref, jnp.where(odd, 7, 3), tile_count)
+        start_if(between, tile_copies(from_inner, tile, to_far, sems, 4))
+        start_if(jnp.logical_not(between), tile_copies(own, tile, to_far, sems, 4))
         zeros[...] = jnp.zeros_like(zeros)
         start_if(jnp.logical_not(edge), zero_copies(zeros, to_one, sems, 2))
-        between = (plane == 1) | (plane == 2)
-        start_if(
-            jnp.logical_not(between),
-            zero_copies(zeros, to_outer, sems, 4) + zero_copies(zeros, to_inner, sems, 6),
-        )
-        if not again:
-            for read in reads:
-                read.wait()
-            wants[0] = read_note(notes[0], jnp.where(plane == 1, 7, 3), tile_count)
-            wants[1] = read_note(notes[1], jnp.where(plane == 1, 3, 7), tile_count)
-        start_if(
-            between,
-            tile_copies(from_inner, wants[0], to_outer, sems, 4)
-            + tile_copies(from_outer, wants[1], to_inner, sems, 6),
-        )
-        for n, target in enumerate((to_two, to_one, to_outer, to_inner)):
-            for copy in tile_copies(from_outer, 0, target, sems, 2 * n):
+        for n, target in enumerate((to_two, to_one, to_far)):
+            for copy in zero_copies(zeros, target, sems, 2 * n):
                 copy.wait()
 
-    sent = [jax.ShapeDtypeStruct((2 * TILE, width), jnp.bfloat16)] * 4
     return move(
-        "choose_again" if again else "choose",
+        "choose",
         build,
-        (meta, corner_tile, *([wants] if again else []), outer, inner, *after),
-        [SCALAR] * (2 + again) + [WHOLE] * (2 + len(after)),
-        ([] if again else [jax.ShapeDtypeStruct((2,), jnp.int32)]) + sent,
-        [SCALAR] * (not again) + [WHOLE] * 4,
-        10,
-        32 * TILE * width,
-        ([] if again else [pltpu.VMEM((2, NOTE_ROWS, HD), jnp.bfloat16)])
-        + [pltpu.VMEM((TILE, width), jnp.bfloat16)],
+        (meta, corner_tile, far_list, in_hbm(keys), in_hbm(values), outer, inner, *after),
+        [SCALAR] * 3 + [WHOLE] * (4 + len(after)),
+        [jax.ShapeDtypeStruct((2 * TILE, width), jnp.bfloat16)] * 3,
+        [WHOLE] * 3,
+        6,
+        24 * TILE * width,
+        [pltpu.VMEM((TILE, width), jnp.bfloat16)],
     )
 
 
@@ -450,6 +406,7 @@
     corner_out = [(i, i ^ 3 if i % 4 in (0, 3) else i) for i in every]
     outer = [(i, i ^ 4) for i in every]
     inner = [(i, i ^ 12 if i // 4 in (1, 2) else i) for i in every]
+    far = [(i, i + (8, -4, 4, -8)[i // 4]) for i in every]
 
     def right(meta):
         return meta[8] % 4 >= 2
@@ -489,24 +446,27 @@
     first_width = parts[0][1] * block
     meta, first, to_across = begin(tile_lists, me, across_list, key_heads, value_heads, first_width)
     over = send(to_across, across)
-    corner_tile, to_beside, to_corner = choose_near(meta, beside_list, corner_list, key_heads, value_heads)
+    corner_tile, listing, to_beside, to_corner = choose_near(
+        meta, tile_lists, beside_list, corner_list, key_heads, value_heads
+    )
+    far_list = send(listing, [(j, i) for i, j in far])
     next_to = send(to_beside, beside)
     one_in = send(to_corner, corner_in)
     second = pack(key_heads, value_heads, first_width, width - first_width, [to_beside])
     near = [own_frame(), sent_tile([(next_to, 0)]), sent_tile([(over, 0)])]
     begun = attend(queries, meta, near, 0, width // block, heads)
 
-    after, wants = [begun[0], one_in], None
+    after = [begun[0], one_in]
     middles, finals = [], []
     for (at, steps), packed in zip(parts, (first, second)):
         from_outer = send(packed, outer)
         from_inner = send(packed, inner)
-        sent = choose(meta, corner_tile, wants, from_outer, from_inner, after)
-        if wants is None:
-            wants, *sent = sent
-        two = send(sent[0], across)
-        one = send(sent[1], corner_out)
-        far = [send(sent[2], outer), send(sent[3], inner)]
+        to_two, to_one, to_far = choose(
+            meta, corner_tile, far_list, key_heads, value_heads, at * block, from_outer, from_inner, after
+        )
+        two = send(to_two, across)
+        one = send(to_one, corner_out)
+        from_far = send(to_far, far)
         middle = attend(
             queries,
             meta,
@@ -526,7 +486,7 @@
             [
                 sent_tile([(two, 0)], two_there),
                 sent_tile([(one_in, at), (one, 0)], one_there),
-                sent_tile([(a, 0) for a in far]),
+                sent_tile([(from_far, 0)]),
             ]
         )
     out = None

time: 70.5 us -> 79.9 us (1.13)
  waiting for transfers between devices: 22.4 us -> 34.1 us
  Pallas kernels: 24.7 us -> 23.4 us
  starting transfers between devices: 22.7 us -> 21.4 us
    ppermute x18 -> x17, waiting for transfers between devices: 22.4 us -> 34.1 us  [send(): return lax.ppermute(array, 'frame', route)]
    ppermute x18 -> x17, starting transfers between devices: 22.7 us -> 21.4 us  [send(): return lax.ppermute(array, 'frame', route)]
    pallas_call x5, Pallas kernels: 10.9 us -> 9.69 us  [move(): pl.pallas_call(build, name=name, out_shape=out_shape, in_specs=specs, out...]
  transfers between devices with their start and end apart: 18 -> 17, of which waited for: 9 -> 6; matrix products, arithmetic and copies ran while one was open for 0% -> 0% of each run, Pallas kernels for 28% -> 23%
where the time goes in v12:
time: 79.9 us; the launch traced here: 79.1 us
  waiting for transfers between devices  34.1 us (43%)
  Pallas kernels  23.4 us (29%)
  starting transfers between devices  21.4 us (27%)
    ppermute x17, waiting for transfers between devices, send(): return lax.ppermute(array, 'frame', route)  34.1 us
    ppermute x17, starting transfers between devices, send(): return lax.ppermute(array, 'frame', route)  21.4 us
    pallas_call x5, Pallas kernels, attend(): pl.pallas_call(functools.partial(attend_kernel, plan, heads, carry is not...  13.7 us
    pallas_call x5, Pallas kernels, move(): pl.pallas_call(build, name=name, out_shape=out_shape, in_specs=specs, out...  9.69 us
  transfers between devices with their start and end apart: 17, of which 6 were waited for; matrix products, arithmetic and copies ran while one was open for 0% of the time, Pallas kernels for 23%

profile of v12, /device:TPU:12, one launch (start us, length us, event | category | flops | bytes accessed | tf_op | source)
XLA Modules:
  0.0 79.1 jit_solution(6368862819176216354)
XLA Ops:
  0.0 1.5 %collective-permute-start = (s32[1,8]{1,0:T(1,128)}, s32[1,8]{1,0:T(1,128)S(1)}, u32[]{:S(2)}, u32[]{:S(2)}) collective-permute-start(s32[1,8]{1,0:T(1,128)} %list_hbm.3), channel_id=1, source_target_pairs={{0,2},{1,3},{2,0},{3,1},{4,6},{5,7},{6,4},{7,5},{8,10},{9,11},{10,... | collective-permute-start | bytes 104 | tf_op jit(solution)/shard_map/ppermute | solution.py:366
  1.5 2.2 %collective-permute-done.across_ref = s32[1,8]{1,0:T(1,128)S(1)} collective-permute-done((s32[1,8]{1,0:T(1,128)}, s32[1,8]{1,0:T(1,128)S(1)}, u32[]{:S(2)}, u32[]{:S(2)}) %collective-permute-start) | collective-permute-done | bytes 64 | tf_op jit(solution)/shard_map/ppermute | solution.py:366
  3.7 2.6 %begin.1 = (s32[10]{0:T(128)S(1)}, bf16[512,1024]{1,0:T(8,128)(2,1)S(1)}, bf16[256,1536]{1,0:T(8,128)(2,1)S(1)}) custom-call(s32[1]{0:T(128)} %bitcast.me_ref, s32[1,8]{1,0:T(1,128)S(1)} %collective-permute-done.across_ref, s32[1,8]{1,0:T(1,128)} %list_hbm.3, bf16[256,1536]{1,0:T(8,128)(2,1)} %k_ref.9, bf16[256,1536]{1,0:T(8,128)(2,1)} %v_ref.9), custom_call_target="tpu_custom_call" | custom-call | bytes 3670016 | tf_op jit(solution)/shard_map/begin/pallas_call | solution.py:162
  6.3 0.5 collective-permute-start.6
  6.8 4.6 %collective-permute-start.7 = (bf16[512,1024]{1,0:T(8,128)(2,1)S(1)}, bf16[512,1024]{1,0:T(8,128)(2,1)S(1)}, u32[]{:S(2)}, u32[]{:S(2)}) collective-permute-start(bf16[512,1024]{1,0:T(8,128)(2,1)S(1)} %get-tuple-element.31), channel_id=1, source_target_pairs={{0,0},{1,1},{2,2},{3,3},{4,8},{5,9},{6,10},{7,11},{8,4},{9,5},{10,... | collective-permute-start | bytes 3145736 | tf_op jit(solution)/shard_map/ppermute | solution.py:366
  11.4 0.1 collective-permute-start.1
  11.5 1.6 %collective-permute-start.9 = (bf16[256,1536]{1,0:T(8,128)(2,1)S(1)}, bf16[256,1536]{1,0:T(8,128)(2,1)S(1)}, u32[]{:S(2)}, u32[]{:S(2)}) collective-permute-start(bf16[256,1536]{1,0:T(8,128)(2,1)S(1)} %get-tuple-element.32), channel_id=1, source_target_pairs={{0,2},{1,3},{2,0},{3,1},{4,6},{5,7},{6,4},{7,5},{8,10},{9,11},{10,... | collective-permute-start | bytes 2359304 | tf_op jit(solution)/shard_map/ppermute | solution.py:366
  13.1 0.2 collective-permute-start.2
  13.3 1.0 %collective-permute-done.2.corner_ref = s32[1,8]{1,0:T(1,128)S(1)} collective-permute-done((s32[1,8]{1,0:T(1,128)S(1)}, s32[1,8]{1,0:T(1,128)S(1)}, u32[]{:S(2)}, u32[]{:S(2)}) %collective-permute-start.2) | collective-permute-done | bytes 64 | tf_op jit(solution)/shard_map/ppermute | solution.py:366
  14.2 2.2 %choose_near.1 = (s32[1]{0:T(128)}, s32[1,8]{1,0:T(1,128)S(1)}, bf16[256,1536]{1,0:T(8,128)(2,1)S(1)}, bf16[256,1536]{1,0:T(8,128)(2,1)S(1)}) custom-call(s32[10]{0:T(128)S(1)} %get-tuple-element.27.meta, s32[1,8]{1,0:T(1,128)} %list_hbm.3, s32[1,8]{1,0:T(1,128)S(1)} %collective-permute-done.1.beside_ref, s32[1,8]{1,0:T(1,128)S(1)} %collective-permute-done.2.corner_ref, ...), custom_call_target="tpu_custom_call" | custom-call | bytes 3145728 | tf_op jit(solution)/shard_map/choose_near/pallas_call | solution.py:162
  16.5 0.6 collective-permute-start.8
  17.1 0.8 %collective-permute-start.11 = (bf16[256,1536]{1,0:T(8,128)(2,1)S(1)}, bf16[256,1536]{1,0:T(8,128)(2,1)S(1)}, u32[]{:S(2)}, u32[]{:S(2)}) collective-permute-start(bf16[256,1536]{1,0:T(8,128)(2,1)S(1)} %get-tuple-element.38), channel_id=1, source_target_pairs={{0,0},{1,2},{2,1},{3,3},{4,4},{5,6},{6,5},{7,7},{8,8},{9,10},{10,9... | collective-permute-start | bytes 2359304 | tf_op jit(solution)/shard_map/ppermute | solution.py:366
  17.9 1.1 %pack.1 = bf16[512,512]{1,0:T(8,128)(2,1)S(1)} custom-call(bf16[256,1536]{1,0:T(8,128)(2,1)} %k_ref.9, bf16[256,1536]{1,0:T(8,128)(2,1)} %v_ref.9, bf16[256,1536]{1,0:T(8,128)(2,1)S(1)} %get-tuple-element.30.refs_0_), custom_call_target="tpu_custom_call" | custom-call | bytes 1048576 | tf_op jit(solution)/shard_map/pack/pallas_call | solution.py:162
  19.0 12.4 %collective-permute-done.9.refs_5_.refs_6_ = bf16[256,1536]{1,0:T(8,128)(2,1)S(1)} collective-permute-done((bf16[256,1536]{1,0:T(8,128)(2,1)S(1)}, bf16[256,1536]{1,0:T(8,128)(2,1)S(1)}, u32[]{:S(2)}, u32[]{:S(2)}) %collective-permute-start.9) | collective-permute-done | bytes 786464 | tf_op jit(solution)/shard_map/ppermute | solution.py:366
  31.5 2.0 %collective-permute-start.4 = (bf16[512,512]{1,0:T(8,128)(2,1)S(1)}, bf16[512,512]{1,0:T(8,128)(2,1)S(1)}, u32[]{:S(2)}, u32[]{:S(2)}) collective-permute-start(bf16[512,512]{1,0:T(8,128)(2,1)S(1)} %pack.1), channel_id=1, source_target_pairs={{0,4},{1,5},{2,6},{3,7},{4,0},{5,1},{6,2},{7,3},{8,12},{9,13},{10,... | collective-permute-start | bytes 1572872 | tf_op jit(solution)/shard_map/ppermute | solution.py:366
  33.5 4.1 %attend_own.1 = (f32[256,1536]{1,0:T(8,128)S(1)}, f32[256,1536]{1,0:T(8,128)S(1)}, f32[256,1536]{1,0:T(8,128)S(1)}) custom-call(s32[10]{0:T(128)S(1)} %get-tuple-element.27.meta, bf16[256,1536]{1,0:T(8,128)(2,1)S(1)} %copy-done.2, bf16[256,1536]{1,0:T(8,128)(2,1)S(1)} %copy-done, bf16[256,1536]{1,0:T(8,128)(2,1)S(1)} %copy-done.1, ...), custom_call_target="tpu_custom_call" | custom-call | flops 805306368 | bytes 3932160 | tf_op jit(solution)/shard_map/attend_own/pallas_call | solution.py:140
  37.6 1.9 %collective-permute-start.5 = (bf16[512,512]{1,0:T(8,128)(2,1)S(1)}, bf16[512,512]{1,0:T(8,128)(2,1)S(1)}, u32[]{:S(2)}, u32[]{:S(2)}) collective-permute-start(bf16[512,512]{1,0:T(8,128)(2,1)S(1)} %pack.1), channel_id=1, source_target_pairs={{0,0},{1,1},{2,2},{3,3},{4,8},{5,9},{6,10},{7,11},{8,4},{9,5},{10,... | collective-permute-start | bytes 1572872 | tf_op jit(solution)/shard_map/ppermute | solution.py:366
  39.6 1.4 %choose.3 = (bf16[256,1024]{1,0:T(8,128)(2,1)S(1)}, bf16[256,1024]{1,0:T(8,128)(2,1)S(1)}, bf16[256,1024]{1,0:T(8,128)(2,1)S(1)}) custom-call(s32[10]{0:T(128)S(1)} %get-tuple-element.27.meta, s32[1]{0:T(128)} %get-tuple-element.28.corner_ref, s32[1,8]{1,0:T(1,128)S(1)} %collective-permute-done.3.far_ref, bf16[256,1536]{1,0:T(8,128)(2,1)} %k_ref.9, ...), custom_call_target="tpu_custom_call" | custom-call | bytes 3145728 | tf_op jit(solution)/shard_map/choose/pallas_call | solution.py:162
  41.0 2.0 %collective-permute-start.14 = (bf16[256,1024]{1,0:T(8,128)(2,1)S(1)}, bf16[256,1024]{1,0:T(8,128)(2,1)S(1)}, u32[]{:S(2)}, u32[]{:S(2)}) collective-permute-start(bf16[256,1024]{1,0:T(8,128)(2,1)S(1)} %get-tuple-element.44), channel_id=1, source_target_pairs={{0,2},{1,3},{2,0},{3,1},{4,6},{5,7},{6,4},{7,5},{8,10},{9,11},{10,... | collective-permute-start | bytes 1572872 | tf_op jit(solution)/shard_map/ppermute | solution.py:366
  43.0 1.9 %collective-permute-start.15 = (bf16[256,1024]{1,0:T(8,128)(2,1)S(1)}, bf16[256,1024]{1,0:T(8,128)(2,1)S(1)}, u32[]{:S(2)}, u32[]{:S(2)}) collective-permute-start(bf16[256,1024]{1,0:T(8,128)(2,1)S(1)} %get-tuple-element.45), channel_id=1, source_target_pairs={{0,3},{1,1},{2,2},{3,0},{4,7},{5,5},{6,6},{7,4},{8,11},{9,9},{10,1... | collective-permute-start | bytes 1572872 | tf_op jit(solution)/shard_map/ppermute | solution.py:366
  45.0 0.1 collective-permute-start.16
  45.0 2.6 %attend_more.2 = (f32[256,1024]{1,0:T(8,128)S(1)}, f32[256,1024]{1,0:T(8,128)S(1)}, f32[256,1024]{1,0:T(8,128)S(1)}) custom-call(s32[10]{0:T(128)S(1)} %get-tuple-element.27.meta, bf16[256,1536]{1,0:T(8,128)(2,1)S(1)} %copy-done.2, bf16[512,1024]{1,0:T(8,128)(2,1)S(1)} %collective-permute-done.6.refs_1_.refs_2_.outer, ...), custom_call_target="tpu_custom_call" | custom-call | flops 268435456 | bytes 1572864 | tf_op jit(solution)/shard_map/attend_more/pallas_call | solution.py:140
  47.7 16.0 %collective-permute-done.5.inner.refs_3_.refs_4_ = bf16[512,512]{1,0:T(8,128)(2,1)S(1)} collective-permute-done((bf16[512,512]{1,0:T(8,128)(2,1)S(1)}, bf16[512,512]{1,0:T(8,128)(2,1)S(1)}, u32[]{:S(2)}, u32[]{:S(2)}) %collective-permute-start.5) | collective-permute-done | bytes 524320 | tf_op jit(solution)/shard_map/ppermute | solution.py:366
  63.7 2.3 %choose.2 = (bf16[256,512]{1,0:T(8,128)(2,1)S(1)}, bf16[256,512]{1,0:T(8,128)(2,1)S(1)}, bf16[256,512]{1,0:T(8,128)(2,1)S(1)}) custom-call(s32[10]{0:T(128)S(1)} %get-tuple-element.27.meta, s32[1]{0:T(128)} %get-tuple-element.28.corner_ref, s32[1,8]{1,0:T(1,128)S(1)} %collective-permute-done.3.far_ref, bf16[256,1536]{1,0:T(8,128)(2,1)} %k_ref.9, ...), custom_call_target="tpu_custom_call" | custom-call | bytes 1572864 | tf_op jit(solution)/shard_map/choose/pallas_call | solution.py:162
  66.0 1.6 %collective-permute-start.10 = (bf16[256,512]{1,0:T(8,128)(2,1)S(1)}, bf16[256,512]{1,0:T(8,128)(2,1)S(1)}, u32[]{:S(2)}, u32[]{:S(2)}) collective-permute-start(bf16[256,512]{1,0:T(8,128)(2,1)S(1)} %get-tuple-element.37), channel_id=1, source_target_pairs={{0,2},{1,3},{2,0},{3,1},{4,6},{5,7},{6,4},{7,5},{8,10},{9,11},{10,... | collective-permute-start | bytes 786440 | tf_op jit(solution)/shard_map/ppermute | solution.py:366
  67.6 1.9 %collective-permute-start.12 = (bf16[256,512]{1,0:T(8,128)(2,1)S(1)}, bf16[256,512]{1,0:T(8,128)(2,1)S(1)}, u32[]{:S(2)}, u32[]{:S(2)}) collective-permute-start(bf16[256,512]{1,0:T(8,128)(2,1)S(1)} %get-tuple-element.39), channel_id=1, source_target_pairs={{0,3},{1,1},{2,2},{3,0},{4,7},{5,5},{6,6},{7,4},{8,11},{9,9},{10,1... | collective-permute-start | bytes 786440 | tf_op jit(solution)/shard_map/ppermute | solution.py:366
  69.5 0.1 collective-permute-start.13
  69.6 1.2 %attend_more.3 = (f32[256,512]{1,0:T(8,128)S(1)}, f32[256,512]{1,0:T(8,128)S(1)}, f32[256,512]{1,0:T(8,128)S(1)}) custom-call(s32[10]{0:T(128)S(1)} %get-tuple-element.27.meta, bf16[256,1536]{1,0:T(8,128)(2,1)S(1)} %copy-done.2, bf16[512,512]{1,0:T(8,128)(2,1)S(1)} %collective-permute-done.4.outer.refs_1_.refs_2_, ...), custom_call_target="tpu_custom_call" | custom-call | flops 134217728 | bytes 786432 | tf_op jit(solution)/shard_map/attend_more/pallas_call | solution.py:140
  70.8 3.5 %attend_last.2.refs_12_ = bf16[256,1536]{1,0:T(8,128)(2,1)} custom-call(s32[10]{0:T(128)S(1)} %get-tuple-element.27.meta, bf16[256,1536]{1,0:T(8,128)(2,1)S(1)} %copy-done.2, bf16[256,1024]{1,0:T(8,128)(2,1)S(1)} %collective-permute-done.14.refs_1_.refs_2_, bf16[256,1024]{1,0:T(8,128)(2,1)S(1)} %collective-permute-done.14.refs_1_.refs_2_, ...), custom_call_target="tpu_custom_call" | custom-call | flops 402653184 | bytes 2097152 | tf_op jit(solution)/shard_map/attend_last/pallas_call | solution.py:140
  74.3 0.9 %collective-permute-done.12.refs_4_.refs_6_ = bf16[256,512]{1,0:T(8,128)(2,1)S(1)} collective-permute-done((bf16[256,512]{1,0:T(8,128)(2,1)S(1)}, bf16[256,512]{1,0:T(8,128)(2,1)S(1)}, u32[]{:S(2)}, u32[]{:S(2)}) %collective-permute-start.12) | collective-permute-done | bytes 262176 | tf_op jit(solution)/shard_map/ppermute | solution.py:366
  75.3 1.6 %collective-permute-done.13.refs_7_.refs_8_ = bf16[256,512]{1,0:T(8,128)(2,1)S(1)} collective-permute-done((bf16[256,512]{1,0:T(8,128)(2,1)S(1)}, bf16[256,512]{1,0:T(8,128)(2,1)S(1)}, u32[]{:S(2)}, u32[]{:S(2)}) %collective-permute-start.13) | collective-permute-done | bytes 262176 | tf_op jit(solution)/shard_map/ppermute | solution.py:366
  76.8 2.2 %attend_last.3 = bf16[256,1536]{1,0:T(8,128)(2,1)} custom-call(s32[10]{0:T(128)S(1)} %get-tuple-element.27.meta, bf16[256,1536]{1,0:T(8,128)(2,1)S(1)} %copy-done.2, bf16[256,512]{1,0:T(8,128)(2,1)S(1)} %collective-permute-done.10.refs_1_.refs_2_, bf16[256,512]{1,0:T(8,128)(2,1)S(1)} %collective-permute-done.10.refs_1_.refs_2_, ...), custom_call_target="tpu_custom_call", output_to_operand_aliasing={{}: (13, {})} | custom-call | flops 201326592 | bytes 1048576 | tf_op jit(solution)/shard_map/attend_last/pallas_call | solution.py:140
  (20 shorter events, 0.1 us)
Async XLA Ops:
  0.0 11.4 %copy-start.3 = (s32[1,8]{1,0:T(1,128)S(1)}, s32[1,8]{1,0:T(1,128)}, u32[]{:S(2)}) copy-start(s32[1,8]{1,0:T(1,128)} %list_hbm.3) | copy-start | bytes 100
  0.0 3.7 %collective-permute-start = (s32[1,8]{1,0:T(1,128)}, s32[1,8]{1,0:T(1,128)S(1)}, u32[]{:S(2)}, u32[]{:S(2)}) collective-permute-start(s32[1,8]{1,0:T(1,128)} %list_hbm.3), channel_id=1, source_target_pairs={{0,2},{1,3},{2,0},{3,1},{4,6},{5,7},{6,4},{7,5},{8,10},{9,11},{10,... | collective-permute-start | bytes 104 | tf_op jit(solution)/shard_map/ppermute | solution.py:366
  6.3 33.2 %collective-permute-start.6 = (bf16[512,1024]{1,0:T(8,128)(2,1)S(1)}, bf16[512,1024]{1,0:T(8,128)(2,1)S(1)}, u32[]{:S(2)}, u32[]{:S(2)}) collective-permute-start(bf16[512,1024]{1,0:T(8,128)(2,1)S(1)} %get-tuple-element.31), channel_id=1, source_target_pairs={{0,4},{1,5},{2,6},{3,7},{4,0},{5,1},{6,2},{7,3},{8,12},{9,13},{10,... | collective-permute-start | bytes 3145736 | tf_op jit(solution)/shard_map/ppermute | solution.py:366
  6.8 32.7 %collective-permute-start.7 = (bf16[512,1024]{1,0:T(8,128)(2,1)S(1)}, bf16[512,1024]{1,0:T(8,128)(2,1)S(1)}, u32[]{:S(2)}, u32[]{:S(2)}) collective-permute-start(bf16[512,1024]{1,0:T(8,128)(2,1)S(1)} %get-tuple-element.31), channel_id=1, source_target_pairs={{0,0},{1,1},{2,2},{3,3},{4,8},{5,9},{6,10},{7,11},{8,4},{9,5},{10,... | collective-permute-start | bytes 3145736 | tf_op jit(solution)/shard_map/ppermute | solution.py:366
  11.4 1.8 %collective-permute-start.1 = (s32[1,8]{1,0:T(1,128)S(1)}, s32[1,8]{1,0:T(1,128)S(1)}, u32[]{:S(2)}, u32[]{:S(2)}) collective-permute-start(s32[1,8]{1,0:T(1,128)S(1)} %copy-done.3), channel_id=1, source_target_pairs={{0,1},{1,0},{2,3},{3,2},{4,5},{5,4},{6,7},{7,6},{8,9},{9,8},{10,11... | collective-permute-start | bytes 104 | tf_op jit(solution)/shard_map/ppermute | solution.py:366
  11.5 20.0 %collective-permute-start.9 = (bf16[256,1536]{1,0:T(8,128)(2,1)S(1)}, bf16[256,1536]{1,0:T(8,128)(2,1)S(1)}, u32[]{:S(2)}, u32[]{:S(2)}) collective-permute-start(bf16[256,1536]{1,0:T(8,128)(2,1)S(1)} %get-tuple-element.32), channel_id=1, source_target_pairs={{0,2},{1,3},{2,0},{3,1},{4,6},{5,7},{6,4},{7,5},{8,10},{9,11},{10,... | collective-permute-start | bytes 2359304 | tf_op jit(solution)/shard_map/ppermute | solution.py:366
  13.1 1.1 %collective-permute-start.2 = (s32[1,8]{1,0:T(1,128)S(1)}, s32[1,8]{1,0:T(1,128)S(1)}, u32[]{:S(2)}, u32[]{:S(2)}) collective-permute-start(s32[1,8]{1,0:T(1,128)S(1)} %collective-permute-done.across_ref), channel_id=1, source_target_pairs={{0,1},{1,0},{2,3},{3,2},{4,5},{5,4},{6,7},{7,6},{8,9},{9,8},{10,11... | collective-permute-start | bytes 104 | tf_op jit(solution)/shard_map/ppermute | solution.py:366
  16.5 17.0 %copy-start = (bf16[256,1536]{1,0:T(8,128)(2,1)S(1)}, bf16[256,1536]{1,0:T(8,128)(2,1)}, u32[]{:S(2)}) copy-start(bf16[256,1536]{1,0:T(8,128)(2,1)} %k_ref.9) | copy-start | bytes 2359300
  16.5 17.0 %copy-start.1 = (bf16[256,1536]{1,0:T(8,128)(2,1)S(1)}, bf16[256,1536]{1,0:T(8,128)(2,1)}, u32[]{:S(2)}) copy-start(bf16[256,1536]{1,0:T(8,128)(2,1)} %v_ref.9) | copy-start | bytes 2359300
  16.5 17.0 %copy-start.2 = (bf16[256,1536]{1,0:T(8,128)(2,1)S(1)}, bf16[256,1536]{1,0:T(8,128)(2,1)}, u32[]{:S(2)}) copy-start(bf16[256,1536]{1,0:T(8,128)(2,1)} %refs_0_.9) | copy-start | bytes 2359300
  16.5 15.0 %collective-permute-start.8 = (bf16[256,1536]{1,0:T(8,128)(2,1)S(1)}, bf16[256,1536]{1,0:T(8,128)(2,1)S(1)}, u32[]{:S(2)}, u32[]{:S(2)}) collective-permute-start(bf16[256,1536]{1,0:T(8,128)(2,1)S(1)} %get-tuple-element.30.refs_0_), channel_id=1, source_target_pairs={{0,1},{1,0},{2,3},{3,2},{4,5},{5,4},{6,7},{7,6},{8,9},{9,8},{10,11... | collective-permute-start | bytes 2359304 | tf_op jit(solution)/shard_map/ppermute | solution.py:366
  17.1 22.4 %collective-permute-start.11 = (bf16[256,1536]{1,0:T(8,128)(2,1)S(1)}, bf16[256,1536]{1,0:T(8,128)(2,1)S(1)}, u32[]{:S(2)}, u32[]{:S(2)}) collective-permute-start(bf16[256,1536]{1,0:T(8,128)(2,1)S(1)} %get-tuple-element.38), channel_id=1, source_target_pairs={{0,0},{1,2},{2,1},{3,3},{4,4},{5,6},{6,5},{7,7},{8,8},{9,10},{10,9... | collective-permute-start | bytes 2359304 | tf_op jit(solution)/shard_map/ppermute | solution.py:366
  31.5 6.1 %collective-permute-start.3 = (s32[1,8]{1,0:T(1,128)S(1)}, s32[1,8]{1,0:T(1,128)S(1)}, u32[]{:S(2)}, u32[]{:S(2)}) collective-permute-start(s32[1,8]{1,0:T(1,128)S(1)} %get-tuple-element.29), channel_id=1, source_target_pairs={{8,0},{9,1},{10,2},{11,3},{0,4},{1,5},{2,6},{3,7},{12,8},{13,9},{1... | collective-permute-start | bytes 104 | tf_op jit(solution)/shard_map/ppermute | solution.py:366
  31.5 16.2 %collective-permute-start.4 = (bf16[512,512]{1,0:T(8,128)(2,1)S(1)}, bf16[512,512]{1,0:T(8,128)(2,1)S(1)}, u32[]{:S(2)}, u32[]{:S(2)}) collective-permute-start(bf16[512,512]{1,0:T(8,128)(2,1)S(1)} %pack.1), channel_id=1, source_target_pairs={{0,4},{1,5},{2,6},{3,7},{4,0},{5,1},{6,2},{7,3},{8,12},{9,13},{10,... | collective-permute-start | bytes 1572872 | tf_op jit(solution)/shard_map/ppermute | solution.py:366
  37.6 26.1 %collective-permute-start.5 = (bf16[512,512]{1,0:T(8,128)(2,1)S(1)}, bf16[512,512]{1,0:T(8,128)(2,1)S(1)}, u32[]{:S(2)}, u32[]{:S(2)}) collective-permute-start(bf16[512,512]{1,0:T(8,128)(2,1)S(1)} %pack.1), channel_id=1, source_target_pairs={{0,0},{1,1},{2,2},{3,3},{4,8},{5,9},{6,10},{7,11},{8,4},{9,5},{10,... | collective-permute-start | bytes 1572872 | tf_op jit(solution)/shard_map/ppermute | solution.py:366
  41.0 28.5 %collective-permute-start.14 = (bf16[256,1024]{1,0:T(8,128)(2,1)S(1)}, bf16[256,1024]{1,0:T(8,128)(2,1)S(1)}, u32[]{:S(2)}, u32[]{:S(2)}) collective-permute-start(bf16[256,1024]{1,0:T(8,128)(2,1)S(1)} %get-tuple-element.44), channel_id=1, source_target_pairs={{0,2},{1,3},{2,0},{3,1},{4,6},{5,7},{6,4},{7,5},{8,10},{9,11},{10,... | collective-permute-start | bytes 1572872 | tf_op jit(solution)/shard_map/ppermute | solution.py:366
  43.0 27.8 %collective-permute-start.15 = (bf16[256,1024]{1,0:T(8,128)(2,1)S(1)}, bf16[256,1024]{1,0:T(8,128)(2,1)S(1)}, u32[]{:S(2)}, u32[]{:S(2)}) collective-permute-start(bf16[256,1024]{1,0:T(8,128)(2,1)S(1)} %get-tuple-element.45), channel_id=1, source_target_pairs={{0,3},{1,1},{2,2},{3,0},{4,7},{5,5},{6,6},{7,4},{8,11},{9,9},{10,1... | collective-permute-start | bytes 1572872 | tf_op jit(solution)/shard_map/ppermute | solution.py:366
  45.0 25.9 %collective-permute-start.16 = (bf16[256,1024]{1,0:T(8,128)(2,1)S(1)}, bf16[256,1024]{1,0:T(8,128)(2,1)S(1)}, u32[]{:S(2)}, u32[]{:S(2)}) collective-permute-start(bf16[256,1024]{1,0:T(8,128)(2,1)S(1)} %get-tuple-element.46), channel_id=1, source_target_pairs={{0,8},{1,9},{2,10},{3,11},{4,0},{5,1},{6,2},{7,3},{8,12},{9,13},{1... | collective-permute-start | bytes 1572872 | tf_op jit(solution)/shard_map/ppermute | solution.py:366
  66.0 8.4 %collective-permute-start.10 = (bf16[256,512]{1,0:T(8,128)(2,1)S(1)}, bf16[256,512]{1,0:T(8,128)(2,1)S(1)}, u32[]{:S(2)}, u32[]{:S(2)}) collective-permute-start(bf16[256,512]{1,0:T(8,128)(2,1)S(1)} %get-tuple-element.37), channel_id=1, source_target_pairs={{0,2},{1,3},{2,0},{3,1},{4,6},{5,7},{6,4},{7,5},{8,10},{9,11},{10,... | collective-permute-start | bytes 786440 | tf_op jit(solution)/shard_map/ppermute | solution.py:366
  67.6 7.7 %collective-permute-start.12 = (bf16[256,512]{1,0:T(8,128)(2,1)S(1)}, bf16[256,512]{1,0:T(8,128)(2,1)S(1)}, u32[]{:S(2)}, u32[]{:S(2)}) collective-permute-start(bf16[256,512]{1,0:T(8,128)(2,1)S(1)} %get-tuple-element.39), channel_id=1, source_target_pairs={{0,3},{1,1},{2,2},{3,0},{4,7},{5,5},{6,6},{7,4},{8,11},{9,9},{10,1... | collective-permute-start | bytes 786440 | tf_op jit(solution)/shard_map/ppermute | solution.py:366
  69.5 7.3 %collective-permute-start.13 = (bf16[256,512]{1,0:T(8,128)(2,1)S(1)}, bf16[256,512]{1,0:T(8,128)(2,1)S(1)}, u32[]{:S(2)}, u32[]{:S(2)}) collective-permute-start(bf16[256,512]{1,0:T(8,128)(2,1)S(1)} %get-tuple-element.40), channel_id=1, source_target_pairs={{0,8},{1,9},{2,10},{3,11},{4,0},{5,1},{6,2},{7,3},{8,12},{9,13},{1... | collective-permute-start | bytes 786440 | tf_op jit(solution)/shard_map/ppermute | solution.py:366

commit v13 on v12

--- a/solution.py
+++ b/solution.py
@@ -213,11 +213,12 @@
     ]
 
 
-def begin(tile_lists, me, across_list, keys, values, width):
+def begin(tile_lists, me, across_list, keys, values, width, after):
     rows, all_width = keys.shape
     tile_count = rows // TILE
 
-    def build(me_ref, across_ref, list_hbm, k_ref, v_ref, meta, packed, to_across, list_ref, sems):
+    def build(me_ref, across_ref, list_hbm, k_ref, v_ref, *refs):
+        meta, packed, to_across, list_ref, sems = refs[-5:]
         read = pltpu.make_async_copy(list_hbm, list_ref, sems.at[4])
         read.start()
         me = me_ref[0]
@@ -238,8 +239,8 @@
     return move(
         "begin",
         build,
-        (me, across_list, in_hbm(tile_lists), in_hbm(keys), in_hbm(values)),
-        [SCALAR] * 2 + [WHOLE] * 3,
+        (me, across_list, in_hbm(tile_lists), in_hbm(keys), in_hbm(values), *after),
+        [SCALAR] * 2 + [WHOLE] * (3 + len(after)),
         [
             jax.ShapeDtypeStruct((10,), jnp.int32),
             jax.ShapeDtypeStruct((2 * rows, width), jnp.bfloat16),
@@ -252,15 +253,14 @@
     )
 
 
-def choose_near(meta, tile_lists, beside_list, corner_list, keys, values):
+def choose_near(meta, beside_list, corner_list, keys, values):
     rows, width = keys.shape
     tile_count = rows // TILE
 
-    def build(meta, list_hbm, beside_ref, corner_ref, k_ref, v_ref, wanted, listing, to_beside, to_corner, zeros, sems):
+    def build(meta, beside_ref, corner_ref, k_ref, v_ref, wanted, to_beside, to_corner, zeros, sems):
         even = meta[8] % 2 == 0
         own = ((k_ref, 0, 0), (v_ref, 0, 0))
         copies = tile_copies(own, tile_at(beside_ref, jnp.where(even, 0, 4), tile_count), to_beside, sems, 0)
-        copies.append(pltpu.make_async_copy(list_hbm, listing, sems.at[4]))
         for copy in copies:
             copy.start()
         wanted[0] = tile_at(corner_ref, jnp.where(even, 4, 0), tile_count)
@@ -276,16 +276,11 @@
     return move(
         "choose_near",
         build,
-        (meta, in_hbm(tile_lists), beside_list, corner_list, in_hbm(keys), in_hbm(values)),
-        [SCALAR, WHOLE] + [SCALAR] * 2 + [WHOLE] * 2,
-        [
-            jax.ShapeDtypeStruct((1,), jnp.int32),
-            jax.ShapeDtypeStruct(tile_lists.shape, jnp.int32),
-            tile,
-            tile,
-        ],
-        [SCALAR, WHOLE, WHOLE, WHOLE],
-        5,
+        (meta, beside_list, corner_list, in_hbm(keys), in_hbm(values)),
+        [SCALAR] * 3 + [WHOLE] * 2,
+        [jax.ShapeDtypeStruct((1,), jnp.int32), tile, tile],
+        [SCALAR, WHOLE, WHOLE],
+        4,
         16 * TILE * width,
         [pltpu.VMEM((TILE, width), jnp.bfloat16)],
     )
@@ -441,22 +436,20 @@
 
     me = lax.axis_index("frame").astype(jnp.int32).reshape(1)
     across_list = send(tile_lists, across)
+    far_list = send(tile_lists, [(j, i) for i, j in far])
     beside_list = send(tile_lists, beside)
     corner_list = send(across_list, beside)
     first_width = parts[0][1] * block
-    meta, first, to_across = begin(tile_lists, me, across_list, key_heads, value_heads, first_width)
+    meta, first, to_across = begin(tile_lists, me, across_list, key_heads, value_heads, first_width, [far_list])
     over = send(to_across, across)
-    corner_tile, listing, to_beside, to_corner = choose_near(
-        meta, tile_lists, beside_list, corner_list, key_heads, value_heads
-    )
-    far_list = send(listing, [(j, i) for i, j in far])
+    corner_tile, to_beside, to_corner = choose_near(meta, beside_list, corner_list, key_heads, value_heads)
     next_to = send(to_beside, beside)
     one_in = send(to_corner, corner_in)
-    second = pack(key_heads, value_heads, first_width, width - first_width, [to_beside])
+    second = pack(key_heads, value_heads, first_width, width - first_width, [over])
     near = [own_frame(), sent_tile([(next_to, 0)]), sent_tile([(over, 0)])]
     begun = attend(queries, meta, near, 0, width // block, heads)
 
-    after = [begun[0], one_in]
+    after = [begun[0]]
     middles, finals = [], []
     for (at, steps), packed in zip(parts, (first, second)):
         from_outer = send(packed, outer)

time: 79.9 us -> 75.1 us (0.940)
  waiting for transfers between devices: 34.1 us -> 25.6 us
  starting transfers between devices: 21.4 us -> 24.5 us
    ppermute x17, waiting for transfers between devices: 34.1 us -> 25.6 us  [send(): return lax.ppermute(array, 'frame', route)]
    ppermute x17, starting transfers between devices: 21.4 us -> 24.5 us  [send(): return lax.ppermute(array, 'frame', route)]
  transfers between devices with their start and end apart: 17 -> 17, of which waited for: 6 -> 8; matrix products, arithmetic and copies ran while one was open for 0% -> 0% of each run, Pallas kernels for 23% -> 25%
where the time goes in v13:
time: 75.1 us; the launch traced here: 73.7 us
  waiting for transfers between devices  25.6 us (34%)
  starting transfers between devices  24.5 us (33%)
  Pallas kernels  23.4 us (31%)
    ppermute x17, waiting for transfers between devices, send(): return lax.ppermute(array, 'frame', route)  25.6 us
    ppermute x17, starting transfers between devices, send(): return lax.ppermute(array, 'frame', route)  24.5 us
    pallas_call x5, Pallas kernels, attend(): pl.pallas_call(functools.partial(attend_kernel, plan, heads, carry is not...  13.7 us
    pallas_call x5, Pallas kernels, move(): pl.pallas_call(build, name=name, out_shape=out_shape, in_specs=specs, out...  9.71 us
  transfers between devices with their start and end apart: 17, of which 8 were waited for; matrix products, arithmetic and copies ran while one was open for 0% of the time, Pallas kernels for 25%

profile of v13, /device:TPU:12, one launch (start us, length us, event | category | flops | bytes accessed | tf_op | source)
XLA Modules:
  0.0 73.7 jit_solution(10703737618240018983)
XLA Ops:
  0.0 2.6 %collective-permute-start.1 = (s32[1,8]{1,0:T(1,128)}, s32[1,8]{1,0:T(1,128)S(1)}, u32[]{:S(2)}, u32[]{:S(2)}) collective-permute-start(s32[1,8]{1,0:T(1,128)} %list_hbm.1), channel_id=1, source_target_pairs={{8,0},{9,1},{10,2},{11,3},{0,4},{1,5},{2,6},{3,7},{12,8},{13,9},{1... | collective-permute-start | bytes 104 | tf_op jit(solution)/shard_map/ppermute | solution.py:361
  2.6 1.5 %collective-permute-start = (s32[1,8]{1,0:T(1,128)}, s32[1,8]{1,0:T(1,128)S(1)}, u32[]{:S(2)}, u32[]{:S(2)}) collective-permute-start(s32[1,8]{1,0:T(1,128)} %list_hbm.1), channel_id=1, source_target_pairs={{0,2},{1,3},{2,0},{3,1},{4,6},{5,7},{6,4},{7,5},{8,10},{9,11},{10,... | collective-permute-start | bytes 104 | tf_op jit(solution)/shard_map/ppermute | solution.py:361
  4.1 2.2 %collective-permute-done.across_ref = s32[1,8]{1,0:T(1,128)S(1)} collective-permute-done((s32[1,8]{1,0:T(1,128)}, s32[1,8]{1,0:T(1,128)S(1)}, u32[]{:S(2)}, u32[]{:S(2)}) %collective-permute-start) | collective-permute-done | bytes 64 | tf_op jit(solution)/shard_map/ppermute | solution.py:361
  6.3 2.6 %begin.1 = (s32[10]{0:T(128)S(1)}, bf16[512,1024]{1,0:T(8,128)(2,1)S(1)}, bf16[256,1536]{1,0:T(8,128)(2,1)S(1)}) custom-call(s32[1]{0:T(128)} %bitcast.me_ref, s32[1,8]{1,0:T(1,128)S(1)} %collective-permute-done.across_ref, s32[1,8]{1,0:T(1,128)} %list_hbm.1, bf16[256,1536]{1,0:T(8,128)(2,1)} %k_ref.9, bf16[256,1536]{1,0:T(8,128)(2,1)} %v_ref.9, ...), custom_call_target="tpu_custom_call" | custom-call | bytes 3670016 | tf_op jit(solution)/shard_map/begin/pallas_call | solution.py:162
  8.9 1.5 %collective-permute-start.4 = (bf16[256,1536]{1,0:T(8,128)(2,1)S(1)}, bf16[256,1536]{1,0:T(8,128)(2,1)S(1)}, u32[]{:S(2)}, u32[]{:S(2)}) collective-permute-start(bf16[256,1536]{1,0:T(8,128)(2,1)S(1)} %get-tuple-element.28), channel_id=1, source_target_pairs={{0,2},{1,3},{2,0},{3,1},{4,6},{5,7},{6,4},{7,5},{8,10},{9,11},{10,... | collective-permute-start | bytes 2359304 | tf_op jit(solution)/shard_map/ppermute | solution.py:361
  10.4 3.4 %collective-permute-start.8 = (bf16[512,1024]{1,0:T(8,128)(2,1)S(1)}, bf16[512,1024]{1,0:T(8,128)(2,1)S(1)}, u32[]{:S(2)}, u32[]{:S(2)}) collective-permute-start(bf16[512,1024]{1,0:T(8,128)(2,1)S(1)} %get-tuple-element.29), channel_id=1, source_target_pairs={{0,0},{1,1},{2,2},{3,3},{4,8},{5,9},{6,10},{7,11},{8,4},{9,5},{10,... | collective-permute-start | bytes 3145736 | tf_op jit(solution)/shard_map/ppermute | solution.py:361
  13.8 0.1 collective-permute-start.2
  13.9 0.5 collective-permute-start.3
  14.4 0.6 collective-permute-done.2.beside_ref
  15.0 0.2 collective-permute-done.3.corner_ref
  15.2 2.2 %choose_near.1 = (s32[1]{0:T(128)}, bf16[256,1536]{1,0:T(8,128)(2,1)S(1)}, bf16[256,1536]{1,0:T(8,128)(2,1)S(1)}) custom-call(s32[10]{0:T(128)S(1)} %get-tuple-element.26.meta, s32[1,8]{1,0:T(1,128)S(1)} %collective-permute-done.2.beside_ref, s32[1,8]{1,0:T(1,128)S(1)} %collective-permute-done.3.corner_ref, bf16[256,1536]{1,0:T(8,128)(2,1)} %k_ref.9, ...), custom_call_target="tpu_custom_call" | custom-call | bytes 3145728 | tf_op jit(solution)/shard_map/choose_near/pallas_call | solution.py:162
  17.5 0.6 collective-permute-start.9
  18.1 8.7 %collective-permute-done.4.refs_0_.refs_5_.refs_6_ = bf16[256,1536]{1,0:T(8,128)(2,1)S(1)} collective-permute-done((bf16[256,1536]{1,0:T(8,128)(2,1)S(1)}, bf16[256,1536]{1,0:T(8,128)(2,1)S(1)}, u32[]{:S(2)}, u32[]{:S(2)}) %collective-permute-start.4) | collective-permute-done | bytes 786464 | tf_op jit(solution)/shard_map/ppermute | solution.py:361
  26.8 1.1 %pack.1 = bf16[512,512]{1,0:T(8,128)(2,1)S(1)} custom-call(bf16[256,1536]{1,0:T(8,128)(2,1)} %k_ref.9, bf16[256,1536]{1,0:T(8,128)(2,1)} %v_ref.9, bf16[256,1536]{1,0:T(8,128)(2,1)S(1)} %collective-permute-done.4.refs_0_.refs_5_.refs_6_), custom_call_target="tpu_custom_call" | custom-call | bytes 1048576 | tf_op jit(solution)/shard_map/pack/pallas_call | solution.py:162
  27.9 0.1 collective-permute-start.5
  28.0 0.7 collective-permute-start.11
  28.7 3.6 %collective-permute-start.6 = (bf16[512,512]{1,0:T(8,128)(2,1)S(1)}, bf16[512,512]{1,0:T(8,128)(2,1)S(1)}, u32[]{:S(2)}, u32[]{:S(2)}) collective-permute-start(bf16[512,512]{1,0:T(8,128)(2,1)S(1)} %pack.1), channel_id=1, source_target_pairs={{0,0},{1,1},{2,2},{3,3},{4,8},{5,9},{6,10},{7,11},{8,4},{9,5},{10,... | collective-permute-start | bytes 1572872 | tf_op jit(solution)/shard_map/ppermute | solution.py:361
  32.4 4.1 %attend_own.1 = (f32[256,1536]{1,0:T(8,128)S(1)}, f32[256,1536]{1,0:T(8,128)S(1)}, f32[256,1536]{1,0:T(8,128)S(1)}) custom-call(s32[10]{0:T(128)S(1)} %get-tuple-element.26.meta, bf16[256,1536]{1,0:T(8,128)(2,1)S(1)} %copy-done.2, bf16[256,1536]{1,0:T(8,128)(2,1)S(1)} %copy-done, bf16[256,1536]{1,0:T(8,128)(2,1)S(1)} %copy-done.1, ...), custom_call_target="tpu_custom_call" | custom-call | flops 805306368 | bytes 3932160 | tf_op jit(solution)/shard_map/attend_own/pallas_call | solution.py:140
  36.5 1.4 %choose.3 = (bf16[256,1024]{1,0:T(8,128)(2,1)S(1)}, bf16[256,1024]{1,0:T(8,128)(2,1)S(1)}, bf16[256,1024]{1,0:T(8,128)(2,1)S(1)}) custom-call(s32[10]{0:T(128)S(1)} %get-tuple-element.26.meta, s32[1]{0:T(128)} %get-tuple-element.27.corner_ref, s32[1,8]{1,0:T(1,128)S(1)} %collective-permute-done.1.refs_0_.far_ref, bf16[256,1536]{1,0:T(8,128)(2,1)} %k_ref.9, ...), custom_call_target="tpu_custom_call" | custom-call | bytes 3145728 | tf_op jit(solution)/shard_map/choose/pallas_call | solution.py:162
  38.0 2.7 %collective-permute-start.14 = (bf16[256,1024]{1,0:T(8,128)(2,1)S(1)}, bf16[256,1024]{1,0:T(8,128)(2,1)S(1)}, u32[]{:S(2)}, u32[]{:S(2)}) collective-permute-start(bf16[256,1024]{1,0:T(8,128)(2,1)S(1)} %get-tuple-element.42), channel_id=1, source_target_pairs={{0,2},{1,3},{2,0},{3,1},{4,6},{5,7},{6,4},{7,5},{8,10},{9,11},{10,... | collective-permute-start | bytes 1572872 | tf_op jit(solution)/shard_map/ppermute | solution.py:361
  40.7 3.1 %collective-permute-start.15 = (bf16[256,1024]{1,0:T(8,128)(2,1)S(1)}, bf16[256,1024]{1,0:T(8,128)(2,1)S(1)}, u32[]{:S(2)}, u32[]{:S(2)}) collective-permute-start(bf16[256,1024]{1,0:T(8,128)(2,1)S(1)} %get-tuple-element.43), channel_id=1, source_target_pairs={{0,3},{1,1},{2,2},{3,0},{4,7},{5,5},{6,6},{7,4},{8,11},{9,9},{10,1... | collective-permute-start | bytes 1572872 | tf_op jit(solution)/shard_map/ppermute | solution.py:361
  43.8 1.2 %collective-permute-done.5.outer.refs_1_.refs_2_ = bf16[512,512]{1,0:T(8,128)(2,1)S(1)} collective-permute-done((bf16[512,512]{1,0:T(8,128)(2,1)S(1)}, bf16[512,512]{1,0:T(8,128)(2,1)S(1)}, u32[]{:S(2)}, u32[]{:S(2)}) %collective-permute-start.5) | collective-permute-done | bytes 524320 | tf_op jit(solution)/shard_map/ppermute | solution.py:361
  45.0 0.1 collective-permute-start.16
  45.1 2.6 %attend_more.2 = (f32[256,1024]{1,0:T(8,128)S(1)}, f32[256,1024]{1,0:T(8,128)S(1)}, f32[256,1024]{1,0:T(8,128)S(1)}) custom-call(s32[10]{0:T(128)S(1)} %get-tuple-element.26.meta, bf16[256,1536]{1,0:T(8,128)(2,1)S(1)} %copy-done.2, bf16[512,1024]{1,0:T(8,128)(2,1)S(1)} %collective-permute-done.7.refs_1_.refs_2_.outer, ...), custom_call_target="tpu_custom_call" | custom-call | flops 268435456 | bytes 1572864 | tf_op jit(solution)/shard_map/attend_more/pallas_call | solution.py:140
  47.8 9.7 %collective-permute-done.6.inner.refs_3_.refs_4_ = bf16[512,512]{1,0:T(8,128)(2,1)S(1)} collective-permute-done((bf16[512,512]{1,0:T(8,128)(2,1)S(1)}, bf16[512,512]{1,0:T(8,128)(2,1)S(1)}, u32[]{:S(2)}, u32[]{:S(2)}) %collective-permute-start.6) | collective-permute-done | bytes 524320 | tf_op jit(solution)/shard_map/ppermute | solution.py:361
  57.4 2.3 %choose.2 = (bf16[256,512]{1,0:T(8,128)(2,1)S(1)}, bf16[256,512]{1,0:T(8,128)(2,1)S(1)}, bf16[256,512]{1,0:T(8,128)(2,1)S(1)}) custom-call(s32[10]{0:T(128)S(1)} %get-tuple-element.26.meta, s32[1]{0:T(128)} %get-tuple-element.27.corner_ref, s32[1,8]{1,0:T(1,128)S(1)} %collective-permute-done.1.refs_0_.far_ref, bf16[256,1536]{1,0:T(8,128)(2,1)} %k_ref.9, ...), custom_call_target="tpu_custom_call" | custom-call | bytes 1572864 | tf_op jit(solution)/shard_map/choose/pallas_call | solution.py:162
  59.9 3.9 %collective-permute-start.12 = (bf16[256,512]{1,0:T(8,128)(2,1)S(1)}, bf16[256,512]{1,0:T(8,128)(2,1)S(1)}, u32[]{:S(2)}, u32[]{:S(2)}) collective-permute-start(bf16[256,512]{1,0:T(8,128)(2,1)S(1)} %get-tuple-element.37), channel_id=1, source_target_pairs={{0,3},{1,1},{2,2},{3,0},{4,7},{5,5},{6,6},{7,4},{8,11},{9,9},{10,1... | collective-permute-start | bytes 786440 | tf_op jit(solution)/shard_map/ppermute | solution.py:361
  63.8 1.2 %attend_more.3 = (f32[256,512]{1,0:T(8,128)S(1)}, f32[256,512]{1,0:T(8,128)S(1)}, f32[256,512]{1,0:T(8,128)S(1)}) custom-call(s32[10]{0:T(128)S(1)} %get-tuple-element.26.meta, bf16[256,1536]{1,0:T(8,128)(2,1)S(1)} %copy-done.2, bf16[512,512]{1,0:T(8,128)(2,1)S(1)} %collective-permute-done.5.outer.refs_1_.refs_2_, ...), custom_call_target="tpu_custom_call" | custom-call | flops 134217728 | bytes 786432 | tf_op jit(solution)/shard_map/attend_more/pallas_call | solution.py:140
  65.1 3.5 %attend_last.2.refs_12_ = bf16[256,1536]{1,0:T(8,128)(2,1)} custom-call(s32[10]{0:T(128)S(1)} %get-tuple-element.26.meta, bf16[256,1536]{1,0:T(8,128)(2,1)S(1)} %copy-done.2, bf16[256,1024]{1,0:T(8,128)(2,1)S(1)} %collective-permute-done.14.refs_1_.refs_2_, bf16[256,1024]{1,0:T(8,128)(2,1)S(1)} %collective-permute-done.14.refs_1_.refs_2_, ...), custom_call_target="tpu_custom_call" | custom-call | flops 402653184 | bytes 2097152 | tf_op jit(solution)/shard_map/attend_last/pallas_call | solution.py:140
  68.6 0.4 collective-permute-done.10.refs_1_.refs_2_
  69.0 2.5 %collective-permute-done.12.refs_4_.refs_6_ = bf16[256,512]{1,0:T(8,128)(2,1)S(1)} collective-permute-done((bf16[256,512]{1,0:T(8,128)(2,1)S(1)}, bf16[256,512]{1,0:T(8,128)(2,1)S(1)}, u32[]{:S(2)}, u32[]{:S(2)}) %collective-permute-start.12) | collective-permute-done | bytes 262176 | tf_op jit(solution)/shard_map/ppermute | solution.py:361
  71.5 2.2 %attend_last.3 = bf16[256,1536]{1,0:T(8,128)(2,1)} custom-call(s32[10]{0:T(128)S(1)} %get-tuple-element.26.meta, bf16[256,1536]{1,0:T(8,128)(2,1)S(1)} %copy-done.2, bf16[256,512]{1,0:T(8,128)(2,1)S(1)} %collective-permute-done.10.refs_1_.refs_2_, bf16[256,512]{1,0:T(8,128)(2,1)S(1)} %collective-permute-done.10.refs_1_.refs_2_, ...), custom_call_target="tpu_custom_call", output_to_operand_aliasing={{}: (13, {})} | custom-call | flops 201326592 | bytes 1048576 | tf_op jit(solution)/shard_map/attend_last/pallas_call | solution.py:140
  (20 shorter events, 0.2 us)
Async XLA Ops:
  0.0 13.8 %copy-start.3 = (s32[1,8]{1,0:T(1,128)S(1)}, s32[1,8]{1,0:T(1,128)}, u32[]{:S(2)}) copy-start(s32[1,8]{1,0:T(1,128)} %list_hbm.1) | copy-start | bytes 100
  0.0 4.1 %collective-permute-start.1 = (s32[1,8]{1,0:T(1,128)}, s32[1,8]{1,0:T(1,128)S(1)}, u32[]{:S(2)}, u32[]{:S(2)}) collective-permute-start(s32[1,8]{1,0:T(1,128)} %list_hbm.1), channel_id=1, source_target_pairs={{8,0},{9,1},{10,2},{11,3},{0,4},{1,5},{2,6},{3,7},{12,8},{13,9},{1... | collective-permute-start | bytes 104 | tf_op jit(solution)/shard_map/ppermute | solution.py:361
  2.6 3.7 %collective-permute-start = (s32[1,8]{1,0:T(1,128)}, s32[1,8]{1,0:T(1,128)S(1)}, u32[]{:S(2)}, u32[]{:S(2)}) collective-permute-start(s32[1,8]{1,0:T(1,128)} %list_hbm.1), channel_id=1, source_target_pairs={{0,2},{1,3},{2,0},{3,1},{4,6},{5,7},{6,4},{7,5},{8,10},{9,11},{10,... | collective-permute-start | bytes 104 | tf_op jit(solution)/shard_map/ppermute | solution.py:361
  8.9 17.9 %collective-permute-start.4 = (bf16[256,1536]{1,0:T(8,128)(2,1)S(1)}, bf16[256,1536]{1,0:T(8,128)(2,1)S(1)}, u32[]{:S(2)}, u32[]{:S(2)}) collective-permute-start(bf16[256,1536]{1,0:T(8,128)(2,1)S(1)} %get-tuple-element.28), channel_id=1, source_target_pairs={{0,2},{1,3},{2,0},{3,1},{4,6},{5,7},{6,4},{7,5},{8,10},{9,11},{10,... | collective-permute-start | bytes 2359304 | tf_op jit(solution)/shard_map/ppermute | solution.py:361
  10.4 26.1 %collective-permute-start.7 = (bf16[512,1024]{1,0:T(8,128)(2,1)S(1)}, bf16[512,1024]{1,0:T(8,128)(2,1)S(1)}, u32[]{:S(2)}, u32[]{:S(2)}) collective-permute-start(bf16[512,1024]{1,0:T(8,128)(2,1)S(1)} %get-tuple-element.29), channel_id=1, source_target_pairs={{0,4},{1,5},{2,6},{3,7},{4,0},{5,1},{6,2},{7,3},{8,12},{9,13},{10,... | collective-permute-start | bytes 3145736 | tf_op jit(solution)/shard_map/ppermute | solution.py:361
  10.4 26.1 %collective-permute-start.8 = (bf16[512,1024]{1,0:T(8,128)(2,1)S(1)}, bf16[512,1024]{1,0:T(8,128)(2,1)S(1)}, u32[]{:S(2)}, u32[]{:S(2)}) collective-permute-start(bf16[512,1024]{1,0:T(8,128)(2,1)S(1)} %get-tuple-element.29), channel_id=1, source_target_pairs={{0,0},{1,1},{2,2},{3,3},{4,8},{5,9},{6,10},{7,11},{8,4},{9,5},{10,... | collective-permute-start | bytes 3145736 | tf_op jit(solution)/shard_map/ppermute | solution.py:361
  13.8 1.2 %collective-permute-start.2 = (s32[1,8]{1,0:T(1,128)S(1)}, s32[1,8]{1,0:T(1,128)S(1)}, u32[]{:S(2)}, u32[]{:S(2)}) collective-permute-start(s32[1,8]{1,0:T(1,128)S(1)} %copy-done.3), channel_id=1, source_target_pairs={{0,1},{1,0},{2,3},{3,2},{4,5},{5,4},{6,7},{7,6},{8,9},{9,8},{10,11... | collective-permute-start | bytes 104 | tf_op jit(solution)/shard_map/ppermute | solution.py:361
  13.9 1.3 %collective-permute-start.3 = (s32[1,8]{1,0:T(1,128)S(1)}, s32[1,8]{1,0:T(1,128)S(1)}, u32[]{:S(2)}, u32[]{:S(2)}) collective-permute-start(s32[1,8]{1,0:T(1,128)S(1)} %collective-permute-done.across_ref), channel_id=1, source_target_pairs={{0,1},{1,0},{2,3},{3,2},{4,5},{5,4},{6,7},{7,6},{8,9},{9,8},{10,11... | collective-permute-start | bytes 104 | tf_op jit(solution)/shard_map/ppermute | solution.py:361
  17.5 14.9 %copy-start = (bf16[256,1536]{1,0:T(8,128)(2,1)S(1)}, bf16[256,1536]{1,0:T(8,128)(2,1)}, u32[]{:S(2)}) copy-start(bf16[256,1536]{1,0:T(8,128)(2,1)} %k_ref.9) | copy-start | bytes 2359300
  17.5 14.9 %copy-start.1 = (bf16[256,1536]{1,0:T(8,128)(2,1)S(1)}, bf16[256,1536]{1,0:T(8,128)(2,1)}, u32[]{:S(2)}) copy-start(bf16[256,1536]{1,0:T(8,128)(2,1)} %v_ref.9) | copy-start | bytes 2359300
  17.5 14.9 %copy-start.2 = (bf16[256,1536]{1,0:T(8,128)(2,1)S(1)}, bf16[256,1536]{1,0:T(8,128)(2,1)}, u32[]{:S(2)}) copy-start(bf16[256,1536]{1,0:T(8,128)(2,1)} %refs_0_.9) | copy-start | bytes 2359300
  17.5 11.2 %collective-permute-start.9 = (bf16[256,1536]{1,0:T(8,128)(2,1)S(1)}, bf16[256,1536]{1,0:T(8,128)(2,1)S(1)}, u32[]{:S(2)}, u32[]{:S(2)}) collective-permute-start(bf16[256,1536]{1,0:T(8,128)(2,1)S(1)} %get-tuple-element.30), channel_id=1, source_target_pairs={{0,1},{1,0},{2,3},{3,2},{4,5},{5,4},{6,7},{7,6},{8,9},{9,8},{10,11... | collective-permute-start | bytes 2359304 | tf_op jit(solution)/shard_map/ppermute | solution.py:361
  27.9 17.1 %collective-permute-start.5 = (bf16[512,512]{1,0:T(8,128)(2,1)S(1)}, bf16[512,512]{1,0:T(8,128)(2,1)S(1)}, u32[]{:S(2)}, u32[]{:S(2)}) collective-permute-start(bf16[512,512]{1,0:T(8,128)(2,1)S(1)} %pack.1), channel_id=1, source_target_pairs={{0,4},{1,5},{2,6},{3,7},{4,0},{5,1},{6,2},{7,3},{8,12},{9,13},{10,... | collective-permute-start | bytes 1572872 | tf_op jit(solution)/shard_map/ppermute | solution.py:361
  28.0 31.8 %collective-permute-start.11 = (bf16[256,1536]{1,0:T(8,128)(2,1)S(1)}, bf16[256,1536]{1,0:T(8,128)(2,1)S(1)}, u32[]{:S(2)}, u32[]{:S(2)}) collective-permute-start(bf16[256,1536]{1,0:T(8,128)(2,1)S(1)} %get-tuple-element.36), channel_id=1, source_target_pairs={{0,0},{1,2},{2,1},{3,3},{4,4},{5,6},{6,5},{7,7},{8,8},{9,10},{10,9... | collective-permute-start | bytes 2359304 | tf_op jit(solution)/shard_map/ppermute | solution.py:361
  28.7 28.7 %collective-permute-start.6 = (bf16[512,512]{1,0:T(8,128)(2,1)S(1)}, bf16[512,512]{1,0:T(8,128)(2,1)S(1)}, u32[]{:S(2)}, u32[]{:S(2)}) collective-permute-start(bf16[512,512]{1,0:T(8,128)(2,1)S(1)} %pack.1), channel_id=1, source_target_pairs={{0,0},{1,1},{2,2},{3,3},{4,8},{5,9},{6,10},{7,11},{8,4},{9,5},{10,... | collective-permute-start | bytes 1572872 | tf_op jit(solution)/shard_map/ppermute | solution.py:361
  38.0 25.8 %collective-permute-start.14 = (bf16[256,1024]{1,0:T(8,128)(2,1)S(1)}, bf16[256,1024]{1,0:T(8,128)(2,1)S(1)}, u32[]{:S(2)}, u32[]{:S(2)}) collective-permute-start(bf16[256,1024]{1,0:T(8,128)(2,1)S(1)} %get-tuple-element.42), channel_id=1, source_target_pairs={{0,2},{1,3},{2,0},{3,1},{4,6},{5,7},{6,4},{7,5},{8,10},{9,11},{10,... | collective-permute-start | bytes 1572872 | tf_op jit(solution)/shard_map/ppermute | solution.py:361
  40.7 24.4 %collective-permute-start.15 = (bf16[256,1024]{1,0:T(8,128)(2,1)S(1)}, bf16[256,1024]{1,0:T(8,128)(2,1)S(1)}, u32[]{:S(2)}, u32[]{:S(2)}) collective-permute-start(bf16[256,1024]{1,0:T(8,128)(2,1)S(1)} %get-tuple-element.43), channel_id=1, source_target_pairs={{0,3},{1,1},{2,2},{3,0},{4,7},{5,5},{6,6},{7,4},{8,11},{9,9},{10,1... | collective-permute-start | bytes 1572872 | tf_op jit(solution)/shard_map/ppermute | solution.py:361
  45.0 20.1 %collective-permute-start.16 = (bf16[256,1024]{1,0:T(8,128)(2,1)S(1)}, bf16[256,1024]{1,0:T(8,128)(2,1)S(1)}, u32[]{:S(2)}, u32[]{:S(2)}) collective-permute-start(bf16[256,1024]{1,0:T(8,128)(2,1)S(1)} %get-tuple-element.44), channel_id=1, source_target_pairs={{0,8},{1,9},{2,10},{3,11},{4,0},{5,1},{6,2},{7,3},{8,12},{9,13},{1... | collective-permute-start | bytes 1572872 | tf_op jit(solution)/shard_map/ppermute | solution.py:361
  59.8 9.2 %collective-permute-start.10 = (bf16[256,512]{1,0:T(8,128)(2,1)S(1)}, bf16[256,512]{1,0:T(8,128)(2,1)S(1)}, u32[]{:S(2)}, u32[]{:S(2)}) collective-permute-start(bf16[256,512]{1,0:T(8,128)(2,1)S(1)} %get-tuple-element.35), channel_id=1, source_target_pairs={{0,2},{1,3},{2,0},{3,1},{4,6},{5,7},{6,4},{7,5},{8,10},{9,11},{10,... | collective-permute-start | bytes 786440 | tf_op jit(solution)/shard_map/ppermute | solution.py:361
  59.9 11.7 %collective-permute-start.12 = (bf16[256,512]{1,0:T(8,128)(2,1)S(1)}, bf16[256,512]{1,0:T(8,128)(2,1)S(1)}, u32[]{:S(2)}, u32[]{:S(2)}) collective-permute-start(bf16[256,512]{1,0:T(8,128)(2,1)S(1)} %get-tuple-element.37), channel_id=1, source_target_pairs={{0,3},{1,1},{2,2},{3,0},{4,7},{5,5},{6,6},{7,4},{8,11},{9,9},{10,1... | collective-permute-start | bytes 786440 | tf_op jit(solution)/shard_map/ppermute | solution.py:361
  63.8 7.8 %collective-permute-start.13 = (bf16[256,512]{1,0:T(8,128)(2,1)S(1)}, bf16[256,512]{1,0:T(8,128)(2,1)S(1)}, u32[]{:S(2)}, u32[]{:S(2)}) collective-permute-start(bf16[256,512]{1,0:T(8,128)(2,1)S(1)} %get-tuple-element.38), channel_id=1, source_target_pairs={{0,8},{1,9},{2,10},{3,11},{4,0},{5,1},{6,2},{7,3},{8,12},{9,13},{1... | collective-permute-start | bytes 786440 | tf_op jit(solution)/shard_map/ppermute | solution.py:361

commit v14 on v10

--- a/solution.py
+++ b/solution.py
@@ -497,7 +497,7 @@
     begun = attend(queries, meta, near, 0, width // block, heads)
 
     after, wants = [begun[0], one_in], None
-    middles, finals = [], []
+    calls = []
     for (at, steps), packed in zip(parts, (first, second)):
         from_outer = send(packed, outer)
         from_inner = send(packed, inner)
@@ -507,32 +507,19 @@
         two = send(sent[0], across)
         one = send(sent[1], corner_out)
         far = [send(sent[2], outer), send(sent[3], inner)]
-        middle = attend(
-            queries,
-            meta,
-            [
-                tile_of(from_outer, outer_tile),
-                tile_of(from_inner, inner_tile, inner_there),
-            ],
-            at,
-            steps,
-            heads,
-            begun,
-            held=at,
-        )
-        after = [middle[0]]
-        middles.append(middle)
-        finals.append(
-            [
-                sent_tile([(two, 0)], two_there),
-                sent_tile([(one_in, at), (one, 0)], one_there),
-                sent_tile([(a, 0) for a in far]),
-            ]
-        )
-    out = None
-    for (at, steps), sources, middle in zip(parts, finals, middles):
-        out = attend(queries, meta, sources, at, steps, heads, middle, True, out)
-    return out
+        z_tiles = [tile_of(from_outer, outer_tile), tile_of(from_inner, inner_tile, inner_there)]
+        late_tiles = [
+            sent_tile([(two, 0)], two_there),
+            sent_tile([(one_in, at), (one, 0)], one_there),
+            sent_tile([(a, 0) for a in far]),
+        ]
+        after = []
+        calls.append((at, steps, z_tiles, late_tiles))
+    at, steps, z_tiles, late_tiles = calls[0]
+    out = attend(queries, meta, z_tiles + late_tiles, at, steps, heads, begun, True, held=at)
+    at, steps, z_tiles, late_tiles = calls[1]
+    middle = attend(queries, meta, z_tiles, at, steps, heads, begun, held=at)
+    return attend(queries, meta, late_tiles, at, steps, heads, middle, True, out)
 
 
 def solution(mesh):

time: 70.5 us -> 70.4 us (level)
  starting transfers between devices: 22.7 us -> 30 us
  waiting for transfers between devices: 22.4 us -> 16.5 us
  Pallas kernels: 24.7 us -> 23.3 us
    ppermute x18, starting transfers between devices: 22.7 us -> 30 us  [send(): return lax.ppermute(array, 'frame', route)]
    ppermute x18, waiting for transfers between devices: 22.4 us -> 16.5 us  [send(): return lax.ppermute(array, 'frame', route)]
    pallas_call x5 -> x4, Pallas kernels: 13.9 us -> 12.4 us  [attend(): pl.pallas_call(functools.partial(attend_kernel, plan, heads, carry is not...]
  transfers between devices with their start and end apart: 18 -> 18, of which waited for: 9 -> 7; matrix products, arithmetic and copies ran while one was open for 0% -> 0% of each run, Pallas kernels for 28% -> 26%
where the time goes in v14:
time: 70.4 us; the launch traced here: 70 us
  starting transfers between devices  30 us (43%)
  Pallas kernels  23.3 us (33%)
  waiting for transfers between devices  16.5 us (23%)
    ppermute x18, starting transfers between devices, send(): return lax.ppermute(array, 'frame', route)  30 us
    ppermute x18, waiting for transfers between devices, send(): return lax.ppermute(array, 'frame', route)  16.5 us
    pallas_call x4, Pallas kernels, attend(): pl.pallas_call(functools.partial(attend_kernel, plan, heads, carry is not...  12.4 us
    pallas_call x5, Pallas kernels, move(): pl.pallas_call(build, name=name, out_shape=out_shape, in_specs=specs, out...  10.9 us
  transfers between devices with their start and end apart: 18, of which 7 were waited for; matrix products, arithmetic and copies ran while one was open for 0% of the time, Pallas kernels for 26%

profile of v14, /device:TPU:12, one launch (start us, length us, event | category | flops | bytes accessed | tf_op | source)
XLA Modules:
  0.0 70.0 jit_solution(458535079014896816)
XLA Ops:
  0.0 1.5 %collective-permute-start = (s32[1,8]{1,0:T(1,128)}, s32[1,8]{1,0:T(1,128)S(1)}, u32[]{:S(2)}, u32[]{:S(2)}) collective-permute-start(s32[1,8]{1,0:T(1,128)} %list_hbm.1), channel_id=1, source_target_pairs={{0,2},{1,3},{2,0},{3,1},{4,6},{5,7},{6,4},{7,5},{8,10},{9,11},{10,... | collective-permute-start | bytes 104 | tf_op jit(solution)/shard_map/ppermute | solution.py:410
  1.5 2.2 %collective-permute-done.across_ref = s32[1,8]{1,0:T(1,128)S(1)} collective-permute-done((s32[1,8]{1,0:T(1,128)}, s32[1,8]{1,0:T(1,128)S(1)}, u32[]{:S(2)}, u32[]{:S(2)}) %collective-permute-start) | collective-permute-done | bytes 64 | tf_op jit(solution)/shard_map/ppermute | solution.py:410
  3.7 2.6 %begin.1 = (s32[10]{0:T(128)S(1)}, bf16[528,1024]{1,0:T(8,128)(2,1)S(1)}, bf16[256,1536]{1,0:T(8,128)(2,1)S(1)}) custom-call(s32[1]{0:T(128)} %bitcast.me_ref, s32[1,8]{1,0:T(1,128)S(1)} %collective-permute-done.across_ref, s32[1,8]{1,0:T(1,128)} %list_hbm.1, bf16[256,1536]{1,0:T(8,128)(2,1)} %k_ref.5, bf16[256,1536]{1,0:T(8,128)(2,1)} %v_ref.5), custom_call_target="tpu_custom_call" | custom-call | bytes 3670016 | tf_op jit(solution)/shard_map/begin/pallas_call | solution.py:163
  6.3 1.6 %collective-permute-start.6 = (bf16[256,1536]{1,0:T(8,128)(2,1)S(1)}, bf16[256,1536]{1,0:T(8,128)(2,1)S(1)}, u32[]{:S(2)}, u32[]{:S(2)}) collective-permute-start(bf16[256,1536]{1,0:T(8,128)(2,1)S(1)} %get-tuple-element.30), channel_id=1, source_target_pairs={{0,2},{1,3},{2,0},{3,1},{4,6},{5,7},{6,4},{7,5},{8,10},{9,11},{10,... | collective-permute-start | bytes 2359304 | tf_op jit(solution)/shard_map/ppermute | solution.py:410
  7.9 0.4 collective-permute-start.3
  8.3 4.6 %collective-permute-start.4 = (bf16[528,1024]{1,0:T(8,128)(2,1)S(1)}, bf16[528,1024]{1,0:T(8,128)(2,1)S(1)}, u32[]{:S(2)}, u32[]{:S(2)}) collective-permute-start(bf16[528,1024]{1,0:T(8,128)(2,1)S(1)} %get-tuple-element.28), channel_id=1, source_target_pairs={{0,0},{1,1},{2,2},{3,3},{4,8},{5,9},{6,10},{7,11},{8,4},{9,5},{10,... | collective-permute-start | bytes 3244040 | tf_op jit(solution)/shard_map/ppermute | solution.py:410
  13.0 0.1 collective-permute-start.1
  13.0 0.5 collective-permute-start.2
  13.5 0.6 collective-permute-done.1.beside_ref
  14.2 0.2 collective-permute-done.2.corner_ref
  14.4 2.2 %choose_near.1 = (s32[1]{0:T(128)}, bf16[256,1536]{1,0:T(8,128)(2,1)S(1)}, bf16[256,1536]{1,0:T(8,128)(2,1)S(1)}) custom-call(s32[10]{0:T(128)S(1)} %get-tuple-element.26.meta, s32[1,8]{1,0:T(1,128)S(1)} %collective-permute-done.1.beside_ref, s32[1,8]{1,0:T(1,128)S(1)} %collective-permute-done.2.corner_ref, bf16[256,1536]{1,0:T(8,128)(2,1)} %k_ref.5, ...), custom_call_target="tpu_custom_call" | custom-call | bytes 3145728 | tf_op jit(solution)/shard_map/choose_near/pallas_call | solution.py:163
  16.6 0.7 collective-permute-start.5
  17.3 0.8 %collective-permute-start.7 = (bf16[256,1536]{1,0:T(8,128)(2,1)S(1)}, bf16[256,1536]{1,0:T(8,128)(2,1)S(1)}, u32[]{:S(2)}, u32[]{:S(2)}) collective-permute-start(bf16[256,1536]{1,0:T(8,128)(2,1)S(1)} %get-tuple-element.32), channel_id=1, source_target_pairs={{0,0},{1,2},{2,1},{3,3},{4,4},{5,6},{6,5},{7,7},{8,8},{9,10},{10,9... | collective-permute-start | bytes 2359304 | tf_op jit(solution)/shard_map/ppermute | solution.py:410
  18.1 1.1 %pack.1 = bf16[512,512]{1,0:T(8,128)(2,1)S(1)} custom-call(bf16[256,1536]{1,0:T(8,128)(2,1)} %k_ref.5, bf16[256,1536]{1,0:T(8,128)(2,1)} %v_ref.5, bf16[256,1536]{1,0:T(8,128)(2,1)S(1)} %get-tuple-element.29.refs_0_), custom_call_target="tpu_custom_call" | custom-call | bytes 1048576 | tf_op jit(solution)/shard_map/pack/pallas_call | solution.py:163
  19.2 6.6 %collective-permute-done.6.refs_5_.refs_6_ = bf16[256,1536]{1,0:T(8,128)(2,1)S(1)} collective-permute-done((bf16[256,1536]{1,0:T(8,128)(2,1)S(1)}, bf16[256,1536]{1,0:T(8,128)(2,1)S(1)}, u32[]{:S(2)}, u32[]{:S(2)}) %collective-permute-start.6) | collective-permute-done | bytes 786464 | tf_op jit(solution)/shard_map/ppermute | solution.py:410
  25.9 0.4 collective-permute-start.8
  26.3 4.6 %collective-permute-start.9 = (bf16[512,512]{1,0:T(8,128)(2,1)S(1)}, bf16[512,512]{1,0:T(8,128)(2,1)S(1)}, u32[]{:S(2)}, u32[]{:S(2)}) collective-permute-start(bf16[512,512]{1,0:T(8,128)(2,1)S(1)} %pack.1), channel_id=1, source_target_pairs={{0,0},{1,1},{2,2},{3,3},{4,8},{5,9},{6,10},{7,11},{8,4},{9,5},{10,... | collective-permute-start | bytes 1572872 | tf_op jit(solution)/shard_map/ppermute | solution.py:410
  31.0 4.1 %attend_own.1 = (f32[256,1536]{1,0:T(8,128)S(1)}, f32[256,1536]{1,0:T(8,128)S(1)}, f32[256,1536]{1,0:T(8,128)S(1)}) custom-call(s32[10]{0:T(128)S(1)} %get-tuple-element.26.meta, bf16[256,1536]{1,0:T(8,128)(2,1)S(1)} %copy-done, bf16[256,1536]{1,0:T(8,128)(2,1)S(1)} %copy-done.1, bf16[256,1536]{1,0:T(8,128)(2,1)S(1)} %copy-done.2, ...), custom_call_target="tpu_custom_call" | custom-call | flops 805306368 | bytes 3932160 | tf_op jit(solution)/shard_map/attend_own/pallas_call | solution.py:141
  35.1 2.6 %collective-permute-done.4.refs_1_.refs_3_.refs_4_ = bf16[528,1024]{1,0:T(8,128)(2,1)S(1)} collective-permute-done((bf16[528,1024]{1,0:T(8,128)(2,1)S(1)}, bf16[528,1024]{1,0:T(8,128)(2,1)S(1)}, u32[]{:S(2)}, u32[]{:S(2)}) %collective-permute-start.4) | collective-permute-done | bytes 1081376 | tf_op jit(solution)/shard_map/ppermute | solution.py:410
  37.7 2.2 %choose.1 = (s32[2]{0:T(128)S(1)}, bf16[256,1024]{1,0:T(8,128)(2,1)S(1)}, bf16[256,1024]{1,0:T(8,128)(2,1)S(1)}, bf16[256,1024]{1,0:T(8,128)(2,1)S(1)}, bf16[256,1024]{1,0:T(8,128)(2,1)S(1)}) custom-call(s32[10]{0:T(128)S(1)} %get-tuple-element.26.meta, s32[1]{0:T(128)} %get-tuple-element.27.corner_ref, ...), custom_call_target="tpu_custom_call" | custom-call | bytes 4194304 | tf_op jit(solution)/shard_map/choose/pallas_call | solution.py:163
  40.0 0.6 collective-permute-start.14
  40.5 1.9 %collective-permute-start.15 = (bf16[256,1024]{1,0:T(8,128)(2,1)S(1)}, bf16[256,1024]{1,0:T(8,128)(2,1)S(1)}, u32[]{:S(2)}, u32[]{:S(2)}) collective-permute-start(bf16[256,1024]{1,0:T(8,128)(2,1)S(1)} %get-tuple-element.44), channel_id=1, source_target_pairs={{0,3},{1,1},{2,2},{3,0},{4,7},{5,5},{6,6},{7,4},{8,11},{9,9},{10,1... | collective-permute-start | bytes 1572872 | tf_op jit(solution)/shard_map/ppermute | solution.py:410
  42.5 3.4 %collective-permute-done.8.refs_1_.refs_2_ = bf16[512,512]{1,0:T(8,128)(2,1)S(1)} collective-permute-done((bf16[512,512]{1,0:T(8,128)(2,1)S(1)}, bf16[512,512]{1,0:T(8,128)(2,1)S(1)}, u32[]{:S(2)}, u32[]{:S(2)}) %collective-permute-start.8) | collective-permute-done | bytes 524320 | tf_op jit(solution)/shard_map/ppermute | solution.py:410
  45.9 3.5 %collective-permute-start.17 = (bf16[256,1024]{1,0:T(8,128)(2,1)S(1)}, bf16[256,1024]{1,0:T(8,128)(2,1)S(1)}, u32[]{:S(2)}, u32[]{:S(2)}) collective-permute-start(bf16[256,1024]{1,0:T(8,128)(2,1)S(1)} %get-tuple-element.46), channel_id=1, source_target_pairs={{0,0},{1,1},{2,2},{3,3},{4,8},{5,9},{6,10},{7,11},{8,4},{9,5},{10,... | collective-permute-start | bytes 1572872 | tf_op jit(solution)/shard_map/ppermute | solution.py:410
  49.4 2.7 %choose_again.1 = (bf16[256,512]{1,0:T(8,128)(2,1)S(1)}, bf16[256,512]{1,0:T(8,128)(2,1)S(1)}, bf16[256,512]{1,0:T(8,128)(2,1)S(1)}, bf16[256,512]{1,0:T(8,128)(2,1)S(1)}) custom-call(s32[10]{0:T(128)S(1)} %get-tuple-element.26.meta, s32[1]{0:T(128)} %get-tuple-element.27.corner_ref, s32[2]{0:T(128)S(1)} %get-tuple-element.33.refs_0_, ...), custom_call_target="tpu_custom_call" | custom-call | bytes 2097152 | tf_op jit(solution)/shard_map/choose_again/pallas_call | solution.py:163
  52.2 0.8 %collective-permute-done.14.refs_5_.refs_6_ = bf16[256,1024]{1,0:T(8,128)(2,1)S(1)} collective-permute-done((bf16[256,1024]{1,0:T(8,128)(2,1)S(1)}, bf16[256,1024]{1,0:T(8,128)(2,1)S(1)}, u32[]{:S(2)}, u32[]{:S(2)}) %collective-permute-start.14) | collective-permute-done | bytes 524320 | tf_op jit(solution)/shard_map/ppermute | solution.py:410
  53.0 1.9 %collective-permute-start.11 = (bf16[256,512]{1,0:T(8,128)(2,1)S(1)}, bf16[256,512]{1,0:T(8,128)(2,1)S(1)}, u32[]{:S(2)}, u32[]{:S(2)}) collective-permute-start(bf16[256,512]{1,0:T(8,128)(2,1)S(1)} %get-tuple-element.35), channel_id=1, source_target_pairs={{0,3},{1,1},{2,2},{3,0},{4,7},{5,5},{6,6},{7,4},{8,11},{9,9},{10,1... | collective-permute-start | bytes 786440 | tf_op jit(solution)/shard_map/ppermute | solution.py:410
  54.9 2.2 %collective-permute-start.12 = (bf16[256,512]{1,0:T(8,128)(2,1)S(1)}, bf16[256,512]{1,0:T(8,128)(2,1)S(1)}, u32[]{:S(2)}, u32[]{:S(2)}) collective-permute-start(bf16[256,512]{1,0:T(8,128)(2,1)S(1)} %get-tuple-element.36), channel_id=1, source_target_pairs={{0,4},{1,5},{2,6},{3,7},{4,0},{5,1},{6,2},{7,3},{8,12},{9,13},{10,... | collective-permute-start | bytes 786440 | tf_op jit(solution)/shard_map/ppermute | solution.py:410
  57.1 4.5 %collective-permute-start.13 = (bf16[256,512]{1,0:T(8,128)(2,1)S(1)}, bf16[256,512]{1,0:T(8,128)(2,1)S(1)}, u32[]{:S(2)}, u32[]{:S(2)}) collective-permute-start(bf16[256,512]{1,0:T(8,128)(2,1)S(1)} %get-tuple-element.37), channel_id=1, source_target_pairs={{0,0},{1,1},{2,2},{3,3},{4,8},{5,9},{6,10},{7,11},{8,4},{9,5},{10,... | collective-permute-start | bytes 786440 | tf_op jit(solution)/shard_map/ppermute | solution.py:410
  61.6 1.2 %attend_more.1 = (f32[256,512]{1,0:T(8,128)S(1)}, f32[256,512]{1,0:T(8,128)S(1)}, f32[256,512]{1,0:T(8,128)S(1)}) custom-call(s32[10]{0:T(128)S(1)} %get-tuple-element.26.meta, bf16[256,1536]{1,0:T(8,128)(2,1)S(1)} %copy-done, bf16[512,512]{1,0:T(8,128)(2,1)S(1)} %collective-permute-done.8.refs_1_.refs_2_, ...), custom_call_target="tpu_custom_call" | custom-call | flops 134217728 | bytes 786432 | tf_op jit(solution)/shard_map/attend_more/pallas_call | solution.py:141
  62.9 4.8 %attend_last.2.refs_14_ = bf16[256,1536]{1,0:T(8,128)(2,1)} custom-call(s32[10]{0:T(128)S(1)} %get-tuple-element.26.meta, bf16[256,1536]{1,0:T(8,128)(2,1)S(1)} %copy-done, bf16[528,1024]{1,0:T(8,128)(2,1)S(1)} %collective-permute-done.3.refs_0_.refs_1_.refs_2_, bf16[528,1024]{1,0:T(8,128)(2,1)S(1)} %collective-permute-done.3.refs_0_.refs_1_.refs_2_, ...), custom_call_target="tpu_custom_call" | custom-call | flops 671088640 | bytes 3145728 | tf_op jit(solution)/shard_map/attend_last/pallas_call | solution.py:141
  67.7 2.3 %attend_last.3 = bf16[256,1536]{1,0:T(8,128)(2,1)} custom-call(s32[10]{0:T(128)S(1)} %get-tuple-element.26.meta, bf16[256,1536]{1,0:T(8,128)(2,1)S(1)} %copy-done, bf16[256,512]{1,0:T(8,128)(2,1)S(1)} %collective-permute-done.10.refs_1_.refs_2_, bf16[256,512]{1,0:T(8,128)(2,1)S(1)} %collective-permute-done.10.refs_1_.refs_2_, ...), custom_call_target="tpu_custom_call", output_to_operand_aliasing={{}: (15, {})} | custom-call | flops 201326592 | bytes 1048576 | tf_op jit(solution)/shard_map/attend_last/pallas_call | solution.py:141
  (21 shorter events, 0.2 us)
Async XLA Ops:
  0.0 13.0 %copy-start.3 = (s32[1,8]{1,0:T(1,128)S(1)}, s32[1,8]{1,0:T(1,128)}, u32[]{:S(2)}) copy-start(s32[1,8]{1,0:T(1,128)} %list_hbm.1) | copy-start | bytes 100
  0.0 3.7 %collective-permute-start = (s32[1,8]{1,0:T(1,128)}, s32[1,8]{1,0:T(1,128)S(1)}, u32[]{:S(2)}, u32[]{:S(2)}) collective-permute-start(s32[1,8]{1,0:T(1,128)} %list_hbm.1), channel_id=1, source_target_pairs={{0,2},{1,3},{2,0},{3,1},{4,6},{5,7},{6,4},{7,5},{8,10},{9,11},{10,... | collective-permute-start | bytes 104 | tf_op jit(solution)/shard_map/ppermute | solution.py:410
  6.3 19.6 %collective-permute-start.6 = (bf16[256,1536]{1,0:T(8,128)(2,1)S(1)}, bf16[256,1536]{1,0:T(8,128)(2,1)S(1)}, u32[]{:S(2)}, u32[]{:S(2)}) collective-permute-start(bf16[256,1536]{1,0:T(8,128)(2,1)S(1)} %get-tuple-element.30), channel_id=1, source_target_pairs={{0,2},{1,3},{2,0},{3,1},{4,6},{5,7},{6,4},{7,5},{8,10},{9,11},{10,... | collective-permute-start | bytes 2359304 | tf_op jit(solution)/shard_map/ppermute | solution.py:410
  7.9 27.2 %collective-permute-start.3 = (bf16[528,1024]{1,0:T(8,128)(2,1)S(1)}, bf16[528,1024]{1,0:T(8,128)(2,1)S(1)}, u32[]{:S(2)}, u32[]{:S(2)}) collective-permute-start(bf16[528,1024]{1,0:T(8,128)(2,1)S(1)} %get-tuple-element.28), channel_id=1, source_target_pairs={{0,4},{1,5},{2,6},{3,7},{4,0},{5,1},{6,2},{7,3},{8,12},{9,13},{10,... | collective-permute-start | bytes 3244040 | tf_op jit(solution)/shard_map/ppermute | solution.py:410
  8.3 29.4 %collective-permute-start.4 = (bf16[528,1024]{1,0:T(8,128)(2,1)S(1)}, bf16[528,1024]{1,0:T(8,128)(2,1)S(1)}, u32[]{:S(2)}, u32[]{:S(2)}) collective-permute-start(bf16[528,1024]{1,0:T(8,128)(2,1)S(1)} %get-tuple-element.28), channel_id=1, source_target_pairs={{0,0},{1,1},{2,2},{3,3},{4,8},{5,9},{6,10},{7,11},{8,4},{9,5},{10,... | collective-permute-start | bytes 3244040 | tf_op jit(solution)/shard_map/ppermute | solution.py:410
  13.0 1.2 %collective-permute-start.1 = (s32[1,8]{1,0:T(1,128)S(1)}, s32[1,8]{1,0:T(1,128)S(1)}, u32[]{:S(2)}, u32[]{:S(2)}) collective-permute-start(s32[1,8]{1,0:T(1,128)S(1)} %copy-done.3), channel_id=1, source_target_pairs={{0,1},{1,0},{2,3},{3,2},{4,5},{5,4},{6,7},{7,6},{8,9},{9,8},{10,11... | collective-permute-start | bytes 104 | tf_op jit(solution)/shard_map/ppermute | solution.py:410
  13.0 1.3 %collective-permute-start.2 = (s32[1,8]{1,0:T(1,128)S(1)}, s32[1,8]{1,0:T(1,128)S(1)}, u32[]{:S(2)}, u32[]{:S(2)}) collective-permute-start(s32[1,8]{1,0:T(1,128)S(1)} %collective-permute-done.across_ref), channel_id=1, source_target_pairs={{0,1},{1,0},{2,3},{3,2},{4,5},{5,4},{6,7},{7,6},{8,9},{9,8},{10,11... | collective-permute-start | bytes 104 | tf_op jit(solution)/shard_map/ppermute | solution.py:410
  16.6 14.4 %copy-start = (bf16[256,1536]{1,0:T(8,128)(2,1)S(1)}, bf16[256,1536]{1,0:T(8,128)(2,1)}, u32[]{:S(2)}) copy-start(bf16[256,1536]{1,0:T(8,128)(2,1)} %refs_0_.7) | copy-start | bytes 2359300
  16.6 14.4 %copy-start.1 = (bf16[256,1536]{1,0:T(8,128)(2,1)S(1)}, bf16[256,1536]{1,0:T(8,128)(2,1)}, u32[]{:S(2)}) copy-start(bf16[256,1536]{1,0:T(8,128)(2,1)} %k_ref.5) | copy-start | bytes 2359300
  16.6 14.4 %copy-start.2 = (bf16[256,1536]{1,0:T(8,128)(2,1)S(1)}, bf16[256,1536]{1,0:T(8,128)(2,1)}, u32[]{:S(2)}) copy-start(bf16[256,1536]{1,0:T(8,128)(2,1)} %v_ref.5) | copy-start | bytes 2359300
  16.6 9.7 %collective-permute-start.5 = (bf16[256,1536]{1,0:T(8,128)(2,1)S(1)}, bf16[256,1536]{1,0:T(8,128)(2,1)S(1)}, u32[]{:S(2)}, u32[]{:S(2)}) collective-permute-start(bf16[256,1536]{1,0:T(8,128)(2,1)S(1)} %get-tuple-element.29.refs_0_), channel_id=1, source_target_pairs={{0,1},{1,0},{2,3},{3,2},{4,5},{5,4},{6,7},{7,6},{8,9},{9,8},{10,11... | collective-permute-start | bytes 2359304 | tf_op jit(solution)/shard_map/ppermute | solution.py:410
  17.3 17.8 %collective-permute-start.7 = (bf16[256,1536]{1,0:T(8,128)(2,1)S(1)}, bf16[256,1536]{1,0:T(8,128)(2,1)S(1)}, u32[]{:S(2)}, u32[]{:S(2)}) collective-permute-start(bf16[256,1536]{1,0:T(8,128)(2,1)S(1)} %get-tuple-element.32), channel_id=1, source_target_pairs={{0,0},{1,2},{2,1},{3,3},{4,4},{5,6},{6,5},{7,7},{8,8},{9,10},{10,9... | collective-permute-start | bytes 2359304 | tf_op jit(solution)/shard_map/ppermute | solution.py:410
  25.9 20.0 %collective-permute-start.8 = (bf16[512,512]{1,0:T(8,128)(2,1)S(1)}, bf16[512,512]{1,0:T(8,128)(2,1)S(1)}, u32[]{:S(2)}, u32[]{:S(2)}) collective-permute-start(bf16[512,512]{1,0:T(8,128)(2,1)S(1)} %pack.1), channel_id=1, source_target_pairs={{0,4},{1,5},{2,6},{3,7},{4,0},{5,1},{6,2},{7,3},{8,12},{9,13},{10,... | collective-permute-start | bytes 1572872 | tf_op jit(solution)/shard_map/ppermute | solution.py:410
  26.3 23.1 %collective-permute-start.9 = (bf16[512,512]{1,0:T(8,128)(2,1)S(1)}, bf16[512,512]{1,0:T(8,128)(2,1)S(1)}, u32[]{:S(2)}, u32[]{:S(2)}) collective-permute-start(bf16[512,512]{1,0:T(8,128)(2,1)S(1)} %pack.1), channel_id=1, source_target_pairs={{0,0},{1,1},{2,2},{3,3},{4,8},{5,9},{6,10},{7,11},{8,4},{9,5},{10,... | collective-permute-start | bytes 1572872 | tf_op jit(solution)/shard_map/ppermute | solution.py:410
  40.0 13.0 %collective-permute-start.14 = (bf16[256,1024]{1,0:T(8,128)(2,1)S(1)}, bf16[256,1024]{1,0:T(8,128)(2,1)S(1)}, u32[]{:S(2)}, u32[]{:S(2)}) collective-permute-start(bf16[256,1024]{1,0:T(8,128)(2,1)S(1)} %get-tuple-element.43), channel_id=1, source_target_pairs={{0,2},{1,3},{2,0},{3,1},{4,6},{5,7},{6,4},{7,5},{8,10},{9,11},{10,... | collective-permute-start | bytes 1572872 | tf_op jit(solution)/shard_map/ppermute | solution.py:410
  40.5 14.4 %collective-permute-start.15 = (bf16[256,1024]{1,0:T(8,128)(2,1)S(1)}, bf16[256,1024]{1,0:T(8,128)(2,1)S(1)}, u32[]{:S(2)}, u32[]{:S(2)}) collective-permute-start(bf16[256,1024]{1,0:T(8,128)(2,1)S(1)} %get-tuple-element.44), channel_id=1, source_target_pairs={{0,3},{1,1},{2,2},{3,0},{4,7},{5,5},{6,6},{7,4},{8,11},{9,9},{10,1... | collective-permute-start | bytes 1572872 | tf_op jit(solution)/shard_map/ppermute | solution.py:410
  42.4 14.7 %collective-permute-start.16 = (bf16[256,1024]{1,0:T(8,128)(2,1)S(1)}, bf16[256,1024]{1,0:T(8,128)(2,1)S(1)}, u32[]{:S(2)}, u32[]{:S(2)}) collective-permute-start(bf16[256,1024]{1,0:T(8,128)(2,1)S(1)} %get-tuple-element.45), channel_id=1, source_target_pairs={{0,4},{1,5},{2,6},{3,7},{4,0},{5,1},{6,2},{7,3},{8,12},{9,13},{10,... | collective-permute-start | bytes 1572872 | tf_op jit(solution)/shard_map/ppermute | solution.py:410
  45.9 17.0 %collective-permute-start.17 = (bf16[256,1024]{1,0:T(8,128)(2,1)S(1)}, bf16[256,1024]{1,0:T(8,128)(2,1)S(1)}, u32[]{:S(2)}, u32[]{:S(2)}) collective-permute-start(bf16[256,1024]{1,0:T(8,128)(2,1)S(1)} %get-tuple-element.46), channel_id=1, source_target_pairs={{0,0},{1,1},{2,2},{3,3},{4,8},{5,9},{6,10},{7,11},{8,4},{9,5},{10,... | collective-permute-start | bytes 1572872 | tf_op jit(solution)/shard_map/ppermute | solution.py:410
  52.1 15.6 %collective-permute-start.10 = (bf16[256,512]{1,0:T(8,128)(2,1)S(1)}, bf16[256,512]{1,0:T(8,128)(2,1)S(1)}, u32[]{:S(2)}, u32[]{:S(2)}) collective-permute-start(bf16[256,512]{1,0:T(8,128)(2,1)S(1)} %get-tuple-element.34), channel_id=1, source_target_pairs={{0,2},{1,3},{2,0},{3,1},{4,6},{5,7},{6,4},{7,5},{8,10},{9,11},{10,... | collective-permute-start | bytes 786440 | tf_op jit(solution)/shard_map/ppermute | solution.py:410
  53.0 14.7 %collective-permute-start.11 = (bf16[256,512]{1,0:T(8,128)(2,1)S(1)}, bf16[256,512]{1,0:T(8,128)(2,1)S(1)}, u32[]{:S(2)}, u32[]{:S(2)}) collective-permute-start(bf16[256,512]{1,0:T(8,128)(2,1)S(1)} %get-tuple-element.35), channel_id=1, source_target_pairs={{0,3},{1,1},{2,2},{3,0},{4,7},{5,5},{6,6},{7,4},{8,11},{9,9},{10,1... | collective-permute-start | bytes 786440 | tf_op jit(solution)/shard_map/ppermute | solution.py:410
  54.9 12.8 %collective-permute-start.12 = (bf16[256,512]{1,0:T(8,128)(2,1)S(1)}, bf16[256,512]{1,0:T(8,128)(2,1)S(1)}, u32[]{:S(2)}, u32[]{:S(2)}) collective-permute-start(bf16[256,512]{1,0:T(8,128)(2,1)S(1)} %get-tuple-element.36), channel_id=1, source_target_pairs={{0,4},{1,5},{2,6},{3,7},{4,0},{5,1},{6,2},{7,3},{8,12},{9,13},{10,... | collective-permute-start | bytes 786440 | tf_op jit(solution)/shard_map/ppermute | solution.py:410
  57.1 10.6 %collective-permute-start.13 = (bf16[256,512]{1,0:T(8,128)(2,1)S(1)}, bf16[256,512]{1,0:T(8,128)(2,1)S(1)}, u32[]{:S(2)}, u32[]{:S(2)}) collective-permute-start(bf16[256,512]{1,0:T(8,128)(2,1)S(1)} %get-tuple-element.37), channel_id=1, source_target_pairs={{0,0},{1,1},{2,2},{3,3},{4,8},{5,9},{6,10},{7,11},{8,4},{9,5},{10,... | collective-permute-start | bytes 786440 | tf_op jit(solution)/shard_map/ppermute | solution.py:410

commit v15 on v14

--- a/solution.py
+++ b/solution.py
@@ -278,28 +278,31 @@
     rows, width = keys.shape
     tile_count = rows // TILE
 
-    def build(meta, beside_ref, corner_ref, k_ref, v_ref, wanted, to_beside, to_corner, zeros, sems):
+    def build(meta, beside_ref, corner_ref, k_ref, v_ref, known, to_beside, to_corner, zeros, sems):
         even = meta[8] % 2 == 0
         own = ((k_ref, 0, 0), (v_ref, 0, 0))
         copies = tile_copies(own, tile_at(beside_ref, jnp.where(even, 0, 4), tile_count), to_beside, sems, 0)
         for copy in copies:
             copy.start()
-        wanted[0] = tile_at(corner_ref, jnp.where(even, 4, 0), tile_count)
+        for entry in range(10):
+            known[entry] = meta[entry]
+        tile = tile_at(corner_ref, jnp.where(even, 4, 0), tile_count)
+        known[10] = tile
         inside = (meta[8] % 4 == 1) | (meta[8] % 4 == 2)
-        start_if(inside, tile_copies(own, wanted[0], to_corner, sems, 2))
+        start_if(inside, tile_copies(own, tile, to_corner, sems, 2))
         zeros[...] = jnp.zeros_like(zeros)
         blank = zero_copies(zeros, to_corner, sems, 2)
         start_if(jnp.logical_not(inside), blank)
         for copy in copies + blank:
             copy.wait()
 
-    tile = jax.ShapeDtypeStruct((2 * TILE, width), jnp.bfloat16)
+    sent = jax.ShapeDtypeStruct((2 * TILE, width), jnp.bfloat16)
     return move(
         "choose_near",
         build,
         (meta, beside_list, corner_list, in_hbm(keys), in_hbm(values)),
         [SCALAR] * 3 + [WHOLE] * 2,
-        [jax.ShapeDtypeStruct((1,), jnp.int32), tile, tile],
+        [jax.ShapeDtypeStruct((11,), jnp.int32), sent, sent],
         [SCALAR, WHOLE, WHOLE],
         4,
         16 * TILE * width,
@@ -340,18 +343,16 @@
     )
 
 
-def choose(meta, corner_tile, wants, outer, inner, after):
+def choose(meta, again, outer, inner, after):
     rows, width = outer.shape[0] // 2 // TILE * TILE, outer.shape[1]
     tile_count = rows // TILE
-    again = wants is not None
-
-    def build(meta, corner_ref, *refs):
+
+    def build(meta, outer, inner, *refs):
         if again:
-            wants, outer, inner = refs[:3]
             to_two, to_one, to_outer, to_inner = refs[-6:-2]
+            wants = meta[11], meta[12]
         else:
-            outer, inner, wants = refs[:2] + refs[-8:-7]
-            to_two, to_one, to_outer, to_inner, notes = refs[-7:-2]
+            known, to_two, to_one, to_outer, to_inner, notes = refs[-8:-2]
         zeros, sems = refs[-2:]
         spot, plane = meta[8] % 4, meta[8] // 4
         right, odd = spot >= 2, plane % 2 == 1
@@ -369,7 +370,7 @@
         edge = (spot == 0) | (spot == 3)
         for source, here in ((from_outer, right == odd), (from_inner, right != odd)):
             start_if(here, tile_copies(source, meta[9], to_two, sems, 0))
-            start_if(here & edge, tile_copies(source, corner_ref[0], to_one, sems, 2))
+            start_if(here & edge, tile_copies(source, meta[10], to_one, sems, 2))
         zeros[...] = jnp.zeros_like(zeros)
         start_if(jnp.logical_not(edge), zero_copies(zeros, to_one, sems, 2))
         between = (plane == 1) | (plane == 2)
@@ -380,8 +381,13 @@
         if not again:
             for read in reads:
                 read.wait()
-            wants[0] = read_note(notes[0], jnp.where(plane == 1, 7, 3), tile_count)
-            wants[1] = read_note(notes[1], jnp.where(plane == 1, 3, 7), tile_count)
+            wants = (
+                read_note(notes[0], jnp.where(plane == 1, 7, 3), tile_count),
+                read_note(notes[1], jnp.where(plane == 1, 3, 7), tile_count),
+            )
+            for entry in range(11):
+                known[entry] = meta[entry]
+            known[11], known[12] = wants
         start_if(
             between,
             tile_copies(from_inner, wants[0], to_outer, sems, 4)
@@ -395,9 +401,9 @@
     return move(
         "choose_again" if again else "choose",
         build,
-        (meta, corner_tile, *([wants] if again else []), outer, inner, *after),
-        [SCALAR] * (2 + again) + [WHOLE] * (2 + len(after)),
-        ([] if again else [jax.ShapeDtypeStruct((2,), jnp.int32)]) + sent,
+        (meta, outer, inner, *after),
+        [SCALAR] + [WHOLE] * (2 + len(after)),
+        ([] if again else [jax.ShapeDtypeStruct((13,), jnp.int32)]) + sent,
         [SCALAR] * (not again) + [WHOLE] * 4,
         10,
         32 * TILE * width,
@@ -489,21 +495,22 @@
     first_width = parts[0][1] * block
     meta, first, to_across = begin(tile_lists, me, across_list, key_heads, value_heads, first_width)
     over = send(to_across, across)
-    corner_tile, to_beside, to_corner = choose_near(meta, beside_list, corner_list, key_heads, value_heads)
+    known, to_beside, to_corner = choose_near(meta, beside_list, corner_list, key_heads, value_heads)
     next_to = send(to_beside, beside)
     one_in = send(to_corner, corner_in)
     second = pack(key_heads, value_heads, first_width, width - first_width, [to_beside])
     near = [own_frame(), sent_tile([(next_to, 0)]), sent_tile([(over, 0)])]
     begun = attend(queries, meta, near, 0, width // block, heads)
 
-    after, wants = [begun[0], one_in], None
+    after, again = [begun[0], one_in], False
     calls = []
     for (at, steps), packed in zip(parts, (first, second)):
         from_outer = send(packed, outer)
         from_inner = send(packed, inner)
-        sent = choose(meta, corner_tile, wants, from_outer, from_inner, after)
-        if wants is None:
-            wants, *sent = sent
+        sent = choose(known, again, from_outer, from_inner, after)
+        if not again:
+            known, *sent = sent
+        again = True
         two = send(sent[0], across)
         one = send(sent[1], corner_out)
         far = [send(sent[2], outer), send(sent[3], inner)]

time: 70.4 us -> 69.8 us (level)
  Pallas kernels: 23.3 us -> 22.1 us
    pallas_call x5, Pallas kernels: 10.9 us -> 9.66 us  [move(): pl.pallas_call(build, name=name, out_shape=out_shape, in_specs=specs, out...]
    ppermute x18, waiting for transfers between devices: 16.5 us -> 17.2 us  [send(): return lax.ppermute(array, 'frame', route)]
  transfers between devices with their start and end apart: 18 -> 18, of which waited for: 7 -> 8; matrix products, arithmetic and copies ran while one was open for 0% -> 0% of each run, Pallas kernels for 26% -> 25%
where the time goes in v15:
time: 69.8 us; the launch traced here: 69.4 us
  starting transfers between devices  29.9 us (43%)
  Pallas kernels  22.1 us (32%)
  waiting for transfers between devices  17.2 us (25%)
    ppermute x18, starting transfers between devices, send(): return lax.ppermute(array, 'frame', route)  29.9 us
    ppermute x18, waiting for transfers between devices, send(): return lax.ppermute(array, 'frame', route)  17.2 us
    pallas_call x4, Pallas kernels, attend(): pl.pallas_call(functools.partial(attend_kernel, plan, heads, carry is not...  12.4 us
    pallas_call x5, Pallas kernels, move(): pl.pallas_call(build, name=name, out_shape=out_shape, in_specs=specs, out...  9.66 us
  transfers between devices with their start and end apart: 18, of which 8 were waited for; matrix products, arithmetic and copies ran while one was open for 0% of the time, Pallas kernels for 25%

profile of v15, /device:TPU:12, one launch (start us, length us, event | category | flops | bytes accessed | tf_op | source)
XLA Modules:
  0.0 69.4 jit_solution(16567998174781837505)
XLA Ops:
  0.0 1.5 %collective-permute-start = (s32[1,8]{1,0:T(1,128)}, s32[1,8]{1,0:T(1,128)S(1)}, u32[]{:S(2)}, u32[]{:S(2)}) collective-permute-start(s32[1,8]{1,0:T(1,128)} %list_hbm.1), channel_id=1, source_target_pairs={{0,2},{1,3},{2,0},{3,1},{4,6},{5,7},{6,4},{7,5},{8,10},{9,11},{10,... | collective-permute-start | bytes 104 | tf_op jit(solution)/shard_map/ppermute | solution.py:416
  1.5 2.2 %collective-permute-done.across_ref = s32[1,8]{1,0:T(1,128)S(1)} collective-permute-done((s32[1,8]{1,0:T(1,128)}, s32[1,8]{1,0:T(1,128)S(1)}, u32[]{:S(2)}, u32[]{:S(2)}) %collective-permute-start) | collective-permute-done | bytes 64 | tf_op jit(solution)/shard_map/ppermute | solution.py:416
  3.7 2.6 %begin.1 = (s32[10]{0:T(128)S(1)}, bf16[528,1024]{1,0:T(8,128)(2,1)S(1)}, bf16[256,1536]{1,0:T(8,128)(2,1)S(1)}) custom-call(s32[1]{0:T(128)} %bitcast.me_ref, s32[1,8]{1,0:T(1,128)S(1)} %collective-permute-done.across_ref, s32[1,8]{1,0:T(1,128)} %list_hbm.1, bf16[256,1536]{1,0:T(8,128)(2,1)} %k_ref.5, bf16[256,1536]{1,0:T(8,128)(2,1)} %v_ref.5), custom_call_target="tpu_custom_call" | custom-call | bytes 3670016 | tf_op jit(solution)/shard_map/begin/pallas_call | solution.py:163
  6.3 1.6 %collective-permute-start.6 = (bf16[256,1536]{1,0:T(8,128)(2,1)S(1)}, bf16[256,1536]{1,0:T(8,128)(2,1)S(1)}, u32[]{:S(2)}, u32[]{:S(2)}) collective-permute-start(bf16[256,1536]{1,0:T(8,128)(2,1)S(1)} %get-tuple-element.30), channel_id=1, source_target_pairs={{0,2},{1,3},{2,0},{3,1},{4,6},{5,7},{6,4},{7,5},{8,10},{9,11},{10,... | collective-permute-start | bytes 2359304 | tf_op jit(solution)/shard_map/ppermute | solution.py:416
  7.9 0.5 collective-permute-start.3
  8.3 4.6 %collective-permute-start.4 = (bf16[528,1024]{1,0:T(8,128)(2,1)S(1)}, bf16[528,1024]{1,0:T(8,128)(2,1)S(1)}, u32[]{:S(2)}, u32[]{:S(2)}) collective-permute-start(bf16[528,1024]{1,0:T(8,128)(2,1)S(1)} %get-tuple-element.28), channel_id=1, source_target_pairs={{0,0},{1,1},{2,2},{3,3},{4,8},{5,9},{6,10},{7,11},{8,4},{9,5},{10,... | collective-permute-start | bytes 3244040 | tf_op jit(solution)/shard_map/ppermute | solution.py:416
  13.0 0.5 collective-permute-start.2
  13.5 0.6 collective-permute-done.1.beside_ref
  14.2 0.2 collective-permute-done.2.corner_ref
  14.4 2.3 %choose_near.1 = (s32[11]{0:T(128)S(1)}, bf16[256,1536]{1,0:T(8,128)(2,1)S(1)}, bf16[256,1536]{1,0:T(8,128)(2,1)S(1)}) custom-call(s32[10]{0:T(128)S(1)} %get-tuple-element.26.meta, s32[1,8]{1,0:T(1,128)S(1)} %collective-permute-done.1.beside_ref, s32[1,8]{1,0:T(1,128)S(1)} %collective-permute-done.2.corner_ref, bf16[256,1536]{1,0:T(8,128)(2,1)} %k_ref.5, ...), custom_call_target="tpu_custom_call" | custom-call | bytes 3145728 | tf_op jit(solution)/shard_map/choose_near/pallas_call | solution.py:163
  16.7 0.7 collective-permute-start.5
  17.4 0.8 %collective-permute-start.7 = (bf16[256,1536]{1,0:T(8,128)(2,1)S(1)}, bf16[256,1536]{1,0:T(8,128)(2,1)S(1)}, u32[]{:S(2)}, u32[]{:S(2)}) collective-permute-start(bf16[256,1536]{1,0:T(8,128)(2,1)S(1)} %get-tuple-element.32), channel_id=1, source_target_pairs={{0,0},{1,2},{2,1},{3,3},{4,4},{5,6},{6,5},{7,7},{8,8},{9,10},{10,9... | collective-permute-start | bytes 2359304 | tf_op jit(solution)/shard_map/ppermute | solution.py:416
  18.2 1.1 %pack.1 = bf16[512,512]{1,0:T(8,128)(2,1)S(1)} custom-call(bf16[256,1536]{1,0:T(8,128)(2,1)} %k_ref.5, bf16[256,1536]{1,0:T(8,128)(2,1)} %v_ref.5, bf16[256,1536]{1,0:T(8,128)(2,1)S(1)} %get-tuple-element.29.refs_0_), custom_call_target="tpu_custom_call" | custom-call | bytes 1048576 | tf_op jit(solution)/shard_map/pack/pallas_call | solution.py:163
  19.3 6.5 %collective-permute-done.6.refs_5_.refs_6_ = bf16[256,1536]{1,0:T(8,128)(2,1)S(1)} collective-permute-done((bf16[256,1536]{1,0:T(8,128)(2,1)S(1)}, bf16[256,1536]{1,0:T(8,128)(2,1)S(1)}, u32[]{:S(2)}, u32[]{:S(2)}) %collective-permute-start.6) | collective-permute-done | bytes 786464 | tf_op jit(solution)/shard_map/ppermute | solution.py:416
  25.9 0.5 collective-permute-start.8
  26.4 4.6 %collective-permute-start.9 = (bf16[512,512]{1,0:T(8,128)(2,1)S(1)}, bf16[512,512]{1,0:T(8,128)(2,1)S(1)}, u32[]{:S(2)}, u32[]{:S(2)}) collective-permute-start(bf16[512,512]{1,0:T(8,128)(2,1)S(1)} %pack.1), channel_id=1, source_target_pairs={{0,0},{1,1},{2,2},{3,3},{4,8},{5,9},{6,10},{7,11},{8,4},{9,5},{10,... | collective-permute-start | bytes 1572872 | tf_op jit(solution)/shard_map/ppermute | solution.py:416
  31.0 4.1 %attend_own.1 = (f32[256,1536]{1,0:T(8,128)S(1)}, f32[256,1536]{1,0:T(8,128)S(1)}, f32[256,1536]{1,0:T(8,128)S(1)}) custom-call(s32[10]{0:T(128)S(1)} %get-tuple-element.26.meta, bf16[256,1536]{1,0:T(8,128)(2,1)S(1)} %copy-done, bf16[256,1536]{1,0:T(8,128)(2,1)S(1)} %copy-done.1, bf16[256,1536]{1,0:T(8,128)(2,1)S(1)} %copy-done.2, ...), custom_call_target="tpu_custom_call" | custom-call | flops 805306368 | bytes 3932160 | tf_op jit(solution)/shard_map/attend_own/pallas_call | solution.py:141
  35.1 2.6 %collective-permute-done.4.inner.refs_3_.refs_4_ = bf16[528,1024]{1,0:T(8,128)(2,1)S(1)} collective-permute-done((bf16[528,1024]{1,0:T(8,128)(2,1)S(1)}, bf16[528,1024]{1,0:T(8,128)(2,1)S(1)}, u32[]{:S(2)}, u32[]{:S(2)}) %collective-permute-start.4) | collective-permute-done | bytes 1081376 | tf_op jit(solution)/shard_map/ppermute | solution.py:416
  37.7 1.6 %choose.1 = (s32[13]{0:T(128)S(1)}, bf16[256,1024]{1,0:T(8,128)(2,1)S(1)}, bf16[256,1024]{1,0:T(8,128)(2,1)S(1)}, bf16[256,1024]{1,0:T(8,128)(2,1)S(1)}, bf16[256,1024]{1,0:T(8,128)(2,1)S(1)}) custom-call(s32[11]{0:T(128)S(1)} %get-tuple-element.27.meta, bf16[528,1024]{1,0:T(8,128)(2,1)S(1)} %collective-permute-done.3.outer.refs_1_.refs_2_, ...), custom_call_target="tpu_custom_call" | custom-call | bytes 4194304 | tf_op jit(solution)/shard_map/choose/pallas_call | solution.py:163
  39.3 0.6 collective-permute-start.14
  39.9 1.9 %collective-permute-start.15 = (bf16[256,1024]{1,0:T(8,128)(2,1)S(1)}, bf16[256,1024]{1,0:T(8,128)(2,1)S(1)}, u32[]{:S(2)}, u32[]{:S(2)}) collective-permute-start(bf16[256,1024]{1,0:T(8,128)(2,1)S(1)} %get-tuple-element.44), channel_id=1, source_target_pairs={{0,3},{1,1},{2,2},{3,0},{4,7},{5,5},{6,6},{7,4},{8,11},{9,9},{10,1... | collective-permute-start | bytes 1572872 | tf_op jit(solution)/shard_map/ppermute | solution.py:416
  41.9 4.0 %collective-permute-done.8.outer.refs_1_.refs_2_ = bf16[512,512]{1,0:T(8,128)(2,1)S(1)} collective-permute-done((bf16[512,512]{1,0:T(8,128)(2,1)S(1)}, bf16[512,512]{1,0:T(8,128)(2,1)S(1)}, u32[]{:S(2)}, u32[]{:S(2)}) %collective-permute-start.8) | collective-permute-done | bytes 524320 | tf_op jit(solution)/shard_map/ppermute | solution.py:416
  45.9 3.5 %collective-permute-start.17 = (bf16[256,1024]{1,0:T(8,128)(2,1)S(1)}, bf16[256,1024]{1,0:T(8,128)(2,1)S(1)}, u32[]{:S(2)}, u32[]{:S(2)}) collective-permute-start(bf16[256,1024]{1,0:T(8,128)(2,1)S(1)} %get-tuple-element.46), channel_id=1, source_target_pairs={{0,0},{1,1},{2,2},{3,3},{4,8},{5,9},{6,10},{7,11},{8,4},{9,5},{10,... | collective-permute-start | bytes 1572872 | tf_op jit(solution)/shard_map/ppermute | solution.py:416
  49.4 2.1 %choose_again.1 = (bf16[256,512]{1,0:T(8,128)(2,1)S(1)}, bf16[256,512]{1,0:T(8,128)(2,1)S(1)}, bf16[256,512]{1,0:T(8,128)(2,1)S(1)}, bf16[256,512]{1,0:T(8,128)(2,1)S(1)}) custom-call(s32[13]{0:T(128)S(1)} %get-tuple-element.33.meta, bf16[512,512]{1,0:T(8,128)(2,1)S(1)} %collective-permute-done.8.outer.refs_1_.refs_2_, ...), custom_call_target="tpu_custom_call" | custom-call | bytes 2097152 | tf_op jit(solution)/shard_map/choose_again/pallas_call | solution.py:163
  51.5 0.8 %collective-permute-done.14.refs_5_.refs_6_ = bf16[256,1024]{1,0:T(8,128)(2,1)S(1)} collective-permute-done((bf16[256,1024]{1,0:T(8,128)(2,1)S(1)}, bf16[256,1024]{1,0:T(8,128)(2,1)S(1)}, u32[]{:S(2)}, u32[]{:S(2)}) %collective-permute-start.14) | collective-permute-done | bytes 524320 | tf_op jit(solution)/shard_map/ppermute | solution.py:416
  52.3 1.9 %collective-permute-start.11 = (bf16[256,512]{1,0:T(8,128)(2,1)S(1)}, bf16[256,512]{1,0:T(8,128)(2,1)S(1)}, u32[]{:S(2)}, u32[]{:S(2)}) collective-permute-start(bf16[256,512]{1,0:T(8,128)(2,1)S(1)} %get-tuple-element.35), channel_id=1, source_target_pairs={{0,3},{1,1},{2,2},{3,0},{4,7},{5,5},{6,6},{7,4},{8,11},{9,9},{10,1... | collective-permute-start | bytes 786440 | tf_op jit(solution)/shard_map/ppermute | solution.py:416
  54.2 0.2 collective-permute-done.15.refs_8_.refs_10_
  54.4 2.0 %collective-permute-start.12 = (bf16[256,512]{1,0:T(8,128)(2,1)S(1)}, bf16[256,512]{1,0:T(8,128)(2,1)S(1)}, u32[]{:S(2)}, u32[]{:S(2)}) collective-permute-start(bf16[256,512]{1,0:T(8,128)(2,1)S(1)} %get-tuple-element.36), channel_id=1, source_target_pairs={{0,4},{1,5},{2,6},{3,7},{4,0},{5,1},{6,2},{7,3},{8,12},{9,13},{10,... | collective-permute-start | bytes 786440 | tf_op jit(solution)/shard_map/ppermute | solution.py:416
  56.4 4.7 %collective-permute-start.13 = (bf16[256,512]{1,0:T(8,128)(2,1)S(1)}, bf16[256,512]{1,0:T(8,128)(2,1)S(1)}, u32[]{:S(2)}, u32[]{:S(2)}) collective-permute-start(bf16[256,512]{1,0:T(8,128)(2,1)S(1)} %get-tuple-element.37), channel_id=1, source_target_pairs={{0,0},{1,1},{2,2},{3,3},{4,8},{5,9},{6,10},{7,11},{8,4},{9,5},{10,... | collective-permute-start | bytes 786440 | tf_op jit(solution)/shard_map/ppermute | solution.py:416
  61.0 1.2 %attend_more.1 = (f32[256,512]{1,0:T(8,128)S(1)}, f32[256,512]{1,0:T(8,128)S(1)}, f32[256,512]{1,0:T(8,128)S(1)}) custom-call(s32[10]{0:T(128)S(1)} %get-tuple-element.26.meta, bf16[256,1536]{1,0:T(8,128)(2,1)S(1)} %copy-done, bf16[512,512]{1,0:T(8,128)(2,1)S(1)} %collective-permute-done.8.outer.refs_1_.refs_2_, ...), custom_call_target="tpu_custom_call" | custom-call | flops 134217728 | bytes 786432 | tf_op jit(solution)/shard_map/attend_more/pallas_call | solution.py:141
  62.3 4.8 %attend_last.2.refs_14_ = bf16[256,1536]{1,0:T(8,128)(2,1)} custom-call(s32[10]{0:T(128)S(1)} %get-tuple-element.26.meta, bf16[256,1536]{1,0:T(8,128)(2,1)S(1)} %copy-done, bf16[528,1024]{1,0:T(8,128)(2,1)S(1)} %collective-permute-done.3.outer.refs_1_.refs_2_, bf16[528,1024]{1,0:T(8,128)(2,1)S(1)} %collective-permute-done.3.outer.refs_1_.refs_2_, ...), custom_call_target="tpu_custom_call" | custom-call | flops 671088640 | bytes 3145728 | tf_op jit(solution)/shard_map/attend_last/pallas_call | solution.py:141
  67.2 2.3 %attend_last.3 = bf16[256,1536]{1,0:T(8,128)(2,1)} custom-call(s32[10]{0:T(128)S(1)} %get-tuple-element.26.meta, bf16[256,1536]{1,0:T(8,128)(2,1)S(1)} %copy-done, bf16[256,512]{1,0:T(8,128)(2,1)S(1)} %collective-permute-done.10.refs_1_.refs_2_, bf16[256,512]{1,0:T(8,128)(2,1)S(1)} %collective-permute-done.10.refs_1_.refs_2_, ...), custom_call_target="tpu_custom_call", output_to_operand_aliasing={{}: (15, {})} | custom-call | flops 201326592 | bytes 1048576 | tf_op jit(solution)/shard_map/attend_last/pallas_call | solution.py:141
  (21 shorter events, 0.3 us)
Async XLA Ops:
  0.0 13.0 %copy-start.3 = (s32[1,8]{1,0:T(1,128)S(1)}, s32[1,8]{1,0:T(1,128)}, u32[]{:S(2)}) copy-start(s32[1,8]{1,0:T(1,128)} %list_hbm.1) | copy-start | bytes 100
  0.0 3.7 %collective-permute-start = (s32[1,8]{1,0:T(1,128)}, s32[1,8]{1,0:T(1,128)S(1)}, u32[]{:S(2)}, u32[]{:S(2)}) collective-permute-start(s32[1,8]{1,0:T(1,128)} %list_hbm.1), channel_id=1, source_target_pairs={{0,2},{1,3},{2,0},{3,1},{4,6},{5,7},{6,4},{7,5},{8,10},{9,11},{10,... | collective-permute-start | bytes 104 | tf_op jit(solution)/shard_map/ppermute | solution.py:416
  6.3 19.6 %collective-permute-start.6 = (bf16[256,1536]{1,0:T(8,128)(2,1)S(1)}, bf16[256,1536]{1,0:T(8,128)(2,1)S(1)}, u32[]{:S(2)}, u32[]{:S(2)}) collective-permute-start(bf16[256,1536]{1,0:T(8,128)(2,1)S(1)} %get-tuple-element.30), channel_id=1, source_target_pairs={{0,2},{1,3},{2,0},{3,1},{4,6},{5,7},{6,4},{7,5},{8,10},{9,11},{10,... | collective-permute-start | bytes 2359304 | tf_op jit(solution)/shard_map/ppermute | solution.py:416
  7.9 27.2 %collective-permute-start.3 = (bf16[528,1024]{1,0:T(8,128)(2,1)S(1)}, bf16[528,1024]{1,0:T(8,128)(2,1)S(1)}, u32[]{:S(2)}, u32[]{:S(2)}) collective-permute-start(bf16[528,1024]{1,0:T(8,128)(2,1)S(1)} %get-tuple-element.28), channel_id=1, source_target_pairs={{0,4},{1,5},{2,6},{3,7},{4,0},{5,1},{6,2},{7,3},{8,12},{9,13},{10,... | collective-permute-start | bytes 3244040 | tf_op jit(solution)/shard_map/ppermute | solution.py:416
  8.3 29.4 %collective-permute-start.4 = (bf16[528,1024]{1,0:T(8,128)(2,1)S(1)}, bf16[528,1024]{1,0:T(8,128)(2,1)S(1)}, u32[]{:S(2)}, u32[]{:S(2)}) collective-permute-start(bf16[528,1024]{1,0:T(8,128)(2,1)S(1)} %get-tuple-element.28), channel_id=1, source_target_pairs={{0,0},{1,1},{2,2},{3,3},{4,8},{5,9},{6,10},{7,11},{8,4},{9,5},{10,... | collective-permute-start | bytes 3244040 | tf_op jit(solution)/shard_map/ppermute | solution.py:416
  13.0 1.2 %collective-permute-start.1 = (s32[1,8]{1,0:T(1,128)S(1)}, s32[1,8]{1,0:T(1,128)S(1)}, u32[]{:S(2)}, u32[]{:S(2)}) collective-permute-start(s32[1,8]{1,0:T(1,128)S(1)} %copy-done.3), channel_id=1, source_target_pairs={{0,1},{1,0},{2,3},{3,2},{4,5},{5,4},{6,7},{7,6},{8,9},{9,8},{10,11... | collective-permute-start | bytes 104 | tf_op jit(solution)/shard_map/ppermute | solution.py:416
  13.0 1.3 %collective-permute-start.2 = (s32[1,8]{1,0:T(1,128)S(1)}, s32[1,8]{1,0:T(1,128)S(1)}, u32[]{:S(2)}, u32[]{:S(2)}) collective-permute-start(s32[1,8]{1,0:T(1,128)S(1)} %collective-permute-done.across_ref), channel_id=1, source_target_pairs={{0,1},{1,0},{2,3},{3,2},{4,5},{5,4},{6,7},{7,6},{8,9},{9,8},{10,11... | collective-permute-start | bytes 104 | tf_op jit(solution)/shard_map/ppermute | solution.py:416
  16.7 14.3 %copy-start = (bf16[256,1536]{1,0:T(8,128)(2,1)S(1)}, bf16[256,1536]{1,0:T(8,128)(2,1)}, u32[]{:S(2)}) copy-start(bf16[256,1536]{1,0:T(8,128)(2,1)} %refs_0_.7) | copy-start | bytes 2359300
  16.7 14.3 %copy-start.1 = (bf16[256,1536]{1,0:T(8,128)(2,1)S(1)}, bf16[256,1536]{1,0:T(8,128)(2,1)}, u32[]{:S(2)}) copy-start(bf16[256,1536]{1,0:T(8,128)(2,1)} %k_ref.5) | copy-start | bytes 2359300
  16.7 14.3 %copy-start.2 = (bf16[256,1536]{1,0:T(8,128)(2,1)S(1)}, bf16[256,1536]{1,0:T(8,128)(2,1)}, u32[]{:S(2)}) copy-start(bf16[256,1536]{1,0:T(8,128)(2,1)} %v_ref.5) | copy-start | bytes 2359300
  16.7 9.6 %collective-permute-start.5 = (bf16[256,1536]{1,0:T(8,128)(2,1)S(1)}, bf16[256,1536]{1,0:T(8,128)(2,1)S(1)}, u32[]{:S(2)}, u32[]{:S(2)}) collective-permute-start(bf16[256,1536]{1,0:T(8,128)(2,1)S(1)} %get-tuple-element.29.refs_0_), channel_id=1, source_target_pairs={{0,1},{1,0},{2,3},{3,2},{4,5},{5,4},{6,7},{7,6},{8,9},{9,8},{10,11... | collective-permute-start | bytes 2359304 | tf_op jit(solution)/shard_map/ppermute | solution.py:416
  17.4 17.7 %collective-permute-start.7 = (bf16[256,1536]{1,0:T(8,128)(2,1)S(1)}, bf16[256,1536]{1,0:T(8,128)(2,1)S(1)}, u32[]{:S(2)}, u32[]{:S(2)}) collective-permute-start(bf16[256,1536]{1,0:T(8,128)(2,1)S(1)} %get-tuple-element.32), channel_id=1, source_target_pairs={{0,0},{1,2},{2,1},{3,3},{4,4},{5,6},{6,5},{7,7},{8,8},{9,10},{10,9... | collective-permute-start | bytes 2359304 | tf_op jit(solution)/shard_map/ppermute | solution.py:416
  25.9 20.0 %collective-permute-start.8 = (bf16[512,512]{1,0:T(8,128)(2,1)S(1)}, bf16[512,512]{1,0:T(8,128)(2,1)S(1)}, u32[]{:S(2)}, u32[]{:S(2)}) collective-permute-start(bf16[512,512]{1,0:T(8,128)(2,1)S(1)} %pack.1), channel_id=1, source_target_pairs={{0,4},{1,5},{2,6},{3,7},{4,0},{5,1},{6,2},{7,3},{8,12},{9,13},{10,... | collective-permute-start | bytes 1572872 | tf_op jit(solution)/shard_map/ppermute | solution.py:416
  26.4 23.0 %collective-permute-start.9 = (bf16[512,512]{1,0:T(8,128)(2,1)S(1)}, bf16[512,512]{1,0:T(8,128)(2,1)S(1)}, u32[]{:S(2)}, u32[]{:S(2)}) collective-permute-start(bf16[512,512]{1,0:T(8,128)(2,1)S(1)} %pack.1), channel_id=1, source_target_pairs={{0,0},{1,1},{2,2},{3,3},{4,8},{5,9},{6,10},{7,11},{8,4},{9,5},{10,... | collective-permute-start | bytes 1572872 | tf_op jit(solution)/shard_map/ppermute | solution.py:416
  39.3 13.0 %collective-permute-start.14 = (bf16[256,1024]{1,0:T(8,128)(2,1)S(1)}, bf16[256,1024]{1,0:T(8,128)(2,1)S(1)}, u32[]{:S(2)}, u32[]{:S(2)}) collective-permute-start(bf16[256,1024]{1,0:T(8,128)(2,1)S(1)} %get-tuple-element.43), channel_id=1, source_target_pairs={{0,2},{1,3},{2,0},{3,1},{4,6},{5,7},{6,4},{7,5},{8,10},{9,11},{10,... | collective-permute-start | bytes 1572872 | tf_op jit(solution)/shard_map/ppermute | solution.py:416
  39.9 14.5 %collective-permute-start.15 = (bf16[256,1024]{1,0:T(8,128)(2,1)S(1)}, bf16[256,1024]{1,0:T(8,128)(2,1)S(1)}, u32[]{:S(2)}, u32[]{:S(2)}) collective-permute-start(bf16[256,1024]{1,0:T(8,128)(2,1)S(1)} %get-tuple-element.44), channel_id=1, source_target_pairs={{0,3},{1,1},{2,2},{3,0},{4,7},{5,5},{6,6},{7,4},{8,11},{9,9},{10,1... | collective-permute-start | bytes 1572872 | tf_op jit(solution)/shard_map/ppermute | solution.py:416
  41.8 14.6 %collective-permute-start.16 = (bf16[256,1024]{1,0:T(8,128)(2,1)S(1)}, bf16[256,1024]{1,0:T(8,128)(2,1)S(1)}, u32[]{:S(2)}, u32[]{:S(2)}) collective-permute-start(bf16[256,1024]{1,0:T(8,128)(2,1)S(1)} %get-tuple-element.45), channel_id=1, source_target_pairs={{0,4},{1,5},{2,6},{3,7},{4,0},{5,1},{6,2},{7,3},{8,12},{9,13},{10,... | collective-permute-start | bytes 1572872 | tf_op jit(solution)/shard_map/ppermute | solution.py:416
  45.9 16.4 %collective-permute-start.17 = (bf16[256,1024]{1,0:T(8,128)(2,1)S(1)}, bf16[256,1024]{1,0:T(8,128)(2,1)S(1)}, u32[]{:S(2)}, u32[]{:S(2)}) collective-permute-start(bf16[256,1024]{1,0:T(8,128)(2,1)S(1)} %get-tuple-element.46), channel_id=1, source_target_pairs={{0,0},{1,1},{2,2},{3,3},{4,8},{5,9},{6,10},{7,11},{8,4},{9,5},{10,... | collective-permute-start | bytes 1572872 | tf_op jit(solution)/shard_map/ppermute | solution.py:416
  51.4 15.7 %collective-permute-start.10 = (bf16[256,512]{1,0:T(8,128)(2,1)S(1)}, bf16[256,512]{1,0:T(8,128)(2,1)S(1)}, u32[]{:S(2)}, u32[]{:S(2)}) collective-permute-start(bf16[256,512]{1,0:T(8,128)(2,1)S(1)} %get-tuple-element.34), channel_id=1, source_target_pairs={{0,2},{1,3},{2,0},{3,1},{4,6},{5,7},{6,4},{7,5},{8,10},{9,11},{10,... | collective-permute-start | bytes 786440 | tf_op jit(solution)/shard_map/ppermute | solution.py:416
  52.3 14.8 %collective-permute-start.11 = (bf16[256,512]{1,0:T(8,128)(2,1)S(1)}, bf16[256,512]{1,0:T(8,128)(2,1)S(1)}, u32[]{:S(2)}, u32[]{:S(2)}) collective-permute-start(bf16[256,512]{1,0:T(8,128)(2,1)S(1)} %get-tuple-element.35), channel_id=1, source_target_pairs={{0,3},{1,1},{2,2},{3,0},{4,7},{5,5},{6,6},{7,4},{8,11},{9,9},{10,1... | collective-permute-start | bytes 786440 | tf_op jit(solution)/shard_map/ppermute | solution.py:416
  54.4 12.7 %collective-permute-start.12 = (bf16[256,512]{1,0:T(8,128)(2,1)S(1)}, bf16[256,512]{1,0:T(8,128)(2,1)S(1)}, u32[]{:S(2)}, u32[]{:S(2)}) collective-permute-start(bf16[256,512]{1,0:T(8,128)(2,1)S(1)} %get-tuple-element.36), channel_id=1, source_target_pairs={{0,4},{1,5},{2,6},{3,7},{4,0},{5,1},{6,2},{7,3},{8,12},{9,13},{10,... | collective-permute-start | bytes 786440 | tf_op jit(solution)/shard_map/ppermute | solution.py:416
  56.4 10.8 %collective-permute-start.13 = (bf16[256,512]{1,0:T(8,128)(2,1)S(1)}, bf16[256,512]{1,0:T(8,128)(2,1)S(1)}, u32[]{:S(2)}, u32[]{:S(2)}) collective-permute-start(bf16[256,512]{1,0:T(8,128)(2,1)S(1)} %get-tuple-element.37), channel_id=1, source_target_pairs={{0,0},{1,1},{2,2},{3,3},{4,8},{5,9},{6,10},{7,11},{8,4},{9,5},{10,... | collective-permute-start | bytes 786440 | tf_op jit(solution)/shard_map/ppermute | solution.py:416

commit v16 on v15

--- a/solution.py
+++ b/solution.py
@@ -234,16 +234,22 @@
     rows, all_width = keys.shape
     tile_count = rows // TILE
 
-    def build(me_ref, across_ref, list_hbm, k_ref, v_ref, meta, packed, to_across, list_ref, note, sems):
+    def build(me_ref, across_any, list_hbm, k_ref, v_ref, meta, packed, to_across, list_ref, across_ref, note, sems):
         read = pltpu.make_async_copy(list_hbm, list_ref, sems.at[5])
+        read_across = pltpu.make_async_copy(across_any, across_ref, sems.at[6])
+        read_across.start()
         read.start()
         me = me_ref[0]
         right = me % 4 >= 2
         copies = part_copies(k_ref, v_ref, 0, width, packed, sems, 0)
-        tile = tile_at(across_ref, jnp.where(right, 5, 1), tile_count)
-        copies += tile_copies(((k_ref, 0, 0), (v_ref, 0, 0)), tile, to_across, sems, 2)
         for copy in copies:
             copy.start()
+        read_across.wait()
+        tile = tile_at(across_ref, jnp.where(right, 5, 1), tile_count)
+        tiles = tile_copies(((k_ref, 0, 0), (v_ref, 0, 0)), tile, to_across, sems, 2)
+        for copy in tiles:
+            copy.start()
+        copies += tiles
         read.wait()
         write_note(note, list_ref, tile_count)
         last = pltpu.make_async_copy(
@@ -261,16 +267,16 @@
         "begin",
         build,
         (me, across_list, in_hbm(tile_lists), in_hbm(keys), in_hbm(values)),
-        [SCALAR] * 2 + [WHOLE] * 3,
+        [SCALAR] + [WHOLE] * 4,
         [
             jax.ShapeDtypeStruct((10,), jnp.int32),
             jax.ShapeDtypeStruct((2 * rows + NOTE_ROWS, width), jnp.bfloat16),
             jax.ShapeDtypeStruct((2 * TILE, all_width), jnp.bfloat16),
         ],
         [SCALAR, WHOLE, WHOLE],
-        6,
+        7,
         8 * rows * width + 8 * TILE * all_width,
-        [pltpu.SMEM(tile_lists.shape, jnp.int32), pltpu.VMEM((NOTE_ROWS, HD), jnp.bfloat16)],
+        [pltpu.SMEM(tile_lists.shape, jnp.int32)] * 2 + [pltpu.VMEM((NOTE_ROWS, HD), jnp.bfloat16)],
     )
 
 

time: 69.8 us -> 69.5 us (level)
  no operation moved by 1% of the time
where the time goes in v16:
time: 69.5 us; the launch traced here: 69.2 us
  starting transfers between devices  29.8 us (43%)
  Pallas kernels  21.8 us (31%)
  waiting for transfers between devices  17.3 us (25%)
    ppermute x18, starting transfers between devices, send(): return lax.ppermute(array, 'frame', route)  29.8 us
    ppermute x18, waiting for transfers between devices, send(): return lax.ppermute(array, 'frame', route)  17.3 us
    pallas_call x4, Pallas kernels, attend(): pl.pallas_call(functools.partial(attend_kernel, plan, heads, carry is not...  12.4 us
    pallas_call x5, Pallas kernels, move(): pl.pallas_call(build, name=name, out_shape=out_shape, in_specs=specs, out...  9.43 us
  transfers between devices with their start and end apart: 18, of which 8 were waited for; matrix products, arithmetic and copies ran while one was open for 0% of the time, Pallas kernels for 25%

profile of v16, /device:TPU:12, one launch (start us, length us, event | category | flops | bytes accessed | tf_op | source)
XLA Modules:
  0.0 69.2 jit_solution(4661163779987662266)
XLA Ops:
  0.0 1.5 %collective-permute-start = (s32[1,8]{1,0:T(1,128)}, s32[1,8]{1,0:T(1,128)S(1)}, u32[]{:S(2)}, u32[]{:S(2)}) collective-permute-start(s32[1,8]{1,0:T(1,128)} %list_hbm.1), channel_id=1, source_target_pairs={{0,2},{1,3},{2,0},{3,1},{4,6},{5,7},{6,4},{7,5},{8,10},{9,11},{10,... | collective-permute-start | bytes 104 | tf_op jit(solution)/shard_map/ppermute | solution.py:422
  1.5 2.2 %collective-permute-done.across_any = s32[1,8]{1,0:T(1,128)S(1)} collective-permute-done((s32[1,8]{1,0:T(1,128)}, s32[1,8]{1,0:T(1,128)S(1)}, u32[]{:S(2)}, u32[]{:S(2)}) %collective-permute-start) | collective-permute-done | bytes 64 | tf_op jit(solution)/shard_map/ppermute | solution.py:422
  3.7 2.4 %begin.1 = (s32[10]{0:T(128)S(1)}, bf16[528,1024]{1,0:T(8,128)(2,1)S(1)}, bf16[256,1536]{1,0:T(8,128)(2,1)S(1)}) custom-call(s32[1]{0:T(128)} %bitcast.me_ref, s32[1,8]{1,0:T(1,128)S(1)} %collective-permute-done.across_any, s32[1,8]{1,0:T(1,128)} %list_hbm.1, bf16[256,1536]{1,0:T(8,128)(2,1)} %k_ref.5, bf16[256,1536]{1,0:T(8,128)(2,1)} %v_ref.5), custom_call_target="tpu_custom_call" | custom-call | bytes 3670016 | tf_op jit(solution)/shard_map/begin/pallas_call | solution.py:163
  6.1 1.6 %collective-permute-start.6 = (bf16[256,1536]{1,0:T(8,128)(2,1)S(1)}, bf16[256,1536]{1,0:T(8,128)(2,1)S(1)}, u32[]{:S(2)}, u32[]{:S(2)}) collective-permute-start(bf16[256,1536]{1,0:T(8,128)(2,1)S(1)} %get-tuple-element.30), channel_id=1, source_target_pairs={{0,2},{1,3},{2,0},{3,1},{4,6},{5,7},{6,4},{7,5},{8,10},{9,11},{10,... | collective-permute-start | bytes 2359304 | tf_op jit(solution)/shard_map/ppermute | solution.py:422
  7.6 0.4 collective-permute-start.3
  8.1 4.6 %collective-permute-start.4 = (bf16[528,1024]{1,0:T(8,128)(2,1)S(1)}, bf16[528,1024]{1,0:T(8,128)(2,1)S(1)}, u32[]{:S(2)}, u32[]{:S(2)}) collective-permute-start(bf16[528,1024]{1,0:T(8,128)(2,1)S(1)} %get-tuple-element.28), channel_id=1, source_target_pairs={{0,0},{1,1},{2,2},{3,3},{4,8},{5,9},{6,10},{7,11},{8,4},{9,5},{10,... | collective-permute-start | bytes 3244040 | tf_op jit(solution)/shard_map/ppermute | solution.py:422
  12.8 0.5 collective-permute-start.2
  13.3 0.6 collective-permute-done.1.beside_ref
  13.9 0.2 collective-permute-done.2.corner_ref
  14.1 2.3 %choose_near.1 = (s32[11]{0:T(128)S(1)}, bf16[256,1536]{1,0:T(8,128)(2,1)S(1)}, bf16[256,1536]{1,0:T(8,128)(2,1)S(1)}) custom-call(s32[10]{0:T(128)S(1)} %get-tuple-element.26.meta, s32[1,8]{1,0:T(1,128)S(1)} %collective-permute-done.1.beside_ref, s32[1,8]{1,0:T(1,128)S(1)} %collective-permute-done.2.corner_ref, bf16[256,1536]{1,0:T(8,128)(2,1)} %k_ref.5, ...), custom_call_target="tpu_custom_call" | custom-call | bytes 3145728 | tf_op jit(solution)/shard_map/choose_near/pallas_call | solution.py:163
  16.5 0.6 collective-permute-start.5
  17.1 0.8 %collective-permute-start.7 = (bf16[256,1536]{1,0:T(8,128)(2,1)S(1)}, bf16[256,1536]{1,0:T(8,128)(2,1)S(1)}, u32[]{:S(2)}, u32[]{:S(2)}) collective-permute-start(bf16[256,1536]{1,0:T(8,128)(2,1)S(1)} %get-tuple-element.32), channel_id=1, source_target_pairs={{0,0},{1,2},{2,1},{3,3},{4,4},{5,6},{6,5},{7,7},{8,8},{9,10},{10,9... | collective-permute-start | bytes 2359304 | tf_op jit(solution)/shard_map/ppermute | solution.py:422
  17.9 1.1 %pack.1 = bf16[512,512]{1,0:T(8,128)(2,1)S(1)} custom-call(bf16[256,1536]{1,0:T(8,128)(2,1)} %k_ref.5, bf16[256,1536]{1,0:T(8,128)(2,1)} %v_ref.5, bf16[256,1536]{1,0:T(8,128)(2,1)S(1)} %get-tuple-element.29.refs_0_), custom_call_target="tpu_custom_call" | custom-call | bytes 1048576 | tf_op jit(solution)/shard_map/pack/pallas_call | solution.py:163
  19.0 6.6 %collective-permute-done.6.refs_5_.refs_6_ = bf16[256,1536]{1,0:T(8,128)(2,1)S(1)} collective-permute-done((bf16[256,1536]{1,0:T(8,128)(2,1)S(1)}, bf16[256,1536]{1,0:T(8,128)(2,1)S(1)}, u32[]{:S(2)}, u32[]{:S(2)}) %collective-permute-start.6) | collective-permute-done | bytes 786464 | tf_op jit(solution)/shard_map/ppermute | solution.py:422
  25.6 0.4 collective-permute-start.8
  26.1 4.6 %collective-permute-start.9 = (bf16[512,512]{1,0:T(8,128)(2,1)S(1)}, bf16[512,512]{1,0:T(8,128)(2,1)S(1)}, u32[]{:S(2)}, u32[]{:S(2)}) collective-permute-start(bf16[512,512]{1,0:T(8,128)(2,1)S(1)} %pack.1), channel_id=1, source_target_pairs={{0,0},{1,1},{2,2},{3,3},{4,8},{5,9},{6,10},{7,11},{8,4},{9,5},{10,... | collective-permute-start | bytes 1572872 | tf_op jit(solution)/shard_map/ppermute | solution.py:422
  30.7 4.1 %attend_own.1 = (f32[256,1536]{1,0:T(8,128)S(1)}, f32[256,1536]{1,0:T(8,128)S(1)}, f32[256,1536]{1,0:T(8,128)S(1)}) custom-call(s32[10]{0:T(128)S(1)} %get-tuple-element.26.meta, bf16[256,1536]{1,0:T(8,128)(2,1)S(1)} %copy-done, bf16[256,1536]{1,0:T(8,128)(2,1)S(1)} %copy-done.1, bf16[256,1536]{1,0:T(8,128)(2,1)S(1)} %copy-done.2, ...), custom_call_target="tpu_custom_call" | custom-call | flops 805306368 | bytes 3932160 | tf_op jit(solution)/shard_map/attend_own/pallas_call | solution.py:141
  34.8 2.6 %collective-permute-done.4.inner.refs_3_.refs_4_ = bf16[528,1024]{1,0:T(8,128)(2,1)S(1)} collective-permute-done((bf16[528,1024]{1,0:T(8,128)(2,1)S(1)}, bf16[528,1024]{1,0:T(8,128)(2,1)S(1)}, u32[]{:S(2)}, u32[]{:S(2)}) %collective-permute-start.4) | collective-permute-done | bytes 1081376 | tf_op jit(solution)/shard_map/ppermute | solution.py:422
  37.5 1.6 %choose.1 = (s32[13]{0:T(128)S(1)}, bf16[256,1024]{1,0:T(8,128)(2,1)S(1)}, bf16[256,1024]{1,0:T(8,128)(2,1)S(1)}, bf16[256,1024]{1,0:T(8,128)(2,1)S(1)}, bf16[256,1024]{1,0:T(8,128)(2,1)S(1)}) custom-call(s32[11]{0:T(128)S(1)} %get-tuple-element.27.meta, bf16[528,1024]{1,0:T(8,128)(2,1)S(1)} %collective-permute-done.3.outer.refs_1_.refs_2_, ...), custom_call_target="tpu_custom_call" | custom-call | bytes 4194304 | tf_op jit(solution)/shard_map/choose/pallas_call | solution.py:163
  39.1 0.6 collective-permute-start.14
  39.6 1.9 %collective-permute-start.15 = (bf16[256,1024]{1,0:T(8,128)(2,1)S(1)}, bf16[256,1024]{1,0:T(8,128)(2,1)S(1)}, u32[]{:S(2)}, u32[]{:S(2)}) collective-permute-start(bf16[256,1024]{1,0:T(8,128)(2,1)S(1)} %get-tuple-element.44), channel_id=1, source_target_pairs={{0,3},{1,1},{2,2},{3,0},{4,7},{5,5},{6,6},{7,4},{8,11},{9,9},{10,1... | collective-permute-start | bytes 1572872 | tf_op jit(solution)/shard_map/ppermute | solution.py:422
  41.6 4.0 %collective-permute-done.8.outer.refs_1_.refs_2_ = bf16[512,512]{1,0:T(8,128)(2,1)S(1)} collective-permute-done((bf16[512,512]{1,0:T(8,128)(2,1)S(1)}, bf16[512,512]{1,0:T(8,128)(2,1)S(1)}, u32[]{:S(2)}, u32[]{:S(2)}) %collective-permute-start.8) | collective-permute-done | bytes 524320 | tf_op jit(solution)/shard_map/ppermute | solution.py:422
  45.7 3.5 %collective-permute-start.17 = (bf16[256,1024]{1,0:T(8,128)(2,1)S(1)}, bf16[256,1024]{1,0:T(8,128)(2,1)S(1)}, u32[]{:S(2)}, u32[]{:S(2)}) collective-permute-start(bf16[256,1024]{1,0:T(8,128)(2,1)S(1)} %get-tuple-element.46), channel_id=1, source_target_pairs={{0,0},{1,1},{2,2},{3,3},{4,8},{5,9},{6,10},{7,11},{8,4},{9,5},{10,... | collective-permute-start | bytes 1572872 | tf_op jit(solution)/shard_map/ppermute | solution.py:422
  49.2 2.1 %choose_again.1 = (bf16[256,512]{1,0:T(8,128)(2,1)S(1)}, bf16[256,512]{1,0:T(8,128)(2,1)S(1)}, bf16[256,512]{1,0:T(8,128)(2,1)S(1)}, bf16[256,512]{1,0:T(8,128)(2,1)S(1)}) custom-call(s32[13]{0:T(128)S(1)} %get-tuple-element.33.meta, bf16[512,512]{1,0:T(8,128)(2,1)S(1)} %collective-permute-done.8.outer.refs_1_.refs_2_, ...), custom_call_target="tpu_custom_call" | custom-call | bytes 2097152 | tf_op jit(solution)/shard_map/choose_again/pallas_call | solution.py:163
  51.3 0.7 %collective-permute-done.14.refs_5_.refs_6_ = bf16[256,1024]{1,0:T(8,128)(2,1)S(1)} collective-permute-done((bf16[256,1024]{1,0:T(8,128)(2,1)S(1)}, bf16[256,1024]{1,0:T(8,128)(2,1)S(1)}, u32[]{:S(2)}, u32[]{:S(2)}) %collective-permute-start.14) | collective-permute-done | bytes 524320 | tf_op jit(solution)/shard_map/ppermute | solution.py:422
  52.0 1.9 %collective-permute-start.11 = (bf16[256,512]{1,0:T(8,128)(2,1)S(1)}, bf16[256,512]{1,0:T(8,128)(2,1)S(1)}, u32[]{:S(2)}, u32[]{:S(2)}) collective-permute-start(bf16[256,512]{1,0:T(8,128)(2,1)S(1)} %get-tuple-element.35), channel_id=1, source_target_pairs={{0,3},{1,1},{2,2},{3,0},{4,7},{5,5},{6,6},{7,4},{8,11},{9,9},{10,1... | collective-permute-start | bytes 786440 | tf_op jit(solution)/shard_map/ppermute | solution.py:422
  54.0 0.2 collective-permute-done.15.refs_8_.refs_10_
  54.2 2.0 %collective-permute-start.12 = (bf16[256,512]{1,0:T(8,128)(2,1)S(1)}, bf16[256,512]{1,0:T(8,128)(2,1)S(1)}, u32[]{:S(2)}, u32[]{:S(2)}) collective-permute-start(bf16[256,512]{1,0:T(8,128)(2,1)S(1)} %get-tuple-element.36), channel_id=1, source_target_pairs={{0,4},{1,5},{2,6},{3,7},{4,0},{5,1},{6,2},{7,3},{8,12},{9,13},{10,... | collective-permute-start | bytes 786440 | tf_op jit(solution)/shard_map/ppermute | solution.py:422
  56.2 4.6 %collective-permute-start.13 = (bf16[256,512]{1,0:T(8,128)(2,1)S(1)}, bf16[256,512]{1,0:T(8,128)(2,1)S(1)}, u32[]{:S(2)}, u32[]{:S(2)}) collective-permute-start(bf16[256,512]{1,0:T(8,128)(2,1)S(1)} %get-tuple-element.37), channel_id=1, source_target_pairs={{0,0},{1,1},{2,2},{3,3},{4,8},{5,9},{6,10},{7,11},{8,4},{9,5},{10,... | collective-permute-start | bytes 786440 | tf_op jit(solution)/shard_map/ppermute | solution.py:422
  60.8 1.2 %attend_more.1 = (f32[256,512]{1,0:T(8,128)S(1)}, f32[256,512]{1,0:T(8,128)S(1)}, f32[256,512]{1,0:T(8,128)S(1)}) custom-call(s32[10]{0:T(128)S(1)} %get-tuple-element.26.meta, bf16[256,1536]{1,0:T(8,128)(2,1)S(1)} %copy-done, bf16[512,512]{1,0:T(8,128)(2,1)S(1)} %collective-permute-done.8.outer.refs_1_.refs_2_, ...), custom_call_target="tpu_custom_call" | custom-call | flops 134217728 | bytes 786432 | tf_op jit(solution)/shard_map/attend_more/pallas_call | solution.py:141
  62.0 4.8 %attend_last.2.refs_14_ = bf16[256,1536]{1,0:T(8,128)(2,1)} custom-call(s32[10]{0:T(128)S(1)} %get-tuple-element.26.meta, bf16[256,1536]{1,0:T(8,128)(2,1)S(1)} %copy-done, bf16[528,1024]{1,0:T(8,128)(2,1)S(1)} %collective-permute-done.3.outer.refs_1_.refs_2_, bf16[528,1024]{1,0:T(8,128)(2,1)S(1)} %collective-permute-done.3.outer.refs_1_.refs_2_, ...), custom_call_target="tpu_custom_call" | custom-call | flops 671088640 | bytes 3145728 | tf_op jit(solution)/shard_map/attend_last/pallas_call | solution.py:141
  66.9 2.3 %attend_last.3 = bf16[256,1536]{1,0:T(8,128)(2,1)} custom-call(s32[10]{0:T(128)S(1)} %get-tuple-element.26.meta, bf16[256,1536]{1,0:T(8,128)(2,1)S(1)} %copy-done, bf16[256,512]{1,0:T(8,128)(2,1)S(1)} %collective-permute-done.10.refs_1_.refs_2_, bf16[256,512]{1,0:T(8,128)(2,1)S(1)} %collective-permute-done.10.refs_1_.refs_2_, ...), custom_call_target="tpu_custom_call", output_to_operand_aliasing={{}: (15, {})} | custom-call | flops 201326592 | bytes 1048576 | tf_op jit(solution)/shard_map/attend_last/pallas_call | solution.py:141
  (21 shorter events, 0.3 us)
Async XLA Ops:
  0.0 12.7 %copy-start.3 = (s32[1,8]{1,0:T(1,128)S(1)}, s32[1,8]{1,0:T(1,128)}, u32[]{:S(2)}) copy-start(s32[1,8]{1,0:T(1,128)} %list_hbm.1) | copy-start | bytes 100
  0.0 3.7 %collective-permute-start = (s32[1,8]{1,0:T(1,128)}, s32[1,8]{1,0:T(1,128)S(1)}, u32[]{:S(2)}, u32[]{:S(2)}) collective-permute-start(s32[1,8]{1,0:T(1,128)} %list_hbm.1), channel_id=1, source_target_pairs={{0,2},{1,3},{2,0},{3,1},{4,6},{5,7},{6,4},{7,5},{8,10},{9,11},{10,... | collective-permute-start | bytes 104 | tf_op jit(solution)/shard_map/ppermute | solution.py:422
  6.1 19.6 %collective-permute-start.6 = (bf16[256,1536]{1,0:T(8,128)(2,1)S(1)}, bf16[256,1536]{1,0:T(8,128)(2,1)S(1)}, u32[]{:S(2)}, u32[]{:S(2)}) collective-permute-start(bf16[256,1536]{1,0:T(8,128)(2,1)S(1)} %get-tuple-element.30), channel_id=1, source_target_pairs={{0,2},{1,3},{2,0},{3,1},{4,6},{5,7},{6,4},{7,5},{8,10},{9,11},{10,... | collective-permute-start | bytes 2359304 | tf_op jit(solution)/shard_map/ppermute | solution.py:422
  7.6 27.2 %collective-permute-start.3 = (bf16[528,1024]{1,0:T(8,128)(2,1)S(1)}, bf16[528,1024]{1,0:T(8,128)(2,1)S(1)}, u32[]{:S(2)}, u32[]{:S(2)}) collective-permute-start(bf16[528,1024]{1,0:T(8,128)(2,1)S(1)} %get-tuple-element.28), channel_id=1, source_target_pairs={{0,4},{1,5},{2,6},{3,7},{4,0},{5,1},{6,2},{7,3},{8,12},{9,13},{10,... | collective-permute-start | bytes 3244040 | tf_op jit(solution)/shard_map/ppermute | solution.py:422
  8.1 29.4 %collective-permute-start.4 = (bf16[528,1024]{1,0:T(8,128)(2,1)S(1)}, bf16[528,1024]{1,0:T(8,128)(2,1)S(1)}, u32[]{:S(2)}, u32[]{:S(2)}) collective-permute-start(bf16[528,1024]{1,0:T(8,128)(2,1)S(1)} %get-tuple-element.28), channel_id=1, source_target_pairs={{0,0},{1,1},{2,2},{3,3},{4,8},{5,9},{6,10},{7,11},{8,4},{9,5},{10,... | collective-permute-start | bytes 3244040 | tf_op jit(solution)/shard_map/ppermute | solution.py:422
  12.7 1.2 %collective-permute-start.1 = (s32[1,8]{1,0:T(1,128)S(1)}, s32[1,8]{1,0:T(1,128)S(1)}, u32[]{:S(2)}, u32[]{:S(2)}) collective-permute-start(s32[1,8]{1,0:T(1,128)S(1)} %copy-done.3), channel_id=1, source_target_pairs={{0,1},{1,0},{2,3},{3,2},{4,5},{5,4},{6,7},{7,6},{8,9},{9,8},{10,11... | collective-permute-start | bytes 104 | tf_op jit(solution)/shard_map/ppermute | solution.py:422
  12.8 1.3 %collective-permute-start.2 = (s32[1,8]{1,0:T(1,128)S(1)}, s32[1,8]{1,0:T(1,128)S(1)}, u32[]{:S(2)}, u32[]{:S(2)}) collective-permute-start(s32[1,8]{1,0:T(1,128)S(1)} %collective-permute-done.across_any), channel_id=1, source_target_pairs={{0,1},{1,0},{2,3},{3,2},{4,5},{5,4},{6,7},{7,6},{8,9},{9,8},{10,11... | collective-permute-start | bytes 104 | tf_op jit(solution)/shard_map/ppermute | solution.py:422
  16.4 14.3 %copy-start = (bf16[256,1536]{1,0:T(8,128)(2,1)S(1)}, bf16[256,1536]{1,0:T(8,128)(2,1)}, u32[]{:S(2)}) copy-start(bf16[256,1536]{1,0:T(8,128)(2,1)} %refs_0_.7) | copy-start | bytes 2359300
  16.4 14.3 %copy-start.1 = (bf16[256,1536]{1,0:T(8,128)(2,1)S(1)}, bf16[256,1536]{1,0:T(8,128)(2,1)}, u32[]{:S(2)}) copy-start(bf16[256,1536]{1,0:T(8,128)(2,1)} %k_ref.5) | copy-start | bytes 2359300
  16.4 14.3 %copy-start.2 = (bf16[256,1536]{1,0:T(8,128)(2,1)S(1)}, bf16[256,1536]{1,0:T(8,128)(2,1)}, u32[]{:S(2)}) copy-start(bf16[256,1536]{1,0:T(8,128)(2,1)} %v_ref.5) | copy-start | bytes 2359300
  16.5 9.6 %collective-permute-start.5 = (bf16[256,1536]{1,0:T(8,128)(2,1)S(1)}, bf16[256,1536]{1,0:T(8,128)(2,1)S(1)}, u32[]{:S(2)}, u32[]{:S(2)}) collective-permute-start(bf16[256,1536]{1,0:T(8,128)(2,1)S(1)} %get-tuple-element.29.refs_0_), channel_id=1, source_target_pairs={{0,1},{1,0},{2,3},{3,2},{4,5},{5,4},{6,7},{7,6},{8,9},{9,8},{10,11... | collective-permute-start | bytes 2359304 | tf_op jit(solution)/shard_map/ppermute | solution.py:422
  17.1 17.8 %collective-permute-start.7 = (bf16[256,1536]{1,0:T(8,128)(2,1)S(1)}, bf16[256,1536]{1,0:T(8,128)(2,1)S(1)}, u32[]{:S(2)}, u32[]{:S(2)}) collective-permute-start(bf16[256,1536]{1,0:T(8,128)(2,1)S(1)} %get-tuple-element.32), channel_id=1, source_target_pairs={{0,0},{1,2},{2,1},{3,3},{4,4},{5,6},{6,5},{7,7},{8,8},{9,10},{10,9... | collective-permute-start | bytes 2359304 | tf_op jit(solution)/shard_map/ppermute | solution.py:422
  25.6 20.0 %collective-permute-start.8 = (bf16[512,512]{1,0:T(8,128)(2,1)S(1)}, bf16[512,512]{1,0:T(8,128)(2,1)S(1)}, u32[]{:S(2)}, u32[]{:S(2)}) collective-permute-start(bf16[512,512]{1,0:T(8,128)(2,1)S(1)} %pack.1), channel_id=1, source_target_pairs={{0,4},{1,5},{2,6},{3,7},{4,0},{5,1},{6,2},{7,3},{8,12},{9,13},{10,... | collective-permute-start | bytes 1572872 | tf_op jit(solution)/shard_map/ppermute | solution.py:422
  26.1 23.1 %collective-permute-start.9 = (bf16[512,512]{1,0:T(8,128)(2,1)S(1)}, bf16[512,512]{1,0:T(8,128)(2,1)S(1)}, u32[]{:S(2)}, u32[]{:S(2)}) collective-permute-start(bf16[512,512]{1,0:T(8,128)(2,1)S(1)} %pack.1), channel_id=1, source_target_pairs={{0,0},{1,1},{2,2},{3,3},{4,8},{5,9},{6,10},{7,11},{8,4},{9,5},{10,... | collective-permute-start | bytes 1572872 | tf_op jit(solution)/shard_map/ppermute | solution.py:422
  39.1 13.0 %collective-permute-start.14 = (bf16[256,1024]{1,0:T(8,128)(2,1)S(1)}, bf16[256,1024]{1,0:T(8,128)(2,1)S(1)}, u32[]{:S(2)}, u32[]{:S(2)}) collective-permute-start(bf16[256,1024]{1,0:T(8,128)(2,1)S(1)} %get-tuple-element.43), channel_id=1, source_target_pairs={{0,2},{1,3},{2,0},{3,1},{4,6},{5,7},{6,4},{7,5},{8,10},{9,11},{10,... | collective-permute-start | bytes 1572872 | tf_op jit(solution)/shard_map/ppermute | solution.py:422
  39.6 14.5 %collective-permute-start.15 = (bf16[256,1024]{1,0:T(8,128)(2,1)S(1)}, bf16[256,1024]{1,0:T(8,128)(2,1)S(1)}, u32[]{:S(2)}, u32[]{:S(2)}) collective-permute-start(bf16[256,1024]{1,0:T(8,128)(2,1)S(1)} %get-tuple-element.44), channel_id=1, source_target_pairs={{0,3},{1,1},{2,2},{3,0},{4,7},{5,5},{6,6},{7,4},{8,11},{9,9},{10,1... | collective-permute-start | bytes 1572872 | tf_op jit(solution)/shard_map/ppermute | solution.py:422
  41.6 14.6 %collective-permute-start.16 = (bf16[256,1024]{1,0:T(8,128)(2,1)S(1)}, bf16[256,1024]{1,0:T(8,128)(2,1)S(1)}, u32[]{:S(2)}, u32[]{:S(2)}) collective-permute-start(bf16[256,1024]{1,0:T(8,128)(2,1)S(1)} %get-tuple-element.45), channel_id=1, source_target_pairs={{0,4},{1,5},{2,6},{3,7},{4,0},{5,1},{6,2},{7,3},{8,12},{9,13},{10,... | collective-permute-start | bytes 1572872 | tf_op jit(solution)/shard_map/ppermute | solution.py:422
  45.7 16.4 %collective-permute-start.17 = (bf16[256,1024]{1,0:T(8,128)(2,1)S(1)}, bf16[256,1024]{1,0:T(8,128)(2,1)S(1)}, u32[]{:S(2)}, u32[]{:S(2)}) collective-permute-start(bf16[256,1024]{1,0:T(8,128)(2,1)S(1)} %get-tuple-element.46), channel_id=1, source_target_pairs={{0,0},{1,1},{2,2},{3,3},{4,8},{5,9},{6,10},{7,11},{8,4},{9,5},{10,... | collective-permute-start | bytes 1572872 | tf_op jit(solution)/shard_map/ppermute | solution.py:422
  51.2 15.7 %collective-permute-start.10 = (bf16[256,512]{1,0:T(8,128)(2,1)S(1)}, bf16[256,512]{1,0:T(8,128)(2,1)S(1)}, u32[]{:S(2)}, u32[]{:S(2)}) collective-permute-start(bf16[256,512]{1,0:T(8,128)(2,1)S(1)} %get-tuple-element.34), channel_id=1, source_target_pairs={{0,2},{1,3},{2,0},{3,1},{4,6},{5,7},{6,4},{7,5},{8,10},{9,11},{10,... | collective-permute-start | bytes 786440 | tf_op jit(solution)/shard_map/ppermute | solution.py:422
  52.0 14.8 %collective-permute-start.11 = (bf16[256,512]{1,0:T(8,128)(2,1)S(1)}, bf16[256,512]{1,0:T(8,128)(2,1)S(1)}, u32[]{:S(2)}, u32[]{:S(2)}) collective-permute-start(bf16[256,512]{1,0:T(8,128)(2,1)S(1)} %get-tuple-element.35), channel_id=1, source_target_pairs={{0,3},{1,1},{2,2},{3,0},{4,7},{5,5},{6,6},{7,4},{8,11},{9,9},{10,1... | collective-permute-start | bytes 786440 | tf_op jit(solution)/shard_map/ppermute | solution.py:422
  54.2 12.7 %collective-permute-start.12 = (bf16[256,512]{1,0:T(8,128)(2,1)S(1)}, bf16[256,512]{1,0:T(8,128)(2,1)S(1)}, u32[]{:S(2)}, u32[]{:S(2)}) collective-permute-start(bf16[256,512]{1,0:T(8,128)(2,1)S(1)} %get-tuple-element.36), channel_id=1, source_target_pairs={{0,4},{1,5},{2,6},{3,7},{4,0},{5,1},{6,2},{7,3},{8,12},{9,13},{10,... | collective-permute-start | bytes 786440 | tf_op jit(solution)/shard_map/ppermute | solution.py:422
  56.2 10.7 %collective-permute-start.13 = (bf16[256,512]{1,0:T(8,128)(2,1)S(1)}, bf16[256,512]{1,0:T(8,128)(2,1)S(1)}, u32[]{:S(2)}, u32[]{:S(2)}) collective-permute-start(bf16[256,512]{1,0:T(8,128)(2,1)S(1)} %get-tuple-element.37), channel_id=1, source_target_pairs={{0,0},{1,1},{2,2},{3,3},{4,8},{5,9},{6,10},{7,11},{8,4},{9,5},{10,... | collective-permute-start | bytes 786440 | tf_op jit(solution)/shard_map/ppermute | solution.py:422
